TPU v7x, 32 devices: a whole 2x2x4 slice. The times are simulated.
32 devices in a mesh: dp: 4 (over z), seq: 8 (over y, x, core).
Axes of the slice: x: 2, y: 2, z: 4, core: 2. Of those that a mesh axis runs over, the one named last changes fastest.
Arguments:
- hidden: bfloat16 [4096, 5120], P(('dp', 'seq')), may hold values from -6 to 6
- queries: bfloat16 [4096, 4096], P(('dp', 'seq')), may hold values from -330 to 330
- key_states: bfloat16 [4096, 4096], P(('dp', 'seq')), may hold values from -18 to 18
- value_states: bfloat16 [4096, 4096], P(('dp', 'seq')), may hold values from -6 to 6
- attention_out: bfloat16 [4096, 4096], P(('dp', 'seq')), may hold values from -6 to 6
- grad_out: bfloat16 [4096, 4096], P(('dp', 'seq')), may hold values from -6 to 6
- lengths: int32 [4, 4], P('dp'), may hold values from 1 to 512, 1024 in all within a row
- down_query: bfloat16 [8, 5120], replicated, may hold values from -0.0012207031 to 0.0012207031
- up_query: bfloat16 [8, 4096], replicated, may hold values from -0.0014648438 to 0.0014648438
- down_value: bfloat16 [8, 5120], replicated, may hold values from -0.0012207031 to 0.0012207031
- up_value: bfloat16 [8, 4096], replicated, may hold values from -0.0014648438 to 0.0014648438
Outputs:
- grad_queries: bfloat16 [4096, 4096], P(('dp', 'seq'))
- grad_keys: bfloat16 [4096, 4096], P(('dp', 'seq'))
- value_gradients: bfloat16 [4096, 4096], P(('dp', 'seq'))
- query_down_gradient: float32 [8, 5120], P(None, 'dp')
- query_up_gradient: float32 [8, 4096], P(None, 'dp')
- value_down_gradient: float32 [8, 5120], P(None, 'dp')
- value_up_gradient: float32 [8, 4096], P(None, 'dp')
Inputs may be any that keep to these rules, and one draw needn't show every extreme that they name: Each row lists the lengths of the 4 sequences of one pack in packing order; a row sums to 1024.
All inputs are finite; a program needn't handle non-finite values.
Results may differ from a plain program's by a relative error of at most 0.0067.
Values may be sent and summed in bfloat16 or wider, within the bound.
No kernel may reach another device: no remote copies, remote signals or barrier semaphores. Data moves between devices by JAX's collectives and lax.ppermute only.
A program may use at most 64 MiB of HBM per device.

v0:
```python
import math

import jax
import jax.numpy as jnp
from jax import lax
from jax.sharding import PartitionSpec as P

H = 32
HD = 128
ADAPTER_RANK = 8
ADAPTER_ALPHA = 16


def pack_begin(lengths_row, total):
    seq_ends = jnp.cumsum(lengths_row)
    starts = seq_ends - lengths_row
    positions = jnp.arange(total, dtype=jnp.int32)
    inside = (positions[:, None] >= starts[None, :]) & (positions[:, None] < seq_ends[None, :])
    return jnp.sum(jnp.where(inside, starts[None, :], 0), axis=1)


def rotate_back(grads, seq_positions):
    rows = grads.shape[0]
    half = HD // 2
    inverse = jnp.exp(-(jnp.arange(half, dtype=jnp.float32) * (2.0 / HD)) * math.log(10000.0))
    angles = seq_positions.astype(jnp.float32)[:, None] * inverse[None, :]
    cosine = jnp.cos(angles)[:, None, :]
    sine = jnp.sin(angles)[:, None, :]
    split = grads.astype(jnp.float32).reshape(rows, H, HD)
    first = split[:, :, :half]
    second = split[:, :, half:]
    new_first = first * cosine + second * sine
    new_second = second * cosine - first * sine
    joined = jnp.concatenate([new_first, new_second], axis=2)
    return joined.reshape(rows, H * HD).astype(jnp.bfloat16)


def head_backward(head_query, head_key, head_value, head_grad, delta_column, begin, block_rows):
    total = head_query.shape[0]
    width = head_query.shape[1]
    block_count = total // block_rows
    scaling = 1.0 / math.sqrt(width)
    offsets = jnp.arange(block_rows, dtype=jnp.int32)

    def block_of(array, index):
        return lax.dynamic_slice_in_dim(array, index * block_rows, block_rows, 0)

    def outer(query_block, running):
        grad_query_all, grad_key_all, grad_value_all = running
        query_rows = block_of(head_query, query_block)
        grad_rows = block_of(head_grad, query_block)
        delta_rows = block_of(delta_column, query_block)[:, None]
        row_begin = block_of(begin, query_block)
        row_positions = query_block * block_rows + offsets
        first_block = row_begin[0] // block_rows

        def allowed_at(key_block):
            key_positions = key_block * block_rows + offsets
            return (key_positions[None, :] >= row_begin[:, None]) & (
                key_positions[None, :] <= row_positions[:, None]
            )

        def scores_at(key_block):
            key_rows = block_of(head_key, key_block)
            return jnp.dot(query_rows, key_rows.T, preferred_element_type=jnp.float32) * scaling

        def statistics(key_block, running_stats):
            row_top, row_total = running_stats
            allowed = allowed_at(key_block)
            masked = jnp.where(allowed, scores_at(key_block), -1e30)
            new_top = jnp.maximum(row_top, jnp.max(masked, axis=1, keepdims=True))
            weights = jnp.where(allowed, jnp.exp(masked - new_top), 0.0)
            row_total = row_total * jnp.exp(row_top - new_top) + jnp.sum(
                weights, axis=1, keepdims=True
            )
            return (new_top, row_total)

        start_stats = (
            jnp.full((block_rows, 1), -1e30, jnp.float32),
            jnp.zeros((block_rows, 1), jnp.float32),
        )
        row_top, row_total = lax.fori_loop(first_block, query_block + 1, statistics, start_stats)

        def gradients(key_block, running_grads):
            grad_query_rows, grad_key_acc, grad_value_acc = running_grads
            key_rows = block_of(head_key, key_block)
            value_rows = block_of(head_value, key_block)
            allowed = allowed_at(key_block)
            prob_rows = jnp.where(allowed, jnp.exp(scores_at(key_block) - row_top) / row_total, 0.0)
            prob_low = prob_rows.astype(jnp.bfloat16)
            grad_prob = jnp.dot(grad_rows, value_rows.T, preferred_element_type=jnp.float32)
            grad_score = (prob_rows * (grad_prob - delta_rows)).astype(jnp.bfloat16)
            grad_query_rows = grad_query_rows + jnp.dot(
                grad_score, key_rows, preferred_element_type=jnp.float32
            )
            key_piece = jnp.dot(grad_score.T, query_rows, preferred_element_type=jnp.float32)
            value_piece = jnp.dot(prob_low.T, grad_rows, preferred_element_type=jnp.float32)
            grad_key_acc = lax.dynamic_update_slice_in_dim(
                grad_key_acc,
                block_of(grad_key_acc, key_block) + key_piece,
                key_block * block_rows,
                0,
            )
            grad_value_acc = lax.dynamic_update_slice_in_dim(
                grad_value_acc,
                block_of(grad_value_acc, key_block) + value_piece,
                key_block * block_rows,
                0,
            )
            return (grad_query_rows, grad_key_acc, grad_value_acc)

        start_grads = (jnp.zeros((block_rows, width), jnp.float32), grad_key_all, grad_value_all)
        grad_query_rows, grad_key_all, grad_value_all = lax.fori_loop(
            first_block, query_block + 1, gradients, start_grads
        )
        grad_query_all = lax.dynamic_update_slice_in_dim(
            grad_query_all, grad_query_rows * scaling, query_block * block_rows, 0
        )
        return (grad_query_all, grad_key_all, grad_value_all)

    empty_rows = jnp.zeros((total, width), jnp.float32)
    grad_query_all, grad_key_all, grad_value_all = lax.fori_loop(
        0, block_count, outer, (empty_rows, empty_rows, empty_rows)
    )
    return (
        grad_query_all.astype(jnp.bfloat16),
        (grad_key_all * scaling).astype(jnp.bfloat16),
        grad_value_all.astype(jnp.bfloat16),
    )


def shards(
    hidden,
    queries,
    key_states,
    value_states,
    attention_out,
    grad_out,
    lengths,
    down_query,
    up_query,
    down_value,
    up_value,
):
    tok_rows = queries.shape[0]
    members = lax.axis_size("seq")
    total = tok_rows * members
    heads_here = H // members
    block_rows = min(512, total)
    begin = pack_begin(lengths[0], total)
    head_query, head_key, head_value, head_out, head_grad = (
        lax.all_to_all(queries, "seq", split_axis=1, concat_axis=0, tiled=True),
        lax.all_to_all(key_states, "seq", split_axis=1, concat_axis=0, tiled=True),
        lax.all_to_all(value_states, "seq", split_axis=1, concat_axis=0, tiled=True),
        lax.all_to_all(attention_out, "seq", split_axis=1, concat_axis=0, tiled=True),
        lax.all_to_all(grad_out, "seq", split_axis=1, concat_axis=0, tiled=True),
    )
    products = head_out.astype(jnp.float32) * head_grad.astype(jnp.float32)
    row_delta = jnp.sum(products.reshape(total, heads_here, HD), axis=2)
    query_parts = []
    key_parts = []
    value_parts = []
    for head_index in range(heads_here):
        low_col = head_index * HD
        grad_query, grad_key, grad_value = head_backward(
            head_query[:, low_col : low_col + HD],
            head_key[:, low_col : low_col + HD],
            head_value[:, low_col : low_col + HD],
            head_grad[:, low_col : low_col + HD],
            row_delta[:, head_index],
            begin,
            block_rows,
        )
        query_parts.append(grad_query)
        key_parts.append(grad_key)
        value_parts.append(grad_value)
    grad_queries, grad_keys, value_gradients = (
        lax.all_to_all(
            jnp.concatenate(query_parts, axis=1), "seq", split_axis=0, concat_axis=1, tiled=True
        ),
        lax.all_to_all(
            jnp.concatenate(key_parts, axis=1), "seq", split_axis=0, concat_axis=1, tiled=True
        ),
        lax.all_to_all(
            jnp.concatenate(value_parts, axis=1), "seq", split_axis=0, concat_axis=1, tiled=True
        ),
    )
    first_row = lax.axis_index("seq") * tok_rows
    local_begin = lax.dynamic_slice_in_dim(begin, first_row, tok_rows, 0)
    seq_positions = first_row + jnp.arange(tok_rows, dtype=jnp.int32) - local_begin
    query_gradient_before = rotate_back(grad_queries, seq_positions)
    query_lowrank = jnp.dot(hidden, down_query.T, preferred_element_type=jnp.float32).astype(
        jnp.bfloat16
    )
    value_lowrank = jnp.dot(hidden, down_value.T, preferred_element_type=jnp.float32).astype(
        jnp.bfloat16
    )
    query_backprop = jnp.dot(
        query_gradient_before, up_query.T, preferred_element_type=jnp.float32
    ).astype(jnp.bfloat16)
    value_backprop = jnp.dot(
        value_gradients, up_value.T, preferred_element_type=jnp.float32
    ).astype(jnp.bfloat16)
    terms = (
        jnp.dot(query_backprop.T, hidden, preferred_element_type=jnp.float32),
        jnp.dot(query_lowrank.T, query_gradient_before, preferred_element_type=jnp.float32),
        jnp.dot(value_backprop.T, hidden, preferred_element_type=jnp.float32),
        jnp.dot(value_lowrank.T, value_gradients, preferred_element_type=jnp.float32),
    )
    summed = lax.psum((terms[0], terms[1], terms[2], terms[3]), "seq")
    group_portions = (
        lax.psum_scatter(summed[0], "dp", scatter_dimension=1, tiled=True),
        lax.psum_scatter(summed[1], "dp", scatter_dimension=1, tiled=True),
        lax.psum_scatter(summed[2], "dp", scatter_dimension=1, tiled=True),
        lax.psum_scatter(summed[3], "dp", scatter_dimension=1, tiled=True),
    )
    adapter_scale = ADAPTER_ALPHA / ADAPTER_RANK
    return (
        grad_queries,
        grad_keys,
        value_gradients,
        group_portions[0] * adapter_scale,
        group_portions[1] * adapter_scale,
        group_portions[2] * adapter_scale,
        group_portions[3] * adapter_scale,
    )


def solution(mesh):
    placed = (
        P(("dp", "seq"), None),
        P(("dp", "seq"), None),
        P(("dp", "seq"), None),
        P(("dp", "seq"), None),
        P(("dp", "seq"), None),
        P(("dp", "seq"), None),
        P("dp", None),
        P(),
        P(),
        P(),
        P(),
    )
    return jax.shard_map(
        shards,
        mesh=mesh,
        in_specs=placed,
        out_specs=(
            P(("dp", "seq"), None),
            P(("dp", "seq"), None),
            P(("dp", "seq"), None),
            P(None, "dp"),
            P(None, "dp"),
            P(None, "dp"),
            P(None, "dp"),
        ),
        check_vma=False,
    )
```

profile of v0, /device:TPU:0, one launch (start us, length us, event | category | flops | bytes accessed | tf_op | source)
XLA Modules:
  0.0 376.4 jit_solution(5690483224862346361)
XLA Ops:
  7.2 2.4 copy.73
  9.6 5.2 %all-to-all-start.2 = ((bf16[128,8,512]{2,0,1:T(8,128)(2,1)}), bf16[128,8,512]{2,0,1:T(8,128)(2,1)S(1)}, u32[]{:S(2)}, u32[]{:S(2)}) async-start(bf16[128,8,512]{2,0,1:T(8,128)(2,1)} %bitcast.349), calls=%async_computation.2 | async-start | bytes 2097152 | tf_op jit(solution)/shard_map/all_to_all | solution.py:156
  14.7 2.3 copy.72
  17.0 13.1 %all-to-all-done.2 = bf16[128,8,512]{2,0,1:T(8,128)(2,1)S(1)} async-done(((bf16[128,8,512]{2,0,1:T(8,128)(2,1)}), bf16[128,8,512]{2,0,1:T(8,128)(2,1)S(1)}, u32[]{:S(2)}, u32[]{:S(2)}) %all-to-all-start.2) | async-done | bytes 1048608 | tf_op jit(solution)/shard_map/all_to_all | solution.py:156
  30.2 4.2 %all-to-all-start.3 = ((bf16[128,8,512]{2,0,1:T(8,128)(2,1)}), bf16[128,8,512]{2,0,1:T(8,128)(2,1)}, u32[]{:S(2)}, u32[]{:S(2)}) async-start(bf16[128,8,512]{2,0,1:T(8,128)(2,1)} %bitcast.347), calls=%async_computation.3 | async-start | bytes 2097152 | tf_op jit(solution)/shard_map/all_to_all | solution.py:155
  34.4 2.3 copy.75
  36.7 13.1 %all-to-all-done.3 = bf16[128,8,512]{2,0,1:T(8,128)(2,1)} async-done(((bf16[128,8,512]{2,0,1:T(8,128)(2,1)}), bf16[128,8,512]{2,0,1:T(8,128)(2,1)}, u32[]{:S(2)}, u32[]{:S(2)}) %all-to-all-start.3) | async-done | bytes 1048608 | tf_op jit(solution)/shard_map/all_to_all | solution.py:155
  49.8 4.2 %all-to-all-start = ((bf16[128,8,512]{2,0,1:T(8,128)(2,1)}), bf16[128,8,512]{2,0,1:T(8,128)(2,1)}, u32[]{:S(2)}, u32[]{:S(2)}) async-start(bf16[128,8,512]{2,0,1:T(8,128)(2,1)} %bitcast.348), calls=%async_computation | async-start | bytes 2097152 | tf_op jit(solution)/shard_map/all_to_all | solution.py:152
  54.1 2.3 copy.74
  56.4 13.1 %all-to-all-done = bf16[128,8,512]{2,0,1:T(8,128)(2,1)} async-done(((bf16[128,8,512]{2,0,1:T(8,128)(2,1)}), bf16[128,8,512]{2,0,1:T(8,128)(2,1)}, u32[]{:S(2)}, u32[]{:S(2)}) %all-to-all-start) | async-done | bytes 1048608 | tf_op jit(solution)/shard_map/all_to_all | solution.py:152
  69.5 4.2 %all-to-all-start.1 = ((bf16[128,8,512]{2,0,1:T(8,128)(2,1)}), bf16[128,8,512]{2,0,1:T(8,128)(2,1)}, u32[]{:S(2)}, u32[]{:S(2)}) async-start(bf16[128,8,512]{2,0,1:T(8,128)(2,1)} %bitcast.346), calls=%async_computation.1 | async-start | bytes 2097152 | tf_op jit(solution)/shard_map/all_to_all | solution.py:153
  76.1 2.3 copy.71
  78.5 2.9 bitcast_multiply_fusion
  81.4 2.9 mul.323
  84.2 2.8 reduce_sum.55
  87.0 2.1 all-to-all-done.1
  89.2 4.4 %all-to-all-start.4 = ((bf16[128,8,512]{2,0,1:T(8,128)(2,1)}), bf16[128,8,512]{2,0,1:T(8,128)(2,1)}, u32[]{:S(2)}, u32[]{:S(2)}) async-start(bf16[128,8,512]{2,0,1:T(8,128)(2,1)} %bitcast.345), calls=%async_computation.4 | async-start | bytes 2097152 | tf_op jit(solution)/shard_map/all_to_all | solution.py:154
  93.6 1.5 slice_reduce_fusion.3
  96.2 2.2 fusion.105
  98.4 2.1 fusion.104
  100.5 8.3 %all-to-all-done.4 = bf16[128,8,512]{2,0,1:T(8,128)(2,1)} async-done(((bf16[128,8,512]{2,0,1:T(8,128)(2,1)}), bf16[128,8,512]{2,0,1:T(8,128)(2,1)}, u32[]{:S(2)}, u32[]{:S(2)}) %all-to-all-start.4) | async-done | bytes 1048608 | tf_op jit(solution)/shard_map/all_to_all | solution.py:154
  108.8 2.1 fusion.102
  111.0 15.8 %while.418 = (s32[]{:T(128)}, bf16[1024,128]{1,0:T(8,128)(2,1)}, f32[1024,128]{1,0:T(8,128)S(1)}, f32[1024,128]{1,0:T(8,128)S(1)}, s32[1024]{0:T(1024)S(1)}, /*i...) while((s32[]{:T(128)}, bf16[1024,128]{1,0:T(8,128)(2,1)}, ...), condition=%wide.region_10.11_spmd.clone.clone, body=%wide.region_3.10_spmd.clone.clone.sunk | while | flops 408947232 | bytes 10955911 | solution.py:122
  116.4 1.8 while.429
  124.3 1.8 while.429
  127.8 19.7 %while.421 = (s32[]{:T(128)}, bf16[1024,128]{1,0:T(8,128)(2,1)}, f32[1024,128]{1,0:T(8,128)S(1)}, f32[1024,128]{1,0:T(8,128)S(1)}, s32[1024]{0:T(1024)S(1)}, /*i...) while((s32[]{:T(128)}, bf16[1024,128]{1,0:T(8,128)(2,1)}, ...), condition=%wide.region_18.19_spmd.clone.clone, body=%wide.region_11.18_spmd.clone.clone.sunk | while | flops 408947232 | bytes 13053119 | solution.py:122
  132.0 1.7 while.430
  132.1 1.3 fusion.244
  133.9 3.1 while.431
  133.9 1.4 fusion.255
  141.9 1.7 while.430
  141.9 1.3 fusion.244
  143.7 3.1 while.431
  143.8 1.4 fusion.255
  148.4 19.7 %while.424 = (s32[]{:T(128)}, bf16[1024,128]{1,0:T(8,128)(2,1)}, f32[1024,128]{1,0:T(8,128)S(1)}, f32[1024,128]{1,0:T(8,128)S(1)}, s32[1024]{0:T(1024)S(1)}, /*i...) while((s32[]{:T(128)}, bf16[1024,128]{1,0:T(8,128)(2,1)}, ...), condition=%wide.region_26.27_spmd.clone.clone, body=%wide.region_19.26_spmd.clone.clone.sunk | while | flops 408947232 | bytes 13053119 | solution.py:122
  152.7 1.7 while.432
  154.5 3.1 while.433
  154.5 1.4 fusion.239
  162.5 1.7 while.432
  164.3 3.1 while.433
  164.4 1.4 fusion.239
  169.1 16.7 %while.427 = (s32[]{:T(128)}, bf16[1024,128]{1,0:T(8,128)(2,1)}, f32[1024,128]{1,0:T(8,128)}, f32[1024,128]{1,0:T(8,128)S(1)}, s32[1024]{0:T(1024)S(1)}, /*index...) while((s32[]{:T(128)}, bf16[1024,128]{1,0:T(8,128)(2,1)}, ...), condition=%wide.region_34.35_spmd.clone.clone, body=%wide.region_27.34_spmd.clone.clone.sunk | while | flops 408947232 | bytes 16198883 | solution.py:122
  174.3 2.5 while.435
  182.6 2.5 while.435
  185.8 2.4 pad_maximum_fusion
  188.1 4.2 %all-to-all-start.5 = ((bf16[8,128,512]{2,1,0:T(8,128)(2,1)}), bf16[8,128,512]{2,1,0:T(8,128)(2,1)}, u32[]{:S(2)}, u32[]{:S(2)}) async-start(bf16[8,128,512]{2,1,0:T(8,128)(2,1)} %bitcast.344), calls=%async_computation.5 | async-start | bytes 2097152 | tf_op jit(solution)/shard_map/all_to_all | solution.py:178
  194.2 13.6 %all-to-all-done.5 = bf16[8,128,512]{2,1,0:T(8,128)(2,1)} async-done(((bf16[8,128,512]{2,1,0:T(8,128)(2,1)}), bf16[8,128,512]{2,1,0:T(8,128)(2,1)}, u32[]{:S(2)}, u32[]{:S(2)}) %all-to-all-start.5) | async-done | bytes 1048608 | tf_op jit(solution)/shard_map/all_to_all | solution.py:178
  207.8 4.2 %all-to-all-start.7 = ((bf16[8,128,512]{2,1,0:T(8,128)(2,1)}), bf16[8,128,512]{2,1,0:T(8,128)(2,1)}, u32[]{:S(2)}, u32[]{:S(2)}) async-start(bf16[8,128,512]{2,1,0:T(8,128)(2,1)} %bitcast.59), calls=%async_computation.7 | async-start | bytes 2097152 | tf_op jit(solution)/shard_map/all_to_all | solution.py:184
  213.6 1.6 copy.55
  216.3 2.0 fusion.92
  218.3 9.2 %all-to-all-done.7 = bf16[8,128,512]{2,1,0:T(8,128)(2,1)} async-done(((bf16[8,128,512]{2,1,0:T(8,128)(2,1)}), bf16[8,128,512]{2,1,0:T(8,128)(2,1)}, u32[]{:S(2)}, u32[]{:S(2)}) %all-to-all-start.7) | async-done | bytes 1048608 | tf_op jit(solution)/shard_map/all_to_all | solution.py:184
  227.5 4.4 %all-to-all-start.6 = ((bf16[8,128,512]{2,1,0:T(8,128)(2,1)}), bf16[8,128,512]{2,1,0:T(8,128)(2,1)}, u32[]{:S(2)}, u32[]{:S(2)}) async-start(bf16[8,128,512]{2,1,0:T(8,128)(2,1)} %bitcast.343), calls=%async_computation.6 | async-start | bytes 2097152 | tf_op jit(solution)/shard_map/all_to_all | solution.py:181
  231.9 1.6 copy.57
  233.6 2.0 fusion.93
  235.7 2.4 fusion.94
  239.4 13.0 %reduce-scatter.7.cloned.1.call-done = f32[8,1024]{1,0:T(8,128)} async-done(((f32[8,4096]{1,0:T(8,128)}), f32[8,1024]{1,0:T(8,128)}) %reduce-scatter.7.cloned.1.call-update) | async-done | bytes 32784 | tf_op jit(solution)/shard_map/reduce_scatter | solution.py:213
  252.4 19.7 %reduce-scatter.11.cloned.1.call-done = f32[8,1024]{1,0:T(8,128)} async-done(((f32[8,4096]{1,0:T(8,128)}), f32[8,1024]{1,0:T(8,128)}) %reduce-scatter.11.cloned.1.call-update) | async-done | bytes 32784 | tf_op jit(solution)/shard_map/reduce_scatter | solution.py:215
  272.1 20.3 %reduce-scatter.5.cloned.1.call-done = f32[8,1280]{1,0:T(8,128)} async-done(((f32[8,5120]{1,0:T(8,128)}), f32[8,1280]{1,0:T(8,128)}) %reduce-scatter.5.cloned.1.call-update) | async-done | bytes 40976 | tf_op jit(solution)/shard_map/reduce_scatter | solution.py:212
  292.4 20.2 %reduce-scatter.9.cloned.1.call-done = f32[8,1280]{1,0:T(8,128)} async-done(((f32[8,5120]{1,0:T(8,128)}), f32[8,1280]{1,0:T(8,128)}) %reduce-scatter.9.cloned.1.call-update) | async-done | bytes 40976 | tf_op jit(solution)/shard_map/reduce_scatter | solution.py:214
  312.6 1.3 copy.60
  313.9 1.6 copy.56
  318.2 48.9 %all-reduce.3.cloned.1.call-done = (f32[8,1280]{1,0:T(8,128)}, f32[8,1024]{1,0:T(8,128)}, f32[8,1280]{1,0:T(8,128)}, f32[8,1024]{1,0:T(8,128)}) async-done(((f32[8,1280]{1,0:T(8,128)}, f32[8,1024]{1,0:T(8,128)}, f32[8,1280]{1,0:T(8,128)}, f32[8,1024]{1,0:T(8,128)}), (f32[8,1280]{1,0:T(8,128)}, f32[8,1024]{1,0:T(8,128)}, f32[8,1280]{1,0:T(8,128)}, f32[8,1024]{1,0:T(8,128)})) %all-reduce.3.cloned.1.call-update) | async-done | bytes 147472 | tf_op jit(solution)/shard_map/psum | solution.py:210
  367.1 1.4 broadcast_multiply_fusion.2
  368.5 1.4 broadcast_multiply_fusion
  (290 shorter events, 58.7 us)
Async XLA Ops:
  7.2 208.7 %copy-start = (bf16[128,5120]{1,0:T(8,128)(2,1)S(1)}, bf16[128,5120]{1,0:T(8,128)(2,1)}, u32[]{:S(2)}) copy-start(bf16[128,5120]{1,0:T(8,128)(2,1)} %param.35) | copy-start | bytes 3932164
  9.6 20.6 %all-to-all-start.2 = ((bf16[128,8,512]{2,0,1:T(8,128)(2,1)}), bf16[128,8,512]{2,0,1:T(8,128)(2,1)S(1)}, u32[]{:S(2)}, u32[]{:S(2)}) async-start(bf16[128,8,512]{2,0,1:T(8,128)(2,1)} %bitcast.349), calls=%async_computation.2 | async-start | bytes 2097152 | tf_op jit(solution)/shard_map/all_to_all | solution.py:156
  30.2 19.7 %all-to-all-start.3 = ((bf16[128,8,512]{2,0,1:T(8,128)(2,1)}), bf16[128,8,512]{2,0,1:T(8,128)(2,1)}, u32[]{:S(2)}, u32[]{:S(2)}) async-start(bf16[128,8,512]{2,0,1:T(8,128)(2,1)} %bitcast.347), calls=%async_computation.3 | async-start | bytes 2097152 | tf_op jit(solution)/shard_map/all_to_all | solution.py:155
  49.8 19.7 %all-to-all-start = ((bf16[128,8,512]{2,0,1:T(8,128)(2,1)}), bf16[128,8,512]{2,0,1:T(8,128)(2,1)}, u32[]{:S(2)}, u32[]{:S(2)}) async-start(bf16[128,8,512]{2,0,1:T(8,128)(2,1)} %bitcast.348), calls=%async_computation | async-start | bytes 2097152 | tf_op jit(solution)/shard_map/all_to_all | solution.py:152
  56.4 19.6 %copy-start.28 = (s32[1,4]{1,0:T(1,128)S(1)}, s32[1,4]{1,0:T(1,128)}, u32[]{:S(2)}) copy-start(s32[1,4]{1,0:T(1,128)} %param.41) | copy-start | bytes 52
  69.5 19.7 %all-to-all-start.1 = ((bf16[128,8,512]{2,0,1:T(8,128)(2,1)}), bf16[128,8,512]{2,0,1:T(8,128)(2,1)}, u32[]{:S(2)}, u32[]{:S(2)}) async-start(bf16[128,8,512]{2,0,1:T(8,128)(2,1)} %bitcast.346), calls=%async_computation.1 | async-start | bytes 2097152 | tf_op jit(solution)/shard_map/all_to_all | solution.py:153
  73.8 7.6 %copy-start.21 = (bf16[1024,128]{1,0:T(8,128)(2,1)}, bf16[1024,128]{1,0:T(8,128)(2,1)S(1)}, u32[]{:S(2)}) copy-start(bf16[1024,128]{1,0:T(8,128)(2,1)S(1)} %fusion.106) | copy-start | bytes 786436
  89.2 19.7 %all-to-all-start.4 = ((bf16[128,8,512]{2,0,1:T(8,128)(2,1)}), bf16[128,8,512]{2,0,1:T(8,128)(2,1)}, u32[]{:S(2)}, u32[]{:S(2)}) async-start(bf16[128,8,512]{2,0,1:T(8,128)(2,1)} %bitcast.345), calls=%async_computation.4 | async-start | bytes 2097152 | tf_op jit(solution)/shard_map/all_to_all | solution.py:154
  126.8 0.8 copy-start.5
  126.8 1.0 copy-start.1
  127.7 20.7 %copy-start.27 = (f32[1024]{0:T(1024)S(1)}, f32[1024]{0:T(1024)}, u32[]{:S(2)}) copy-start(f32[1024]{0:T(1024)} %get-tuple-element.3818) | copy-start | bytes 12292
  132.0 1.9 copy-start.19
  135.3 1.0 copy-start.18
  141.9 1.9 copy-start.19
  145.2 1.0 copy-start.18
  147.5 0.8 copy-start.7
  147.5 1.0 copy-start.3
  148.4 20.7 %copy-start.14 = (bf16[1024,128]{1,0:T(8,128)(2,1)S(1)}, bf16[1024,128]{1,0:T(8,128)(2,1)}, u32[]{:S(2)}) copy-start(bf16[1024,128]{1,0:T(8,128)(2,1)} %get-tuple-element.3735) | copy-start | bytes 786436
  148.4 20.7 %copy-start.26 = (f32[1024]{0:T(1024)S(1)}, f32[1024]{0:T(1024)}, u32[]{:S(2)}) copy-start(f32[1024]{0:T(1024)} %get-tuple-element.3737) | copy-start | bytes 12292
  154.5 1.4 copy-start.17
  156.0 1.0 copy-start.16
  164.4 1.4 copy-start.17
  165.8 1.0 copy-start.16
  168.1 1.0 copy-start.9
  173.4 1.0 copy-start.15
  174.3 1.0 copy-start.11
  175.7 0.8 copy-start.12
  181.7 1.0 copy-start.15
  182.7 1.0 copy-start.11
  184.0 0.8 copy-start.12
  185.8 6.9 %copy-start.2 = (f32[1024,128]{1,0:T(8,128)S(1)}, f32[1024,128]{1,0:T(8,128)}, u32[]{:S(2)}) copy-start(f32[1024,128]{1,0:T(8,128)} %copy-done.1) | copy-start | bytes 1572868
  185.8 7.0 %copy-start.4 = (f32[1024,128]{1,0:T(8,128)S(1)}, f32[1024,128]{1,0:T(8,128)}, u32[]{:S(2)}) copy-start(f32[1024,128]{1,0:T(8,128)} %copy-done.3) | copy-start | bytes 1572868
  188.1 19.7 %all-to-all-start.5 = ((bf16[8,128,512]{2,1,0:T(8,128)(2,1)}), bf16[8,128,512]{2,1,0:T(8,128)(2,1)}, u32[]{:S(2)}, u32[]{:S(2)}) async-start(bf16[8,128,512]{2,1,0:T(8,128)(2,1)} %bitcast.344), calls=%async_computation.5 | async-start | bytes 2097152 | tf_op jit(solution)/shard_map/all_to_all | solution.py:178
  192.8 1.2 copy-start.6
  192.8 1.3 copy-start.8
  194.0 18.4 %copy-start.10 = (f32[1024,128]{1,0:T(8,128)S(1)}, f32[1024,128]{1,0:T(8,128)}, u32[]{:S(2)}) copy-start(f32[1024,128]{1,0:T(8,128)} %copy-done.9) | copy-start | bytes 1572868
  194.0 18.4 %copy-start.13 = (f32[1024,128]{1,0:T(8,128)S(1)}, f32[1024,128]{1,0:T(8,128)}, u32[]{:S(2)}) copy-start(f32[1024,128]{1,0:T(8,128)} %get-tuple-element.4071) | copy-start | bytes 1572868
  207.8 19.7 %all-to-all-start.7 = ((bf16[8,128,512]{2,1,0:T(8,128)(2,1)}), bf16[8,128,512]{2,1,0:T(8,128)(2,1)}, u32[]{:S(2)}, u32[]{:S(2)}) async-start(bf16[8,128,512]{2,1,0:T(8,128)(2,1)} %bitcast.59), calls=%async_computation.7 | async-start | bytes 2097152 | tf_op jit(solution)/shard_map/all_to_all | solution.py:184
  212.1 40.3 %reduce-scatter.7.cloned.1.call-start = ((), (), s32[]{:S(2)}) async-start(), calls=%async_computation.13 | async-start | bytes 163840 | tf_op jit(solution)/shard_map/reduce_scatter | solution.py:213
  215.4 0.9 copy-start.22
  215.8 11.7 %copy-start.20 = (bf16[128,32,128]{0,2,1:T(8,128)(2,1)}, bf16[128,32,128]{0,2,1:T(8,128)(2,1)S(1)}, u32[]{:S(2)}) copy-start(bf16[128,32,128]{0,2,1:T(8,128)(2,1)S(1)} %pad_maximum_fusion.3) | copy-start | bytes 3145732
  227.5 6.1 %copy-start.23 = (bf16[8,5120]{1,0:T(8,128)(2,1)S(1)}, bf16[8,5120]{1,0:T(8,128)(2,1)}, u32[]{:S(2)}) copy-start(bf16[8,5120]{1,0:T(8,128)(2,1)} %param.44) | copy-start | bytes 245764
  227.5 86.4 %all-to-all-start.6 = ((bf16[8,128,512]{2,1,0:T(8,128)(2,1)}), bf16[8,128,512]{2,1,0:T(8,128)(2,1)}, u32[]{:S(2)}, u32[]{:S(2)}) async-start(bf16[8,128,512]{2,1,0:T(8,128)(2,1)} %bitcast.343), calls=%async_computation.6 | async-start | bytes 2097152 | tf_op jit(solution)/shard_map/all_to_all | solution.py:181
  231.9 3.8 %copy-start.24 = (bf16[8,4096]{1,0:T(8,128)(2,1)S(1)}, bf16[8,4096]{1,0:T(8,128)(2,1)}, u32[]{:S(2)}) copy-start(bf16[8,4096]{1,0:T(8,128)(2,1)} %param.43) | copy-start | bytes 196612
  231.9 40.2 %reduce-scatter.11.cloned.1.call-start = ((), (), s32[]{:S(2)}) async-start(), calls=%async_computation.15 | async-start | bytes 163840 | tf_op jit(solution)/shard_map/reduce_scatter | solution.py:215
  235.6 2.6 copy-start.25
  235.6 56.8 %reduce-scatter.5.cloned.1.call-start = ((), (), s32[]{:S(2)}) async-start(), calls=%async_computation.12 | async-start | bytes 204800 | tf_op jit(solution)/shard_map/reduce_scatter | solution.py:212
  238.1 74.5 %reduce-scatter.9.cloned.1.call-start = ((), (), s32[]{:S(2)}) async-start(), calls=%async_computation.14 | async-start | bytes 204800 | tf_op jit(solution)/shard_map/reduce_scatter | solution.py:214
  239.4 127.7 %all-reduce.3.cloned.1.call-start = ((), (), s32[]{:S(2)}) async-start(), calls=%async_computation.16 | async-start | bytes 294912 | tf_op jit(solution)/shard_map/psum | solution.py:210
Sparse Core Ops, SparseCore 0:
  218.4 33.8 reduce-scatter.6
  254.7 17.3 reduce-scatter.10
  274.9 17.4 reduce-scatter.4
  295.2 17.3 reduce-scatter.8
  316.0 51.0 all-reduce.2
where the time goes:
time: 378 us; the launch traced here: 376 us
  waiting for transfers between devices  195 us (52%)
  local copies, waits for them, and re-layouts  54.4 us (14%)
  starting transfers between devices  35.6 us (9%)
  matrix products  31.9 us (8%)
  other arithmetic  22.8 us (6%)
  loops' own time  22.8 us (6%)
  between operations  14.2 us (4%)
    psum x1, waiting for transfers between devices, shards(): summed = lax.psum((terms[0], terms[1], terms[2], terms[3]), 'seq')  48.9 us
    another operation x4, loops' own time, head_backward(): lax.fori_loop(0, block_count, outer, (empty_rows, empty_rows, empty_rows))  21.7 us
    reduce_scatter x1, waiting for transfers between devices, shards(): lax.psum_scatter(summed[0], 'dp', scatter_dimension=1, tiled=True)  20.3 us
    reduce_scatter x1, waiting for transfers between devices, shards(): lax.psum_scatter(summed[2], 'dp', scatter_dimension=1, tiled=True)  20.2 us
    reduce_scatter x1, waiting for transfers between devices, shards(): lax.psum_scatter(summed[3], 'dp', scatter_dimension=1, tiled=True)  19.7 us
    dot_general x16, matrix products, scores_at(): jnp.dot(query_rows, key_rows.T, preferred_element_type=jnp.float32)  14.3 us
    all_to_all x1, waiting for transfers between devices, shards(): lax.all_to_all(jnp.concatenate(query_parts, axis=1), 'seq', split_axis=0,...  13.6 us
    all_to_all x1, waiting for transfers between devices, shards(): lax.all_to_all(attention_out, 'seq', split_axis=1, concat_axis=0, tiled=T...  13.1 us
  transfers between devices with their start and end apart: 13, of which 12 were waited for; matrix products, arithmetic and copies ran while one was open for 12% of the time, Pallas kernels for 0%

commit v1 on v0

v1 whole, which is shorter than its diff:
```python
import functools
import math

import jax
import jax.numpy as jnp
from jax import lax
from jax.experimental import pallas as pl
from jax.experimental.pallas import tpu as pltpu
from jax.sharding import PartitionSpec as P

H = 32
HD = 128
RANK = 8
ADAPTER_ALPHA = 16
SCALING = 1.0 / math.sqrt(HD)
LOG2E = 1.4426950408889634
BF16 = jnp.bfloat16
F32 = jnp.float32
NT = (((1,), (1,)), ((), ()))
VMEM_LIMIT = 56 * 1024 * 1024


def params():
    return pltpu.CompilerParams(vmem_limit_bytes=VMEM_LIMIT)


def any_specs(count):
    return [pl.BlockSpec(memory_space=pl.ANY)] * count


def vmem_specs(count):
    return [pl.BlockSpec(memory_space=pltpu.VMEM)] * count


def dot_nt(left, right):
    return lax.dot_general(left, right, NT, preferred_element_type=F32)


def two_parts(value):
    high = value.astype(BF16)
    low = (value - high.astype(F32)).astype(BF16)
    return high, low


def three_parts(value):
    high, _ = two_parts(value)
    rest = value - high.astype(F32)
    middle, low = two_parts(rest)
    return high, middle, low


def pack_kernel(members, heads_here, first_head, stage_heads, *refs):
    sources = refs[:4]
    messages = refs[4 : 4 + members]
    sems = refs[4 + members]
    me = lax.axis_index("seq")
    copies = []
    for offset in range(members):
        target = me ^ offset
        start = pl.multiple_of((target * heads_here + first_head) * HD, HD)
        for which in range(4):
            copies.append(
                pltpu.make_async_copy(
                    sources[which].at[:, pl.ds(start, stage_heads * HD)],
                    messages[offset].at[which],
                    sems.at[offset, which],
                )
            )
    for copy in copies:
        copy.start()
    for copy in copies:
        copy.wait()


def pack(sources, members, heads_here, first_head, stage_heads):
    rows = sources[0].shape[0]
    shape = jax.ShapeDtypeStruct((4, rows, stage_heads * HD), BF16)
    size = 2 * 4 * rows * stage_heads * HD * members * 2
    return pl.pallas_call(
        functools.partial(pack_kernel, members, heads_here, first_head, stage_heads),
        out_shape=[shape] * members,
        in_specs=any_specs(4),
        out_specs=any_specs(members),
        scratch_shapes=[pltpu.SemaphoreType.DMA((members, 4))],
        compiler_params=params(),
        cost_estimate=pl.CostEstimate(flops=0, bytes_accessed=size, transcendentals=0),
        name="pack",
    )(*sources)


def side_kernel(members, heads_here, out_ref, grad_ref, hidden_ref, downq_ref, downv_ref, *refs):
    messages = refs[:members]
    held, sems = refs[members:]
    me = lax.axis_index("seq")
    low_query = dot_nt(downq_ref[...], hidden_ref[...]).astype(BF16)
    low_value = dot_nt(downv_ref[...], hidden_ref[...]).astype(BF16)
    rows = out_ref.shape[0]
    ones = jnp.ones((8, HD), BF16)
    for member in range(members):
        parts = []
        for head in range(heads_here):
            low_col = (member * heads_here + head) * HD
            product = out_ref[:, low_col : low_col + HD].astype(F32) * grad_ref[
                :, low_col : low_col + HD
            ].astype(F32)
            high, middle, low = three_parts(product)
            total = dot_nt(ones, high) + (dot_nt(ones, middle) + dot_nt(ones, low))
            parts.extend(three_parts(total[0:1, :]))
        parts.append(jnp.zeros((16 - 3 * heads_here, rows), BF16))
        held[member] = jnp.concatenate(parts + [low_query, low_value], axis=0)
    copies = [
        pltpu.make_async_copy(held.at[me ^ offset], messages[offset], sems.at[offset])
        for offset in range(members)
    ]
    for copy in copies:
        copy.start()
    for copy in copies:
        copy.wait()


def side(attention_out, grad_out, hidden, down_query, down_value, members, heads_here):
    rows = hidden.shape[0]
    return pl.pallas_call(
        functools.partial(side_kernel, members, heads_here),
        out_shape=[jax.ShapeDtypeStruct((32, rows), BF16)] * members,
        in_specs=vmem_specs(5),
        out_specs=any_specs(members),
        scratch_shapes=[
            pltpu.VMEM((members, 32, rows), BF16),
            pltpu.SemaphoreType.DMA((members,)),
        ],
        compiler_params=params(),
        cost_estimate=pl.CostEstimate(flops=10**9, bytes_accessed=4 * 2**20, transcendentals=0),
        name="side",
    )(attention_out, grad_out, hidden, down_query, down_value)


def begin_of(lengths_ref, positions):
    begin = jnp.zeros_like(positions)
    start = jnp.int32(0)
    for index in range(lengths_ref.shape[1] - 1):
        start = start + lengths_ref[0, index]
        begin = jnp.where(positions >= start, start, begin)
    return begin


def attention_kernel(
    members,
    heads_here,
    first_head,
    stage_heads,
    lengths_ref,
    upq_ref,
    upv_ref,
    cos_ref,
    sin_ref,
    *refs,
):
    refs = list(refs)
    messages = [refs.pop(0) for _ in range(members)]
    sides = [refs.pop(0) for _ in range(members)]
    outs = [refs.pop(0) for _ in range(members)]
    back_ref = refs.pop(0)
    terms_ref = refs.pop(0)
    held, side_held, key_flip, grads, key_acc, value_acc, in_sems, side_sems, out_sems = refs
    me = lax.axis_index("seq")
    rows = messages[0].shape[1]
    total = rows * members
    block = min(256, total)
    reach = total // 2
    rows_of = [
        pl.ds(pl.multiple_of((me ^ offset) * rows, rows), rows) for offset in range(members)
    ]
    copies = []
    for offset in range(members):
        copies.append(
            pltpu.make_async_copy(
                messages[offset], held.at[:, rows_of[offset], :], in_sems.at[offset]
            )
        )
        copies.append(
            pltpu.make_async_copy(
                sides[offset], side_held.at[:, rows_of[offset]], side_sems.at[offset]
            )
        )
    for copy in copies:
        copy.start()
    key_acc[...] = jnp.zeros_like(key_acc)
    value_acc[...] = jnp.zeros_like(value_acc)
    terms_ref[...] = jnp.zeros_like(terms_ref)
    for copy in copies:
        copy.wait()
    columns = [slice(head * HD, (head + 1) * HD) for head in range(stage_heads)]
    for head in range(stage_heads):
        key_flip[head] = held[1, :, columns[head]].astype(F32).T.astype(BF16)

    def query_block(low, key_low, width):
        positions = low + lax.broadcasted_iota(jnp.int32, (1, block), 1)
        begin = begin_of(lengths_ref, positions)
        key_positions = key_low + lax.broadcasted_iota(jnp.int32, (width, block), 0)
        allowed = (key_positions >= begin) & (key_positions <= positions)
        bias = jnp.where(allowed, 0.0, -1e30).astype(F32)
        here = pl.ds(low, block)
        keys_here = pl.ds(key_low, width)
        cosine = cos_ref[:, here]
        sine = sin_ref[:, here]
        back_query = jnp.zeros((RANK, block), F32)
        for head in range(stage_heads):
            cols = columns[head]
            query = held[0, here, cols]
            grad = held[3, here, cols]
            scores = dot_nt(held[1, keys_here, cols], query) + bias
            grad_prob = dot_nt(held[2, keys_here, cols], grad)
            top = jnp.max(scores, axis=0, keepdims=True)
            weights = jnp.exp2((scores - top) * (SCALING * LOG2E))
            inverse = 1.0 / jnp.sum(weights, axis=0, keepdims=True)
            probs = weights * inverse
            row = 3 * (first_head + head)
            parts = side_held[0:16, here].astype(F32)
            delta = parts[row : row + 1] + parts[row + 1 : row + 2] + parts[row + 2 : row + 3]
            grad_score = (probs * (grad_prob - delta)).astype(BF16)
            value_acc[head, keys_here, :] += jnp.dot(
                probs.astype(BF16), grad, preferred_element_type=F32
            )
            key_acc[head, keys_here, :] += jnp.dot(grad_score, query, preferred_element_type=F32)
            flipped = SCALING * jnp.dot(
                key_flip[head, :, keys_here], grad_score, preferred_element_type=F32
            )
            grads[0, here, cols] = flipped.T.astype(BF16)
            rounded = flipped.astype(BF16).astype(F32)
            first = rounded[: HD // 2]
            second = rounded[HD // 2 :]
            before = jnp.concatenate(
                [first * cosine + second * sine, second * cosine - first * sine], axis=0
            ).astype(BF16)
            back_query += jnp.dot(upq_ref[:, cols], before, preferred_element_type=F32)
            terms_ref[0:RANK, cols] += dot_nt(side_held[16:24, here], before)
        back_ref[0:RANK, here] = back_query

    if total <= 1024:
        for low in range(0, total, block):
            key_low = max(0, low - reach)
            query_block(low, key_low, low + block - key_low)
    else:

        @pl.loop(0, total // block)
        def _(index):
            low = pl.multiple_of(index * block, block)
            key_low = pl.multiple_of(jnp.maximum(low - reach, 0), block)
            query_block(low, key_low, reach + block)

    back_value = jnp.zeros((RANK, total), F32)
    for head in range(stage_heads):
        cols = columns[head]
        grads[1, :, cols] = (key_acc[head] * SCALING).astype(BF16)
        value_grad = value_acc[head].astype(BF16)
        grads[2, :, cols] = value_grad
        back_value += dot_nt(upv_ref[:, cols], value_grad)
        terms_ref[RANK : 2 * RANK, cols] = jnp.dot(
            side_held[24:32, :], value_grad, preferred_element_type=F32
        )
    back_ref[RANK : 2 * RANK, :] = back_value
    copies = [
        pltpu.make_async_copy(grads.at[:, rows_of[offset], :], outs[offset], out_sems.at[offset])
        for offset in range(members)
    ]
    for copy in copies:
        copy.start()
    for copy in copies:
        copy.wait()


def attention(lengths, ups, turns, messages, sides, heads_here, first_head, stage_heads):
    members = len(messages)
    rows = messages[0].shape[1]
    total = rows * members
    width = stage_heads * HD
    message = jax.ShapeDtypeStruct((3, rows, width), BF16)
    return pl.pallas_call(
        functools.partial(attention_kernel, members, heads_here, first_head, stage_heads),
        out_shape=[message] * members
        + [
            jax.ShapeDtypeStruct((2 * RANK, total), F32),
            jax.ShapeDtypeStruct((2 * RANK, width), F32),
        ],
        in_specs=[pl.BlockSpec(memory_space=pltpu.SMEM)] + vmem_specs(4) + any_specs(2 * members),
        out_specs=any_specs(members) + vmem_specs(2),
        scratch_shapes=[
            pltpu.VMEM((4, total, width), BF16),
            pltpu.VMEM((32, total), BF16),
            pltpu.VMEM((stage_heads, HD, total), BF16),
            pltpu.VMEM((3, total, width), BF16),
            pltpu.VMEM((stage_heads, total, HD), F32),
            pltpu.VMEM((stage_heads, total, HD), F32),
            pltpu.SemaphoreType.DMA((members,)),
            pltpu.SemaphoreType.DMA((members,)),
            pltpu.SemaphoreType.DMA((members,)),
        ],
        compiler_params=params(),
        cost_estimate=pl.CostEstimate(
            flops=stage_heads * 5 * 10**9, bytes_accessed=4 * 2**20, transcendentals=0
        ),
        name="attention",
    )(lengths, *ups, *turns, *messages, *sides)


def spread_kernel(members, stages, *refs):
    backs = refs[:stages]
    messages = refs[stages : stages + members]
    held, sems = refs[stages + members :]
    me = lax.axis_index("seq")
    rows = held.shape[2]
    for member in range(members):
        here = slice(member * rows, (member + 1) * rows)
        total = backs[0][:, here]
        for back in backs[1:]:
            total = total + back[:, here]
        high, low = two_parts(total)
        held[member] = jnp.concatenate([high, low], axis=0)
    copies = [
        pltpu.make_async_copy(held.at[me ^ offset], messages[offset], sems.at[offset])
        for offset in range(members)
    ]
    for copy in copies:
        copy.start()
    for copy in copies:
        copy.wait()


def spread(backs, members, rows):
    return pl.pallas_call(
        functools.partial(spread_kernel, members, len(backs)),
        out_shape=[jax.ShapeDtypeStruct((4 * RANK, rows), BF16)] * members,
        in_specs=vmem_specs(len(backs)),
        out_specs=any_specs(members),
        scratch_shapes=[
            pltpu.VMEM((members, 4 * RANK, rows), BF16),
            pltpu.SemaphoreType.DMA((members,)),
        ],
        compiler_params=params(),
        cost_estimate=pl.CostEstimate(flops=10**6, bytes_accessed=10**5, transcendentals=0),
        name="spread",
    )(*backs)


def down_kernel(members, packs, stage_sizes, hidden_ref, *refs):
    backs = refs[:members]
    ups = refs[members : members + len(stage_sizes)]
    messages = refs[members + len(stage_sizes) : members + len(stage_sizes) + packs]
    held, sems = refs[members + len(stage_sizes) + packs :]
    me = lax.axis_index("seq")
    pack_here = lax.axis_index("dp")
    total = backs[0][...].astype(F32)
    for back in backs[1:]:
        total = total + back[...].astype(F32)
    back = (total[: 2 * RANK] + total[2 * RANK :]).astype(BF16)
    terms = jnp.dot(back, hidden_ref[...], preferred_element_type=F32)
    down_cols = terms.shape[1] // packs
    sharers = members // packs
    head_cols = sum(stage_sizes) * HD
    for target in range(packs):
        held[target, :, :down_cols] = terms[:, target * down_cols : (target + 1) * down_cols]
        for place in range(sharers):
            low = down_cols + place * head_cols
            mine = me == target * sharers + place
            for size, up in zip(stage_sizes, ups):
                held[target, :, low : low + size * HD] = jnp.where(mine, up[...], 0.0)
                low += size * HD
    copies = [
        pltpu.make_async_copy(held.at[pack_here ^ offset], messages[offset], sems.at[offset])
        for offset in range(packs)
    ]
    for copy in copies:
        copy.start()
    for copy in copies:
        copy.wait()


def down_terms(hidden, backs, ups, packs):
    members = len(backs)
    stage_sizes = [up.shape[1] // HD for up in ups]
    width = hidden.shape[1] // packs + (members // packs) * sum(stage_sizes) * HD
    return pl.pallas_call(
        functools.partial(down_kernel, members, packs, stage_sizes),
        out_shape=[jax.ShapeDtypeStruct((2 * RANK, width), F32)] * packs,
        in_specs=vmem_specs(1 + members + len(ups)),
        out_specs=any_specs(packs),
        scratch_shapes=[
            pltpu.VMEM((packs, 2 * RANK, width), F32),
            pltpu.SemaphoreType.DMA((packs,)),
        ],
        compiler_params=params(),
        cost_estimate=pl.CostEstimate(flops=10**7, bytes_accessed=2 * 10**6, transcendentals=0),
        name="down_terms",
    )(hidden, *backs, *ups)


def unpack_kernel(members, heads_here, stages, *refs):
    count = members * len(stages)
    messages = refs[:count]
    outs = refs[count : count + 3]
    sems = refs[count + 3]
    me = lax.axis_index("seq")
    copies = []
    for stage, (first_head, stage_heads) in enumerate(stages):
        for offset in range(members):
            source = me ^ offset
            start = pl.multiple_of((source * heads_here + first_head) * HD, HD)
            for which in range(3):
                copies.append(
                    pltpu.make_async_copy(
                        messages[stage * members + offset].at[which],
                        outs[which].at[:, pl.ds(start, stage_heads * HD)],
                        sems.at[stage, offset, which],
                    )
                )
    for copy in copies:
        copy.start()
    for copy in copies:
        copy.wait()


def unpack(messages, members, heads_here, stages):
    rows = messages[0].shape[1]
    width = members * heads_here * HD
    return pl.pallas_call(
        functools.partial(unpack_kernel, members, heads_here, stages),
        out_shape=[jax.ShapeDtypeStruct((rows, width), BF16)] * 3,
        in_specs=any_specs(len(messages)),
        out_specs=any_specs(3),
        scratch_shapes=[pltpu.SemaphoreType.DMA((len(stages), members, 3))],
        compiler_params=params(),
        cost_estimate=pl.CostEstimate(
            flops=0, bytes_accessed=2 * 3 * rows * width * 2, transcendentals=0
        ),
        name="unpack",
    )(*messages)


def exchange(messages, axis):
    count = len(messages)
    return [messages[0]] + [
        lax.ppermute(messages[offset], axis, [(i, i ^ offset) for i in range(count)])
        for offset in range(1, count)
    ]


def turn_tables(lengths_row, total):
    positions = jnp.arange(total, dtype=jnp.int32)
    ends = jnp.cumsum(lengths_row)
    starts = ends - lengths_row
    begin = jnp.max(jnp.where(positions[:, None] >= starts[None, :], starts[None, :], 0), axis=1)
    half = HD // 2
    inverse = jnp.exp(-(jnp.arange(half, dtype=F32) * (2.0 / HD)) * math.log(10000.0))
    angles = inverse[:, None] * (positions - begin).astype(F32)[None, :]
    return jnp.cos(angles), jnp.sin(angles)


def shards(
    hidden,
    queries,
    key_states,
    value_states,
    attention_out,
    grad_out,
    lengths,
    down_query,
    up_query,
    down_value,
    up_value,
):
    rows = queries.shape[0]
    members = lax.axis_size("seq")
    packs = lax.axis_size("dp")
    total = rows * members
    heads_here = H // members
    stages = [(0, heads_here)]
    if heads_here > 1:
        stages = [(0, heads_here // 2), (heads_here // 2, heads_here - heads_here // 2)]
    sources = (queries, key_states, value_states, grad_out)
    me = lax.axis_index("seq")

    arrived = []
    sides = None
    for first_head, stage_heads in stages:
        packed = pack(sources, members, heads_here, first_head, stage_heads)
        arrived.append(exchange(packed, "seq"))
        if sides is None:
            sides = exchange(
                side(
                    attention_out, grad_out, hidden, down_query, down_value, members, heads_here
                ),
                "seq",
            )
    turns = turn_tables(lengths[0], total)
    returned = []
    backs = []
    ups = []
    for (first_head, stage_heads), messages in zip(stages, arrived):
        start = (me * heads_here + first_head) * HD
        up_here = tuple(
            lax.dynamic_slice_in_dim(up, start, stage_heads * HD, 1) for up in (up_query, up_value)
        )
        *grads, back, up_terms = attention(
            lengths, up_here, turns, messages, sides, heads_here, first_head, stage_heads
        )
        returned.append(grads)
        backs.append(back)
        ups.append(up_terms)
    back_messages = exchange(spread(backs, members, rows), "seq")
    home = []
    for grads in returned:
        home.extend(exchange(grads, "seq"))
    pieces = exchange(down_terms(hidden, back_messages, ups, packs), "dp")
    summed = pieces[0]
    for piece in pieces[1:]:
        summed = summed + piece
    step = 1
    while step < members:
        summed = summed + lax.ppermute(summed, "seq", [(i, i ^ step) for i in range(members)])
        step *= 2
    summed = summed * (ADAPTER_ALPHA / RANK)
    down_cols = hidden.shape[1] // packs
    grad_queries, grad_keys, value_gradients = unpack(home, members, heads_here, stages)
    return (
        grad_queries,
        grad_keys,
        value_gradients,
        summed[:RANK, :down_cols],
        summed[:RANK, down_cols:],
        summed[RANK:, :down_cols],
        summed[RANK:, down_cols:],
    )


def solution(mesh):
    tokens = P(("dp", "seq"), None)
    placed = (tokens,) * 6 + (P("dp", None),) + (P(),) * 4
    return jax.shard_map(
        shards,
        mesh=mesh,
        in_specs=placed,
        out_specs=(tokens,) * 3 + (P(None, "dp"),) * 4,
        check_vma=False,
    )
```

time: 378 us -> 375 us (level)
  Pallas kernels: 0 us -> 258 us
  waiting for transfers between devices: 195 us -> 55 us
  local copies, waits for them, and re-layouts: 54.4 us -> 4.93 us
  matrix products: 31.9 us -> 0 us
  loops' own time: 22.8 us -> 0 us
  other arithmetic: 22.8 us -> 3.1 us
  starting transfers between devices: 35.6 us -> 51.9 us
  between operations: 14.2 us -> 1.34 us
    pallas_call x0 -> x8, Pallas kernels: none -> 258 us  [the longest x2 130 us: pack(): pl.pallas_call(functools.partial(pack_kernel, members, heads_here, first_...]
    reduce_scatter x4 -> x0, waiting for transfers between devices: 73.2 us -> none  [the longest x1 20.3 us: shards(): lax.psum_scatter(summed[0], 'dp', scatter_dimension=1, tiled=True)]
    all_to_all x8 -> x0, waiting for transfers between devices: 72.6 us -> none  [the longest x1 13.6 us: shards(): lax.all_to_all(jnp.concatenate(query_parts, axis=1), 'seq', split_axis=0,...]
    ppermute x0 -> x48, waiting for transfers between devices: none -> 55 us  [the longest x45 54 us: exchange(): lax.ppermute(messages[offset], axis, [(i, i ^ offset) for i in range(coun...]
    ppermute x0 -> x48, starting transfers between devices: none -> 51.9 us  [the longest x45 48.8 us: exchange(): lax.ppermute(messages[offset], axis, [(i, i ^ offset) for i in range(coun...]
    psum x1 -> x0, waiting for transfers between devices: 48.9 us -> none  [shards(): summed = lax.psum((terms[0], terms[1], terms[2], terms[3]), 'seq')]
    all_to_all x8 -> x0, starting transfers between devices: 35.2 us -> none  [the longest x1 5.17 us: shards(): lax.all_to_all(grad_out, 'seq', split_axis=1, concat_axis=0, tiled=True)]
    dot_general x52 -> x0, matrix products: 31.9 us -> none  [the longest x16 14.3 us: scores_at(): jnp.dot(query_rows, key_rows.T, preferred_element_type=jnp.float32)]
  transfers between devices with their start and end apart: 13 -> 48, of which waited for: 12 -> 10; matrix products, arithmetic and copies ran while one was open for 12% -> 1% of each run, Pallas kernels for 0% -> 64%
where the time goes in v1:
time: 375 us; the launch traced here: 374 us
  Pallas kernels  258 us (69%)
  waiting for transfers between devices  55 us (15%)
  starting transfers between devices  51.9 us (14%)
  local copies, waits for them, and re-layouts  4.93 us (1%)
    pallas_call x2, Pallas kernels, pack(): pl.pallas_call(functools.partial(pack_kernel, members, heads_here, first_...  130 us
    pallas_call x1, Pallas kernels, unpack(): pl.pallas_call(functools.partial(unpack_kernel, members, heads_here, stag...  96.8 us
    ppermute x45, waiting for transfers between devices, exchange(): lax.ppermute(messages[offset], axis, [(i, i ^ offset) for i in range(coun...  54 us
    ppermute x45, starting transfers between devices, exchange(): lax.ppermute(messages[offset], axis, [(i, i ^ offset) for i in range(coun...  48.8 us
    pallas_call x2, Pallas kernels, attention(): pl.pallas_call(functools.partial(attention_kernel, members, heads_here, f...  21.7 us
  transfers between devices with their start and end apart: 48, of which 10 were waited for; matrix products, arithmetic and copies ran while one was open for 1% of the time, Pallas kernels for 64%

profile of v1, /device:TPU:0, one launch (start us, length us, event | category | flops | bytes accessed | tf_op | source)
XLA Modules:
  0.0 374.0 jit_solution(7947993186245118295)
XLA Ops:
  0.6 5.1 %side.1 = (bf16[32,128]{1,0:T(8,128)(2,1)}, bf16[32,128]{1,0:T(8,128)(2,1)}, bf16[32,128]{1,0:T(8,128)(2,1)}, bf16[32,128]{1,0:T(8,128)(2,1)}, bf16[32,128]{1,0:...) custom-call(bf16[128,4096]{1,0:T(8,128)(2,1)} %out_ref.1, ...), custom_call_target="tpu_custom_call" | custom-call | flops 1000000000 | bytes 4194304 | tf_op jit(solution)/shard_map/side/pallas_call | solution.py:123
  5.8 0.5 collective-permute-start.7
  6.3 2.6 collective-permute-start.8
  8.9 1.8 collective-permute-start.10
  11.0 64.9 %pack.3 = (bf16[4,128,256]{2,1,0:T(8,128)(2,1)}, bf16[4,128,256]{2,1,0:T(8,128)(2,1)}, bf16[4,128,256]{2,1,0:T(8,128)(2,1)}, bf16[4,128,256]{2,1,0:T(8,128)(2,1)...) custom-call(bf16[128,4096]{1,0:T(8,128)(2,1)} %refs_0_.3, ...), custom_call_target="tpu_custom_call" | custom-call | bytes 4194304 | tf_op jit(solution)/shard_map/pack/pallas_call | solution.py:79
  76.0 2.7 collective-permute-start.12
  78.8 0.6 collective-permute-start.22
  79.4 1.1 collective-permute-start.23
  80.5 0.5 collective-permute-start.24
  81.0 1.3 collective-permute-start.13
  82.4 1.3 constant_dynamic-slice_fusion
  83.7 64.9 %pack.2 = (bf16[4,128,256]{2,1,0:T(8,128)(2,1)}, bf16[4,128,256]{2,1,0:T(8,128)(2,1)}, bf16[4,128,256]{2,1,0:T(8,128)(2,1)}, bf16[4,128,256]{2,1,0:T(8,128)(2,1)...) custom-call(bf16[128,4096]{1,0:T(8,128)(2,1)} %refs_0_.3, ...), custom_call_target="tpu_custom_call" | custom-call | bytes 4194304 | tf_op jit(solution)/shard_map/pack/pallas_call | solution.py:79
  148.8 1.1 collective-permute-start.25
  149.9 1.9 collective-permute-start.26
  152.2 0.9 collective-permute-start
  153.0 0.9 collective-permute-start.1
  154.0 1.8 multiply_sine_fusion
  155.8 11.8 %collective-permute-done.25.refs_5_ = bf16[4,128,256]{2,1,0:T(8,128)(2,1)S(1)} collective-permute-done((bf16[4,128,256]{2,1,0:T(8,128)(2,1)S(1)}, bf16[4,128,256]{2,1,0:T(8,128)(2,1)S(1)}, u32[]{:S(2)}, u32[]{:S(2)}) %collective-permute-start.25) | collective-permute-done | bytes 262176 | tf_op jit(solution)/shard_map/ppermute | solution.py:443
  167.6 2.3 collective-permute-start.2
  169.9 0.5 collective-permute-start.3
  170.4 0.8 collective-permute-start.4
  171.2 0.8 collective-permute-start.5
  172.0 2.3 collective-permute-start.6
  174.3 10.9 %attention.3 = (bf16[3,128,256]{2,1,0:T(8,128)(2,1)}, bf16[3,128,256]{2,1,0:T(8,128)(2,1)}, bf16[3,128,256]{2,1,0:T(8,128)(2,1)}, bf16[3,128,256]{2,1,0:T(8,128)...) custom-call(s32[1,4]{1,0:T(1,128)} %lengths_ref.3, ...), custom_call_target="tpu_custom_call" | custom-call | flops 10000000000 | bytes 4194304 | tf_op jit(solution)/shard_map/attention/pallas_call | solution.py:279
  185.2 5.3 %collective-permute-done.3.refs_4_ = bf16[4,128,256]{2,1,0:T(8,128)(2,1)S(1)} collective-permute-done((bf16[4,128,256]{2,1,0:T(8,128)(2,1)}, bf16[4,128,256]{2,1,0:T(8,128)(2,1)S(1)}, u32[]{:S(2)}, u32[]{:S(2)}) %collective-permute-start.3) | collective-permute-done | bytes 262176 | tf_op jit(solution)/shard_map/ppermute | solution.py:443
  190.5 3.6 collective-permute-done.4.refs_5_
  194.1 0.7 copy-done.34
  195.0 10.8 %attention.2 = (bf16[3,128,256]{2,1,0:T(8,128)(2,1)}, bf16[3,128,256]{2,1,0:T(8,128)(2,1)}, bf16[3,128,256]{2,1,0:T(8,128)(2,1)}, bf16[3,128,256]{2,1,0:T(8,128)...) custom-call(s32[1,4]{1,0:T(1,128)} %lengths_ref.3, ...), custom_call_target="tpu_custom_call" | custom-call | flops 10000000000 | bytes 4194304 | tf_op jit(solution)/shard_map/attention/pallas_call | solution.py:279
  205.9 1.7 spread.1
  207.6 0.9 collective-permute-start.35
  208.5 0.5 collective-permute-start.36
  209.0 0.9 collective-permute-start.37
  209.9 0.5 collective-permute-start.38
  210.4 1.6 collective-permute-start.39
  212.0 0.5 collective-permute-start.40
  212.5 1.8 collective-permute-start.41
  214.3 2.4 collective-permute-done.40.refs_6_
  216.8 0.5 copy-done.19
  217.4 2.6 down_terms.1
  219.9 1.6 collective-permute-start.42
  221.6 2.6 collective-permute-start.43
  224.4 1.5 collective-permute-start.29
  225.9 2.5 collective-permute-done.42
  228.5 7.3 %collective-permute-done.43 = f32[16,2304]{1,0:T(8,128)S(1)} collective-permute-done((f32[16,2304]{1,0:T(8,128)}, f32[16,2304]{1,0:T(8,128)S(1)}, u32[]{:S(2)}, u32[]{:S(2)}) %collective-permute-start.43) | collective-permute-done | bytes 147488 | tf_op jit(solution)/shard_map/ppermute | solution.py:443
  235.8 1.4 collective-permute-start.31
  237.2 1.0 add_add_fusion
  238.3 0.7 collective-permute-start.32
  239.0 2.5 collective-permute-start.33
  241.6 0.7 collective-permute-start.14
  242.2 1.5 collective-permute-start.15
  243.7 9.8 %collective-permute-done.32.refs_13_ = bf16[3,128,256]{2,1,0:T(8,128)(2,1)S(1)} collective-permute-done((bf16[3,128,256]{2,1,0:T(8,128)(2,1)S(1)}, bf16[3,128,256]{2,1,0:T(8,128)(2,1)S(1)}, u32[]{:S(2)}, u32[]{:S(2)}) %collective-permute-start.32) | collective-permute-done | bytes 196640 | tf_op jit(solution)/shard_map/ppermute | solution.py:443
  253.6 1.4 collective-permute-start.46
  255.0 0.6 collective-permute-start.16
  255.6 1.5 collective-permute-start.17
  257.3 1.9 collective-permute-start.19
  259.2 1.0 collective-permute-done.46
  260.2 1.9 collective-permute-start.20
  262.1 1.8 collective-permute-done.16.refs_3_
  263.9 1.7 collective-permute-start.47
  265.6 9.4 %collective-permute-done.18.refs_5_ = bf16[3,128,256]{2,1,0:T(8,128)(2,1)S(1)} collective-permute-done((bf16[3,128,256]{2,1,0:T(8,128)(2,1)S(1)}, bf16[3,128,256]{2,1,0:T(8,128)(2,1)S(1)}, u32[]{:S(2)}, u32[]{:S(2)}) %collective-permute-start.18) | collective-permute-done | bytes 196640 | tf_op jit(solution)/shard_map/ppermute | solution.py:443
  275.2 0.5 copy-done.11
  275.9 96.8 %unpack.1 = (bf16[128,4096]{1,0:T(8,128)(2,1)}, bf16[128,4096]{1,0:T(8,128)(2,1)}, bf16[128,4096]{1,0:T(8,128)(2,1)}) custom-call(bf16[3,128,256]{2,1,0:T(8,128)(2,1)} %get-tuple-element.82.refs_0_, bf16[3,128,256]{2,1,0:T(8,128)(2,1)} %copy-done.7, bf16[3,128,256]{2,1,0:T(8,128)(2,1)} %copy-done.8, bf16[3,128,256]{2,1,0:T(8,128)(2,1)} %copy-done.9, ...), custom_call_target="tpu_custom_call" | custom-call | bytes 6291456 | tf_op jit(solution)/shard_map/unpack/pallas_call | solution.py:426
  372.8 0.6 fusion
  373.4 0.6 fusion.1
  (177 shorter events, 2.2 us)
Async XLA Ops:
  5.8 70.2 %collective-permute-start.7 = (bf16[32,128]{1,0:T(8,128)(2,1)}, bf16[32,128]{1,0:T(8,128)(2,1)S(1)}, u32[]{:S(2)}, u32[]{:S(2)}) collective-permute-start(bf16[32,128]{1,0:T(8,128)(2,1)} %get-tuple-element.75), channel_id=1, source_target_pairs={{0,1},{1,0},{2,3},{3,2},{4,5},{5,4},{6,7},{7,6},{8,9},{9,8},{10,11... | collective-permute-start | bytes 24584 | tf_op jit(solution)/shard_map/ppermute | solution.py:443
  6.3 72.3 %collective-permute-start.8 = (bf16[32,128]{1,0:T(8,128)(2,1)}, bf16[32,128]{1,0:T(8,128)(2,1)S(1)}, u32[]{:S(2)}, u32[]{:S(2)}) collective-permute-start(bf16[32,128]{1,0:T(8,128)(2,1)} %get-tuple-element.76), channel_id=1, source_target_pairs={{0,2},{1,3},{2,0},{3,1},{4,6},{5,7},{6,4},{7,5},{8,10},{9,11},{10,... | collective-permute-start | bytes 24584 | tf_op jit(solution)/shard_map/ppermute | solution.py:443
  8.8 70.0 %collective-permute-start.9 = (bf16[32,128]{1,0:T(8,128)(2,1)}, bf16[32,128]{1,0:T(8,128)(2,1)S(1)}, u32[]{:S(2)}, u32[]{:S(2)}) collective-permute-start(bf16[32,128]{1,0:T(8,128)(2,1)} %get-tuple-element.77), channel_id=1, source_target_pairs={{0,3},{1,2},{2,1},{3,0},{4,7},{5,6},{6,5},{7,4},{8,11},{9,10},{10,... | collective-permute-start | bytes 24584 | tf_op jit(solution)/shard_map/ppermute | solution.py:443
  8.9 70.4 %collective-permute-start.10 = (bf16[32,128]{1,0:T(8,128)(2,1)}, bf16[32,128]{1,0:T(8,128)(2,1)S(1)}, u32[]{:S(2)}, u32[]{:S(2)}) collective-permute-start(bf16[32,128]{1,0:T(8,128)(2,1)} %get-tuple-element.78), channel_id=1, source_target_pairs={{0,4},{1,5},{2,6},{3,7},{4,0},{5,1},{6,2},{7,3},{8,12},{9,13},{10,... | collective-permute-start | bytes 24584 | tf_op jit(solution)/shard_map/ppermute | solution.py:443
  10.7 69.8 %collective-permute-start.11 = (bf16[32,128]{1,0:T(8,128)(2,1)}, bf16[32,128]{1,0:T(8,128)(2,1)S(1)}, u32[]{:S(2)}, u32[]{:S(2)}) collective-permute-start(bf16[32,128]{1,0:T(8,128)(2,1)} %get-tuple-element.79), channel_id=1, source_target_pairs={{0,5},{1,4},{2,7},{3,6},{4,1},{5,0},{6,3},{7,2},{8,13},{9,12},{10,... | collective-permute-start | bytes 24584 | tf_op jit(solution)/shard_map/ppermute | solution.py:443
  11.0 65.0 %copy-start.60 = (bf16[32,128]{1,0:T(8,128)(2,1)S(1)}, bf16[32,128]{1,0:T(8,128)(2,1)}, u32[]{:S(2)}) copy-start(bf16[32,128]{1,0:T(8,128)(2,1)} %get-tuple-element.80) | copy-start | bytes 24580
  11.0 70.1 %copy-start.59 = (bf16[32,128]{1,0:T(8,128)(2,1)S(1)}, bf16[32,128]{1,0:T(8,128)(2,1)}, u32[]{:S(2)}) copy-start(bf16[32,128]{1,0:T(8,128)(2,1)} %get-tuple-element.81) | copy-start | bytes 24580
  75.9 72.7 %copy-start.52 = (bf16[32,128]{1,0:T(8,128)(2,1)}, bf16[32,128]{1,0:T(8,128)(2,1)S(1)}, u32[]{:S(2)}) copy-start(bf16[32,128]{1,0:T(8,128)(2,1)S(1)} %collective-permute-done.7.refs_9_) | copy-start | bytes 24580
  76.0 5.1 %collective-permute-start.12 = (bf16[32,128]{1,0:T(8,128)(2,1)S(1)}, bf16[32,128]{1,0:T(8,128)(2,1)S(1)}, u32[]{:S(2)}, u32[]{:S(2)}) collective-permute-start(bf16[32,128]{1,0:T(8,128)(2,1)S(1)} %copy-done.60), channel_id=1, source_target_pairs={{0,6},{1,7},{2,4},{3,5},{4,2},{5,3},{6,0},{7,1},{8,14},{9,15},{10,... | collective-permute-start | bytes 24584 | tf_op jit(solution)/shard_map/ppermute | solution.py:443
  78.6 70.1 %copy-start.53 = (bf16[32,128]{1,0:T(8,128)(2,1)}, bf16[32,128]{1,0:T(8,128)(2,1)S(1)}, u32[]{:S(2)}) copy-start(bf16[32,128]{1,0:T(8,128)(2,1)S(1)} %collective-permute-done.8.refs_10_) | copy-start | bytes 24580
  78.6 71.2 %collective-permute-start.21 = (bf16[4,128,256]{2,1,0:T(8,128)(2,1)}, bf16[4,128,256]{2,1,0:T(8,128)(2,1)S(1)}, u32[]{:S(2)}, u32[]{:S(2)}) collective-permute-start(bf16[4,128,256]{2,1,0:T(8,128)(2,1)} %get-tuple-element.91), channel_id=1, source_target_pairs={{0,1},{1,0},{2,3},{3,2},{4,5},{5,4},{6,7},{7,6},{8,9},{9,8},{10,11... | collective-permute-start | bytes 786440 | tf_op jit(solution)/shard_map/ppermute | solution.py:443
  78.8 69.9 %copy-start.54 = (bf16[32,128]{1,0:T(8,128)(2,1)}, bf16[32,128]{1,0:T(8,128)(2,1)S(1)}, u32[]{:S(2)}) copy-start(bf16[32,128]{1,0:T(8,128)(2,1)S(1)} %collective-permute-done.9.refs_11_) | copy-start | bytes 24580
  78.8 73.0 %collective-permute-start.22 = (bf16[4,128,256]{2,1,0:T(8,128)(2,1)}, bf16[4,128,256]{2,1,0:T(8,128)(2,1)S(1)}, u32[]{:S(2)}, u32[]{:S(2)}) collective-permute-start(bf16[4,128,256]{2,1,0:T(8,128)(2,1)} %get-tuple-element.92), channel_id=1, source_target_pairs={{0,2},{1,3},{2,0},{3,1},{4,6},{5,7},{6,4},{7,5},{8,10},{9,11},{10,... | collective-permute-start | bytes 786440 | tf_op jit(solution)/shard_map/ppermute | solution.py:443
  79.4 69.3 %copy-start.55 = (bf16[32,128]{1,0:T(8,128)(2,1)}, bf16[32,128]{1,0:T(8,128)(2,1)S(1)}, u32[]{:S(2)}) copy-start(bf16[32,128]{1,0:T(8,128)(2,1)S(1)} %collective-permute-done.10.refs_12_) | copy-start | bytes 24580
  79.4 72.8 %collective-permute-start.23 = (bf16[4,128,256]{2,1,0:T(8,128)(2,1)}, bf16[4,128,256]{2,1,0:T(8,128)(2,1)S(1)}, u32[]{:S(2)}, u32[]{:S(2)}) collective-permute-start(bf16[4,128,256]{2,1,0:T(8,128)(2,1)} %get-tuple-element.93), channel_id=1, source_target_pairs={{0,3},{1,2},{2,1},{3,0},{4,7},{5,6},{6,5},{7,4},{8,11},{9,10},{10,... | collective-permute-start | bytes 786440 | tf_op jit(solution)/shard_map/ppermute | solution.py:443
  80.5 68.2 %copy-start.56 = (bf16[32,128]{1,0:T(8,128)(2,1)}, bf16[32,128]{1,0:T(8,128)(2,1)S(1)}, u32[]{:S(2)}) copy-start(bf16[32,128]{1,0:T(8,128)(2,1)S(1)} %collective-permute-done.11.refs_13_) | copy-start | bytes 24580
  80.5 72.5 %collective-permute-start.24 = (bf16[4,128,256]{2,1,0:T(8,128)(2,1)}, bf16[4,128,256]{2,1,0:T(8,128)(2,1)S(1)}, u32[]{:S(2)}, u32[]{:S(2)}) collective-permute-start(bf16[4,128,256]{2,1,0:T(8,128)(2,1)} %get-tuple-element.94), channel_id=1, source_target_pairs={{0,4},{1,5},{2,6},{3,7},{4,0},{5,1},{6,2},{7,3},{8,12},{9,13},{10,... | collective-permute-start | bytes 786440 | tf_op jit(solution)/shard_map/ppermute | solution.py:443
  81.0 67.7 %copy-start.57 = (bf16[32,128]{1,0:T(8,128)(2,1)}, bf16[32,128]{1,0:T(8,128)(2,1)S(1)}, u32[]{:S(2)}) copy-start(bf16[32,128]{1,0:T(8,128)(2,1)S(1)} %collective-permute-done.12.refs_14_) | copy-start | bytes 24580
  81.0 67.7 %collective-permute-start.13 = (bf16[32,128]{1,0:T(8,128)(2,1)S(1)}, bf16[32,128]{1,0:T(8,128)(2,1)S(1)}, u32[]{:S(2)}, u32[]{:S(2)}) collective-permute-start(bf16[32,128]{1,0:T(8,128)(2,1)S(1)} %copy-done.59), channel_id=1, source_target_pairs={{0,7},{1,6},{2,5},{3,4},{4,3},{5,2},{6,1},{7,0},{8,15},{9,14},{10,... | collective-permute-start | bytes 24584 | tf_op jit(solution)/shard_map/ppermute | solution.py:443
  83.7 65.0 %copy-start.27 = (bf16[4,128,256]{2,1,0:T(8,128)(2,1)S(1)}, bf16[4,128,256]{2,1,0:T(8,128)(2,1)}, u32[]{:S(2)}) copy-start(bf16[4,128,256]{2,1,0:T(8,128)(2,1)} %get-tuple-element.95) | copy-start | bytes 786436
  83.7 66.1 %copy-start.26 = (bf16[4,128,256]{2,1,0:T(8,128)(2,1)S(1)}, bf16[4,128,256]{2,1,0:T(8,128)(2,1)}, u32[]{:S(2)}) copy-start(bf16[4,128,256]{2,1,0:T(8,128)(2,1)} %get-tuple-element.96) | copy-start | bytes 786436
  83.7 68.1 %copy-start.24 = (bf16[4,128,256]{2,1,0:T(8,128)(2,1)S(1)}, bf16[4,128,256]{2,1,0:T(8,128)(2,1)}, u32[]{:S(2)}) copy-start(bf16[4,128,256]{2,1,0:T(8,128)(2,1)} %get-tuple-element.97) | copy-start | bytes 786436
  148.8 18.8 %collective-permute-start.25 = (bf16[4,128,256]{2,1,0:T(8,128)(2,1)S(1)}, bf16[4,128,256]{2,1,0:T(8,128)(2,1)S(1)}, u32[]{:S(2)}, u32[]{:S(2)}) collective-permute-start(bf16[4,128,256]{2,1,0:T(8,128)(2,1)S(1)} %copy-done.27), channel_id=1, source_target_pairs={{0,5},{1,4},{2,7},{3,6},{4,1},{5,0},{6,3},{7,2},{8,13},{9,12},{10,... | collective-permute-start | bytes 786440 | tf_op jit(solution)/shard_map/ppermute | solution.py:443
  149.9 20.0 %collective-permute-start.26 = (bf16[4,128,256]{2,1,0:T(8,128)(2,1)S(1)}, bf16[4,128,256]{2,1,0:T(8,128)(2,1)S(1)}, u32[]{:S(2)}, u32[]{:S(2)}) collective-permute-start(bf16[4,128,256]{2,1,0:T(8,128)(2,1)S(1)} %copy-done.26), channel_id=1, source_target_pairs={{0,6},{1,7},{2,4},{3,5},{4,2},{5,3},{6,0},{7,1},{8,14},{9,15},{10,... | collective-permute-start | bytes 786440 | tf_op jit(solution)/shard_map/ppermute | solution.py:443
  151.8 18.6 %collective-permute-start.27 = (bf16[4,128,256]{2,1,0:T(8,128)(2,1)S(1)}, bf16[4,128,256]{2,1,0:T(8,128)(2,1)S(1)}, u32[]{:S(2)}, u32[]{:S(2)}) collective-permute-start(bf16[4,128,256]{2,1,0:T(8,128)(2,1)S(1)} %copy-done.24), channel_id=1, source_target_pairs={{0,7},{1,6},{2,5},{3,4},{4,3},{5,2},{6,1},{7,0},{8,15},{9,14},{10,... | collective-permute-start | bytes 786440 | tf_op jit(solution)/shard_map/ppermute | solution.py:443
  152.2 19.0 %collective-permute-start = (bf16[4,128,256]{2,1,0:T(8,128)(2,1)}, bf16[4,128,256]{2,1,0:T(8,128)(2,1)S(1)}, u32[]{:S(2)}, u32[]{:S(2)}) collective-permute-start(bf16[4,128,256]{2,1,0:T(8,128)(2,1)} %get-tuple-element.67), channel_id=1, source_target_pairs={{0,1},{1,0},{2,3},{3,2},{4,5},{5,4},{6,7},{7,6},{8,9},{9,8},{10,11... | collective-permute-start | bytes 786440 | tf_op jit(solution)/shard_map/ppermute | solution.py:443
  153.0 18.9 %collective-permute-start.1 = (bf16[4,128,256]{2,1,0:T(8,128)(2,1)}, bf16[4,128,256]{2,1,0:T(8,128)(2,1)S(1)}, u32[]{:S(2)}, u32[]{:S(2)}) collective-permute-start(bf16[4,128,256]{2,1,0:T(8,128)(2,1)} %get-tuple-element.68), channel_id=1, source_target_pairs={{0,2},{1,3},{2,0},{3,1},{4,6},{5,7},{6,4},{7,5},{8,10},{9,11},{10,... | collective-permute-start | bytes 786440 | tf_op jit(solution)/shard_map/ppermute | solution.py:443
  167.6 17.7 %collective-permute-start.2 = (bf16[4,128,256]{2,1,0:T(8,128)(2,1)}, bf16[4,128,256]{2,1,0:T(8,128)(2,1)S(1)}, u32[]{:S(2)}, u32[]{:S(2)}) collective-permute-start(bf16[4,128,256]{2,1,0:T(8,128)(2,1)} %get-tuple-element.69), channel_id=1, source_target_pairs={{0,3},{1,2},{2,1},{3,0},{4,7},{5,6},{6,5},{7,4},{8,11},{9,10},{10,... | collective-permute-start | bytes 786440 | tf_op jit(solution)/shard_map/ppermute | solution.py:443
  169.9 20.6 %collective-permute-start.3 = (bf16[4,128,256]{2,1,0:T(8,128)(2,1)}, bf16[4,128,256]{2,1,0:T(8,128)(2,1)S(1)}, u32[]{:S(2)}, u32[]{:S(2)}) collective-permute-start(bf16[4,128,256]{2,1,0:T(8,128)(2,1)} %get-tuple-element.70), channel_id=1, source_target_pairs={{0,4},{1,5},{2,6},{3,7},{4,0},{5,1},{6,2},{7,3},{8,12},{9,13},{10,... | collective-permute-start | bytes 786440 | tf_op jit(solution)/shard_map/ppermute | solution.py:443
  170.4 23.7 %collective-permute-start.4 = (bf16[4,128,256]{2,1,0:T(8,128)(2,1)}, bf16[4,128,256]{2,1,0:T(8,128)(2,1)S(1)}, u32[]{:S(2)}, u32[]{:S(2)}) collective-permute-start(bf16[4,128,256]{2,1,0:T(8,128)(2,1)} %get-tuple-element.71), channel_id=1, source_target_pairs={{0,5},{1,4},{2,7},{3,6},{4,1},{5,0},{6,3},{7,2},{8,13},{9,12},{10,... | collective-permute-start | bytes 786440 | tf_op jit(solution)/shard_map/ppermute | solution.py:443
  171.2 22.9 %collective-permute-start.5 = (bf16[4,128,256]{2,1,0:T(8,128)(2,1)}, bf16[4,128,256]{2,1,0:T(8,128)(2,1)S(1)}, u32[]{:S(2)}, u32[]{:S(2)}) collective-permute-start(bf16[4,128,256]{2,1,0:T(8,128)(2,1)} %get-tuple-element.72), channel_id=1, source_target_pairs={{0,6},{1,7},{2,4},{3,5},{4,2},{5,3},{6,0},{7,1},{8,14},{9,15},{10,... | collective-permute-start | bytes 786440 | tf_op jit(solution)/shard_map/ppermute | solution.py:443
  172.0 22.1 %collective-permute-start.6 = (bf16[4,128,256]{2,1,0:T(8,128)(2,1)}, bf16[4,128,256]{2,1,0:T(8,128)(2,1)S(1)}, u32[]{:S(2)}, u32[]{:S(2)}) collective-permute-start(bf16[4,128,256]{2,1,0:T(8,128)(2,1)} %get-tuple-element.73), channel_id=1, source_target_pairs={{0,7},{1,6},{2,5},{3,4},{4,3},{5,2},{6,1},{7,0},{8,15},{9,14},{10,... | collective-permute-start | bytes 786440 | tf_op jit(solution)/shard_map/ppermute | solution.py:443
  207.6 4.4 %collective-permute-start.35 = (bf16[32,128]{1,0:T(8,128)(2,1)}, bf16[32,128]{1,0:T(8,128)(2,1)S(1)}, u32[]{:S(2)}, u32[]{:S(2)}) collective-permute-start(bf16[32,128]{1,0:T(8,128)(2,1)} %get-tuple-element.112), channel_id=1, source_target_pairs={{0,1},{1,0},{2,3},{3,2},{4,5},{5,4},{6,7},{7,6},{8,9},{9,8},{10,11... | collective-permute-start | bytes 24584 | tf_op jit(solution)/shard_map/ppermute | solution.py:443
  208.5 4.0 %collective-permute-start.36 = (bf16[32,128]{1,0:T(8,128)(2,1)}, bf16[32,128]{1,0:T(8,128)(2,1)S(1)}, u32[]{:S(2)}, u32[]{:S(2)}) collective-permute-start(bf16[32,128]{1,0:T(8,128)(2,1)} %get-tuple-element.113), channel_id=1, source_target_pairs={{0,2},{1,3},{2,0},{3,1},{4,6},{5,7},{6,4},{7,5},{8,10},{9,11},{10,... | collective-permute-start | bytes 24584 | tf_op jit(solution)/shard_map/ppermute | solution.py:443
  209.0 5.3 %collective-permute-start.37 = (bf16[32,128]{1,0:T(8,128)(2,1)}, bf16[32,128]{1,0:T(8,128)(2,1)S(1)}, u32[]{:S(2)}, u32[]{:S(2)}) collective-permute-start(bf16[32,128]{1,0:T(8,128)(2,1)} %get-tuple-element.114), channel_id=1, source_target_pairs={{0,3},{1,2},{2,1},{3,0},{4,7},{5,6},{6,5},{7,4},{8,11},{9,10},{10,... | collective-permute-start | bytes 24584 | tf_op jit(solution)/shard_map/ppermute | solution.py:443
  209.9 4.4 %collective-permute-start.38 = (bf16[32,128]{1,0:T(8,128)(2,1)}, bf16[32,128]{1,0:T(8,128)(2,1)S(1)}, u32[]{:S(2)}, u32[]{:S(2)}) collective-permute-start(bf16[32,128]{1,0:T(8,128)(2,1)} %get-tuple-element.115), channel_id=1, source_target_pairs={{0,4},{1,5},{2,6},{3,7},{4,0},{5,1},{6,2},{7,3},{8,12},{9,13},{10,... | collective-permute-start | bytes 24584 | tf_op jit(solution)/shard_map/ppermute | solution.py:443
  210.4 3.9 %collective-permute-start.39 = (bf16[32,128]{1,0:T(8,128)(2,1)}, bf16[32,128]{1,0:T(8,128)(2,1)S(1)}, u32[]{:S(2)}, u32[]{:S(2)}) collective-permute-start(bf16[32,128]{1,0:T(8,128)(2,1)} %get-tuple-element.116), channel_id=1, source_target_pairs={{0,5},{1,4},{2,7},{3,6},{4,1},{5,0},{6,3},{7,2},{8,13},{9,12},{10,... | collective-permute-start | bytes 24584 | tf_op jit(solution)/shard_map/ppermute | solution.py:443
  212.0 4.8 %collective-permute-start.40 = (bf16[32,128]{1,0:T(8,128)(2,1)}, bf16[32,128]{1,0:T(8,128)(2,1)S(1)}, u32[]{:S(2)}, u32[]{:S(2)}) collective-permute-start(bf16[32,128]{1,0:T(8,128)(2,1)} %get-tuple-element.117), channel_id=1, source_target_pairs={{0,6},{1,7},{2,4},{3,5},{4,2},{5,3},{6,0},{7,1},{8,14},{9,15},{10,... | collective-permute-start | bytes 24584 | tf_op jit(solution)/shard_map/ppermute | solution.py:443
  212.5 42.5 %copy-start.43 = (bf16[3,128,256]{2,1,0:T(8,128)(2,1)S(1)}, bf16[3,128,256]{2,1,0:T(8,128)(2,1)}, u32[]{:S(2)}) copy-start(bf16[3,128,256]{2,1,0:T(8,128)(2,1)} %get-tuple-element.85) | copy-start | bytes 589828
  212.5 4.3 %collective-permute-start.41 = (bf16[32,128]{1,0:T(8,128)(2,1)}, bf16[32,128]{1,0:T(8,128)(2,1)S(1)}, u32[]{:S(2)}, u32[]{:S(2)}) collective-permute-start(bf16[32,128]{1,0:T(8,128)(2,1)} %get-tuple-element.118), channel_id=1, source_target_pairs={{0,7},{1,6},{2,5},{3,4},{4,3},{5,2},{6,1},{7,0},{8,15},{9,14},{10,... | collective-permute-start | bytes 24584 | tf_op jit(solution)/shard_map/ppermute | solution.py:443
  216.8 38.9 %copy-start.41 = (bf16[3,128,256]{2,1,0:T(8,128)(2,1)S(1)}, bf16[3,128,256]{2,1,0:T(8,128)(2,1)}, u32[]{:S(2)}) copy-start(bf16[3,128,256]{2,1,0:T(8,128)(2,1)} %get-tuple-element.86) | copy-start | bytes 589828
  216.8 40.4 %copy-start.40 = (bf16[3,128,256]{2,1,0:T(8,128)(2,1)S(1)}, bf16[3,128,256]{2,1,0:T(8,128)(2,1)}, u32[]{:S(2)}) copy-start(bf16[3,128,256]{2,1,0:T(8,128)(2,1)} %get-tuple-element.87) | copy-start | bytes 589828
  217.3 39.9 %copy-start.39 = (bf16[3,128,256]{2,1,0:T(8,128)(2,1)S(1)}, bf16[3,128,256]{2,1,0:T(8,128)(2,1)}, u32[]{:S(2)}) copy-start(bf16[3,128,256]{2,1,0:T(8,128)(2,1)} %get-tuple-element.88) | copy-start | bytes 589828
  217.3 42.8 %copy-start.38 = (bf16[3,128,256]{2,1,0:T(8,128)(2,1)S(1)}, bf16[3,128,256]{2,1,0:T(8,128)(2,1)}, u32[]{:S(2)}) copy-start(bf16[3,128,256]{2,1,0:T(8,128)(2,1)} %get-tuple-element.89) | copy-start | bytes 589828
  219.9 8.5 %collective-permute-start.42 = (f32[16,2304]{1,0:T(8,128)}, f32[16,2304]{1,0:T(8,128)S(1)}, u32[]{:S(2)}, u32[]{:S(2)}) collective-permute-start(f32[16,2304]{1,0:T(8,128)} %get-tuple-element.122), channel_id=1, source_target_pairs={{0,8},{8,0},{16,24},{24,16},{1,9},{9,1},{17,25},{25,17},{2,10},{10... | collective-permute-start | bytes 442376 | tf_op jit(solution)/shard_map/ppermute | solution.py:443
  221.6 14.2 %collective-permute-start.43 = (f32[16,2304]{1,0:T(8,128)}, f32[16,2304]{1,0:T(8,128)S(1)}, u32[]{:S(2)}, u32[]{:S(2)}) collective-permute-start(f32[16,2304]{1,0:T(8,128)} %get-tuple-element.123), channel_id=1, source_target_pairs={{0,16},{8,24},{16,0},{24,8},{1,17},{9,25},{17,1},{25,9},{2,18},{10... | collective-permute-start | bytes 442376 | tf_op jit(solution)/shard_map/ppermute | solution.py:443
  224.2 13.0 %collective-permute-start.44 = (f32[16,2304]{1,0:T(8,128)}, f32[16,2304]{1,0:T(8,128)S(1)}, u32[]{:S(2)}, u32[]{:S(2)}) collective-permute-start(f32[16,2304]{1,0:T(8,128)} %get-tuple-element.124), channel_id=1, source_target_pairs={{0,24},{8,16},{16,8},{24,0},{1,25},{9,17},{17,9},{25,1},{2,26},{10... | collective-permute-start | bytes 442376 | tf_op jit(solution)/shard_map/ppermute | solution.py:443
  224.4 13.8 %collective-permute-start.28 = (bf16[3,128,256]{2,1,0:T(8,128)(2,1)S(1)}, bf16[3,128,256]{2,1,0:T(8,128)(2,1)S(1)}, u32[]{:S(2)}, u32[]{:S(2)}) collective-permute-start(bf16[3,128,256]{2,1,0:T(8,128)(2,1)S(1)} %copy-done.51), channel_id=1, source_target_pairs={{0,1},{1,0},{2,3},{3,2},{4,5},{5,4},{6,7},{7,6},{8,9},{9,8},{10,11... | collective-permute-start | bytes 589832 | tf_op jit(solution)/shard_map/ppermute | solution.py:443
  224.4 14.6 %collective-permute-start.29 = (bf16[3,128,256]{2,1,0:T(8,128)(2,1)S(1)}, bf16[3,128,256]{2,1,0:T(8,128)(2,1)S(1)}, u32[]{:S(2)}, u32[]{:S(2)}) collective-permute-start(bf16[3,128,256]{2,1,0:T(8,128)(2,1)S(1)} %copy-done.50), channel_id=1, source_target_pairs={{0,2},{1,3},{2,0},{3,1},{4,6},{5,7},{6,4},{7,5},{8,10},{9,11},{10,... | collective-permute-start | bytes 589832 | tf_op jit(solution)/shard_map/ppermute | solution.py:443
  228.5 13.0 %collective-permute-start.30 = (bf16[3,128,256]{2,1,0:T(8,128)(2,1)S(1)}, bf16[3,128,256]{2,1,0:T(8,128)(2,1)S(1)}, u32[]{:S(2)}, u32[]{:S(2)}) collective-permute-start(bf16[3,128,256]{2,1,0:T(8,128)(2,1)S(1)} %copy-done.49), channel_id=1, source_target_pairs={{0,3},{1,2},{2,1},{3,0},{4,7},{5,6},{6,5},{7,4},{8,11},{9,10},{10,... | collective-permute-start | bytes 589832 | tf_op jit(solution)/shard_map/ppermute | solution.py:443
  235.8 5.8 %collective-permute-start.31 = (bf16[3,128,256]{2,1,0:T(8,128)(2,1)S(1)}, bf16[3,128,256]{2,1,0:T(8,128)(2,1)S(1)}, u32[]{:S(2)}, u32[]{:S(2)}) collective-permute-start(bf16[3,128,256]{2,1,0:T(8,128)(2,1)S(1)} %copy-done.48), channel_id=1, source_target_pairs={{0,4},{1,5},{2,6},{3,7},{4,0},{5,1},{6,2},{7,3},{8,12},{9,13},{10,... | collective-permute-start | bytes 589832 | tf_op jit(solution)/shard_map/ppermute | solution.py:443
  238.2 4.1 %collective-permute-start.45 = (f32[16,2304]{1,0:T(8,128)S(1)}, f32[16,2304]{1,0:T(8,128)S(1)}, u32[]{:S(2)}, u32[]{:S(2)}) collective-permute-start(f32[16,2304]{1,0:T(8,128)S(1)} %add_add_fusion), channel_id=1, source_target_pairs={{0,1},{1,0},{2,3},{3,2},{4,5},{5,4},{6,7},{7,6},{8,9},{9,8},{10,11... | collective-permute-start | bytes 442376 | tf_op jit(solution)/shard_map/ppermute | solution.py:520
  238.3 15.3 %collective-permute-start.32 = (bf16[3,128,256]{2,1,0:T(8,128)(2,1)S(1)}, bf16[3,128,256]{2,1,0:T(8,128)(2,1)S(1)}, u32[]{:S(2)}, u32[]{:S(2)}) collective-permute-start(bf16[3,128,256]{2,1,0:T(8,128)(2,1)S(1)} %copy-done.45), channel_id=1, source_target_pairs={{0,5},{1,4},{2,7},{3,6},{4,1},{5,0},{6,3},{7,2},{8,13},{9,12},{10,... | collective-permute-start | bytes 589832 | tf_op jit(solution)/shard_map/ppermute | solution.py:443
  239.0 16.0 %collective-permute-start.33 = (bf16[3,128,256]{2,1,0:T(8,128)(2,1)S(1)}, bf16[3,128,256]{2,1,0:T(8,128)(2,1)S(1)}, u32[]{:S(2)}, u32[]{:S(2)}) collective-permute-start(bf16[3,128,256]{2,1,0:T(8,128)(2,1)S(1)} %copy-done.44), channel_id=1, source_target_pairs={{0,6},{1,7},{2,4},{3,5},{4,2},{5,3},{6,0},{7,1},{8,14},{9,15},{10,... | collective-permute-start | bytes 589832 | tf_op jit(solution)/shard_map/ppermute | solution.py:443
  241.5 14.1 %collective-permute-start.34 = (bf16[3,128,256]{2,1,0:T(8,128)(2,1)S(1)}, bf16[3,128,256]{2,1,0:T(8,128)(2,1)S(1)}, u32[]{:S(2)}, u32[]{:S(2)}) collective-permute-start(bf16[3,128,256]{2,1,0:T(8,128)(2,1)S(1)} %copy-done.42), channel_id=1, source_target_pairs={{0,7},{1,6},{2,5},{3,4},{4,3},{5,2},{6,1},{7,0},{8,15},{9,14},{10,... | collective-permute-start | bytes 589832 | tf_op jit(solution)/shard_map/ppermute | solution.py:443
  241.6 15.5 %collective-permute-start.14 = (bf16[3,128,256]{2,1,0:T(8,128)(2,1)S(1)}, bf16[3,128,256]{2,1,0:T(8,128)(2,1)S(1)}, u32[]{:S(2)}, u32[]{:S(2)}) collective-permute-start(bf16[3,128,256]{2,1,0:T(8,128)(2,1)S(1)} %copy-done.47), channel_id=1, source_target_pairs={{0,1},{1,0},{2,3},{3,2},{4,5},{5,4},{6,7},{7,6},{8,9},{9,8},{10,11... | collective-permute-start | bytes 589832 | tf_op jit(solution)/shard_map/ppermute | solution.py:443
  242.2 15.0 %collective-permute-start.15 = (bf16[3,128,256]{2,1,0:T(8,128)(2,1)S(1)}, bf16[3,128,256]{2,1,0:T(8,128)(2,1)S(1)}, u32[]{:S(2)}, u32[]{:S(2)}) collective-permute-start(bf16[3,128,256]{2,1,0:T(8,128)(2,1)S(1)} %copy-done.46), channel_id=1, source_target_pairs={{0,2},{1,3},{2,0},{3,1},{4,6},{5,7},{6,4},{7,5},{8,10},{9,11},{10,... | collective-permute-start | bytes 589832 | tf_op jit(solution)/shard_map/ppermute | solution.py:443
  253.6 6.6 %collective-permute-start.46 = (f32[16,2304]{1,0:T(8,128)S(1)}, f32[16,2304]{1,0:T(8,128)S(1)}, u32[]{:S(2)}, u32[]{:S(2)}) collective-permute-start(f32[16,2304]{1,0:T(8,128)S(1)} %add.35), channel_id=1, source_target_pairs={{0,2},{1,3},{2,0},{3,1},{4,6},{5,7},{6,4},{7,5},{8,10},{9,11},{10,... | collective-permute-start | bytes 442376 | tf_op jit(solution)/shard_map/ppermute | solution.py:520
  255.0 8.9 %collective-permute-start.16 = (bf16[3,128,256]{2,1,0:T(8,128)(2,1)S(1)}, bf16[3,128,256]{2,1,0:T(8,128)(2,1)S(1)}, u32[]{:S(2)}, u32[]{:S(2)}) collective-permute-start(bf16[3,128,256]{2,1,0:T(8,128)(2,1)S(1)} %copy-done.43), channel_id=1, source_target_pairs={{0,3},{1,2},{2,1},{3,0},{4,7},{5,6},{6,5},{7,4},{8,11},{9,10},{10,... | collective-permute-start | bytes 589832 | tf_op jit(solution)/shard_map/ppermute | solution.py:443
  255.6 10.0 %collective-permute-start.17 = (bf16[3,128,256]{2,1,0:T(8,128)(2,1)S(1)}, bf16[3,128,256]{2,1,0:T(8,128)(2,1)S(1)}, u32[]{:S(2)}, u32[]{:S(2)}) collective-permute-start(bf16[3,128,256]{2,1,0:T(8,128)(2,1)S(1)} %copy-done.41), channel_id=1, source_target_pairs={{0,4},{1,5},{2,6},{3,7},{4,0},{5,1},{6,2},{7,3},{8,12},{9,13},{10,... | collective-permute-start | bytes 589832 | tf_op jit(solution)/shard_map/ppermute | solution.py:443
  257.1 17.9 %collective-permute-start.18 = (bf16[3,128,256]{2,1,0:T(8,128)(2,1)S(1)}, bf16[3,128,256]{2,1,0:T(8,128)(2,1)S(1)}, u32[]{:S(2)}, u32[]{:S(2)}) collective-permute-start(bf16[3,128,256]{2,1,0:T(8,128)(2,1)S(1)} %copy-done.40), channel_id=1, source_target_pairs={{0,5},{1,4},{2,7},{3,6},{4,1},{5,0},{6,3},{7,2},{8,13},{9,12},{10,... | collective-permute-start | bytes 589832 | tf_op jit(solution)/shard_map/ppermute | solution.py:443
  257.3 17.8 %collective-permute-start.19 = (bf16[3,128,256]{2,1,0:T(8,128)(2,1)S(1)}, bf16[3,128,256]{2,1,0:T(8,128)(2,1)S(1)}, u32[]{:S(2)}, u32[]{:S(2)}) collective-permute-start(bf16[3,128,256]{2,1,0:T(8,128)(2,1)S(1)} %copy-done.39), channel_id=1, source_target_pairs={{0,6},{1,7},{2,4},{3,5},{4,2},{5,3},{6,0},{7,1},{8,14},{9,15},{10,... | collective-permute-start | bytes 589832 | tf_op jit(solution)/shard_map/ppermute | solution.py:443
  260.2 14.9 %collective-permute-start.20 = (bf16[3,128,256]{2,1,0:T(8,128)(2,1)S(1)}, bf16[3,128,256]{2,1,0:T(8,128)(2,1)S(1)}, u32[]{:S(2)}, u32[]{:S(2)}) collective-permute-start(bf16[3,128,256]{2,1,0:T(8,128)(2,1)S(1)} %copy-done.38), channel_id=1, source_target_pairs={{0,7},{1,6},{2,5},{3,4},{4,3},{5,2},{6,1},{7,0},{8,15},{9,14},{10,... | collective-permute-start | bytes 589832 | tf_op jit(solution)/shard_map/ppermute | solution.py:443
  263.9 108.8 %collective-permute-start.47 = (f32[16,2304]{1,0:T(8,128)S(1)}, f32[16,2304]{1,0:T(8,128)S(1)}, u32[]{:S(2)}, u32[]{:S(2)}) collective-permute-start(f32[16,2304]{1,0:T(8,128)S(1)} %add.36), channel_id=1, source_target_pairs={{0,4},{1,5},{2,6},{3,7},{4,0},{5,1},{6,2},{7,3},{8,12},{9,13},{10,... | collective-permute-start | bytes 442376 | tf_op jit(solution)/shard_map/ppermute | solution.py:520
  (46 other events, 735.4 us)

commit v2 on v1

v2 whole, which is shorter than its diff:
```python
import functools
import math

import jax
import jax.numpy as jnp
from jax import lax
from jax.experimental import pallas as pl
from jax.experimental.pallas import tpu as pltpu
from jax.sharding import PartitionSpec as P

H = 32
HD = 128
RANK = 8
ADAPTER_ALPHA = 16
SCALING = 1.0 / math.sqrt(HD)
LOG2E = 1.4426950408889634
BF16 = jnp.bfloat16
F32 = jnp.float32
NT = (((1,), (1,)), ((), ()))
MIB = 1024 * 1024
COST = pl.CostEstimate(flops=0, bytes_accessed=0, transcendentals=0)
ATTENTION_COST = pl.CostEstimate(flops=10**10, bytes_accessed=0, transcendentals=0)
WHOLE_IN = (False, False)
WHOLE_OUT = (False, False)
ORDER = (6, 2, 4, 7, 3, 5, 1)
CHAIN = tuple((place, max(1, place - 3)) for place in range(1, 8))
PLAN = (
    ((6, 2, 4), ()),
    ((), ()),
    ((7, 3), ()),
    ((5, 1), (6, 2)),
    ((), (4,)),
)


def params(mebibytes):
    return pltpu.CompilerParams(vmem_limit_bytes=mebibytes * MIB)


def offsets_of(count):
    return (0,) + ORDER if count == 1 + len(ORDER) else tuple(range(count))


def pair_offsets(members):
    return [offset for offset in offsets_of(members) if offset % 2 == 0]


def part_of(refs, me, offset):
    if len(refs) == 1:
        return refs[0].at[me ^ offset]
    return refs[offsets_of(len(refs)).index(offset)]


def group_shapes(whole, members, shape, dtype):
    if whole:
        return [jax.ShapeDtypeStruct((members,) + shape, dtype)]
    return [jax.ShapeDtypeStruct(shape, dtype)] * members


def any_specs(count):
    return [pl.BlockSpec(memory_space=pl.ANY)] * count


def vmem_specs(count):
    return [pl.BlockSpec(memory_space=pltpu.VMEM)] * count


def dot_nt(left, right):
    return lax.dot_general(left, right, NT, preferred_element_type=F32)


def two_parts(value):
    high = value.astype(BF16)
    low = (value - high.astype(F32)).astype(BF16)
    return high, low


def three_parts(value):
    high, _ = two_parts(value)
    rest = value - high.astype(F32)
    middle, low = two_parts(rest)
    return high, middle, low


def side_rows(out_ref, grad_ref, hidden_ref, downq_ref, downv_ref):
    product = out_ref[...].astype(F32) * grad_ref[...].astype(F32)
    heads_at = lax.broadcasted_iota(jnp.int32, (H * HD, 128), 0) // HD
    lanes = lax.broadcasted_iota(jnp.int32, (H * HD, 128), 1)
    pick = jnp.where(heads_at == lanes, 1.0, 0.0).astype(BF16)
    high, middle, low = (
        jnp.dot(part, pick, preferred_element_type=F32) for part in three_parts(product)
    )
    delta = (high + (middle + low)).T[:H]
    downs = jnp.concatenate([downq_ref[...], downv_ref[...]], axis=0)
    return three_parts(delta), dot_nt(downs, hidden_ref[...]).astype(BF16)


def pack_kernel(members, heads_here, first_head, stage_heads, with_side, whole, *refs):
    refs = list(refs)
    sources = [refs.pop(0) for _ in range(4)]
    side_refs = [refs.pop(0) for _ in range(5 if with_side else 0)]
    messages = [refs.pop(0) for _ in range(1 if whole else members)]
    held, in_sems, out_sems = refs
    me = lax.axis_index("seq")
    rows = sources[0].shape[0]
    reads = []
    for offset in range(members):
        target = me ^ offset
        for head in range(stage_heads):
            start = pl.multiple_of((target * heads_here + first_head + head) * HD, HD)
            for which in range(4):
                place = head * 4 + which
                reads.append(
                    pltpu.make_async_copy(
                        sources[which].at[:, pl.ds(start, HD)],
                        held.at[target, place * rows : (place + 1) * rows],
                        in_sems.at[offset, place],
                    )
                )
    writes = [
        pltpu.make_async_copy(
            held.at[me ^ offset], part_of(messages, me, offset), out_sems.at[offset]
        )
        for offset in range(members)
    ]
    for copy in reads:
        copy.start()
    if with_side:
        parts, lows = side_rows(*side_refs)
        blank = jnp.zeros((16 - 3 * heads_here, rows), BF16)
        for member in range(members):
            here = slice(member * heads_here, (member + 1) * heads_here)
            held[member, 4 * stage_heads * rows :] = jnp.concatenate(
                [part[here] for part in parts] + [blank, lows], axis=0
            )
    per_message = 4 * stage_heads
    for offset in range(members):
        for place in range(per_message):
            reads[offset * per_message + place].wait()
        writes[offset].start()
    for copy in writes:
        copy.wait()


def pack(sources, side_sources, members, heads_here, first_head, stage_heads, whole):
    rows = sources[0].shape[0]
    shape = (4 * stage_heads * rows + (32 if side_sources else 0), HD)
    size = 2 * 4 * rows * stage_heads * HD * members * 2
    return pl.pallas_call(
        functools.partial(
            pack_kernel, members, heads_here, first_head, stage_heads, bool(side_sources), whole
        ),
        out_shape=group_shapes(whole, members, shape, BF16),
        in_specs=any_specs(4) + vmem_specs(len(side_sources)),
        out_specs=any_specs(1 if whole else members),
        scratch_shapes=[
            pltpu.VMEM((members,) + shape, BF16),
            pltpu.SemaphoreType.DMA((members, 4 * stage_heads)),
            pltpu.SemaphoreType.DMA((members,)),
        ],
        compiler_params=params(56),
        cost_estimate=COST,
        name="pack",
    )(*sources, *side_sources)


def begin_of(lengths_ref, positions):
    begin = jnp.int32(0) * positions
    start = jnp.int32(0)
    for index in range(lengths_ref.shape[1] - 1):
        start = start + lengths_ref[0, index]
        begin = jnp.where(positions >= start, start, begin)
    return begin


def attention_kernel(
    members,
    heads_here,
    first_head,
    stage_heads,
    counts,
    lengths_ref,
    upq_ref,
    upv_ref,
    cos_ref,
    sin_ref,
    *refs,
):
    refs = list(refs)
    messages, sides, outs, backs = [], [], [], []
    for group, count in zip((messages, sides), counts):
        group.extend(refs.pop(0) for _ in range(count))
    sides = sides or messages
    earlier_back = None if first_head == 0 else refs.pop(0)
    for group, count in zip((outs, backs), counts[2:]):
        group.extend(refs.pop(0) for _ in range(count))
    last = first_head + stage_heads == heads_here
    terms_ref = refs.pop(0)
    held, side_held, key_flip, grads, key_acc, value_acc, back_ref = refs[:7]
    in_sems, side_sems, out_sems = refs[7:]
    me = lax.axis_index("seq")
    total = held.shape[1]
    rows = total // members
    side_low = sides[0].shape[-2] - 32
    block = min(256, total)
    reach = total // 2
    rows_of = [
        pl.ds(pl.multiple_of((me ^ offset) * rows, rows), rows) for offset in range(members)
    ]
    copies = []
    for offset in range(members):
        for place in range(4 * stage_heads):
            copies.append(
                pltpu.make_async_copy(
                    part_of(messages, me, offset).at[place * rows : (place + 1) * rows],
                    held.at[place, rows_of[offset], :],
                    in_sems.at[offset, place],
                )
            )
        copies.append(
            pltpu.make_async_copy(
                part_of(sides, me, offset).at[side_low : side_low + 32],
                side_held.at[:, rows_of[offset]],
                side_sems.at[offset],
            )
        )
    for copy in copies:
        copy.start()
    key_acc[...] = jnp.zeros_like(key_acc)
    value_acc[...] = jnp.zeros_like(value_acc)
    terms_ref[...] = jnp.zeros_like(terms_ref)
    for copy in copies:
        copy.wait()
    columns = [slice(head * HD, (head + 1) * HD) for head in range(stage_heads)]
    for head in range(stage_heads):
        key_flip[head] = held[4 * head + 1].astype(F32).T.astype(BF16)

    def query_block(low, key_low, width):
        positions = low + lax.broadcasted_iota(jnp.int32, (1, block), 1)
        begin = begin_of(lengths_ref, positions)
        key_positions = key_low + lax.broadcasted_iota(jnp.int32, (width, block), 0)
        allowed = (key_positions >= begin) & (key_positions <= positions)
        bias = jnp.where(allowed, 0.0, -1e30).astype(F32)
        here = pl.ds(low, block)
        keys_here = pl.ds(key_low, width)
        cosine = cos_ref[:, here]
        sine = sin_ref[:, here]
        back_query = jnp.zeros((RANK, block), F32)
        parts = side_held[0:16, here].astype(F32)
        for head in range(stage_heads):
            cols = columns[head]
            query = held[4 * head, here, :]
            grad = held[4 * head + 3, here, :]
            scores = dot_nt(held[4 * head + 1, keys_here, :], query) + bias
            grad_prob = dot_nt(held[4 * head + 2, keys_here, :], grad)
            top = jnp.max(scores, axis=0, keepdims=True)
            weights = jnp.exp2((scores - top) * (SCALING * LOG2E))
            inverse = 1.0 / jnp.sum(weights, axis=0, keepdims=True)
            probs = weights * inverse
            row = first_head + head
            delta = sum(
                parts[place : place + 1] for place in range(row, 3 * heads_here, heads_here)
            )
            grad_score = (probs * (grad_prob - delta)).astype(BF16)
            value_acc[head, keys_here, :] += jnp.dot(
                probs.astype(BF16), grad, preferred_element_type=F32
            )
            key_acc[head, keys_here, :] += jnp.dot(grad_score, query, preferred_element_type=F32)
            flipped = SCALING * jnp.dot(
                key_flip[head, :, keys_here], grad_score, preferred_element_type=F32
            )
            grads[0, here, cols] = flipped.T.astype(BF16)
            rounded = flipped.astype(BF16).astype(F32)
            first = rounded[: HD // 2]
            second = rounded[HD // 2 :]
            before = jnp.concatenate(
                [first * cosine + second * sine, second * cosine - first * sine], axis=0
            ).astype(BF16)
            back_query += jnp.dot(upq_ref[:, cols], before, preferred_element_type=F32)
            terms_ref[0:RANK, cols] += dot_nt(side_held[16:24, here], before)
        back_ref[0:RANK, here] = back_query

    widths = [block + part * reach // 4 for part in range(5)]

    @pl.loop(0, total // block)
    def _(index):
        low = pl.multiple_of(index * block, block)
        needed = low + block - begin_of(lengths_ref, low)
        for place, width in enumerate(widths):
            fits = needed <= width
            if place:
                fits = fits & (needed > widths[place - 1])

            @pl.when(fits)
            def _(width=width):
                key_low = pl.multiple_of(jnp.maximum(low + block - width, 0), 128)
                query_block(low, key_low, width)

    back_value = jnp.zeros((RANK, total), F32)
    for head in range(stage_heads):
        cols = columns[head]
        grads[1, :, cols] = (key_acc[head] * SCALING).astype(BF16)
        value_grad = value_acc[head].astype(BF16)
        grads[2, :, cols] = value_grad
        back_value += dot_nt(upv_ref[:, cols], value_grad)
        terms_ref[RANK : 2 * RANK, cols] = jnp.dot(
            side_held[24:32, :], value_grad, preferred_element_type=F32
        )
    back_ref[RANK : 2 * RANK, :] = back_value
    copies = [
        pltpu.make_async_copy(
            grads.at[:, rows_of[offset], :], part_of(outs, me, offset), out_sems.at[offset]
        )
        for offset in range(members)
    ]
    for copy in copies:
        copy.start()
    back = back_ref[...]
    if earlier_back is not None:
        back = back + earlier_back[...]
    if last:
        back_ref[...] = back
        for place, offset in enumerate(pair_offsets(members)):
            for group, flip in zip(backs, (0, 1)):
                group[place] = back_ref[:, rows_of[offset ^ flip]]
    else:
        backs[0][...] = back
    for copy in copies:
        copy.wait()


def attention(
    lengths,
    ups,
    turns,
    messages,
    sides,
    earlier_back,
    heads_here,
    first_head,
    stage_heads,
    members,
    rows,
    whole_out,
):
    total = rows * members
    width = stage_heads * HD
    last = first_head + stage_heads == heads_here
    out_shapes = group_shapes(whole_out, members, (3, rows, width), BF16)
    back_shapes = [jax.ShapeDtypeStruct((2 * RANK, total), F32)]
    if last:
        back_shapes = [jax.ShapeDtypeStruct((members // 2, 2 * RANK, rows), F32)] * 2
    earlier = [] if first_head == 0 else list(sides) + [earlier_back]
    counts = (len(messages), len(earlier[:-1]), len(out_shapes), len(back_shapes))
    results = pl.pallas_call(
        functools.partial(attention_kernel, members, heads_here, first_head, stage_heads, counts),
        out_shape=out_shapes + back_shapes + [jax.ShapeDtypeStruct((2 * RANK, width), F32)],
        in_specs=[pl.BlockSpec(memory_space=pltpu.SMEM)]
        + vmem_specs(4)
        + any_specs(len(messages))
        + (any_specs(len(sides)) + vmem_specs(1) if earlier else []),
        out_specs=any_specs(len(out_shapes)) + vmem_specs(len(back_shapes) + 1),
        scratch_shapes=[
            pltpu.VMEM((4 * stage_heads, total, HD), BF16),
            pltpu.VMEM((32, total), BF16),
            pltpu.VMEM((stage_heads, HD, total), BF16),
            pltpu.VMEM((3, total, width), BF16),
            pltpu.VMEM((stage_heads, total, HD), F32),
            pltpu.VMEM((stage_heads, total, HD), F32),
            pltpu.VMEM((2 * RANK, total), F32),
            pltpu.SemaphoreType.DMA((members, 4 * stage_heads)),
            pltpu.SemaphoreType.DMA((members,)),
            pltpu.SemaphoreType.DMA((members,)),
        ],
        compiler_params=params(56),
        cost_estimate=ATTENTION_COST,
        name="attention",
    )(lengths, *ups, *turns, *messages, *earlier)
    split = len(out_shapes)
    return results[:split], results[split:-1], results[-1]


def fold_kernel(own_ref, other_ref, *outs):
    for place, out in enumerate(outs):
        out[...] = own_ref[place] + other_ref[place]


def fold(own, other):
    count = own.shape[0]
    return pl.pallas_call(
        fold_kernel,
        out_shape=[jax.ShapeDtypeStruct(own.shape[1:], F32)] * count,
        in_specs=vmem_specs(2),
        out_specs=vmem_specs(count),
        compiler_params=params(4),
        cost_estimate=COST,
        name="fold",
    )(own, other)


def down_kernel(members, packs, stage_sizes, hidden_ref, *refs):
    backs = refs[: members // 2]
    ups = refs[members // 2 : members // 2 + len(stage_sizes)]
    messages = refs[members // 2 + len(stage_sizes) :][:packs]
    held, sems = refs[members // 2 + len(stage_sizes) + packs :]
    me = lax.axis_index("seq")
    pack_here = lax.axis_index("dp")
    total = backs[0][...]
    for back in backs[1:]:
        total = total + back[...]
    terms = jnp.dot(total.astype(BF16), hidden_ref[...], preferred_element_type=F32)
    down_cols = terms.shape[1] // packs
    sharers = members // packs
    for target in range(packs):
        held[target, :, :down_cols] = terms[:, target * down_cols : (target + 1) * down_cols]
        low = down_cols
        for size, up in zip(stage_sizes, ups):
            held[target, :, low : low + size * HD] = jnp.where(
                me // sharers == target, up[...], 0.0
            )
            low += size * HD
    copies = [
        pltpu.make_async_copy(held.at[pack_here ^ offset], messages[offset], sems.at[offset])
        for offset in range(packs)
    ]
    for copy in copies:
        copy.start()
    for copy in copies:
        copy.wait()


def down_terms(hidden, backs, ups, members, packs):
    stage_sizes = [up.shape[1] // HD for up in ups]
    width = hidden.shape[1] // packs + sum(stage_sizes) * HD
    return pl.pallas_call(
        functools.partial(down_kernel, members, packs, stage_sizes),
        out_shape=[jax.ShapeDtypeStruct((2 * RANK, width), F32)] * packs,
        in_specs=vmem_specs(1 + len(backs) + len(ups)),
        out_specs=any_specs(packs),
        scratch_shapes=[
            pltpu.VMEM((packs, 2 * RANK, width), F32),
            pltpu.SemaphoreType.DMA((packs,)),
        ],
        compiler_params=params(8),
        cost_estimate=COST,
        name="down_terms",
    )(hidden, *backs, *ups)


def packs_kernel(sharers, down_cols, *refs):
    pieces, out = refs[:-1], refs[-1]
    me = lax.axis_index("seq")
    total = pieces[0][...]
    for piece in pieces[1:]:
        total = total + piece[...]
    out[:, :down_cols] = total[:, :down_cols]
    size = total.shape[1] - down_cols
    for place in range(sharers):
        low = down_cols + place * size
        out[:, low : low + size] = jnp.where(me % sharers == place, total[:, down_cols:], 0.0)


def sum_packs(pieces, sharers, down_cols):
    width = down_cols + sharers * (pieces[0].shape[1] - down_cols)
    return pl.pallas_call(
        functools.partial(packs_kernel, sharers, down_cols),
        out_shape=jax.ShapeDtypeStruct((2 * RANK, width), F32),
        in_specs=vmem_specs(len(pieces)),
        out_specs=vmem_specs(1)[0],
        compiler_params=params(4),
        cost_estimate=COST,
        name="sum_packs",
    )(*pieces)


def finish_kernel(down_cols, *refs):
    pieces, outs = refs[:-4], refs[-4:]
    total = pieces[0][...]
    for piece in pieces[1:]:
        total = total + piece[...]
    total = total * (ADAPTER_ALPHA / RANK)
    outs[0][...] = total[:RANK, :down_cols]
    outs[1][...] = total[:RANK, down_cols:]
    outs[2][...] = total[RANK:, :down_cols]
    outs[3][...] = total[RANK:, down_cols:]


def finish(pieces, down_cols):
    up_cols = pieces[0].shape[1] - down_cols
    return pl.pallas_call(
        functools.partial(finish_kernel, down_cols),
        out_shape=[jax.ShapeDtypeStruct((RANK, cols), F32) for cols in (down_cols, up_cols)] * 2,
        in_specs=vmem_specs(len(pieces)),
        out_specs=vmem_specs(4),
        compiler_params=params(4),
        cost_estimate=COST,
        name="finish",
    )(*pieces)


def unpack_kernel(members, heads_here, stages, counts, *refs):
    count = sum(counts)
    groups = [refs[sum(counts[:i]) : sum(counts[: i + 1])] for i in range(len(counts))]
    outs = refs[count : count + 3]
    held = refs[count + 3 : count + 3 + len(stages)]
    in_sems, out_sems = refs[count + 3 + len(stages) :]
    me = lax.axis_index("seq")
    reads = []
    writes = []
    for stage, (first_head, stage_heads) in enumerate(stages):
        for offset in range(members):
            source = me ^ offset
            start = pl.multiple_of((source * heads_here + first_head) * HD, HD)
            reads.append(
                pltpu.make_async_copy(
                    part_of(groups[stage], me, offset),
                    held[stage].at[offset],
                    in_sems.at[stage, offset],
                )
            )
            writes.append(
                [
                    pltpu.make_async_copy(
                        held[stage].at[offset, which],
                        outs[which].at[:, pl.ds(start, stage_heads * HD)],
                        out_sems.at[stage, offset, which],
                    )
                    for which in range(3)
                ]
            )
    for copy in reads:
        copy.start()
    for copy, followers in zip(reads, writes):
        copy.wait()
        for follower in followers:
            follower.start()
    for followers in writes:
        for follower in followers:
            follower.wait()


def unpack(groups, members, heads_here, stages):
    rows = groups[0][0].shape[-2]
    counts = [len(group) for group in groups]
    messages = [message for group in groups for message in group]
    width = members * heads_here * HD
    return pl.pallas_call(
        functools.partial(unpack_kernel, members, heads_here, stages, counts),
        out_shape=[jax.ShapeDtypeStruct((rows, width), BF16)] * 3,
        in_specs=any_specs(len(messages)),
        out_specs=any_specs(3),
        scratch_shapes=[
            pltpu.VMEM((members, 3, rows, stage_heads * HD), BF16) for _, stage_heads in stages
        ]
        + [
            pltpu.SemaphoreType.DMA((len(stages), members)),
            pltpu.SemaphoreType.DMA((len(stages), members, 3)),
        ],
        compiler_params=params(56),
        cost_estimate=COST,
        name="unpack",
    )(*messages)


def exchange(messages, axis):
    count = len(messages)
    if count == 1:
        return [lax.all_to_all(messages[0], axis, split_axis=0, concat_axis=0, tiled=True)]
    return [
        lax.ppermute(message, axis, [(i, i ^ offset) for i in range(count)]) if offset else message
        for offset, message in zip(offsets_of(count), messages)
    ]


def turn_tables(lengths_row, total):
    positions = jnp.arange(total, dtype=jnp.int32)
    ends = jnp.cumsum(lengths_row)
    starts = ends - lengths_row
    begin = jnp.max(jnp.where(positions[:, None] >= starts[None, :], starts[None, :], 0), axis=1)
    half = HD // 2
    inverse = jnp.exp(-(jnp.arange(half, dtype=F32) * (2.0 / HD)) * math.log(10000.0))
    angles = inverse[:, None] * (positions - begin).astype(F32)[None, :]
    return jnp.cos(angles), jnp.sin(angles)


def shards(
    hidden,
    queries,
    key_states,
    value_states,
    attention_out,
    grad_out,
    lengths,
    down_query,
    up_query,
    down_value,
    up_value,
):
    rows = queries.shape[0]
    members = lax.axis_size("seq")
    packs = lax.axis_size("dp")
    total = rows * members
    heads_here = H // members
    stages = [(0, heads_here)]
    if heads_here > 1:
        stages = [(0, heads_here // 2), (heads_here // 2, heads_here - heads_here // 2)]
    sources = (queries, key_states, value_states, grad_out)
    me = lax.axis_index("seq")

    side_sources = (attention_out, grad_out, hidden, down_query, down_value)
    turns = turn_tables(lengths[0], total)
    packed = []
    for (first_head, stage_heads), whole in zip(stages, WHOLE_IN):
        extra = () if packed else side_sources
        held_back = sources
        if packed:
            held_back, _ = lax.optimization_barrier((sources, packed[0][0]))
        packed.append(
            list(pack(held_back, extra, members, heads_here, first_head, stage_heads, whole))
        )
    arrived = []
    home = []
    ups = []
    back = [None]
    planned = len(stages) == 2 and members == 8

    def after(value, stage, offsets):
        if not planned or not offsets:
            return value
        places = [offsets_of(members).index(offset) for offset in offsets]
        taken = tuple(home[stage][place] for place in places)
        value, taken = lax.optimization_barrier((value, taken))
        for place, message in zip(places, taken):
            home[stage][place] = message
        return value

    for index, (first_head, stage_heads) in enumerate(stages):
        arrived.append(exchange(packed[index], "seq"))
        if planned and index == 0:
            for place, before in CHAIN:
                packed[1][place], arrived[0][before] = lax.optimization_barrier(
                    (packed[1][place], arrived[0][before])
                )
        start = (me * heads_here + first_head) * HD
        up_here = tuple(
            lax.dynamic_slice_in_dim(up, start, stage_heads * HD, 1) for up in (up_query, up_value)
        )
        grads, back, up_terms = attention(
            lengths,
            up_here,
            turns,
            arrived[index],
            arrived[0],
            back[0],
            heads_here,
            first_head,
            stage_heads,
            members,
            rows,
            WHOLE_OUT[index],
        )
        home.append(exchange(grads, "seq"))
        ups.append(up_terms)
    def swap(value, offset):
        return lax.ppermute(value, "seq", [(i, i ^ offset) for i in range(members)])

    def planned_after(value, place):
        return after(after(value, 0, PLAN[place][0]), 1, PLAN[place][1])

    own, other = planned_after(tuple(back), 0)
    folded = planned_after(tuple(fold(own, swap(other, 1))), 1)
    tiles = [
        swap(tile, offset) if offset else tile
        for offset, tile in zip(pair_offsets(members), folded)
    ]
    tiles = planned_after(tiles, 2)
    pieces = exchange(down_terms(hidden, tiles, ups, members, packs), "dp")
    down_cols = hidden.shape[1] // packs
    summed = planned_after(sum_packs(pieces, members // packs, down_cols), 3)
    summed = planned_after(summed + swap(summed, 1), 4)
    if members == 8:
        pieces = [swap(summed, offset) if offset else summed for offset in pair_offsets(members)]
    else:
        step = 2
        while step < members // 2:
            summed = summed + swap(summed, step)
            step *= 2
        pieces = [summed, swap(summed, step)]
    down_query_grad, up_query_grad, down_value_grad, up_value_grad = finish(pieces, down_cols)
    grad_queries, grad_keys, value_gradients = unpack(home, members, heads_here, stages)
    return (
        grad_queries,
        grad_keys,
        value_gradients,
        down_query_grad,
        up_query_grad,
        down_value_grad,
        up_value_grad,
    )


def solution(mesh):
    tokens = P(("dp", "seq"), None)
    placed = (tokens,) * 6 + (P("dp", None),) + (P(),) * 4
    return jax.shard_map(
        shards,
        mesh=mesh,
        in_specs=placed,
        out_specs=(tokens,) * 3 + (P(None, "dp"),) * 4,
        check_vma=False,
    )
```

time: 375 us -> 125 us (0.33)
  Pallas kernels: 258 us -> 37.1 us
  waiting for transfers between devices: 55 us -> 33.3 us
  starting transfers between devices: 51.9 us -> 46.3 us
    pallas_call x2, Pallas kernels: 130 us -> 8.66 us  [pack(): pl.pallas_call(functools.partial(pack_kernel, members, heads_here, first_...]
    pallas_call x1, Pallas kernels: 96.8 us -> 3.43 us  [unpack(): pl.pallas_call(functools.partial(unpack_kernel, members, heads_here, stag...]
    ppermute x48 -> x39, waiting for transfers between devices: 55 us -> 33.3 us  [the longest x31 26.7 us: exchange(): lax.ppermute(message, axis, [(i, i ^ offset) for i in range(count)])]
    pallas_call x2 -> x3, Pallas kernels: 6.8 us -> 0.7 us  [the longest x1 0.67 us: finish(): pl.pallas_call(functools.partial(finish_kernel, down_cols), out_shape=[ja...]
    ppermute x48 -> x39, starting transfers between devices: 51.9 us -> 46.3 us  [the longest x31 37.9 us: exchange(): lax.ppermute(message, axis, [(i, i ^ offset) for i in range(count)])]
  transfers between devices with their start and end apart: 48 -> 39, of which waited for: 10 -> 14; matrix products, arithmetic and copies ran while one was open for 1% -> 3% of each run, Pallas kernels for 64% -> 24%
where the time goes in v2:
time: 125 us; the launch traced here: 124 us
  starting transfers between devices  46.3 us (37%)
  Pallas kernels  37.1 us (30%)
  waiting for transfers between devices  33.3 us (27%)
  local copies, waits for them, and re-layouts  4.24 us (3%)
  other arithmetic  2.3 us (2%)
    ppermute x31, starting transfers between devices, exchange(): lax.ppermute(message, axis, [(i, i ^ offset) for i in range(count)])  37.9 us
    ppermute x31, waiting for transfers between devices, exchange(): lax.ppermute(message, axis, [(i, i ^ offset) for i in range(count)])  26.7 us
    pallas_call x2, Pallas kernels, attention(): pl.pallas_call(functools.partial(attention_kernel, members, heads_here, f...  23.4 us
    pallas_call x2, Pallas kernels, pack(): pl.pallas_call(functools.partial(pack_kernel, members, heads_here, first_...  8.66 us
    ppermute x8, starting transfers between devices, swap(): return lax.ppermute(value, 'seq', [(i, i ^ offset) for i in range(members)])  8.32 us
    ppermute x8, waiting for transfers between devices, swap(): return lax.ppermute(value, 'seq', [(i, i ^ offset) for i in range(members)])  6.58 us
    pallas_call x1, Pallas kernels, unpack(): pl.pallas_call(functools.partial(unpack_kernel, members, heads_here, stag...  3.43 us
    unnamed x88, local copies, waits for them, and re-layouts  2.89 us
  transfers between devices with their start and end apart: 39, of which 14 were waited for; matrix products, arithmetic and copies ran while one was open for 3% of the time, Pallas kernels for 24%

profile of v2, /device:TPU:0, one launch (start us, length us, event | category | flops | bytes accessed | tf_op | source)
XLA Modules:
  0.0 124.2 jit_solution(7990818691459079768)
XLA Ops:
  0.6 5.7 %pack.2 = (bf16[1056,128]{1,0:T(8,128)(2,1)}, bf16[1056,128]{1,0:T(8,128)(2,1)}, bf16[1056,128]{1,0:T(8,128)(2,1)}, bf16[1056,128]{1,0:T(8,128)(2,1)}, bf16[1056...) custom-call(bf16[128,4096]{1,0:T(8,128)(2,1)} %refs_0_.2, ...), custom_call_target="tpu_custom_call" | custom-call | tf_op jit(solution)/shard_map/pack/pallas_call | solution.py:149
  6.3 4.0 %collective-permute-start = (bf16[1056,128]{1,0:T(8,128)(2,1)}, bf16[1056,128]{1,0:T(8,128)(2,1)S(1)}, u32[]{:S(2)}, u32[]{:S(2)}) collective-permute-start(bf16[1056,128]{1,0:T(8,128)(2,1)} %get-tuple-element.105), channel_id=1, source_target_pairs={{0,6},{1,7},{2,4},{3,5},{4,2},{5,3},{6,0},{7,1},{8,14},{9,15},{10,... | collective-permute-start | bytes 811016 | tf_op jit(solution)/shard_map/ppermute | solution.py:570
  10.3 0.5 collective-permute-start.1
  10.8 0.1 collective-permute-start.2
  10.9 1.4 %collective-permute-start.3 = (bf16[1056,128]{1,0:T(8,128)(2,1)}, bf16[1056,128]{1,0:T(8,128)(2,1)S(1)}, u32[]{:S(2)}, u32[]{:S(2)}) collective-permute-start(bf16[1056,128]{1,0:T(8,128)(2,1)} %get-tuple-element.117), channel_id=1, source_target_pairs={{0,7},{1,6},{2,5},{3,4},{4,3},{5,2},{6,1},{7,0},{8,15},{9,14},{10,... | collective-permute-start | bytes 811016 | tf_op jit(solution)/shard_map/ppermute | solution.py:570
  12.4 1.7 %collective-permute-start.4 = (bf16[1056,128]{1,0:T(8,128)(2,1)}, bf16[1056,128]{1,0:T(8,128)(2,1)S(1)}, u32[]{:S(2)}, u32[]{:S(2)}) collective-permute-start(bf16[1056,128]{1,0:T(8,128)(2,1)} %get-tuple-element.119), channel_id=1, source_target_pairs={{0,3},{1,2},{2,1},{3,0},{4,7},{5,6},{6,5},{7,4},{8,11},{9,10},{10,... | collective-permute-start | bytes 811016 | tf_op jit(solution)/shard_map/ppermute | solution.py:570
  14.0 0.2 reduce-window_clone.1
  14.2 0.1 select_reduce_fusion
  14.3 1.4 %constant_dynamic-slice_fusion = (bf16[8,256]{1,0:T(8,128)(2,1)}, bf16[8,256]{1,0:T(8,128)(2,1)}, bf16[8,256]{1,0:T(8,128)(2,1)}, bf16[8,256]{1,0:T(8,128)(2,1)}) fusion(bf16[8,4096]{1,0:T(8,128)(2,1)} %param.21, s32[]{:T(128)S(6)} %select_n.14, s32[]{:T(128)S(6)} %select_n.12, bf16[8,4096]{1,0:T(8,128)(2,1)} %param.19), kind=kLoop, calls=%fused_computation.5 | loop fusion | bytes 32776 | tf_op jit(solution)/shard_map/dynamic_slice | solution.py:646
  15.7 3.0 %pack.3 = (bf16[1024,128]{1,0:T(8,128)(2,1)}, bf16[1024,128]{1,0:T(8,128)(2,1)}, bf16[1024,128]{1,0:T(8,128)(2,1)}, bf16[1024,128]{1,0:T(8,128)(2,1)}, bf16[1024...) custom-call(bf16[128,4096]{1,0:T(8,128)(2,1)} %refs_0_.2, ...), custom_call_target="tpu_custom_call" | custom-call | tf_op jit(solution)/shard_map/pack/pallas_call | solution.py:149
  18.7 4.9 %collective-permute-done.2.refs_3_.refs_11_ = bf16[1056,128]{1,0:T(8,128)(2,1)S(1)} collective-permute-done((bf16[1056,128]{1,0:T(8,128)(2,1)}, bf16[1056,128]{1,0:T(8,128)(2,1)S(1)}, u32[]{:S(2)}, u32[]{:S(2)}) %collective-permute-start.2) | collective-permute-done | bytes 270368 | tf_op jit(solution)/shard_map/ppermute | solution.py:570
  23.6 1.6 %collective-permute-start.5 = (bf16[1056,128]{1,0:T(8,128)(2,1)S(1)}, bf16[1056,128]{1,0:T(8,128)(2,1)S(1)}, u32[]{:S(2)}, u32[]{:S(2)}) collective-permute-start(bf16[1056,128]{1,0:T(8,128)(2,1)S(1)} %copy-done.26), channel_id=1, source_target_pairs={{0,5},{1,4},{2,7},{3,6},{4,1},{5,0},{6,3},{7,2},{8,13},{9,12},{10,... | collective-permute-start | bytes 811016 | tf_op jit(solution)/shard_map/ppermute | solution.py:570
  25.1 4.0 %collective-permute-done.3.refs_4_.refs_12_ = bf16[1056,128]{1,0:T(8,128)(2,1)S(1)} collective-permute-done((bf16[1056,128]{1,0:T(8,128)(2,1)}, bf16[1056,128]{1,0:T(8,128)(2,1)S(1)}, u32[]{:S(2)}, u32[]{:S(2)}) %collective-permute-start.3) | collective-permute-done | bytes 270368 | tf_op jit(solution)/shard_map/ppermute | solution.py:570
  29.1 0.1 collective-permute-start.6
  29.3 0.4 collective-permute-start.13
  29.6 1.8 %collective-permute-start.12 = (bf16[1024,128]{1,0:T(8,128)(2,1)}, bf16[1024,128]{1,0:T(8,128)(2,1)S(1)}, u32[]{:S(2)}, u32[]{:S(2)}) collective-permute-start(bf16[1024,128]{1,0:T(8,128)(2,1)} %get-tuple-element.129), channel_id=1, source_target_pairs={{0,5},{1,4},{2,7},{3,6},{4,1},{5,0},{6,3},{7,2},{8,13},{9,12},{10,... | collective-permute-start | bytes 786440 | tf_op jit(solution)/shard_map/ppermute | solution.py:570
  31.4 2.0 %multiply_sine_fusion = (f32[64,1024]{1,0:T(8,128)}, f32[64,1024]{1,0:T(8,128)}) fusion(f32[1024]{0:T(1024)S(1)} %subtract_convert_fusion, f32[64]{0:T(128)S(1)} %multiply_exponential_fusion), kind=kLoop, calls=%fused_computation | loop fusion | flops 65536 | bytes 528640 | tf_op jit(solution)/shard_map/sin | solution.py:583
  33.4 0.3 collective-permute-done.4.refs_5_.refs_13_
  33.8 2.1 %collective-permute-start.11 = (bf16[1024,128]{1,0:T(8,128)(2,1)}, bf16[1024,128]{1,0:T(8,128)(2,1)S(1)}, u32[]{:S(2)}, u32[]{:S(2)}) collective-permute-start(bf16[1024,128]{1,0:T(8,128)(2,1)} %get-tuple-element.128), channel_id=1, source_target_pairs={{0,3},{1,2},{2,1},{3,0},{4,7},{5,6},{6,5},{7,4},{8,11},{9,10},{10,... | collective-permute-start | bytes 786440 | tf_op jit(solution)/shard_map/ppermute | solution.py:570
  35.9 0.9 collective-permute-start.10
  36.8 0.7 collective-permute-start.9
  37.4 0.8 collective-permute-start.8
  38.2 1.7 %collective-permute-done.12.refs_6_ = bf16[1024,128]{1,0:T(8,128)(2,1)S(1)} collective-permute-done((bf16[1024,128]{1,0:T(8,128)(2,1)}, bf16[1024,128]{1,0:T(8,128)(2,1)S(1)}, u32[]{:S(2)}, u32[]{:S(2)}) %collective-permute-start.12) | collective-permute-done | bytes 262176 | tf_op jit(solution)/shard_map/ppermute | solution.py:570
  40.0 2.7 %collective-permute-start.7 = (bf16[1024,128]{1,0:T(8,128)(2,1)}, bf16[1024,128]{1,0:T(8,128)(2,1)S(1)}, u32[]{:S(2)}, u32[]{:S(2)}) collective-permute-start(bf16[1024,128]{1,0:T(8,128)(2,1)} %get-tuple-element.124), channel_id=1, source_target_pairs={{0,6},{1,7},{2,4},{3,5},{4,2},{5,3},{6,0},{7,1},{8,14},{9,15},{10,... | collective-permute-start | bytes 786440 | tf_op jit(solution)/shard_map/ppermute | solution.py:570
  42.7 11.5 %attention.2 = (bf16[3,128,256]{2,1,0:T(8,128)(2,1)}, bf16[3,128,256]{2,1,0:T(8,128)(2,1)}, bf16[3,128,256]{2,1,0:T(8,128)(2,1)}, bf16[3,128,256]{2,1,0:T(8,128)...) custom-call(s32[1,4]{1,0:T(1,128)} %lengths_ref.3, ...), custom_call_target="tpu_custom_call" | custom-call | flops 10000000000 | tf_op jit(solution)/shard_map/attention/pallas_call | solution.py:355
  54.3 0.3 collective-permute-start.14
  54.6 1.7 %collective-permute-start.15 = (bf16[3,128,256]{2,1,0:T(8,128)(2,1)}, bf16[3,128,256]{2,1,0:T(8,128)(2,1)S(1)}, u32[]{:S(2)}, u32[]{:S(2)}) collective-permute-start(bf16[3,128,256]{2,1,0:T(8,128)(2,1)} %get-tuple-element.135), channel_id=1, source_target_pairs={{0,2},{1,3},{2,0},{3,1},{4,6},{5,7},{6,4},{7,5},{8,10},{9,11},{10,... | collective-permute-start | bytes 589832 | tf_op jit(solution)/shard_map/ppermute | solution.py:570
  56.3 1.5 %collective-permute-start.16 = (bf16[3,128,256]{2,1,0:T(8,128)(2,1)}, bf16[3,128,256]{2,1,0:T(8,128)(2,1)S(1)}, u32[]{:S(2)}, u32[]{:S(2)}) collective-permute-start(bf16[3,128,256]{2,1,0:T(8,128)(2,1)} %get-tuple-element.136), channel_id=1, source_target_pairs={{0,4},{1,5},{2,6},{3,7},{4,0},{5,1},{6,2},{7,3},{8,12},{9,13},{10,... | collective-permute-start | bytes 589832 | tf_op jit(solution)/shard_map/ppermute | solution.py:570
  57.8 2.6 %collective-permute-done.7.refs_1_ = bf16[1024,128]{1,0:T(8,128)(2,1)S(1)} collective-permute-done((bf16[1024,128]{1,0:T(8,128)(2,1)}, bf16[1024,128]{1,0:T(8,128)(2,1)S(1)}, u32[]{:S(2)}, u32[]{:S(2)}) %collective-permute-start.7) | collective-permute-done | bytes 262176 | tf_op jit(solution)/shard_map/ppermute | solution.py:570
  60.5 0.6 copy-done.33
  61.1 11.9 %attention.3 = (bf16[3,128,256]{2,1,0:T(8,128)(2,1)}, bf16[3,128,256]{2,1,0:T(8,128)(2,1)}, bf16[3,128,256]{2,1,0:T(8,128)(2,1)}, bf16[3,128,256]{2,1,0:T(8,128)...) custom-call(s32[1,4]{1,0:T(1,128)} %lengths_ref.3, ...), custom_call_target="tpu_custom_call" | custom-call | flops 10000000000 | tf_op jit(solution)/shard_map/attention/pallas_call | solution.py:355
  73.1 1.3 %collective-permute-start.17 = (f32[4,16,128]{2,1,0:T(8,128)}, f32[4,16,128]{2,1,0:T(8,128)S(1)}, u32[]{:S(2)}, u32[]{:S(2)}) collective-permute-start(f32[4,16,128]{2,1,0:T(8,128)} %get-tuple-element.141), channel_id=1, source_target_pairs={{0,1},{1,0},{2,3},{3,2},{4,5},{5,4},{6,7},{7,6},{8,9},{9,8},{10,11... | collective-permute-start | bytes 98312 | tf_op jit(solution)/shard_map/ppermute | solution.py:665
  74.4 1.1 collective-permute-done.17.other_ref
  75.5 0.8 copy-done.1
  76.2 1.8 %collective-permute-start.18 = (f32[16,128]{1,0:T(8,128)S(1)}, f32[16,128]{1,0:T(8,128)S(1)}, u32[]{:S(2)}, u32[]{:S(2)}) collective-permute-start(f32[16,128]{1,0:T(8,128)S(1)} %get-tuple-element.143), channel_id=1, source_target_pairs={{0,6},{1,7},{2,4},{3,5},{4,2},{5,3},{6,0},{7,1},{8,14},{9,15},{10,... | collective-permute-start | bytes 24584 | tf_op jit(solution)/shard_map/ppermute | solution.py:665
  78.1 1.2 collective-permute-start.19
  79.2 0.5 collective-permute-start.20
  79.8 1.0 collective-permute-done.18.refs_1_
  80.8 0.9 collective-permute-done.19.refs_2_
  81.7 1.2 collective-permute-done.20.refs_3_
  82.9 0.7 copy-done.3
  83.7 0.9 down_terms.1
  84.5 1.4 %collective-permute-start.23 = (f32[16,1792]{1,0:T(8,128)S(1)}, f32[16,1792]{1,0:T(8,128)S(1)}, u32[]{:S(2)}, u32[]{:S(2)}) collective-permute-start(f32[16,1792]{1,0:T(8,128)S(1)} %get-tuple-element.157), channel_id=1, source_target_pairs={{0,8},{8,0},{16,24},{24,16},{1,9},{9,1},{17,25},{25,17},{2,10},{10... | collective-permute-start | bytes 344072 | tf_op jit(solution)/shard_map/ppermute | solution.py:570
  86.0 2.8 %collective-permute-start.24 = (f32[16,1792]{1,0:T(8,128)S(1)}, f32[16,1792]{1,0:T(8,128)S(1)}, u32[]{:S(2)}, u32[]{:S(2)}) collective-permute-start(f32[16,1792]{1,0:T(8,128)S(1)} %get-tuple-element.158), channel_id=1, source_target_pairs={{0,16},{8,24},{16,0},{24,8},{1,17},{9,25},{17,1},{25,9},{2,18},{10... | collective-permute-start | bytes 344072 | tf_op jit(solution)/shard_map/ppermute | solution.py:570
  88.8 0.6 collective-permute-start.27
  89.4 1.8 %collective-permute-start.28 = (bf16[3,128,256]{2,1,0:T(8,128)(2,1)S(1)}, bf16[3,128,256]{2,1,0:T(8,128)(2,1)S(1)}, u32[]{:S(2)}, u32[]{:S(2)}) collective-permute-start(bf16[3,128,256]{2,1,0:T(8,128)(2,1)S(1)} %copy-done.42), channel_id=1, source_target_pairs={{0,6},{1,7},{2,4},{3,5},{4,2},{5,3},{6,0},{7,1},{8,14},{9,15},{10,... | collective-permute-start | bytes 589832 | tf_op jit(solution)/shard_map/ppermute | solution.py:570
  91.2 1.2 collective-permute-start.29
  92.4 0.4 collective-permute-done.24.refs_2_
  92.8 4.0 %collective-permute-start.25 = (f32[16,1792]{1,0:T(8,128)S(1)}, f32[16,1792]{1,0:T(8,128)S(1)}, u32[]{:S(2)}, u32[]{:S(2)}) collective-permute-start(f32[16,1792]{1,0:T(8,128)S(1)} %get-tuple-element.159), channel_id=1, source_target_pairs={{0,24},{8,16},{16,8},{24,0},{1,25},{9,17},{17,9},{25,1},{2,26},{10... | collective-permute-start | bytes 344072 | tf_op jit(solution)/shard_map/ppermute | solution.py:570
  96.8 2.9 %collective-permute-done.25.refs_3_ = f32[16,1792]{1,0:T(8,128)S(1)} collective-permute-done((f32[16,1792]{1,0:T(8,128)S(1)}, f32[16,1792]{1,0:T(8,128)S(1)}, u32[]{:S(2)}, u32[]{:S(2)}) %collective-permute-start.25) | collective-permute-done | bytes 114720 | tf_op jit(solution)/shard_map/ppermute | solution.py:570
  99.8 1.7 %collective-permute-done.29.refs_10_ = bf16[3,128,256]{2,1,0:T(8,128)(2,1)S(1)} collective-permute-done((bf16[3,128,256]{2,1,0:T(8,128)(2,1)S(1)}, bf16[3,128,256]{2,1,0:T(8,128)(2,1)S(1)}, u32[]{:S(2)}, u32[]{:S(2)}) %collective-permute-start.29) | collective-permute-done | bytes 196640 | tf_op jit(solution)/shard_map/ppermute | solution.py:570
  101.5 0.6 collective-permute-start.31
  102.1 1.6 %collective-permute-start.32 = (bf16[3,128,256]{2,1,0:T(8,128)(2,1)S(1)}, bf16[3,128,256]{2,1,0:T(8,128)(2,1)S(1)}, u32[]{:S(2)}, u32[]{:S(2)}) collective-permute-start(bf16[3,128,256]{2,1,0:T(8,128)(2,1)S(1)} %copy-done.39), channel_id=1, source_target_pairs={{0,7},{1,6},{2,5},{3,4},{4,3},{5,2},{6,1},{7,0},{8,15},{9,14},{10,... | collective-permute-start | bytes 589832 | tf_op jit(solution)/shard_map/ppermute | solution.py:570
  103.7 1.1 collective-permute-start.33
  104.8 0.3 collective-permute-start.34
  105.1 0.4 collective-permute-start.35
  105.5 8.1 %collective-permute-done.31.refs_11_ = bf16[3,128,256]{2,1,0:T(8,128)(2,1)S(1)} collective-permute-done((bf16[3,128,256]{2,1,0:T(8,128)(2,1)S(1)}, bf16[3,128,256]{2,1,0:T(8,128)(2,1)S(1)}, u32[]{:S(2)}, u32[]{:S(2)}) %collective-permute-start.31) | collective-permute-done | bytes 196640 | tf_op jit(solution)/shard_map/ppermute | solution.py:570
  113.5 0.5 collective-permute-start.38
  114.0 0.9 collective-permute-start.37
  114.9 2.1 %collective-permute-start.36 = (f32[16,2304]{1,0:T(8,128)S(1)}, f32[16,2304]{1,0:T(8,128)S(1)}, u32[]{:S(2)}, u32[]{:S(2)}) collective-permute-start(f32[16,2304]{1,0:T(8,128)S(1)} %add.17.refs_0_), channel_id=1, source_target_pairs={{0,6},{1,7},{2,4},{3,5},{4,2},{5,3},{6,0},{7,1},{8,14},{9,15},{10,... | collective-permute-start | bytes 442376 | tf_op jit(solution)/shard_map/ppermute | solution.py:665
  117.1 0.5 copy-done.16
  117.8 3.4 %unpack.1 = (bf16[128,4096]{1,0:T(8,128)(2,1)}, bf16[128,4096]{1,0:T(8,128)(2,1)}, bf16[128,4096]{1,0:T(8,128)(2,1)}) custom-call(bf16[3,128,256]{2,1,0:T(8,128)(2,1)} %get-tuple-element.122.refs_0_, bf16[3,128,256]{2,1,0:T(8,128)(2,1)} %copy-done.4, bf16[3,128,256]{2,1,0:T(8,128)(2,1)} %copy-done.5, bf16[3,128,256]{2,1,0:T(8,128)(2,1)} %copy-done.6, ...), custom_call_target="tpu_custom_call" | custom-call | tf_op jit(solution)/shard_map/unpack/pallas_call | solution.py:547
  121.2 2.4 %collective-permute-done.38.refs_3_ = f32[16,2304]{1,0:T(8,128)S(1)} collective-permute-done((f32[16,2304]{1,0:T(8,128)S(1)}, f32[16,2304]{1,0:T(8,128)S(1)}, u32[]{:S(2)}, u32[]{:S(2)}) %collective-permute-start.38) | collective-permute-done | bytes 147488 | tf_op jit(solution)/shard_map/ppermute | solution.py:665
  123.6 0.7 finish.1
  (119 shorter events, 0.4 us)
Async XLA Ops:
  0.6 13.4 %copy-start.43 = (s32[1,4]{1,0:T(1,128)S(1)}, s32[1,4]{1,0:T(1,128)}, u32[]{:S(2)}) copy-start(s32[1,4]{1,0:T(1,128)} %lengths_ref.3) | copy-start | bytes 52
  6.3 22.9 %collective-permute-start = (bf16[1056,128]{1,0:T(8,128)(2,1)}, bf16[1056,128]{1,0:T(8,128)(2,1)S(1)}, u32[]{:S(2)}, u32[]{:S(2)}) collective-permute-start(bf16[1056,128]{1,0:T(8,128)(2,1)} %get-tuple-element.105), channel_id=1, source_target_pairs={{0,6},{1,7},{2,4},{3,5},{4,2},{5,3},{6,0},{7,1},{8,14},{9,15},{10,... | collective-permute-start | bytes 811016 | tf_op jit(solution)/shard_map/ppermute | solution.py:570
  10.3 19.4 %collective-permute-start.1 = (bf16[1056,128]{1,0:T(8,128)(2,1)}, bf16[1056,128]{1,0:T(8,128)(2,1)S(1)}, u32[]{:S(2)}, u32[]{:S(2)}) collective-permute-start(bf16[1056,128]{1,0:T(8,128)(2,1)} %get-tuple-element.111), channel_id=1, source_target_pairs={{0,2},{1,3},{2,0},{3,1},{4,6},{5,7},{6,4},{7,5},{8,10},{9,11},{10,... | collective-permute-start | bytes 811016 | tf_op jit(solution)/shard_map/ppermute | solution.py:570
  10.8 12.7 %collective-permute-start.2 = (bf16[1056,128]{1,0:T(8,128)(2,1)}, bf16[1056,128]{1,0:T(8,128)(2,1)S(1)}, u32[]{:S(2)}, u32[]{:S(2)}) collective-permute-start(bf16[1056,128]{1,0:T(8,128)(2,1)} %get-tuple-element.114), channel_id=1, source_target_pairs={{0,4},{1,5},{2,6},{3,7},{4,0},{5,1},{6,2},{7,3},{8,12},{9,13},{10,... | collective-permute-start | bytes 811016 | tf_op jit(solution)/shard_map/ppermute | solution.py:570
  10.9 18.2 %collective-permute-start.3 = (bf16[1056,128]{1,0:T(8,128)(2,1)}, bf16[1056,128]{1,0:T(8,128)(2,1)S(1)}, u32[]{:S(2)}, u32[]{:S(2)}) collective-permute-start(bf16[1056,128]{1,0:T(8,128)(2,1)} %get-tuple-element.117), channel_id=1, source_target_pairs={{0,7},{1,6},{2,5},{3,4},{4,3},{5,2},{6,1},{7,0},{8,15},{9,14},{10,... | collective-permute-start | bytes 811016 | tf_op jit(solution)/shard_map/ppermute | solution.py:570
  12.4 21.4 %collective-permute-start.4 = (bf16[1056,128]{1,0:T(8,128)(2,1)}, bf16[1056,128]{1,0:T(8,128)(2,1)S(1)}, u32[]{:S(2)}, u32[]{:S(2)}) collective-permute-start(bf16[1056,128]{1,0:T(8,128)(2,1)} %get-tuple-element.119), channel_id=1, source_target_pairs={{0,3},{1,2},{2,1},{3,0},{4,7},{5,6},{6,5},{7,4},{8,11},{9,10},{10,... | collective-permute-start | bytes 811016 | tf_op jit(solution)/shard_map/ppermute | solution.py:570
  15.7 13.5 %copy-start.25 = (bf16[1056,128]{1,0:T(8,128)(2,1)S(1)}, bf16[1056,128]{1,0:T(8,128)(2,1)}, u32[]{:S(2)}) copy-start(bf16[1056,128]{1,0:T(8,128)(2,1)} %get-tuple-element.121) | copy-start | bytes 811012
  23.5 19.1 %copy-start.20 = (bf16[1056,128]{1,0:T(8,128)(2,1)}, bf16[1056,128]{1,0:T(8,128)(2,1)S(1)}, u32[]{:S(2)}) copy-start(bf16[1056,128]{1,0:T(8,128)(2,1)S(1)} %collective-permute-done.2.refs_3_.refs_11_) | copy-start | bytes 811012
  23.6 12.3 %collective-permute-start.5 = (bf16[1056,128]{1,0:T(8,128)(2,1)S(1)}, bf16[1056,128]{1,0:T(8,128)(2,1)S(1)}, u32[]{:S(2)}, u32[]{:S(2)}) collective-permute-start(bf16[1056,128]{1,0:T(8,128)(2,1)S(1)} %copy-done.26), channel_id=1, source_target_pairs={{0,5},{1,4},{2,7},{3,6},{4,1},{5,0},{6,3},{7,2},{8,13},{9,12},{10,... | collective-permute-start | bytes 811016 | tf_op jit(solution)/shard_map/ppermute | solution.py:570
  29.1 13.5 %copy-start.21 = (bf16[1056,128]{1,0:T(8,128)(2,1)}, bf16[1056,128]{1,0:T(8,128)(2,1)S(1)}, u32[]{:S(2)}) copy-start(bf16[1056,128]{1,0:T(8,128)(2,1)S(1)} %collective-permute-done.3.refs_4_.refs_12_) | copy-start | bytes 811012
  29.1 7.6 %collective-permute-start.6 = (bf16[1056,128]{1,0:T(8,128)(2,1)S(1)}, bf16[1056,128]{1,0:T(8,128)(2,1)S(1)}, u32[]{:S(2)}, u32[]{:S(2)}) collective-permute-start(bf16[1056,128]{1,0:T(8,128)(2,1)S(1)} %copy-done.25), channel_id=1, source_target_pairs={{0,1},{1,0},{2,3},{3,2},{4,5},{5,4},{6,7},{7,6},{8,9},{9,8},{10,11... | collective-permute-start | bytes 811016 | tf_op jit(solution)/shard_map/ppermute | solution.py:570
  29.3 13.4 %copy-start.18 = (bf16[1056,128]{1,0:T(8,128)(2,1)}, bf16[1056,128]{1,0:T(8,128)(2,1)S(1)}, u32[]{:S(2)}) copy-start(bf16[1056,128]{1,0:T(8,128)(2,1)S(1)} %collective-permute-done.refs_1_.refs_9_) | copy-start | bytes 811012
  29.3 8.2 %collective-permute-start.13 = (bf16[1024,128]{1,0:T(8,128)(2,1)}, bf16[1024,128]{1,0:T(8,128)(2,1)S(1)}, u32[]{:S(2)}, u32[]{:S(2)}) collective-permute-start(bf16[1024,128]{1,0:T(8,128)(2,1)} %get-tuple-element.130), channel_id=1, source_target_pairs={{0,1},{1,0},{2,3},{3,2},{4,5},{5,4},{6,7},{7,6},{8,9},{9,8},{10,11... | collective-permute-start | bytes 786440 | tf_op jit(solution)/shard_map/ppermute | solution.py:570
  29.6 10.3 %collective-permute-start.12 = (bf16[1024,128]{1,0:T(8,128)(2,1)}, bf16[1024,128]{1,0:T(8,128)(2,1)S(1)}, u32[]{:S(2)}, u32[]{:S(2)}) collective-permute-start(bf16[1024,128]{1,0:T(8,128)(2,1)} %get-tuple-element.129), channel_id=1, source_target_pairs={{0,5},{1,4},{2,7},{3,6},{4,1},{5,0},{6,3},{7,2},{8,13},{9,12},{10,... | collective-permute-start | bytes 786440 | tf_op jit(solution)/shard_map/ppermute | solution.py:570
  33.8 20.5 %collective-permute-start.11 = (bf16[1024,128]{1,0:T(8,128)(2,1)}, bf16[1024,128]{1,0:T(8,128)(2,1)S(1)}, u32[]{:S(2)}, u32[]{:S(2)}) collective-permute-start(bf16[1024,128]{1,0:T(8,128)(2,1)} %get-tuple-element.128), channel_id=1, source_target_pairs={{0,3},{1,2},{2,1},{3,0},{4,7},{5,6},{6,5},{7,4},{8,11},{9,10},{10,... | collective-permute-start | bytes 786440 | tf_op jit(solution)/shard_map/ppermute | solution.py:570
  35.9 18.7 %collective-permute-start.10 = (bf16[1024,128]{1,0:T(8,128)(2,1)}, bf16[1024,128]{1,0:T(8,128)(2,1)S(1)}, u32[]{:S(2)}, u32[]{:S(2)}) collective-permute-start(bf16[1024,128]{1,0:T(8,128)(2,1)} %get-tuple-element.127), channel_id=1, source_target_pairs={{0,7},{1,6},{2,5},{3,4},{4,3},{5,2},{6,1},{7,0},{8,15},{9,14},{10,... | collective-permute-start | bytes 786440 | tf_op jit(solution)/shard_map/ppermute | solution.py:570
  36.8 19.5 %collective-permute-start.9 = (bf16[1024,128]{1,0:T(8,128)(2,1)}, bf16[1024,128]{1,0:T(8,128)(2,1)S(1)}, u32[]{:S(2)}, u32[]{:S(2)}) collective-permute-start(bf16[1024,128]{1,0:T(8,128)(2,1)} %get-tuple-element.126), channel_id=1, source_target_pairs={{0,4},{1,5},{2,6},{3,7},{4,0},{5,1},{6,2},{7,3},{8,12},{9,13},{10,... | collective-permute-start | bytes 786440 | tf_op jit(solution)/shard_map/ppermute | solution.py:570
  37.4 16.8 %copy-start.27 = (bf16[1024,128]{1,0:T(8,128)(2,1)}, bf16[1024,128]{1,0:T(8,128)(2,1)S(1)}, u32[]{:S(2)}) copy-start(bf16[1024,128]{1,0:T(8,128)(2,1)S(1)} %collective-permute-done.13.refs_7_) | copy-start | bytes 786436
  37.4 20.4 %collective-permute-start.8 = (bf16[1024,128]{1,0:T(8,128)(2,1)}, bf16[1024,128]{1,0:T(8,128)(2,1)S(1)}, u32[]{:S(2)}, u32[]{:S(2)}) collective-permute-start(bf16[1024,128]{1,0:T(8,128)(2,1)} %get-tuple-element.125), channel_id=1, source_target_pairs={{0,2},{1,3},{2,0},{3,1},{4,6},{5,7},{6,4},{7,5},{8,10},{9,11},{10,... | collective-permute-start | bytes 786440 | tf_op jit(solution)/shard_map/ppermute | solution.py:570
  40.0 14.3 %copy-start.28 = (bf16[1024,128]{1,0:T(8,128)(2,1)}, bf16[1024,128]{1,0:T(8,128)(2,1)S(1)}, u32[]{:S(2)}) copy-start(bf16[1024,128]{1,0:T(8,128)(2,1)S(1)} %collective-permute-done.12.refs_6_) | copy-start | bytes 786436
  40.0 20.5 %collective-permute-start.7 = (bf16[1024,128]{1,0:T(8,128)(2,1)}, bf16[1024,128]{1,0:T(8,128)(2,1)S(1)}, u32[]{:S(2)}, u32[]{:S(2)}) collective-permute-start(bf16[1024,128]{1,0:T(8,128)(2,1)} %get-tuple-element.124), channel_id=1, source_target_pairs={{0,6},{1,7},{2,4},{3,5},{4,2},{5,3},{6,0},{7,1},{8,14},{9,15},{10,... | collective-permute-start | bytes 786440 | tf_op jit(solution)/shard_map/ppermute | solution.py:570
  54.3 18.7 %collective-permute-start.14 = (bf16[3,128,256]{2,1,0:T(8,128)(2,1)}, bf16[3,128,256]{2,1,0:T(8,128)(2,1)S(1)}, u32[]{:S(2)}, u32[]{:S(2)}) collective-permute-start(bf16[3,128,256]{2,1,0:T(8,128)(2,1)} %get-tuple-element.134), channel_id=1, source_target_pairs={{0,6},{1,7},{2,4},{3,5},{4,2},{5,3},{6,0},{7,1},{8,14},{9,15},{10,... | collective-permute-start | bytes 589832 | tf_op jit(solution)/shard_map/ppermute | solution.py:570
  54.6 18.5 %collective-permute-start.15 = (bf16[3,128,256]{2,1,0:T(8,128)(2,1)}, bf16[3,128,256]{2,1,0:T(8,128)(2,1)S(1)}, u32[]{:S(2)}, u32[]{:S(2)}) collective-permute-start(bf16[3,128,256]{2,1,0:T(8,128)(2,1)} %get-tuple-element.135), channel_id=1, source_target_pairs={{0,2},{1,3},{2,0},{3,1},{4,6},{5,7},{6,4},{7,5},{8,10},{9,11},{10,... | collective-permute-start | bytes 589832 | tf_op jit(solution)/shard_map/ppermute | solution.py:570
  56.3 16.7 %collective-permute-start.16 = (bf16[3,128,256]{2,1,0:T(8,128)(2,1)}, bf16[3,128,256]{2,1,0:T(8,128)(2,1)S(1)}, u32[]{:S(2)}, u32[]{:S(2)}) collective-permute-start(bf16[3,128,256]{2,1,0:T(8,128)(2,1)} %get-tuple-element.136), channel_id=1, source_target_pairs={{0,4},{1,5},{2,6},{3,7},{4,0},{5,1},{6,2},{7,3},{8,12},{9,13},{10,... | collective-permute-start | bytes 589832 | tf_op jit(solution)/shard_map/ppermute | solution.py:570
  57.8 21.9 %collective-permute-start.21 = (bf16[3,128,256]{2,1,0:T(8,128)(2,1)}, bf16[3,128,256]{2,1,0:T(8,128)(2,1)S(1)}, u32[]{:S(2)}, u32[]{:S(2)}) collective-permute-start(bf16[3,128,256]{2,1,0:T(8,128)(2,1)} %get-tuple-element.146), channel_id=1, source_target_pairs={{0,7},{1,6},{2,5},{3,4},{4,3},{5,2},{6,1},{7,0},{8,15},{9,14},{10,... | collective-permute-start | bytes 589832 | tf_op jit(solution)/shard_map/ppermute | solution.py:570
  60.4 19.3 %collective-permute-start.22 = (bf16[3,128,256]{2,1,0:T(8,128)(2,1)}, bf16[3,128,256]{2,1,0:T(8,128)(2,1)S(1)}, u32[]{:S(2)}, u32[]{:S(2)}) collective-permute-start(bf16[3,128,256]{2,1,0:T(8,128)(2,1)} %get-tuple-element.147), channel_id=1, source_target_pairs={{0,3},{1,2},{2,1},{3,0},{4,7},{5,6},{6,5},{7,4},{8,11},{9,10},{10,... | collective-permute-start | bytes 589832 | tf_op jit(solution)/shard_map/ppermute | solution.py:570
  61.1 21.8 %copy-start = (bf16[128,5120]{1,0:T(8,128)(2,1)S(1)}, bf16[128,5120]{1,0:T(8,128)(2,1)}, u32[]{:S(2)}) copy-start(bf16[128,5120]{1,0:T(8,128)(2,1)} %hidden_ref.1) | copy-start | bytes 3932164
  61.1 21.8 %copy-start.2 = (f32[16,256]{1,0:T(8,128)S(1)}, f32[16,256]{1,0:T(8,128)}, u32[]{:S(2)}) copy-start(f32[16,256]{1,0:T(8,128)} %get-tuple-element.154.refs_4_) | copy-start | bytes 49156
  61.1 27.6 %copy-start.38 = (bf16[3,128,256]{2,1,0:T(8,128)(2,1)S(1)}, bf16[3,128,256]{2,1,0:T(8,128)(2,1)}, u32[]{:S(2)}) copy-start(bf16[3,128,256]{2,1,0:T(8,128)(2,1)} %get-tuple-element.160) | copy-start | bytes 589828
  61.1 27.7 %copy-start.37 = (bf16[3,128,256]{2,1,0:T(8,128)(2,1)S(1)}, bf16[3,128,256]{2,1,0:T(8,128)(2,1)}, u32[]{:S(2)}) copy-start(bf16[3,128,256]{2,1,0:T(8,128)(2,1)} %get-tuple-element.161) | copy-start | bytes 589828
  73.0 44.0 %copy-start.4 = (bf16[3,128,256]{2,1,0:T(8,128)(2,1)}, bf16[3,128,256]{2,1,0:T(8,128)(2,1)S(1)}, u32[]{:S(2)}) copy-start(bf16[3,128,256]{2,1,0:T(8,128)(2,1)S(1)} %collective-permute-done.14.refs_1_) | copy-start | bytes 589828
  73.0 44.0 %copy-start.5 = (bf16[3,128,256]{2,1,0:T(8,128)(2,1)}, bf16[3,128,256]{2,1,0:T(8,128)(2,1)S(1)}, u32[]{:S(2)}) copy-start(bf16[3,128,256]{2,1,0:T(8,128)(2,1)S(1)} %collective-permute-done.15.refs_2_) | copy-start | bytes 589828
  73.1 44.0 %copy-start.6 = (bf16[3,128,256]{2,1,0:T(8,128)(2,1)}, bf16[3,128,256]{2,1,0:T(8,128)(2,1)S(1)}, u32[]{:S(2)}) copy-start(bf16[3,128,256]{2,1,0:T(8,128)(2,1)S(1)} %collective-permute-done.16.refs_3_) | copy-start | bytes 589828
  73.1 2.4 %collective-permute-start.17 = (f32[4,16,128]{2,1,0:T(8,128)}, f32[4,16,128]{2,1,0:T(8,128)S(1)}, u32[]{:S(2)}, u32[]{:S(2)}) collective-permute-start(f32[4,16,128]{2,1,0:T(8,128)} %get-tuple-element.141), channel_id=1, source_target_pairs={{0,1},{1,0},{2,3},{3,2},{4,5},{5,4},{6,7},{7,6},{8,9},{9,8},{10,11... | collective-permute-start | bytes 98312 | tf_op jit(solution)/shard_map/ppermute | solution.py:665
  76.2 4.5 %collective-permute-start.18 = (f32[16,128]{1,0:T(8,128)S(1)}, f32[16,128]{1,0:T(8,128)S(1)}, u32[]{:S(2)}, u32[]{:S(2)}) collective-permute-start(f32[16,128]{1,0:T(8,128)S(1)} %get-tuple-element.143), channel_id=1, source_target_pairs={{0,6},{1,7},{2,4},{3,5},{4,2},{5,3},{6,0},{7,1},{8,14},{9,15},{10,... | collective-permute-start | bytes 24584 | tf_op jit(solution)/shard_map/ppermute | solution.py:665
  78.1 3.7 %collective-permute-start.19 = (f32[16,128]{1,0:T(8,128)S(1)}, f32[16,128]{1,0:T(8,128)S(1)}, u32[]{:S(2)}, u32[]{:S(2)}) collective-permute-start(f32[16,128]{1,0:T(8,128)S(1)} %get-tuple-element.144), channel_id=1, source_target_pairs={{0,2},{1,3},{2,0},{3,1},{4,6},{5,7},{6,4},{7,5},{8,10},{9,11},{10,... | collective-permute-start | bytes 24584 | tf_op jit(solution)/shard_map/ppermute | solution.py:665
  79.2 3.7 %collective-permute-start.20 = (f32[16,128]{1,0:T(8,128)S(1)}, f32[16,128]{1,0:T(8,128)S(1)}, u32[]{:S(2)}, u32[]{:S(2)}) collective-permute-start(f32[16,128]{1,0:T(8,128)S(1)} %get-tuple-element.145), channel_id=1, source_target_pairs={{0,4},{1,5},{2,6},{3,7},{4,0},{5,1},{6,2},{7,3},{8,12},{9,13},{10,... | collective-permute-start | bytes 24584 | tf_op jit(solution)/shard_map/ppermute | solution.py:665
  79.7 37.3 %copy-start.7 = (bf16[3,128,256]{2,1,0:T(8,128)(2,1)}, bf16[3,128,256]{2,1,0:T(8,128)(2,1)S(1)}, u32[]{:S(2)}) copy-start(bf16[3,128,256]{2,1,0:T(8,128)(2,1)S(1)} %collective-permute-done.21.refs_4_) | copy-start | bytes 589828
  79.8 37.3 %copy-start.8 = (bf16[3,128,256]{2,1,0:T(8,128)(2,1)}, bf16[3,128,256]{2,1,0:T(8,128)(2,1)S(1)}, u32[]{:S(2)}) copy-start(bf16[3,128,256]{2,1,0:T(8,128)(2,1)S(1)} %collective-permute-done.22.refs_5_) | copy-start | bytes 589828
  83.6 17.9 %copy-start.40 = (bf16[3,128,256]{2,1,0:T(8,128)(2,1)S(1)}, bf16[3,128,256]{2,1,0:T(8,128)(2,1)}, u32[]{:S(2)}) copy-start(bf16[3,128,256]{2,1,0:T(8,128)(2,1)} %get-tuple-element.171) | copy-start | bytes 589828
  83.6 18.5 %copy-start.39 = (bf16[3,128,256]{2,1,0:T(8,128)(2,1)S(1)}, bf16[3,128,256]{2,1,0:T(8,128)(2,1)}, u32[]{:S(2)}) copy-start(bf16[3,128,256]{2,1,0:T(8,128)(2,1)} %get-tuple-element.173) | copy-start | bytes 589828
  83.6 20.1 %copy-start.36 = (bf16[3,128,256]{2,1,0:T(8,128)(2,1)S(1)}, bf16[3,128,256]{2,1,0:T(8,128)(2,1)}, u32[]{:S(2)}) copy-start(bf16[3,128,256]{2,1,0:T(8,128)(2,1)} %get-tuple-element.174) | copy-start | bytes 589828
  83.6 21.2 %copy-start.35 = (bf16[3,128,256]{2,1,0:T(8,128)(2,1)S(1)}, bf16[3,128,256]{2,1,0:T(8,128)(2,1)}, u32[]{:S(2)}) copy-start(bf16[3,128,256]{2,1,0:T(8,128)(2,1)} %get-tuple-element.175) | copy-start | bytes 589828
  83.6 21.4 %copy-start.34 = (bf16[3,128,256]{2,1,0:T(8,128)(2,1)S(1)}, bf16[3,128,256]{2,1,0:T(8,128)(2,1)}, u32[]{:S(2)}) copy-start(bf16[3,128,256]{2,1,0:T(8,128)(2,1)} %get-tuple-element.176) | copy-start | bytes 589828
  84.5 6.7 %collective-permute-start.23 = (f32[16,1792]{1,0:T(8,128)S(1)}, f32[16,1792]{1,0:T(8,128)S(1)}, u32[]{:S(2)}, u32[]{:S(2)}) collective-permute-start(f32[16,1792]{1,0:T(8,128)S(1)} %get-tuple-element.157), channel_id=1, source_target_pairs={{0,8},{8,0},{16,24},{24,16},{1,9},{9,1},{17,25},{25,17},{2,10},{10... | collective-permute-start | bytes 344072 | tf_op jit(solution)/shard_map/ppermute | solution.py:570
  86.0 6.9 %collective-permute-start.24 = (f32[16,1792]{1,0:T(8,128)S(1)}, f32[16,1792]{1,0:T(8,128)S(1)}, u32[]{:S(2)}, u32[]{:S(2)}) collective-permute-start(f32[16,1792]{1,0:T(8,128)S(1)} %get-tuple-element.158), channel_id=1, source_target_pairs={{0,16},{8,24},{16,0},{24,8},{1,17},{9,25},{17,1},{25,9},{2,18},{10... | collective-permute-start | bytes 344072 | tf_op jit(solution)/shard_map/ppermute | solution.py:570
  88.8 10.9 %collective-permute-start.26 = (bf16[3,128,256]{2,1,0:T(8,128)(2,1)S(1)}, bf16[3,128,256]{2,1,0:T(8,128)(2,1)S(1)}, u32[]{:S(2)}, u32[]{:S(2)}) collective-permute-start(bf16[3,128,256]{2,1,0:T(8,128)(2,1)S(1)} %copy-done.38), channel_id=1, source_target_pairs={{0,5},{1,4},{2,7},{3,6},{4,1},{5,0},{6,3},{7,2},{8,13},{9,12},{10,... | collective-permute-start | bytes 589832 | tf_op jit(solution)/shard_map/ppermute | solution.py:570
  88.8 10.9 %collective-permute-start.27 = (bf16[3,128,256]{2,1,0:T(8,128)(2,1)S(1)}, bf16[3,128,256]{2,1,0:T(8,128)(2,1)S(1)}, u32[]{:S(2)}, u32[]{:S(2)}) collective-permute-start(bf16[3,128,256]{2,1,0:T(8,128)(2,1)S(1)} %copy-done.37), channel_id=1, source_target_pairs={{0,1},{1,0},{2,3},{3,2},{4,5},{5,4},{6,7},{7,6},{8,9},{9,8},{10,11... | collective-permute-start | bytes 589832 | tf_op jit(solution)/shard_map/ppermute | solution.py:570
  89.4 10.3 %collective-permute-start.28 = (bf16[3,128,256]{2,1,0:T(8,128)(2,1)S(1)}, bf16[3,128,256]{2,1,0:T(8,128)(2,1)S(1)}, u32[]{:S(2)}, u32[]{:S(2)}) collective-permute-start(bf16[3,128,256]{2,1,0:T(8,128)(2,1)S(1)} %copy-done.42), channel_id=1, source_target_pairs={{0,6},{1,7},{2,4},{3,5},{4,2},{5,3},{6,0},{7,1},{8,14},{9,15},{10,... | collective-permute-start | bytes 589832 | tf_op jit(solution)/shard_map/ppermute | solution.py:570
  91.2 10.3 %collective-permute-start.29 = (bf16[3,128,256]{2,1,0:T(8,128)(2,1)S(1)}, bf16[3,128,256]{2,1,0:T(8,128)(2,1)S(1)}, u32[]{:S(2)}, u32[]{:S(2)}) collective-permute-start(bf16[3,128,256]{2,1,0:T(8,128)(2,1)S(1)} %copy-done.41), channel_id=1, source_target_pairs={{0,2},{1,3},{2,0},{3,1},{4,6},{5,7},{6,4},{7,5},{8,10},{9,11},{10,... | collective-permute-start | bytes 589832 | tf_op jit(solution)/shard_map/ppermute | solution.py:570
  92.8 6.8 %collective-permute-start.25 = (f32[16,1792]{1,0:T(8,128)S(1)}, f32[16,1792]{1,0:T(8,128)S(1)}, u32[]{:S(2)}, u32[]{:S(2)}) collective-permute-start(f32[16,1792]{1,0:T(8,128)S(1)} %get-tuple-element.159), channel_id=1, source_target_pairs={{0,24},{8,16},{16,8},{24,0},{1,25},{9,17},{17,9},{25,1},{2,26},{10... | collective-permute-start | bytes 344072 | tf_op jit(solution)/shard_map/ppermute | solution.py:570
  99.7 17.4 %copy-start.9 = (bf16[3,128,256]{2,1,0:T(8,128)(2,1)}, bf16[3,128,256]{2,1,0:T(8,128)(2,1)S(1)}, u32[]{:S(2)}) copy-start(bf16[3,128,256]{2,1,0:T(8,128)(2,1)S(1)} %collective-permute-done.26.refs_6_) | copy-start | bytes 589828
  99.7 17.4 %copy-start.10 = (bf16[3,128,256]{2,1,0:T(8,128)(2,1)}, bf16[3,128,256]{2,1,0:T(8,128)(2,1)S(1)}, u32[]{:S(2)}) copy-start(bf16[3,128,256]{2,1,0:T(8,128)(2,1)S(1)} %collective-permute-done.27.refs_7_) | copy-start | bytes 589828
  99.8 17.3 %copy-start.11 = (bf16[3,128,256]{2,1,0:T(8,128)(2,1)}, bf16[3,128,256]{2,1,0:T(8,128)(2,1)S(1)}, u32[]{:S(2)}) copy-start(bf16[3,128,256]{2,1,0:T(8,128)(2,1)S(1)} %collective-permute-done.28.refs_9_) | copy-start | bytes 589828
  101.5 15.6 %copy-start.12 = (bf16[3,128,256]{2,1,0:T(8,128)(2,1)}, bf16[3,128,256]{2,1,0:T(8,128)(2,1)S(1)}, u32[]{:S(2)}) copy-start(bf16[3,128,256]{2,1,0:T(8,128)(2,1)S(1)} %collective-permute-done.29.refs_10_) | copy-start | bytes 589828
  101.5 3.6 %collective-permute-start.30 = (f32[16,2304]{1,0:T(8,128)S(1)}, f32[16,2304]{1,0:T(8,128)S(1)}, u32[]{:S(2)}, u32[]{:S(2)}) collective-permute-start(f32[16,2304]{1,0:T(8,128)S(1)} %sum_packs.1), channel_id=1, source_target_pairs={{0,1},{1,0},{2,3},{3,2},{4,5},{5,4},{6,7},{7,6},{8,9},{9,8},{10,11... | collective-permute-start | bytes 442376 | tf_op jit(solution)/shard_map/ppermute | solution.py:665
  101.5 12.0 %collective-permute-start.31 = (bf16[3,128,256]{2,1,0:T(8,128)(2,1)S(1)}, bf16[3,128,256]{2,1,0:T(8,128)(2,1)S(1)}, u32[]{:S(2)}, u32[]{:S(2)}) collective-permute-start(bf16[3,128,256]{2,1,0:T(8,128)(2,1)S(1)} %copy-done.40), channel_id=1, source_target_pairs={{0,4},{1,5},{2,6},{3,7},{4,0},{5,1},{6,2},{7,3},{8,12},{9,13},{10,... | collective-permute-start | bytes 589832 | tf_op jit(solution)/shard_map/ppermute | solution.py:570
  102.1 11.9 %collective-permute-start.32 = (bf16[3,128,256]{2,1,0:T(8,128)(2,1)S(1)}, bf16[3,128,256]{2,1,0:T(8,128)(2,1)S(1)}, u32[]{:S(2)}, u32[]{:S(2)}) collective-permute-start(bf16[3,128,256]{2,1,0:T(8,128)(2,1)S(1)} %copy-done.39), channel_id=1, source_target_pairs={{0,7},{1,6},{2,5},{3,4},{4,3},{5,2},{6,1},{7,0},{8,15},{9,14},{10,... | collective-permute-start | bytes 589832 | tf_op jit(solution)/shard_map/ppermute | solution.py:570
  103.7 11.2 %collective-permute-start.33 = (bf16[3,128,256]{2,1,0:T(8,128)(2,1)S(1)}, bf16[3,128,256]{2,1,0:T(8,128)(2,1)S(1)}, u32[]{:S(2)}, u32[]{:S(2)}) collective-permute-start(bf16[3,128,256]{2,1,0:T(8,128)(2,1)S(1)} %copy-done.36), channel_id=1, source_target_pairs={{0,3},{1,2},{2,1},{3,0},{4,7},{5,6},{6,5},{7,4},{8,11},{9,10},{10,... | collective-permute-start | bytes 589832 | tf_op jit(solution)/shard_map/ppermute | solution.py:570
  104.8 12.2 %collective-permute-start.34 = (bf16[3,128,256]{2,1,0:T(8,128)(2,1)S(1)}, bf16[3,128,256]{2,1,0:T(8,128)(2,1)S(1)}, u32[]{:S(2)}, u32[]{:S(2)}) collective-permute-start(bf16[3,128,256]{2,1,0:T(8,128)(2,1)S(1)} %copy-done.35), channel_id=1, source_target_pairs={{0,5},{1,4},{2,7},{3,6},{4,1},{5,0},{6,3},{7,2},{8,13},{9,12},{10,... | collective-permute-start | bytes 589832 | tf_op jit(solution)/shard_map/ppermute | solution.py:570
  105.1 11.9 %collective-permute-start.35 = (bf16[3,128,256]{2,1,0:T(8,128)(2,1)S(1)}, bf16[3,128,256]{2,1,0:T(8,128)(2,1)S(1)}, u32[]{:S(2)}, u32[]{:S(2)}) collective-permute-start(bf16[3,128,256]{2,1,0:T(8,128)(2,1)S(1)} %copy-done.34), channel_id=1, source_target_pairs={{0,1},{1,0},{2,3},{3,2},{4,5},{5,4},{6,7},{7,6},{8,9},{9,8},{10,11... | collective-permute-start | bytes 589832 | tf_op jit(solution)/shard_map/ppermute | solution.py:570
  113.5 10.1 %collective-permute-start.38 = (f32[16,2304]{1,0:T(8,128)S(1)}, f32[16,2304]{1,0:T(8,128)S(1)}, u32[]{:S(2)}, u32[]{:S(2)}) collective-permute-start(f32[16,2304]{1,0:T(8,128)S(1)} %add.17.refs_0_), channel_id=1, source_target_pairs={{0,4},{1,5},{2,6},{3,7},{4,0},{5,1},{6,2},{7,3},{8,12},{9,13},{10,... | collective-permute-start | bytes 442376 | tf_op jit(solution)/shard_map/ppermute | solution.py:665
  114.0 9.6 %collective-permute-start.37 = (f32[16,2304]{1,0:T(8,128)S(1)}, f32[16,2304]{1,0:T(8,128)S(1)}, u32[]{:S(2)}, u32[]{:S(2)}) collective-permute-start(f32[16,2304]{1,0:T(8,128)S(1)} %add.17.refs_0_), channel_id=1, source_target_pairs={{0,2},{1,3},{2,0},{3,1},{4,6},{5,7},{6,4},{7,5},{8,10},{9,11},{10,... | collective-permute-start | bytes 442376 | tf_op jit(solution)/shard_map/ppermute | solution.py:665
  114.9 8.7 %collective-permute-start.36 = (f32[16,2304]{1,0:T(8,128)S(1)}, f32[16,2304]{1,0:T(8,128)S(1)}, u32[]{:S(2)}, u32[]{:S(2)}) collective-permute-start(f32[16,2304]{1,0:T(8,128)S(1)} %add.17.refs_0_), channel_id=1, source_target_pairs={{0,6},{1,7},{2,4},{3,5},{4,2},{5,3},{6,0},{7,1},{8,14},{9,15},{10,... | collective-permute-start | bytes 442376 | tf_op jit(solution)/shard_map/ppermute | solution.py:665
  (19 other events, 87.5 us)

commit v3 on v2

--- a/solution.py
+++ b/solution.py
@@ -20,16 +20,18 @@
 MIB = 1024 * 1024
 COST = pl.CostEstimate(flops=0, bytes_accessed=0, transcendentals=0)
 ATTENTION_COST = pl.CostEstimate(flops=10**10, bytes_accessed=0, transcendentals=0)
+LAST_HEADS = 2
+LATE_OUT = 1
 WHOLE_IN = (False, False)
-WHOLE_OUT = (False, False)
+WHOLE_OUT = (False, True)
 ORDER = (6, 2, 4, 7, 3, 5, 1)
 CHAIN = tuple((place, max(1, place - 3)) for place in range(1, 8))
 PLAN = (
     ((6, 2, 4), ()),
     ((), ()),
-    ((7, 3), ()),
-    ((5, 1), (6, 2)),
-    ((), (4,)),
+    ((3, 5), ()),
+    ((), ()),
+    ((7,), (1,)),
 )
 
 
@@ -82,17 +84,16 @@
     return high, middle, low
 
 
-def side_rows(out_ref, grad_ref, hidden_ref, downq_ref, downv_ref):
-    product = out_ref[...].astype(F32) * grad_ref[...].astype(F32)
+def side_rows(out, grad, hidden, downs):
+    rows = out.shape[0]
+    product = out.astype(F32) * grad.astype(F32)
     heads_at = lax.broadcasted_iota(jnp.int32, (H * HD, 128), 0) // HD
     lanes = lax.broadcasted_iota(jnp.int32, (H * HD, 128), 1)
     pick = jnp.where(heads_at == lanes, 1.0, 0.0).astype(BF16)
-    high, middle, low = (
-        jnp.dot(part, pick, preferred_element_type=F32) for part in three_parts(product)
-    )
-    delta = (high + (middle + low)).T[:H]
-    downs = jnp.concatenate([downq_ref[...], downv_ref[...]], axis=0)
-    return three_parts(delta), dot_nt(downs, hidden_ref[...]).astype(BF16)
+    split = jnp.concatenate(three_parts(product), axis=0)
+    sums = jnp.dot(split, pick, preferred_element_type=F32)
+    delta = (sums[:rows] + (sums[rows : 2 * rows] + sums[2 * rows :])).T[:H]
+    return three_parts(delta), dot_nt(hidden, downs).T.astype(BF16)
 
 
 def pack_kernel(members, heads_here, first_head, stage_heads, with_side, whole, *refs):
@@ -100,7 +101,8 @@
     sources = [refs.pop(0) for _ in range(4)]
     side_refs = [refs.pop(0) for _ in range(5 if with_side else 0)]
     messages = [refs.pop(0) for _ in range(1 if whole else members)]
-    held, in_sems, out_sems = refs
+    held, in_sems, out_sems = refs[:3]
+    side_held, side_sems = refs[3:-1], refs[-1]
     me = lax.axis_index("seq")
     rows = sources[0].shape[0]
     reads = []
@@ -117,27 +119,41 @@
                         in_sems.at[offset, place],
                     )
                 )
-    writes = [
-        pltpu.make_async_copy(
-            held.at[me ^ offset], part_of(messages, me, offset), out_sems.at[offset]
+    bulk = 4 * stage_heads * rows
+
+    def write(offset, low, count, sem):
+        return pltpu.make_async_copy(
+            held.at[me ^ offset, low : low + count],
+            part_of(messages, me, offset).at[low : low + count],
+            sem,
         )
-        for offset in range(members)
+
+    writes = [write(offset, 0, bulk, out_sems.at[0, offset]) for offset in range(members)]
+    side_reads = [
+        pltpu.make_async_copy(ref, there, side_sems.at[place])
+        for place, (ref, there) in enumerate(zip(side_refs, side_held))
     ]
-    for copy in reads:
+    for copy in reads + side_reads:
         copy.start()
-    if with_side:
-        parts, lows = side_rows(*side_refs)
-        blank = jnp.zeros((16 - 3 * heads_here, rows), BF16)
-        for member in range(members):
-            here = slice(member * heads_here, (member + 1) * heads_here)
-            held[member, 4 * stage_heads * rows :] = jnp.concatenate(
-                [part[here] for part in parts] + [blank, lows], axis=0
-            )
     per_message = 4 * stage_heads
     for offset in range(members):
         for place in range(per_message):
             reads[offset * per_message + place].wait()
         writes[offset].start()
+    if with_side:
+        for copy in side_reads:
+            copy.wait()
+        out, grad, hidden, downq, downv = (there[...] for there in side_held)
+        parts, lows = side_rows(out, grad, hidden, jnp.concatenate([downq, downv], axis=0))
+        blank = jnp.zeros((16 - 3 * heads_here, rows), BF16)
+        for member in range(members):
+            here = slice(member * heads_here, (member + 1) * heads_here)
+            held[member, bulk:] = jnp.concatenate(
+                [part[here] for part in parts] + [blank, lows], axis=0
+            )
+        for offset in range(members):
+            writes.append(write(offset, bulk, 32, out_sems.at[1, offset]))
+            writes[-1].start()
     for copy in writes:
         copy.wait()
 
@@ -151,13 +167,15 @@
             pack_kernel, members, heads_here, first_head, stage_heads, bool(side_sources), whole
         ),
         out_shape=group_shapes(whole, members, shape, BF16),
-        in_specs=any_specs(4) + vmem_specs(len(side_sources)),
+        in_specs=any_specs(4 + len(side_sources)),
         out_specs=any_specs(1 if whole else members),
         scratch_shapes=[
             pltpu.VMEM((members,) + shape, BF16),
             pltpu.SemaphoreType.DMA((members, 4 * stage_heads)),
-            pltpu.SemaphoreType.DMA((members,)),
-        ],
+            pltpu.SemaphoreType.DMA((2, members)),
+        ]
+        + [pltpu.VMEM(source.shape, BF16) for source in side_sources]
+        + [pltpu.SemaphoreType.DMA((5,))],
         compiler_params=params(56),
         cost_estimate=COST,
         name="pack",
@@ -199,9 +217,9 @@
     held, side_held, key_flip, grads, key_acc, value_acc, back_ref = refs[:7]
     in_sems, side_sems, out_sems = refs[7:]
     me = lax.axis_index("seq")
-    total = held.shape[1]
-    rows = total // members
     side_low = sides[0].shape[-2] - 32
+    rows = side_held.shape[1] // members
+    total = rows * members
     block = min(256, total)
     reach = total // 2
     rows_of = [
@@ -209,14 +227,11 @@
     ]
     copies = []
     for offset in range(members):
-        for place in range(4 * stage_heads):
-            copies.append(
-                pltpu.make_async_copy(
-                    part_of(messages, me, offset).at[place * rows : (place + 1) * rows],
-                    held.at[place, rows_of[offset], :],
-                    in_sems.at[offset, place],
-                )
-            )
+        copies.append(
+            pltpu.make_async_copy(
+                part_of(messages, me, offset), held.at[me ^ offset], in_sems.at[offset]
+            )
+        )
         copies.append(
             pltpu.make_async_copy(
                 part_of(sides, me, offset).at[side_low : side_low + 32],
@@ -232,8 +247,14 @@
     for copy in copies:
         copy.wait()
     columns = [slice(head * HD, (head + 1) * HD) for head in range(stage_heads)]
+
+    def rows_at(place, low, count):
+        first = low // rows
+        taken = held[pl.ds(first, count // rows), place * rows : (place + 1) * rows, :]
+        return taken.reshape(count, HD)
+
     for head in range(stage_heads):
-        key_flip[head] = held[4 * head + 1].astype(F32).T.astype(BF16)
+        key_flip[head] = rows_at(4 * head + 1, 0, total).astype(F32).T.astype(BF16)
 
     def query_block(low, key_low, width):
         positions = low + lax.broadcasted_iota(jnp.int32, (1, block), 1)
@@ -249,10 +270,10 @@
         parts = side_held[0:16, here].astype(F32)
         for head in range(stage_heads):
             cols = columns[head]
-            query = held[4 * head, here, :]
-            grad = held[4 * head + 3, here, :]
-            scores = dot_nt(held[4 * head + 1, keys_here, :], query) + bias
-            grad_prob = dot_nt(held[4 * head + 2, keys_here, :], grad)
+            query = rows_at(4 * head, low, block)
+            grad = rows_at(4 * head + 3, low, block)
+            scores = dot_nt(rows_at(4 * head + 1, key_low, width), query) + bias
+            grad_prob = dot_nt(rows_at(4 * head + 2, key_low, width), grad)
             top = jnp.max(scores, axis=0, keepdims=True)
             weights = jnp.exp2((scores - top) * (SCALING * LOG2E))
             inverse = 1.0 / jnp.sum(weights, axis=0, keepdims=True)
@@ -269,7 +290,9 @@
             flipped = SCALING * jnp.dot(
                 key_flip[head, :, keys_here], grad_score, preferred_element_type=F32
             )
-            grads[0, here, cols] = flipped.T.astype(BF16)
+            grads[pl.ds(low // rows, block // rows), 0, :, cols] = (
+                flipped.T.astype(BF16).reshape(block // rows, rows, HD)
+            )
             rounded = flipped.astype(BF16).astype(F32)
             first = rounded[: HD // 2]
             second = rounded[HD // 2 :]
@@ -299,9 +322,9 @@
     back_value = jnp.zeros((RANK, total), F32)
     for head in range(stage_heads):
         cols = columns[head]
-        grads[1, :, cols] = (key_acc[head] * SCALING).astype(BF16)
+        grads[:, 1, :, cols] = (key_acc[head] * SCALING).astype(BF16).reshape(members, rows, HD)
         value_grad = value_acc[head].astype(BF16)
-        grads[2, :, cols] = value_grad
+        grads[:, 2, :, cols] = value_grad.reshape(members, rows, HD)
         back_value += dot_nt(upv_ref[:, cols], value_grad)
         terms_ref[RANK : 2 * RANK, cols] = jnp.dot(
             side_held[24:32, :], value_grad, preferred_element_type=F32
@@ -309,7 +332,7 @@
     back_ref[RANK : 2 * RANK, :] = back_value
     copies = [
         pltpu.make_async_copy(
-            grads.at[:, rows_of[offset], :], part_of(outs, me, offset), out_sems.at[offset]
+            grads.at[me ^ offset], part_of(outs, me, offset), out_sems.at[offset]
         )
         for offset in range(members)
     ]
@@ -320,9 +343,9 @@
         back = back + earlier_back[...]
     if last:
         back_ref[...] = back
-        for place, offset in enumerate(pair_offsets(members)):
-            for group, flip in zip(backs, (0, 1)):
-                group[place] = back_ref[:, rows_of[offset ^ flip]]
+        for out, offset in zip(backs, pair_offsets(members)):
+            low = pl.multiple_of((me ^ offset) // 2 * 2 * rows, 2 * rows)
+            out[...] = back_ref[:, pl.ds(low, 2 * rows)]
     else:
         backs[0][...] = back
     for copy in copies:
@@ -349,7 +372,7 @@
     out_shapes = group_shapes(whole_out, members, (3, rows, width), BF16)
     back_shapes = [jax.ShapeDtypeStruct((2 * RANK, total), F32)]
     if last:
-        back_shapes = [jax.ShapeDtypeStruct((members // 2, 2 * RANK, rows), F32)] * 2
+        back_shapes = [jax.ShapeDtypeStruct((2 * RANK, 2 * rows), F32)] * (members // 2)
     earlier = [] if first_head == 0 else list(sides) + [earlier_back]
     counts = (len(messages), len(earlier[:-1]), len(out_shapes), len(back_shapes))
     results = pl.pallas_call(
@@ -361,18 +384,18 @@
         + (any_specs(len(sides)) + vmem_specs(1) if earlier else []),
         out_specs=any_specs(len(out_shapes)) + vmem_specs(len(back_shapes) + 1),
         scratch_shapes=[
-            pltpu.VMEM((4 * stage_heads, total, HD), BF16),
+            pltpu.VMEM((members,) + messages[0].shape[-2:], BF16),
             pltpu.VMEM((32, total), BF16),
             pltpu.VMEM((stage_heads, HD, total), BF16),
-            pltpu.VMEM((3, total, width), BF16),
+            pltpu.VMEM((members, 3, rows, width), BF16),
             pltpu.VMEM((stage_heads, total, HD), F32),
             pltpu.VMEM((stage_heads, total, HD), F32),
             pltpu.VMEM((2 * RANK, total), F32),
-            pltpu.SemaphoreType.DMA((members, 4 * stage_heads)),
+            pltpu.SemaphoreType.DMA((members,)),
             pltpu.SemaphoreType.DMA((members,)),
             pltpu.SemaphoreType.DMA((members,)),
         ],
-        compiler_params=params(56),
+        compiler_params=params(32),
         cost_estimate=ATTENTION_COST,
         name="attention",
     )(lengths, *ups, *turns, *messages, *earlier)
@@ -380,45 +403,67 @@
     return results[:split], results[split:-1], results[-1]
 
 
-def fold_kernel(own_ref, other_ref, *outs):
-    for place, out in enumerate(outs):
-        out[...] = own_ref[place] + other_ref[place]
-
-
-def fold(own, other):
-    count = own.shape[0]
+def small_call(kernel, out_shape, *operands, mebibytes=4, name="sum"):
+    outs = len(out_shape) if isinstance(out_shape, list) else 1
     return pl.pallas_call(
-        fold_kernel,
-        out_shape=[jax.ShapeDtypeStruct(own.shape[1:], F32)] * count,
-        in_specs=vmem_specs(2),
-        out_specs=vmem_specs(count),
-        compiler_params=params(4),
+        kernel,
+        out_shape=out_shape,
+        in_specs=vmem_specs(len(operands)),
+        out_specs=vmem_specs(outs) if isinstance(out_shape, list) else vmem_specs(1)[0],
+        compiler_params=params(mebibytes),
         cost_estimate=COST,
-        name="fold",
-    )(own, other)
-
-
-def down_kernel(members, packs, stage_sizes, hidden_ref, *refs):
-    backs = refs[: members // 2]
-    ups = refs[members // 2 : members // 2 + len(stage_sizes)]
-    messages = refs[members // 2 + len(stage_sizes) :][:packs]
-    held, sems = refs[members // 2 + len(stage_sizes) + packs :]
+        name=name,
+    )(*operands)
+
+
+def total_of(refs):
+    total = refs[0][...]
+    for ref in refs[1:]:
+        total = total + ref[...]
+    return total
+
+
+def fold(tiles, ups):
+    def kernel(*refs):
+        out = refs[-1]
+        low = refs[0].shape[1]
+        out[:, :low] = total_of(refs[: len(tiles)])
+        for up in refs[len(tiles) : -1]:
+            out[:, low : low + up.shape[1]] = up[...]
+            low += up.shape[1]
+
+    width = tiles[0].shape[1] + sum(up.shape[1] for up in ups)
+    shape = jax.ShapeDtypeStruct((2 * RANK, width), F32)
+    return small_call(kernel, shape, *tiles, *ups, name="fold")
+
+
+def down_kernel(members, packs, own_ref, other_ref, hidden_ref, beside_ref, *refs):
+    messages = refs[:packs]
+    held, sems = refs[packs:]
     me = lax.axis_index("seq")
     pack_here = lax.axis_index("dp")
-    total = backs[0][...]
-    for back in backs[1:]:
-        total = total + back[...]
-    terms = jnp.dot(total.astype(BF16), hidden_ref[...], preferred_element_type=F32)
+    first_core = me % 2 == 0
+    rows = hidden_ref.shape[0]
+
+    def half(value):
+        return jnp.where(first_core, value[:RANK], value[RANK:])
+
+    own, other = half(own_ref[...]), half(other_ref[...])
+    back = own[:, : 2 * rows] + other[:, : 2 * rows]
+    here = jnp.where(first_core, back[:, :rows], back[:, rows:]).astype(BF16)
+    there = jnp.where(first_core, back[:, rows:], back[:, :rows]).astype(BF16)
+    terms = jnp.dot(here, hidden_ref[...], preferred_element_type=F32) + jnp.dot(
+        there, beside_ref[...], preferred_element_type=F32
+    )
+    own_up, other_up = own[:, 2 * rows :], other[:, 2 * rows :]
+    ups = jnp.concatenate(
+        [jnp.where(first_core, own_up, other_up), jnp.where(first_core, other_up, own_up)], axis=1
+    )
     down_cols = terms.shape[1] // packs
     sharers = members // packs
     for target in range(packs):
         held[target, :, :down_cols] = terms[:, target * down_cols : (target + 1) * down_cols]
-        low = down_cols
-        for size, up in zip(stage_sizes, ups):
-            held[target, :, low : low + size * HD] = jnp.where(
-                me // sharers == target, up[...], 0.0
-            )
-            low += size * HD
+        held[target, :, down_cols:] = jnp.where(me // sharers == target, ups, 0.0)
     copies = [
         pltpu.make_async_copy(held.at[pack_here ^ offset], messages[offset], sems.at[offset])
         for offset in range(packs)
@@ -429,73 +474,63 @@
         copy.wait()
 
 
-def down_terms(hidden, backs, ups, members, packs):
-    stage_sizes = [up.shape[1] // HD for up in ups]
-    width = hidden.shape[1] // packs + sum(stage_sizes) * HD
+def down_terms(own, other, hidden, beside, members, packs):
+    rows = hidden.shape[0]
+    width = hidden.shape[1] // packs + 2 * (own.shape[1] - 2 * rows)
     return pl.pallas_call(
-        functools.partial(down_kernel, members, packs, stage_sizes),
-        out_shape=[jax.ShapeDtypeStruct((2 * RANK, width), F32)] * packs,
-        in_specs=vmem_specs(1 + len(backs) + len(ups)),
+        functools.partial(down_kernel, members, packs),
+        out_shape=[jax.ShapeDtypeStruct((RANK, width), F32)] * packs,
+        in_specs=vmem_specs(4),
         out_specs=any_specs(packs),
         scratch_shapes=[
-            pltpu.VMEM((packs, 2 * RANK, width), F32),
+            pltpu.VMEM((packs, RANK, width), F32),
             pltpu.SemaphoreType.DMA((packs,)),
         ],
         compiler_params=params(8),
         cost_estimate=COST,
         name="down_terms",
-    )(hidden, *backs, *ups)
-
-
-def packs_kernel(sharers, down_cols, *refs):
-    pieces, out = refs[:-1], refs[-1]
-    me = lax.axis_index("seq")
-    total = pieces[0][...]
-    for piece in pieces[1:]:
-        total = total + piece[...]
-    out[:, :down_cols] = total[:, :down_cols]
-    size = total.shape[1] - down_cols
-    for place in range(sharers):
-        low = down_cols + place * size
-        out[:, low : low + size] = jnp.where(me % sharers == place, total[:, down_cols:], 0.0)
-
-
-def sum_packs(pieces, sharers, down_cols):
-    width = down_cols + sharers * (pieces[0].shape[1] - down_cols)
-    return pl.pallas_call(
-        functools.partial(packs_kernel, sharers, down_cols),
-        out_shape=jax.ShapeDtypeStruct((2 * RANK, width), F32),
-        in_specs=vmem_specs(len(pieces)),
-        out_specs=vmem_specs(1)[0],
-        compiler_params=params(4),
-        cost_estimate=COST,
-        name="sum_packs",
-    )(*pieces)
-
-
-def finish_kernel(down_cols, *refs):
-    pieces, outs = refs[:-4], refs[-4:]
-    total = pieces[0][...]
-    for piece in pieces[1:]:
-        total = total + piece[...]
-    total = total * (ADAPTER_ALPHA / RANK)
-    outs[0][...] = total[:RANK, :down_cols]
-    outs[1][...] = total[:RANK, down_cols:]
-    outs[2][...] = total[RANK:, :down_cols]
-    outs[3][...] = total[RANK:, down_cols:]
-
-
-def finish(pieces, down_cols):
-    up_cols = pieces[0].shape[1] - down_cols
-    return pl.pallas_call(
-        functools.partial(finish_kernel, down_cols),
-        out_shape=[jax.ShapeDtypeStruct((RANK, cols), F32) for cols in (down_cols, up_cols)] * 2,
-        in_specs=vmem_specs(len(pieces)),
-        out_specs=vmem_specs(4),
-        compiler_params=params(4),
-        cost_estimate=COST,
-        name="finish",
-    )(*pieces)
+    )(own, other, hidden, beside)
+
+
+def sum_packs(pieces, sharing_chips, down_cols):
+    size = pieces[0].shape[1] - down_cols
+
+    def kernel(*refs):
+        out = refs[-1]
+        me = lax.axis_index("seq")
+        total = total_of(refs[:-1])
+        out[:, :down_cols] = total[:, :down_cols]
+        for place in range(sharing_chips):
+            low = down_cols + place * size
+            mine = (me // 2) % sharing_chips == place
+            out[:, low : low + size] = jnp.where(mine, total[:, down_cols:], 0.0)
+
+    shape = jax.ShapeDtypeStruct((RANK, down_cols + sharing_chips * size), F32)
+    return small_call(kernel, shape, *pieces, name="sum_packs")
+
+
+def sum_chips(pieces):
+    def kernel(*refs):
+        refs[-1][...] = total_of(refs[:-1]) * (ADAPTER_ALPHA / RANK)
+
+    shape = jax.ShapeDtypeStruct(pieces[0].shape, F32)
+    return small_call(kernel, shape, *pieces, name="sum_chips")
+
+
+def finish(own, other, down_cols):
+    def kernel(own_ref, other_ref, *outs):
+        first_core = lax.axis_index("seq") % 2 == 0
+        mine, beside = own_ref[...], other_ref[...]
+        query = jnp.where(first_core, mine, beside)
+        value = jnp.where(first_core, beside, mine)
+        outs[0][...] = query[:, :down_cols]
+        outs[1][...] = query[:, down_cols:]
+        outs[2][...] = value[:, :down_cols]
+        outs[3][...] = value[:, down_cols:]
+
+    up_cols = own.shape[1] - down_cols
+    shapes = [jax.ShapeDtypeStruct((RANK, cols), F32) for cols in (down_cols, up_cols)] * 2
+    return small_call(kernel, shapes, own, other, name="finish")
 
 
 def unpack_kernel(members, heads_here, stages, counts, *refs):
@@ -603,18 +638,19 @@
     heads_here = H // members
     stages = [(0, heads_here)]
     if heads_here > 1:
-        stages = [(0, heads_here // 2), (heads_here // 2, heads_here - heads_here // 2)]
+        stages = [(0, heads_here - LAST_HEADS), (heads_here - LAST_HEADS, LAST_HEADS)]
     sources = (queries, key_states, value_states, grad_out)
     me = lax.axis_index("seq")
 
     side_sources = (attention_out, grad_out, hidden, down_query, down_value)
     turns = turn_tables(lengths[0], total)
+    beside = lax.ppermute(hidden, "seq", [(i, i ^ 1) for i in range(members)])
     packed = []
     for (first_head, stage_heads), whole in zip(stages, WHOLE_IN):
         extra = () if packed else side_sources
         held_back = sources
         if packed:
-            held_back, _ = lax.optimization_barrier((sources, packed[0][0]))
+            held_back, _, beside = lax.optimization_barrier((sources, packed[0][0], beside))
         packed.append(
             list(pack(held_back, extra, members, heads_here, first_head, stage_heads, whole))
         )
@@ -628,6 +664,8 @@
         if not planned or not offsets:
             return value
         places = [offsets_of(members).index(offset) for offset in offsets]
+        if len(home[stage]) == 1:
+            places = [0]
         taken = tuple(home[stage][place] for place in places)
         value, taken = lax.optimization_barrier((value, taken))
         for place, message in zip(places, taken):
@@ -659,25 +697,38 @@
             rows,
             WHOLE_OUT[index],
         )
-        home.append(exchange(grads, "seq"))
+        back = list(back)
+        home.append(list(grads) if index else exchange(grads, "seq"))
         ups.append(up_terms)
+    home_early = not (planned and len(home[-1]) == 1)
+    if len(home) > 1 and home_early:
+        home[1] = exchange(home[1], "seq")
+
     def swap(value, offset):
         return lax.ppermute(value, "seq", [(i, i ^ offset) for i in range(members)])
 
     def planned_after(value, place):
         return after(after(value, 0, PLAN[place][0]), 1, PLAN[place][1])
 
-    own, other = planned_after(tuple(back), 0)
-    folded = planned_after(tuple(fold(own, swap(other, 1))), 1)
+    back = planned_after(list(back), 0)
     tiles = [
         swap(tile, offset) if offset else tile
-        for offset, tile in zip(pair_offsets(members), folded)
+        for offset, tile in zip(pair_offsets(members), back)
     ]
-    tiles = planned_after(tiles, 2)
-    pieces = exchange(down_terms(hidden, tiles, ups, members, packs), "dp")
+    own = planned_after(fold(tiles, ups), 1)
+    if not home_early and LATE_OUT == -1:
+        own, home[1][0] = lax.optimization_barrier((own, home[1][0]))
+    other = planned_after(swap(own, 1), 2)
+    if not home_early and LATE_OUT == 0:
+        other, home[1][0] = lax.optimization_barrier((other, home[1][0]))
+    pieces = list(down_terms(own, other, hidden, beside, members, packs))
+    if not home_early and LATE_OUT == 1:
+        pieces[0], home[1][0] = lax.optimization_barrier((pieces[0], home[1][0]))
+    if not home_early:
+        home[1] = exchange(home[1], "seq")
+    pieces = exchange(pieces, "dp")
     down_cols = hidden.shape[1] // packs
-    summed = planned_after(sum_packs(pieces, members // packs, down_cols), 3)
-    summed = planned_after(summed + swap(summed, 1), 4)
+    summed = planned_after(sum_packs(pieces, members // packs // 2, down_cols), 3)
     if members == 8:
         pieces = [swap(summed, offset) if offset else summed for offset in pair_offsets(members)]
     else:
@@ -686,7 +737,10 @@
             summed = summed + swap(summed, step)
             step *= 2
         pieces = [summed, swap(summed, step)]
-    down_query_grad, up_query_grad, down_value_grad, up_value_grad = finish(pieces, down_cols)
+    summed = planned_after(sum_chips(pieces), 4)
+    down_query_grad, up_query_grad, down_value_grad, up_value_grad = finish(
+        summed, swap(summed, 1), down_cols
+    )
     grad_queries, grad_keys, value_gradients = unpack(home, members, heads_here, stages)
     return (
         grad_queries,

time: 125 us -> 118 us (0.944)
  waiting for transfers between devices: 33.3 us -> 38.1 us
  starting transfers between devices: 46.3 us -> 41.9 us
  Pallas kernels: 37.1 us -> 32.9 us
  local copies, waits for them, and re-layouts: 4.24 us -> 2.15 us
    ppermute x8, waiting for transfers between devices: 6.58 us -> 15.8 us  [swap(): return lax.ppermute(value, 'seq', [(i, i ^ offset) for i in range(members)])]
    ppermute x31 -> x24, starting transfers between devices: 37.9 us -> 29.8 us  [exchange(): lax.ppermute(message, axis, [(i, i ^ offset) for i in range(count)])]
    pallas_call x2, Pallas kernels: 23.4 us -> 18.7 us  [attention(): pl.pallas_call(functools.partial(attention_kernel, members, heads_here, f...]
    ppermute x31 -> x24, waiting for transfers between devices: 26.7 us -> 22.3 us  [exchange(): lax.ppermute(message, axis, [(i, i ^ offset) for i in range(count)])]
    all_to_all x0 -> x1, starting transfers between devices: none -> 4.31 us  [exchange(): lax.all_to_all(messages[0], axis, split_axis=0, concat_axis=0, tiled=True)]
    unnamed x88 -> x28, local copies, waits for them, and re-layouts: 2.89 us -> 1.4 us
  transfers between devices with their start and end apart: 39 -> 34, of which waited for: 14 -> 14; matrix products, arithmetic and copies ran while one was open for 3% -> 2% of each run, Pallas kernels for 24% -> 27%
where the time goes in v3:
time: 118 us; the launch traced here: 117 us
  starting transfers between devices  41.9 us (36%)
  waiting for transfers between devices  38.1 us (32%)
  Pallas kernels  32.9 us (28%)
  local copies, waits for them, and re-layouts  2.15 us (2%)
  other arithmetic  1.27 us (1%)
    ppermute x24, starting transfers between devices, exchange(): lax.ppermute(message, axis, [(i, i ^ offset) for i in range(count)])  29.8 us
    ppermute x24, waiting for transfers between devices, exchange(): lax.ppermute(message, axis, [(i, i ^ offset) for i in range(count)])  22.3 us
    pallas_call x2, Pallas kernels, attention(): pl.pallas_call(functools.partial(attention_kernel, members, heads_here, f...  18.7 us
    ppermute x8, waiting for transfers between devices, swap(): return lax.ppermute(value, 'seq', [(i, i ^ offset) for i in range(members)])  15.8 us
    pallas_call x2, Pallas kernels, pack(): pl.pallas_call(functools.partial(pack_kernel, members, heads_here, first_...  9.25 us
    ppermute x8, starting transfers between devices, swap(): return lax.ppermute(value, 'seq', [(i, i ^ offset) for i in range(members)])  7.24 us
    all_to_all x1, starting transfers between devices, exchange(): lax.all_to_all(messages[0], axis, split_axis=0, concat_axis=0, tiled=True)  4.31 us
    pallas_call x1, Pallas kernels, unpack(): pl.pallas_call(functools.partial(unpack_kernel, members, heads_here, stag...  3.43 us
  transfers between devices with their start and end apart: 34, of which 14 were waited for; matrix products, arithmetic and copies ran while one was open for 2% of the time, Pallas kernels for 27%

profile of v3, /device:TPU:0, one launch (start us, length us, event | category | flops | bytes accessed | tf_op | source)
XLA Modules:
  0.0 117.3 jit_solution(8553640117935722331)
XLA Ops:
  0.6 0.5 collective-permute-start
  1.2 6.2 %pack.2 = (bf16[1056,128]{1,0:T(8,128)(2,1)}, bf16[1056,128]{1,0:T(8,128)(2,1)}, bf16[1056,128]{1,0:T(8,128)(2,1)}, bf16[1056,128]{1,0:T(8,128)(2,1)}, bf16[1056...) custom-call(bf16[128,4096]{1,0:T(8,128)(2,1)} %refs_0_.2, ...), custom_call_target="tpu_custom_call" | custom-call | tf_op jit(solution)/shard_map/pack/pallas_call | solution.py:165
  7.3 3.5 %collective-permute-start.1 = (bf16[1056,128]{1,0:T(8,128)(2,1)}, bf16[1056,128]{1,0:T(8,128)(2,1)S(1)}, u32[]{:S(2)}, u32[]{:S(2)}) collective-permute-start(bf16[1056,128]{1,0:T(8,128)(2,1)} %get-tuple-element.94), channel_id=1, source_target_pairs={{0,6},{1,7},{2,4},{3,5},{4,2},{5,3},{6,0},{7,1},{8,14},{9,15},{10,... | collective-permute-start | bytes 811016 | tf_op jit(solution)/shard_map/ppermute | solution.py:605
  10.9 0.5 collective-permute-start.2
  11.4 0.1 collective-permute-start.3
  11.5 2.1 %collective-permute-start.4 = (bf16[1056,128]{1,0:T(8,128)(2,1)}, bf16[1056,128]{1,0:T(8,128)(2,1)S(1)}, u32[]{:S(2)}, u32[]{:S(2)}) collective-permute-start(bf16[1056,128]{1,0:T(8,128)(2,1)} %get-tuple-element.106), channel_id=1, source_target_pairs={{0,7},{1,6},{2,5},{3,4},{4,3},{5,2},{6,1},{7,0},{8,15},{9,14},{10,... | collective-permute-start | bytes 811016 | tf_op jit(solution)/shard_map/ppermute | solution.py:605
  13.6 0.2 reduce-window_clone.1
  13.8 0.1 select_reduce_fusion
  13.9 0.7 constant_dynamic-slice_fusion
  14.7 1.1 collective-permute-start.5
  15.7 3.1 %pack.3 = (bf16[1024,128]{1,0:T(8,128)(2,1)}, bf16[1024,128]{1,0:T(8,128)(2,1)}, bf16[1024,128]{1,0:T(8,128)(2,1)}, bf16[1024,128]{1,0:T(8,128)(2,1)}, bf16[1024...) custom-call(bf16[128,4096]{1,0:T(8,128)(2,1)} %refs_0_.2, ...), custom_call_target="tpu_custom_call" | custom-call | tf_op jit(solution)/shard_map/pack/pallas_call | solution.py:165
  18.8 5.4 %collective-permute-done.3.refs_3_.refs_11_ = bf16[1056,128]{1,0:T(8,128)(2,1)S(1)} collective-permute-done((bf16[1056,128]{1,0:T(8,128)(2,1)}, bf16[1056,128]{1,0:T(8,128)(2,1)S(1)}, u32[]{:S(2)}, u32[]{:S(2)}) %collective-permute-start.3) | collective-permute-done | bytes 270368 | tf_op jit(solution)/shard_map/ppermute | solution.py:605
  24.2 1.5 %collective-permute-start.6 = (bf16[1056,128]{1,0:T(8,128)(2,1)S(1)}, bf16[1056,128]{1,0:T(8,128)(2,1)S(1)}, u32[]{:S(2)}, u32[]{:S(2)}) collective-permute-start(bf16[1056,128]{1,0:T(8,128)(2,1)S(1)} %copy-done.13), channel_id=1, source_target_pairs={{0,5},{1,4},{2,7},{3,6},{4,1},{5,0},{6,3},{7,2},{8,13},{9,12},{10,... | collective-permute-start | bytes 811016 | tf_op jit(solution)/shard_map/ppermute | solution.py:605
  25.7 4.1 %collective-permute-done.4.refs_4_.refs_12_ = bf16[1056,128]{1,0:T(8,128)(2,1)S(1)} collective-permute-done((bf16[1056,128]{1,0:T(8,128)(2,1)}, bf16[1056,128]{1,0:T(8,128)(2,1)S(1)}, u32[]{:S(2)}, u32[]{:S(2)}) %collective-permute-start.4) | collective-permute-done | bytes 270368 | tf_op jit(solution)/shard_map/ppermute | solution.py:605
  29.7 0.2 collective-permute-start.7
  29.9 0.0 collective-permute-done.1.refs_1_.refs_9_
  29.9 0.3 collective-permute-start.14
  30.2 1.7 %collective-permute-start.13 = (bf16[1024,128]{1,0:T(8,128)(2,1)}, bf16[1024,128]{1,0:T(8,128)(2,1)S(1)}, u32[]{:S(2)}, u32[]{:S(2)}) collective-permute-start(bf16[1024,128]{1,0:T(8,128)(2,1)} %get-tuple-element.118), channel_id=1, source_target_pairs={{0,5},{1,4},{2,7},{3,6},{4,1},{5,0},{6,3},{7,2},{8,13},{9,12},{10,... | collective-permute-start | bytes 786440 | tf_op jit(solution)/shard_map/ppermute | solution.py:605
  32.0 1.0 multiply_sine_fusion
  33.0 2.5 %collective-permute-done.5.refs_5_.refs_13_ = bf16[1056,128]{1,0:T(8,128)(2,1)S(1)} collective-permute-done((bf16[1056,128]{1,0:T(8,128)(2,1)}, bf16[1056,128]{1,0:T(8,128)(2,1)S(1)}, u32[]{:S(2)}, u32[]{:S(2)}) %collective-permute-start.5) | collective-permute-done | bytes 270368 | tf_op jit(solution)/shard_map/ppermute | solution.py:605
  35.5 1.6 %collective-permute-start.12 = (bf16[1024,128]{1,0:T(8,128)(2,1)}, bf16[1024,128]{1,0:T(8,128)(2,1)S(1)}, u32[]{:S(2)}, u32[]{:S(2)}) collective-permute-start(bf16[1024,128]{1,0:T(8,128)(2,1)} %get-tuple-element.117), channel_id=1, source_target_pairs={{0,3},{1,2},{2,1},{3,0},{4,7},{5,6},{6,5},{7,4},{8,11},{9,10},{10,... | collective-permute-start | bytes 786440 | tf_op jit(solution)/shard_map/ppermute | solution.py:605
  37.1 0.8 collective-permute-start.11
  38.0 0.7 collective-permute-start.10
  38.7 1.5 %collective-permute-start.9 = (bf16[1024,128]{1,0:T(8,128)(2,1)}, bf16[1024,128]{1,0:T(8,128)(2,1)S(1)}, u32[]{:S(2)}, u32[]{:S(2)}) collective-permute-start(bf16[1024,128]{1,0:T(8,128)(2,1)} %get-tuple-element.114), channel_id=1, source_target_pairs={{0,2},{1,3},{2,0},{3,1},{4,6},{5,7},{6,4},{7,5},{8,10},{9,11},{10,... | collective-permute-start | bytes 786440 | tf_op jit(solution)/shard_map/ppermute | solution.py:605
  40.2 1.0 collective-permute-done.13.refs_6_
  41.2 2.7 %collective-permute-start.8 = (bf16[1024,128]{1,0:T(8,128)(2,1)}, bf16[1024,128]{1,0:T(8,128)(2,1)S(1)}, u32[]{:S(2)}, u32[]{:S(2)}) collective-permute-start(bf16[1024,128]{1,0:T(8,128)(2,1)} %get-tuple-element.113), channel_id=1, source_target_pairs={{0,6},{1,7},{2,4},{3,5},{4,2},{5,3},{6,0},{7,1},{8,14},{9,15},{10,... | collective-permute-start | bytes 786440 | tf_op jit(solution)/shard_map/ppermute | solution.py:605
  43.9 10.1 %attention.2 = (bf16[3,128,256]{2,1,0:T(8,128)(2,1)S(1)}, bf16[3,128,256]{2,1,0:T(8,128)(2,1)S(1)}, bf16[3,128,256]{2,1,0:T(8,128)(2,1)S(1)}, bf16[3,128,256]{2,...) custom-call(s32[1,4]{1,0:T(1,128)S(1)} %copy-done.4, ...), custom_call_target="tpu_custom_call" | custom-call | flops 10000000000 | tf_op jit(solution)/shard_map/attention/pallas_call | solution.py:378
  54.0 0.7 copy-done.1
  54.7 0.2 collective-permute-start.15
  54.9 1.7 %collective-permute-start.16 = (bf16[3,128,256]{2,1,0:T(8,128)(2,1)S(1)}, bf16[3,128,256]{2,1,0:T(8,128)(2,1)S(1)}, u32[]{:S(2)}, u32[]{:S(2)}) collective-permute-start(bf16[3,128,256]{2,1,0:T(8,128)(2,1)S(1)} %get-tuple-element.126), channel_id=1, source_target_pairs={{0,2},{1,3},{2,0},{3,1},{4,6},{5,7},{6,4},{7,5},{8,10},{9,11},{10,... | collective-permute-start | bytes 589832 | tf_op jit(solution)/shard_map/ppermute | solution.py:605
  56.6 0.0 collective-permute-done.10.refs_3_
  56.6 1.5 %collective-permute-start.17 = (bf16[3,128,256]{2,1,0:T(8,128)(2,1)S(1)}, bf16[3,128,256]{2,1,0:T(8,128)(2,1)S(1)}, u32[]{:S(2)}, u32[]{:S(2)}) collective-permute-start(bf16[3,128,256]{2,1,0:T(8,128)(2,1)S(1)} %get-tuple-element.127), channel_id=1, source_target_pairs={{0,4},{1,5},{2,6},{3,7},{4,0},{5,1},{6,2},{7,3},{8,12},{9,13},{10,... | collective-permute-start | bytes 589832 | tf_op jit(solution)/shard_map/ppermute | solution.py:605
  58.2 0.0 collective-permute-done.9.refs_2_
  58.2 0.0 collective-permute-start.22
  58.2 3.6 %collective-permute-done.8.refs_1_ = bf16[1024,128]{1,0:T(8,128)(2,1)S(1)} collective-permute-done((bf16[1024,128]{1,0:T(8,128)(2,1)}, bf16[1024,128]{1,0:T(8,128)(2,1)S(1)}, u32[]{:S(2)}, u32[]{:S(2)}) %collective-permute-start.8) | collective-permute-done | bytes 262176 | tf_op jit(solution)/shard_map/ppermute | solution.py:605
  61.7 0.0 collective-permute-start.23
  61.8 8.7 %attention.3 = (bf16[8,3,128,256]{3,2,1,0:T(8,128)(2,1)}, f32[16,256]{1,0:T(8,128)S(1)}, f32[16,256]{1,0:T(8,128)S(1)}, f32[16,256]{1,0:T(8,128)S(1)}, f32[16,256]{1,0:T(8,128)S(1)}, /*index=5*/f32[16,256]{1,0:T(8,128)S(1)}) custom-call(s32[1,4]{1,0:T(1,128)S(1)} %copy-done.4, bf16[8,256]{1,0:T(8,128)(2,1)S(1)} %get-tuple-element.170.upq_ref, ...), custom_call_target="tpu_custom_call" | custom-call | flops 10000000000 | tf_op jit(solution)/shard_map/attention/pallas_call | solution.py:378
  70.5 2.8 %collective-permute-start.18 = (f32[16,256]{1,0:T(8,128)S(1)}, f32[16,256]{1,0:T(8,128)S(1)}, u32[]{:S(2)}, u32[]{:S(2)}) collective-permute-start(f32[16,256]{1,0:T(8,128)S(1)} %get-tuple-element.132), channel_id=1, source_target_pairs={{0,6},{1,7},{2,4},{3,5},{4,2},{5,3},{6,0},{7,1},{8,14},{9,15},{10,... | collective-permute-start | bytes 49160 | tf_op jit(solution)/shard_map/ppermute | solution.py:708
  73.2 0.5 collective-permute-start.19
  73.8 0.3 collective-permute-start.20
  74.0 1.1 collective-permute-done.18.refs_1_
  75.2 1.8 %collective-permute-done.19.refs_2_ = f32[16,256]{1,0:T(8,128)S(1)} collective-permute-done((f32[16,256]{1,0:T(8,128)S(1)}, f32[16,256]{1,0:T(8,128)S(1)}, u32[]{:S(2)}, u32[]{:S(2)}) %collective-permute-start.19) | collective-permute-done | bytes 16416 | tf_op jit(solution)/shard_map/ppermute | solution.py:708
  77.0 0.5 collective-permute-done.20.refs_3_
  77.5 0.1 collective-permute-start.21
  77.6 1.2 %collective-permute-done.21.other_ref = f32[16,768]{1,0:T(8,128)S(1)} collective-permute-done((f32[16,768]{1,0:T(8,128)S(1)}, f32[16,768]{1,0:T(8,128)S(1)}, u32[]{:S(2)}, u32[]{:S(2)}) %collective-permute-start.21) | collective-permute-done | bytes 49184 | tf_op jit(solution)/shard_map/ppermute | solution.py:708
  78.8 0.8 down_terms.1
  79.7 4.3 %all-to-all-start = ((bf16[8,3,128,256]{3,2,1,0:T(8,128)(2,1)}), bf16[8,3,128,256]{3,2,1,0:T(8,128)(2,1)}, u32[]{:S(2)}, u32[]{:S(2)}) async-start(bf16[8,3,128,256]{3,2,1,0:T(8,128)(2,1)} %get-tuple-element.153), calls=%async_computation | async-start | bytes 3145728 | tf_op jit(solution)/shard_map/all_to_all | solution.py:603
  84.0 2.6 %collective-permute-start.30 = (bf16[3,128,256]{2,1,0:T(8,128)(2,1)S(1)}, bf16[3,128,256]{2,1,0:T(8,128)(2,1)S(1)}, u32[]{:S(2)}, u32[]{:S(2)}) collective-permute-start(bf16[3,128,256]{2,1,0:T(8,128)(2,1)S(1)} %get-tuple-element.147), channel_id=1, source_target_pairs={{0,7},{1,6},{2,5},{3,4},{4,3},{5,2},{6,1},{7,0},{8,15},{9,14},{10,... | collective-permute-start | bytes 589832 | tf_op jit(solution)/shard_map/ppermute | solution.py:605
  86.6 1.8 %collective-permute-start.24 = (f32[8,2304]{1,0:T(8,128)S(1)}, f32[8,2304]{1,0:T(8,128)S(1)}, u32[]{:S(2)}, u32[]{:S(2)}) collective-permute-start(f32[8,2304]{1,0:T(8,128)S(1)} %get-tuple-element.144), channel_id=1, source_target_pairs={{0,8},{8,0},{16,24},{24,16},{1,9},{9,1},{17,25},{25,17},{2,10},{10... | collective-permute-start | bytes 221192 | tf_op jit(solution)/shard_map/ppermute | solution.py:605
  88.4 2.4 %collective-permute-start.25 = (f32[8,2304]{1,0:T(8,128)S(1)}, f32[8,2304]{1,0:T(8,128)S(1)}, u32[]{:S(2)}, u32[]{:S(2)}) collective-permute-start(f32[8,2304]{1,0:T(8,128)S(1)} %get-tuple-element.145), channel_id=1, source_target_pairs={{0,16},{8,24},{16,0},{24,8},{1,17},{9,25},{17,1},{25,9},{2,18},{10... | collective-permute-start | bytes 221192 | tf_op jit(solution)/shard_map/ppermute | solution.py:605
  90.8 1.1 collective-permute-start.26
  91.9 1.8 %collective-permute-done.25.refs_2_ = f32[8,2304]{1,0:T(8,128)S(1)} collective-permute-done((f32[8,2304]{1,0:T(8,128)S(1)}, f32[8,2304]{1,0:T(8,128)S(1)}, u32[]{:S(2)}, u32[]{:S(2)}) %collective-permute-start.25) | collective-permute-done | bytes 73760 | tf_op jit(solution)/shard_map/ppermute | solution.py:605
  93.7 4.0 %collective-permute-done.26.refs_3_ = f32[8,2304]{1,0:T(8,128)S(1)} collective-permute-done((f32[8,2304]{1,0:T(8,128)S(1)}, f32[8,2304]{1,0:T(8,128)S(1)}, u32[]{:S(2)}, u32[]{:S(2)}) %collective-permute-start.26) | collective-permute-done | bytes 73760 | tf_op jit(solution)/shard_map/ppermute | solution.py:605
  97.7 0.6 collective-permute-start.29
  98.3 0.2 collective-permute-start.28
  98.4 2.8 %collective-permute-start.27 = (f32[8,2304]{1,0:T(8,128)S(1)}, f32[8,2304]{1,0:T(8,128)S(1)}, u32[]{:S(2)}, u32[]{:S(2)}) collective-permute-start(f32[8,2304]{1,0:T(8,128)S(1)} %sum_packs.1.refs_0_), channel_id=1, source_target_pairs={{0,6},{1,7},{2,4},{3,5},{4,2},{5,3},{6,0},{7,1},{8,14},{9,15},{10,... | collective-permute-start | bytes 221192 | tf_op jit(solution)/shard_map/ppermute | solution.py:708
  101.2 8.8 %collective-permute-done.29.refs_3_ = f32[8,2304]{1,0:T(8,128)S(1)} collective-permute-done((f32[8,2304]{1,0:T(8,128)S(1)}, f32[8,2304]{1,0:T(8,128)S(1)}, u32[]{:S(2)}, u32[]{:S(2)}) %collective-permute-start.29) | collective-permute-done | bytes 73760 | tf_op jit(solution)/shard_map/ppermute | solution.py:708
  110.0 0.4 collective-permute-done.28.refs_2_
  110.4 2.0 %collective-permute-done.27.refs_1_ = f32[8,2304]{1,0:T(8,128)S(1)} collective-permute-done((f32[8,2304]{1,0:T(8,128)S(1)}, f32[8,2304]{1,0:T(8,128)S(1)}, u32[]{:S(2)}, u32[]{:S(2)}) %collective-permute-start.27) | collective-permute-done | bytes 73760 | tf_op jit(solution)/shard_map/ppermute | solution.py:708
  112.4 0.1 collective-permute-start.32
  112.5 0.6 copy-done.10
  113.1 0.1 copy-done.11
  113.2 3.4 %unpack.1 = (bf16[128,4096]{1,0:T(8,128)(2,1)}, bf16[128,4096]{1,0:T(8,128)(2,1)}, bf16[128,4096]{1,0:T(8,128)(2,1)}) custom-call(bf16[3,128,256]{2,1,0:T(8,128)(2,1)} %copy-done.1, bf16[3,128,256]{2,1,0:T(8,128)(2,1)} %copy-done.5, bf16[3,128,256]{2,1,0:T(8,128)(2,1)} %copy-done.6, bf16[3,128,256]{2,1,0:T(8,128)(2,1)} %copy-done.7, ...), custom_call_target="tpu_custom_call" | custom-call | tf_op jit(solution)/shard_map/unpack/pallas_call | solution.py:582
  116.7 0.7 finish.1
  (49 shorter events, 0.2 us)
Async XLA Ops:
  0.6 13.0 %copy-start.4 = (s32[1,4]{1,0:T(1,128)S(1)}, s32[1,4]{1,0:T(1,128)}, u32[]{:S(2)}) copy-start(s32[1,4]{1,0:T(1,128)} %lengths_ref.3) | copy-start | bytes 52
  0.6 14.0 %collective-permute-start = (bf16[128,5120]{1,0:T(8,128)(2,1)}, bf16[128,5120]{1,0:T(8,128)(2,1)S(1)}, u32[]{:S(2)}, u32[]{:S(2)}) collective-permute-start(bf16[128,5120]{1,0:T(8,128)(2,1)} %hidden_ref.1), channel_id=1, source_target_pairs={{0,1},{1,0},{2,3},{3,2},{4,5},{5,4},{6,7},{7,6},{8,9},{9,8},{10,11... | collective-permute-start | bytes 3932168 | tf_op jit(solution)/shard_map/ppermute | solution.py:647
  7.3 22.6 %collective-permute-start.1 = (bf16[1056,128]{1,0:T(8,128)(2,1)}, bf16[1056,128]{1,0:T(8,128)(2,1)S(1)}, u32[]{:S(2)}, u32[]{:S(2)}) collective-permute-start(bf16[1056,128]{1,0:T(8,128)(2,1)} %get-tuple-element.94), channel_id=1, source_target_pairs={{0,6},{1,7},{2,4},{3,5},{4,2},{5,3},{6,0},{7,1},{8,14},{9,15},{10,... | collective-permute-start | bytes 811016 | tf_op jit(solution)/shard_map/ppermute | solution.py:605
  10.9 19.4 %collective-permute-start.2 = (bf16[1056,128]{1,0:T(8,128)(2,1)}, bf16[1056,128]{1,0:T(8,128)(2,1)S(1)}, u32[]{:S(2)}, u32[]{:S(2)}) collective-permute-start(bf16[1056,128]{1,0:T(8,128)(2,1)} %get-tuple-element.100), channel_id=1, source_target_pairs={{0,2},{1,3},{2,0},{3,1},{4,6},{5,7},{6,4},{7,5},{8,10},{9,11},{10,... | collective-permute-start | bytes 811016 | tf_op jit(solution)/shard_map/ppermute | solution.py:605
  11.4 12.8 %collective-permute-start.3 = (bf16[1056,128]{1,0:T(8,128)(2,1)}, bf16[1056,128]{1,0:T(8,128)(2,1)S(1)}, u32[]{:S(2)}, u32[]{:S(2)}) collective-permute-start(bf16[1056,128]{1,0:T(8,128)(2,1)} %get-tuple-element.103), channel_id=1, source_target_pairs={{0,4},{1,5},{2,6},{3,7},{4,0},{5,1},{6,2},{7,3},{8,12},{9,13},{10,... | collective-permute-start | bytes 811016 | tf_op jit(solution)/shard_map/ppermute | solution.py:605
  11.5 18.2 %collective-permute-start.4 = (bf16[1056,128]{1,0:T(8,128)(2,1)}, bf16[1056,128]{1,0:T(8,128)(2,1)S(1)}, u32[]{:S(2)}, u32[]{:S(2)}) collective-permute-start(bf16[1056,128]{1,0:T(8,128)(2,1)} %get-tuple-element.106), channel_id=1, source_target_pairs={{0,7},{1,6},{2,5},{3,4},{4,3},{5,2},{6,1},{7,0},{8,15},{9,14},{10,... | collective-permute-start | bytes 811016 | tf_op jit(solution)/shard_map/ppermute | solution.py:605
  14.7 20.8 %collective-permute-start.5 = (bf16[1056,128]{1,0:T(8,128)(2,1)}, bf16[1056,128]{1,0:T(8,128)(2,1)S(1)}, u32[]{:S(2)}, u32[]{:S(2)}) collective-permute-start(bf16[1056,128]{1,0:T(8,128)(2,1)} %get-tuple-element.108), channel_id=1, source_target_pairs={{0,3},{1,2},{2,1},{3,0},{4,7},{5,6},{6,5},{7,4},{8,11},{9,10},{10,... | collective-permute-start | bytes 811016 | tf_op jit(solution)/shard_map/ppermute | solution.py:605
  15.7 8.4 %copy-start.13 = (bf16[1056,128]{1,0:T(8,128)(2,1)S(1)}, bf16[1056,128]{1,0:T(8,128)(2,1)}, u32[]{:S(2)}) copy-start(bf16[1056,128]{1,0:T(8,128)(2,1)} %get-tuple-element.109) | copy-start | bytes 811012
  15.7 14.0 %copy-start.12 = (bf16[1056,128]{1,0:T(8,128)(2,1)S(1)}, bf16[1056,128]{1,0:T(8,128)(2,1)}, u32[]{:S(2)}) copy-start(bf16[1056,128]{1,0:T(8,128)(2,1)} %get-tuple-element.110) | copy-start | bytes 811012
  15.7 28.2 %copy-start.2 = (bf16[1056,128]{1,0:T(8,128)(2,1)S(1)}, bf16[1056,128]{1,0:T(8,128)(2,1)}, u32[]{:S(2)}) copy-start(bf16[1056,128]{1,0:T(8,128)(2,1)} %get-tuple-element.85.refs_0_.refs_8_) | copy-start | bytes 811012
  24.2 13.0 %collective-permute-start.6 = (bf16[1056,128]{1,0:T(8,128)(2,1)S(1)}, bf16[1056,128]{1,0:T(8,128)(2,1)S(1)}, u32[]{:S(2)}, u32[]{:S(2)}) collective-permute-start(bf16[1056,128]{1,0:T(8,128)(2,1)S(1)} %copy-done.13), channel_id=1, source_target_pairs={{0,5},{1,4},{2,7},{3,6},{4,1},{5,0},{6,3},{7,2},{8,13},{9,12},{10,... | collective-permute-start | bytes 811016 | tf_op jit(solution)/shard_map/ppermute | solution.py:605
  29.7 8.3 %collective-permute-start.7 = (bf16[1056,128]{1,0:T(8,128)(2,1)S(1)}, bf16[1056,128]{1,0:T(8,128)(2,1)S(1)}, u32[]{:S(2)}, u32[]{:S(2)}) collective-permute-start(bf16[1056,128]{1,0:T(8,128)(2,1)S(1)} %copy-done.12), channel_id=1, source_target_pairs={{0,1},{1,0},{2,3},{3,2},{4,5},{5,4},{6,7},{7,6},{8,9},{9,8},{10,11... | collective-permute-start | bytes 811016 | tf_op jit(solution)/shard_map/ppermute | solution.py:605
  29.9 8.8 %collective-permute-start.14 = (bf16[1024,128]{1,0:T(8,128)(2,1)}, bf16[1024,128]{1,0:T(8,128)(2,1)S(1)}, u32[]{:S(2)}, u32[]{:S(2)}) collective-permute-start(bf16[1024,128]{1,0:T(8,128)(2,1)} %get-tuple-element.119), channel_id=1, source_target_pairs={{0,1},{1,0},{2,3},{3,2},{4,5},{5,4},{6,7},{7,6},{8,9},{9,8},{10,11... | collective-permute-start | bytes 786440 | tf_op jit(solution)/shard_map/ppermute | solution.py:605
  30.2 11.0 %collective-permute-start.13 = (bf16[1024,128]{1,0:T(8,128)(2,1)}, bf16[1024,128]{1,0:T(8,128)(2,1)S(1)}, u32[]{:S(2)}, u32[]{:S(2)}) collective-permute-start(bf16[1024,128]{1,0:T(8,128)(2,1)} %get-tuple-element.118), channel_id=1, source_target_pairs={{0,5},{1,4},{2,7},{3,6},{4,1},{5,0},{6,3},{7,2},{8,13},{9,12},{10,... | collective-permute-start | bytes 786440 | tf_op jit(solution)/shard_map/ppermute | solution.py:605
  35.5 19.2 %collective-permute-start.12 = (bf16[1024,128]{1,0:T(8,128)(2,1)}, bf16[1024,128]{1,0:T(8,128)(2,1)S(1)}, u32[]{:S(2)}, u32[]{:S(2)}) collective-permute-start(bf16[1024,128]{1,0:T(8,128)(2,1)} %get-tuple-element.117), channel_id=1, source_target_pairs={{0,3},{1,2},{2,1},{3,0},{4,7},{5,6},{6,5},{7,4},{8,11},{9,10},{10,... | collective-permute-start | bytes 786440 | tf_op jit(solution)/shard_map/ppermute | solution.py:605
  37.1 17.8 %collective-permute-start.11 = (bf16[1024,128]{1,0:T(8,128)(2,1)}, bf16[1024,128]{1,0:T(8,128)(2,1)S(1)}, u32[]{:S(2)}, u32[]{:S(2)}) collective-permute-start(bf16[1024,128]{1,0:T(8,128)(2,1)} %get-tuple-element.116), channel_id=1, source_target_pairs={{0,7},{1,6},{2,5},{3,4},{4,3},{5,2},{6,1},{7,0},{8,15},{9,14},{10,... | collective-permute-start | bytes 786440 | tf_op jit(solution)/shard_map/ppermute | solution.py:605
  38.0 18.6 %collective-permute-start.10 = (bf16[1024,128]{1,0:T(8,128)(2,1)}, bf16[1024,128]{1,0:T(8,128)(2,1)S(1)}, u32[]{:S(2)}, u32[]{:S(2)}) collective-permute-start(bf16[1024,128]{1,0:T(8,128)(2,1)} %get-tuple-element.115), channel_id=1, source_target_pairs={{0,4},{1,5},{2,6},{3,7},{4,0},{5,1},{6,2},{7,3},{8,12},{9,13},{10,... | collective-permute-start | bytes 786440 | tf_op jit(solution)/shard_map/ppermute | solution.py:605
  38.7 19.4 %collective-permute-start.9 = (bf16[1024,128]{1,0:T(8,128)(2,1)}, bf16[1024,128]{1,0:T(8,128)(2,1)S(1)}, u32[]{:S(2)}, u32[]{:S(2)}) collective-permute-start(bf16[1024,128]{1,0:T(8,128)(2,1)} %get-tuple-element.114), channel_id=1, source_target_pairs={{0,2},{1,3},{2,0},{3,1},{4,6},{5,7},{6,4},{7,5},{8,10},{9,11},{10,... | collective-permute-start | bytes 786440 | tf_op jit(solution)/shard_map/ppermute | solution.py:605
  41.2 20.5 %collective-permute-start.8 = (bf16[1024,128]{1,0:T(8,128)(2,1)}, bf16[1024,128]{1,0:T(8,128)(2,1)S(1)}, u32[]{:S(2)}, u32[]{:S(2)}) collective-permute-start(bf16[1024,128]{1,0:T(8,128)(2,1)} %get-tuple-element.113), channel_id=1, source_target_pairs={{0,6},{1,7},{2,4},{3,5},{4,2},{5,3},{6,0},{7,1},{8,14},{9,15},{10,... | collective-permute-start | bytes 786440 | tf_op jit(solution)/shard_map/ppermute | solution.py:605
  43.9 17.9 %copy-start.3 = (bf16[1024,128]{1,0:T(8,128)(2,1)S(1)}, bf16[1024,128]{1,0:T(8,128)(2,1)}, u32[]{:S(2)}) copy-start(bf16[1024,128]{1,0:T(8,128)(2,1)} %get-tuple-element.112.refs_0_) | copy-start | bytes 786436
  54.0 0.7 copy-start.1
  54.7 15.8 %collective-permute-start.15 = (bf16[3,128,256]{2,1,0:T(8,128)(2,1)S(1)}, bf16[3,128,256]{2,1,0:T(8,128)(2,1)S(1)}, u32[]{:S(2)}, u32[]{:S(2)}) collective-permute-start(bf16[3,128,256]{2,1,0:T(8,128)(2,1)S(1)} %get-tuple-element.125), channel_id=1, source_target_pairs={{0,6},{1,7},{2,4},{3,5},{4,2},{5,3},{6,0},{7,1},{8,14},{9,15},{10,... | collective-permute-start | bytes 589832 | tf_op jit(solution)/shard_map/ppermute | solution.py:605
  54.9 15.5 %collective-permute-start.16 = (bf16[3,128,256]{2,1,0:T(8,128)(2,1)S(1)}, bf16[3,128,256]{2,1,0:T(8,128)(2,1)S(1)}, u32[]{:S(2)}, u32[]{:S(2)}) collective-permute-start(bf16[3,128,256]{2,1,0:T(8,128)(2,1)S(1)} %get-tuple-element.126), channel_id=1, source_target_pairs={{0,2},{1,3},{2,0},{3,1},{4,6},{5,7},{6,4},{7,5},{8,10},{9,11},{10,... | collective-permute-start | bytes 589832 | tf_op jit(solution)/shard_map/ppermute | solution.py:605
  56.6 13.8 %collective-permute-start.17 = (bf16[3,128,256]{2,1,0:T(8,128)(2,1)S(1)}, bf16[3,128,256]{2,1,0:T(8,128)(2,1)S(1)}, u32[]{:S(2)}, u32[]{:S(2)}) collective-permute-start(bf16[3,128,256]{2,1,0:T(8,128)(2,1)S(1)} %get-tuple-element.127), channel_id=1, source_target_pairs={{0,4},{1,5},{2,6},{3,7},{4,0},{5,1},{6,2},{7,3},{8,12},{9,13},{10,... | collective-permute-start | bytes 589832 | tf_op jit(solution)/shard_map/ppermute | solution.py:605
  58.2 19.4 %collective-permute-start.22 = (bf16[3,128,256]{2,1,0:T(8,128)(2,1)S(1)}, bf16[3,128,256]{2,1,0:T(8,128)(2,1)S(1)}, u32[]{:S(2)}, u32[]{:S(2)}) collective-permute-start(bf16[3,128,256]{2,1,0:T(8,128)(2,1)S(1)} %get-tuple-element.137), channel_id=1, source_target_pairs={{0,3},{1,2},{2,1},{3,0},{4,7},{5,6},{6,5},{7,4},{8,11},{9,10},{10,... | collective-permute-start | bytes 589832 | tf_op jit(solution)/shard_map/ppermute | solution.py:605
  61.7 15.9 %collective-permute-start.23 = (bf16[3,128,256]{2,1,0:T(8,128)(2,1)S(1)}, bf16[3,128,256]{2,1,0:T(8,128)(2,1)S(1)}, u32[]{:S(2)}, u32[]{:S(2)}) collective-permute-start(bf16[3,128,256]{2,1,0:T(8,128)(2,1)S(1)} %get-tuple-element.138), channel_id=1, source_target_pairs={{0,5},{1,4},{2,7},{3,6},{4,1},{5,0},{6,3},{7,2},{8,13},{9,12},{10,... | collective-permute-start | bytes 589832 | tf_op jit(solution)/shard_map/ppermute | solution.py:605
  61.8 17.1 %copy-start = (bf16[128,5120]{1,0:T(8,128)(2,1)S(1)}, bf16[128,5120]{1,0:T(8,128)(2,1)}, u32[]{:S(2)}) copy-start(bf16[128,5120]{1,0:T(8,128)(2,1)} %hidden_ref.1) | copy-start | bytes 3932164
  70.4 9.3 %copy-start.5 = (bf16[3,128,256]{2,1,0:T(8,128)(2,1)}, bf16[3,128,256]{2,1,0:T(8,128)(2,1)S(1)}, u32[]{:S(2)}) copy-start(bf16[3,128,256]{2,1,0:T(8,128)(2,1)S(1)} %collective-permute-done.15.refs_1_) | copy-start | bytes 589828
  70.4 9.3 %copy-start.6 = (bf16[3,128,256]{2,1,0:T(8,128)(2,1)}, bf16[3,128,256]{2,1,0:T(8,128)(2,1)S(1)}, u32[]{:S(2)}) copy-start(bf16[3,128,256]{2,1,0:T(8,128)(2,1)S(1)} %collective-permute-done.16.refs_2_) | copy-start | bytes 589828
  70.5 9.2 %copy-start.7 = (bf16[3,128,256]{2,1,0:T(8,128)(2,1)}, bf16[3,128,256]{2,1,0:T(8,128)(2,1)S(1)}, u32[]{:S(2)}) copy-start(bf16[3,128,256]{2,1,0:T(8,128)(2,1)S(1)} %collective-permute-done.17.refs_3_) | copy-start | bytes 589828
  70.5 4.7 %collective-permute-start.18 = (f32[16,256]{1,0:T(8,128)S(1)}, f32[16,256]{1,0:T(8,128)S(1)}, u32[]{:S(2)}, u32[]{:S(2)}) collective-permute-start(f32[16,256]{1,0:T(8,128)S(1)} %get-tuple-element.132), channel_id=1, source_target_pairs={{0,6},{1,7},{2,4},{3,5},{4,2},{5,3},{6,0},{7,1},{8,14},{9,15},{10,... | collective-permute-start | bytes 49160 | tf_op jit(solution)/shard_map/ppermute | solution.py:708
  73.2 3.7 %collective-permute-start.19 = (f32[16,256]{1,0:T(8,128)S(1)}, f32[16,256]{1,0:T(8,128)S(1)}, u32[]{:S(2)}, u32[]{:S(2)}) collective-permute-start(f32[16,256]{1,0:T(8,128)S(1)} %get-tuple-element.133), channel_id=1, source_target_pairs={{0,2},{1,3},{2,0},{3,1},{4,6},{5,7},{6,4},{7,5},{8,10},{9,11},{10,... | collective-permute-start | bytes 49160 | tf_op jit(solution)/shard_map/ppermute | solution.py:708
  73.8 3.7 %collective-permute-start.20 = (f32[16,256]{1,0:T(8,128)S(1)}, f32[16,256]{1,0:T(8,128)S(1)}, u32[]{:S(2)}, u32[]{:S(2)}) collective-permute-start(f32[16,256]{1,0:T(8,128)S(1)} %get-tuple-element.134), channel_id=1, source_target_pairs={{0,4},{1,5},{2,6},{3,7},{4,0},{5,1},{6,2},{7,3},{8,12},{9,13},{10,... | collective-permute-start | bytes 49160 | tf_op jit(solution)/shard_map/ppermute | solution.py:708
  77.5 1.3 %collective-permute-start.21 = (f32[16,768]{1,0:T(8,128)S(1)}, f32[16,768]{1,0:T(8,128)S(1)}, u32[]{:S(2)}, u32[]{:S(2)}) collective-permute-start(f32[16,768]{1,0:T(8,128)S(1)} %fold.1.own_ref), channel_id=1, source_target_pairs={{0,1},{1,0},{2,3},{3,2},{4,5},{5,4},{6,7},{7,6},{8,9},{9,8},{10,11... | collective-permute-start | bytes 147464 | tf_op jit(solution)/shard_map/ppermute | solution.py:708
  77.6 2.1 %copy-start.8 = (bf16[3,128,256]{2,1,0:T(8,128)(2,1)}, bf16[3,128,256]{2,1,0:T(8,128)(2,1)S(1)}, u32[]{:S(2)}) copy-start(bf16[3,128,256]{2,1,0:T(8,128)(2,1)S(1)} %collective-permute-done.22.refs_5_) | copy-start | bytes 589828
  77.6 2.1 %copy-start.9 = (bf16[3,128,256]{2,1,0:T(8,128)(2,1)}, bf16[3,128,256]{2,1,0:T(8,128)(2,1)S(1)}, u32[]{:S(2)}) copy-start(bf16[3,128,256]{2,1,0:T(8,128)(2,1)S(1)} %collective-permute-done.23.refs_6_) | copy-start | bytes 589828
  79.7 32.7 %all-to-all-start = ((bf16[8,3,128,256]{3,2,1,0:T(8,128)(2,1)}), bf16[8,3,128,256]{3,2,1,0:T(8,128)(2,1)}, u32[]{:S(2)}, u32[]{:S(2)}) async-start(bf16[8,3,128,256]{3,2,1,0:T(8,128)(2,1)} %get-tuple-element.153), calls=%async_computation | async-start | bytes 3145728 | tf_op jit(solution)/shard_map/all_to_all | solution.py:603
  84.0 28.4 %collective-permute-start.30 = (bf16[3,128,256]{2,1,0:T(8,128)(2,1)S(1)}, bf16[3,128,256]{2,1,0:T(8,128)(2,1)S(1)}, u32[]{:S(2)}, u32[]{:S(2)}) collective-permute-start(bf16[3,128,256]{2,1,0:T(8,128)(2,1)S(1)} %get-tuple-element.147), channel_id=1, source_target_pairs={{0,7},{1,6},{2,5},{3,4},{4,3},{5,2},{6,1},{7,0},{8,15},{9,14},{10,... | collective-permute-start | bytes 589832 | tf_op jit(solution)/shard_map/ppermute | solution.py:605
  86.6 5.3 %collective-permute-start.24 = (f32[8,2304]{1,0:T(8,128)S(1)}, f32[8,2304]{1,0:T(8,128)S(1)}, u32[]{:S(2)}, u32[]{:S(2)}) collective-permute-start(f32[8,2304]{1,0:T(8,128)S(1)} %get-tuple-element.144), channel_id=1, source_target_pairs={{0,8},{8,0},{16,24},{24,16},{1,9},{9,1},{17,25},{25,17},{2,10},{10... | collective-permute-start | bytes 221192 | tf_op jit(solution)/shard_map/ppermute | solution.py:605
  88.4 5.3 %collective-permute-start.25 = (f32[8,2304]{1,0:T(8,128)S(1)}, f32[8,2304]{1,0:T(8,128)S(1)}, u32[]{:S(2)}, u32[]{:S(2)}) collective-permute-start(f32[8,2304]{1,0:T(8,128)S(1)} %get-tuple-element.145), channel_id=1, source_target_pairs={{0,16},{8,24},{16,0},{24,8},{1,17},{9,25},{17,1},{25,9},{2,18},{10... | collective-permute-start | bytes 221192 | tf_op jit(solution)/shard_map/ppermute | solution.py:605
  90.8 6.8 %collective-permute-start.26 = (f32[8,2304]{1,0:T(8,128)S(1)}, f32[8,2304]{1,0:T(8,128)S(1)}, u32[]{:S(2)}, u32[]{:S(2)}) collective-permute-start(f32[8,2304]{1,0:T(8,128)S(1)} %get-tuple-element.146), channel_id=1, source_target_pairs={{0,24},{8,16},{16,8},{24,0},{1,25},{9,17},{17,9},{25,1},{2,26},{10... | collective-permute-start | bytes 221192 | tf_op jit(solution)/shard_map/ppermute | solution.py:605
  91.9 20.6 %collective-permute-start.31 = (bf16[3,128,256]{2,1,0:T(8,128)(2,1)S(1)}, bf16[3,128,256]{2,1,0:T(8,128)(2,1)S(1)}, u32[]{:S(2)}, u32[]{:S(2)}) collective-permute-start(bf16[3,128,256]{2,1,0:T(8,128)(2,1)S(1)} %get-tuple-element.151), channel_id=1, source_target_pairs={{0,1},{1,0},{2,3},{3,2},{4,5},{5,4},{6,7},{7,6},{8,9},{9,8},{10,11... | collective-permute-start | bytes 589832 | tf_op jit(solution)/shard_map/ppermute | solution.py:605
  97.7 12.3 %collective-permute-start.29 = (f32[8,2304]{1,0:T(8,128)S(1)}, f32[8,2304]{1,0:T(8,128)S(1)}, u32[]{:S(2)}, u32[]{:S(2)}) collective-permute-start(f32[8,2304]{1,0:T(8,128)S(1)} %sum_packs.1.refs_0_), channel_id=1, source_target_pairs={{0,4},{1,5},{2,6},{3,7},{4,0},{5,1},{6,2},{7,3},{8,12},{9,13},{10,... | collective-permute-start | bytes 221192 | tf_op jit(solution)/shard_map/ppermute | solution.py:708
  98.3 12.1 %collective-permute-start.28 = (f32[8,2304]{1,0:T(8,128)S(1)}, f32[8,2304]{1,0:T(8,128)S(1)}, u32[]{:S(2)}, u32[]{:S(2)}) collective-permute-start(f32[8,2304]{1,0:T(8,128)S(1)} %sum_packs.1.refs_0_), channel_id=1, source_target_pairs={{0,2},{1,3},{2,0},{3,1},{4,6},{5,7},{6,4},{7,5},{8,10},{9,11},{10,... | collective-permute-start | bytes 221192 | tf_op jit(solution)/shard_map/ppermute | solution.py:708
  98.4 13.9 %collective-permute-start.27 = (f32[8,2304]{1,0:T(8,128)S(1)}, f32[8,2304]{1,0:T(8,128)S(1)}, u32[]{:S(2)}, u32[]{:S(2)}) collective-permute-start(f32[8,2304]{1,0:T(8,128)S(1)} %sum_packs.1.refs_0_), channel_id=1, source_target_pairs={{0,6},{1,7},{2,4},{3,5},{4,2},{5,3},{6,0},{7,1},{8,14},{9,15},{10,... | collective-permute-start | bytes 221192 | tf_op jit(solution)/shard_map/ppermute | solution.py:708
  112.4 0.7 copy-start.10
  112.4 4.2 %collective-permute-start.32 = (f32[8,2304]{1,0:T(8,128)S(1)}, f32[8,2304]{1,0:T(8,128)S(1)}, u32[]{:S(2)}, u32[]{:S(2)}) collective-permute-start(f32[8,2304]{1,0:T(8,128)S(1)} %sum_chips.1.own_ref), channel_id=1, source_target_pairs={{0,1},{1,0},{2,3},{3,2},{4,5},{5,4},{6,7},{7,6},{8,9},{9,8},{10,11... | collective-permute-start | bytes 221192 | tf_op jit(solution)/shard_map/ppermute | solution.py:708
  112.5 0.7 copy-start.11

commit v4 on v3

--- a/solution.py
+++ b/solution.py
@@ -24,14 +24,14 @@
 LATE_OUT = 1
 WHOLE_IN = (False, False)
 WHOLE_OUT = (False, True)
-ORDER = (6, 2, 4, 7, 3, 5, 1)
+ORDER = (6, 2, 4, 3, 5, 7, 1)
 CHAIN = tuple((place, max(1, place - 3)) for place in range(1, 8))
 PLAN = (
     ((6, 2, 4), ()),
     ((), ()),
     ((3, 5), ()),
     ((), ()),
-    ((7,), (1,)),
+    ((7, 1), (1,)),
 )
 
 

time: 118 us -> 116 us (0.983); the launches traced: 117 us -> 117 us
  waiting for transfers between devices: 38.1 us -> 33.1 us
  Pallas kernels: 32.9 us -> 35.8 us
  starting transfers between devices: 41.9 us -> 43.5 us
    ppermute x24, waiting for transfers between devices: 22.3 us -> 15.7 us  [exchange(): lax.ppermute(message, axis, [(i, i ^ offset) for i in range(count)])]
    pallas_call x2, Pallas kernels: 18.7 us -> 21.5 us  [attention(): pl.pallas_call(functools.partial(attention_kernel, members, heads_here, f...]
    ppermute x24, starting transfers between devices: 29.8 us -> 31.5 us  [exchange(): lax.ppermute(message, axis, [(i, i ^ offset) for i in range(count)])]
    ppermute x8, waiting for transfers between devices: 15.8 us -> 17.4 us  [swap(): return lax.ppermute(value, 'seq', [(i, i ^ offset) for i in range(members)])]
  transfers between devices with their start and end apart: 34 -> 34, of which waited for: 14 -> 13; matrix products, arithmetic and copies ran while one was open for 2% -> 2% of each run, Pallas kernels for 27% -> 29%
where the time goes in v4:
time: 116 us; the launch traced here: 117 us
  starting transfers between devices  43.5 us (38%)
  Pallas kernels  35.8 us (31%)
  waiting for transfers between devices  33.1 us (29%)
  local copies, waits for them, and re-layouts  2.11 us (2%)
  other arithmetic  1.27 us (1%)
    ppermute x24, starting transfers between devices, exchange(): lax.ppermute(message, axis, [(i, i ^ offset) for i in range(count)])  31.5 us
    pallas_call x2, Pallas kernels, attention(): pl.pallas_call(functools.partial(attention_kernel, members, heads_here, f...  21.5 us
    ppermute x8, waiting for transfers between devices, swap(): return lax.ppermute(value, 'seq', [(i, i ^ offset) for i in range(members)])  17.4 us
    ppermute x24, waiting for transfers between devices, exchange(): lax.ppermute(message, axis, [(i, i ^ offset) for i in range(count)])  15.7 us
    pallas_call x2, Pallas kernels, pack(): pl.pallas_call(functools.partial(pack_kernel, members, heads_here, first_...  9.27 us
    ppermute x8, starting transfers between devices, swap(): return lax.ppermute(value, 'seq', [(i, i ^ offset) for i in range(members)])  7.24 us
    all_to_all x1, starting transfers between devices, exchange(): lax.all_to_all(messages[0], axis, split_axis=0, concat_axis=0, tiled=True)  4.31 us
    pallas_call x1, Pallas kernels, unpack(): pl.pallas_call(functools.partial(unpack_kernel, members, heads_here, stag...  3.43 us
  transfers between devices with their start and end apart: 34, of which 13 were waited for; matrix products, arithmetic and copies ran while one was open for 2% of the time, Pallas kernels for 29%

profile of v4, /device:TPU:0, one launch (start us, length us, event | category | flops | bytes accessed | tf_op | source)
XLA Modules:
  0.0 116.7 jit_solution(6312122141187193360)
XLA Ops:
  0.6 0.5 collective-permute-start
  1.2 6.2 %pack.2 = (bf16[1056,128]{1,0:T(8,128)(2,1)}, bf16[1056,128]{1,0:T(8,128)(2,1)}, bf16[1056,128]{1,0:T(8,128)(2,1)}, bf16[1056,128]{1,0:T(8,128)(2,1)}, bf16[1056...) custom-call(bf16[128,4096]{1,0:T(8,128)(2,1)} %refs_0_.2, ...), custom_call_target="tpu_custom_call" | custom-call | tf_op jit(solution)/shard_map/pack/pallas_call | solution.py:165
  7.3 3.5 %collective-permute-start.1 = (bf16[1056,128]{1,0:T(8,128)(2,1)}, bf16[1056,128]{1,0:T(8,128)(2,1)S(1)}, u32[]{:S(2)}, u32[]{:S(2)}) collective-permute-start(bf16[1056,128]{1,0:T(8,128)(2,1)} %get-tuple-element.95), channel_id=1, source_target_pairs={{0,6},{1,7},{2,4},{3,5},{4,2},{5,3},{6,0},{7,1},{8,14},{9,15},{10,... | collective-permute-start | bytes 811016 | tf_op jit(solution)/shard_map/ppermute | solution.py:605
  10.9 0.5 collective-permute-start.2
  11.4 0.1 collective-permute-start.3
  11.5 1.1 collective-permute-start.4
  12.7 0.2 reduce-window_clone.1
  12.8 0.1 select_reduce_fusion
  12.9 0.7 constant_dynamic-slice_fusion
  13.7 0.0 collective-permute-done.beside_ref
  13.7 2.1 %collective-permute-start.5 = (bf16[1056,128]{1,0:T(8,128)(2,1)}, bf16[1056,128]{1,0:T(8,128)(2,1)S(1)}, u32[]{:S(2)}, u32[]{:S(2)}) collective-permute-start(bf16[1056,128]{1,0:T(8,128)(2,1)} %get-tuple-element.109), channel_id=1, source_target_pairs={{0,5},{1,4},{2,7},{3,6},{4,1},{5,0},{6,3},{7,2},{8,13},{9,12},{10,... | collective-permute-start | bytes 811016 | tf_op jit(solution)/shard_map/ppermute | solution.py:605
  15.8 3.1 %pack.3 = (bf16[1024,128]{1,0:T(8,128)(2,1)}, bf16[1024,128]{1,0:T(8,128)(2,1)}, bf16[1024,128]{1,0:T(8,128)(2,1)}, bf16[1024,128]{1,0:T(8,128)(2,1)}, bf16[1024...) custom-call(bf16[128,4096]{1,0:T(8,128)(2,1)} %refs_0_.2, ...), custom_call_target="tpu_custom_call" | custom-call | tf_op jit(solution)/shard_map/pack/pallas_call | solution.py:165
  18.9 5.2 %collective-permute-done.3.refs_3_.refs_11_ = bf16[1056,128]{1,0:T(8,128)(2,1)S(1)} collective-permute-done((bf16[1056,128]{1,0:T(8,128)(2,1)}, bf16[1056,128]{1,0:T(8,128)(2,1)S(1)}, u32[]{:S(2)}, u32[]{:S(2)}) %collective-permute-start.3) | collective-permute-done | bytes 270368 | tf_op jit(solution)/shard_map/ppermute | solution.py:605
  24.1 2.2 %collective-permute-start.6 = (bf16[1056,128]{1,0:T(8,128)(2,1)S(1)}, bf16[1056,128]{1,0:T(8,128)(2,1)S(1)}, u32[]{:S(2)}, u32[]{:S(2)}) collective-permute-start(bf16[1056,128]{1,0:T(8,128)(2,1)S(1)} %copy-done.13), channel_id=1, source_target_pairs={{0,7},{1,6},{2,5},{3,4},{4,3},{5,2},{6,1},{7,0},{8,15},{9,14},{10,... | collective-permute-start | bytes 811016 | tf_op jit(solution)/shard_map/ppermute | solution.py:605
  26.3 3.4 %collective-permute-done.4.refs_4_.refs_12_ = bf16[1056,128]{1,0:T(8,128)(2,1)S(1)} collective-permute-done((bf16[1056,128]{1,0:T(8,128)(2,1)}, bf16[1056,128]{1,0:T(8,128)(2,1)S(1)}, u32[]{:S(2)}, u32[]{:S(2)}) %collective-permute-start.4) | collective-permute-done | bytes 270368 | tf_op jit(solution)/shard_map/ppermute | solution.py:605
  29.7 1.0 collective-permute-start.7
  30.6 0.0 collective-permute-done.1.refs_1_.refs_9_
  30.6 0.1 collective-permute-start.14
  30.7 1.5 %collective-permute-start.13 = (bf16[1024,128]{1,0:T(8,128)(2,1)}, bf16[1024,128]{1,0:T(8,128)(2,1)S(1)}, u32[]{:S(2)}, u32[]{:S(2)}) collective-permute-start(bf16[1024,128]{1,0:T(8,128)(2,1)} %get-tuple-element.119), channel_id=1, source_target_pairs={{0,7},{1,6},{2,5},{3,4},{4,3},{5,2},{6,1},{7,0},{8,15},{9,14},{10,... | collective-permute-start | bytes 786440 | tf_op jit(solution)/shard_map/ppermute | solution.py:605
  32.2 1.0 multiply_sine_fusion
  33.2 1.3 %collective-permute-start.12 = (bf16[1024,128]{1,0:T(8,128)(2,1)}, bf16[1024,128]{1,0:T(8,128)(2,1)S(1)}, u32[]{:S(2)}, u32[]{:S(2)}) collective-permute-start(bf16[1024,128]{1,0:T(8,128)(2,1)} %get-tuple-element.118), channel_id=1, source_target_pairs={{0,5},{1,4},{2,7},{3,6},{4,1},{5,0},{6,3},{7,2},{8,13},{9,12},{10,... | collective-permute-start | bytes 786440 | tf_op jit(solution)/shard_map/ppermute | solution.py:605
  34.5 0.9 collective-permute-done.6.refs_6_.refs_14_
  35.4 2.0 %collective-permute-start.11 = (bf16[1024,128]{1,0:T(8,128)(2,1)}, bf16[1024,128]{1,0:T(8,128)(2,1)S(1)}, u32[]{:S(2)}, u32[]{:S(2)}) collective-permute-start(bf16[1024,128]{1,0:T(8,128)(2,1)} %get-tuple-element.117), channel_id=1, source_target_pairs={{0,3},{1,2},{2,1},{3,0},{4,7},{5,6},{6,5},{7,4},{8,11},{9,10},{10,... | collective-permute-start | bytes 786440 | tf_op jit(solution)/shard_map/ppermute | solution.py:605
  37.5 0.0 collective-permute-done.7.refs_7_.refs_15_
  37.5 1.5 %collective-permute-start.10 = (bf16[1024,128]{1,0:T(8,128)(2,1)}, bf16[1024,128]{1,0:T(8,128)(2,1)S(1)}, u32[]{:S(2)}, u32[]{:S(2)}) collective-permute-start(bf16[1024,128]{1,0:T(8,128)(2,1)} %get-tuple-element.116), channel_id=1, source_target_pairs={{0,4},{1,5},{2,6},{3,7},{4,0},{5,1},{6,2},{7,3},{8,12},{9,13},{10,... | collective-permute-start | bytes 786440 | tf_op jit(solution)/shard_map/ppermute | solution.py:605
  39.0 0.5 collective-permute-start.9
  39.5 1.6 %collective-permute-done.13.refs_6_ = bf16[1024,128]{1,0:T(8,128)(2,1)S(1)} collective-permute-done((bf16[1024,128]{1,0:T(8,128)(2,1)}, bf16[1024,128]{1,0:T(8,128)(2,1)S(1)}, u32[]{:S(2)}, u32[]{:S(2)}) %collective-permute-start.13) | collective-permute-done | bytes 262176 | tf_op jit(solution)/shard_map/ppermute | solution.py:605
  41.1 2.4 %collective-permute-start.8 = (bf16[1024,128]{1,0:T(8,128)(2,1)}, bf16[1024,128]{1,0:T(8,128)(2,1)S(1)}, u32[]{:S(2)}, u32[]{:S(2)}) collective-permute-start(bf16[1024,128]{1,0:T(8,128)(2,1)} %get-tuple-element.114), channel_id=1, source_target_pairs={{0,6},{1,7},{2,4},{3,5},{4,2},{5,3},{6,0},{7,1},{8,14},{9,15},{10,... | collective-permute-start | bytes 786440 | tf_op jit(solution)/shard_map/ppermute | solution.py:605
  43.6 11.5 %attention.2 = (bf16[3,128,256]{2,1,0:T(8,128)(2,1)S(1)}, bf16[3,128,256]{2,1,0:T(8,128)(2,1)S(1)}, bf16[3,128,256]{2,1,0:T(8,128)(2,1)S(1)}, bf16[3,128,256]{2,...) custom-call(s32[1,4]{1,0:T(1,128)S(1)} %copy-done.4, ...), custom_call_target="tpu_custom_call" | custom-call | flops 10000000000 | tf_op jit(solution)/shard_map/attention/pallas_call | solution.py:378
  55.1 0.7 copy-done.1
  55.7 0.5 collective-permute-start.15
  56.2 0.0 collective-permute-done.11.refs_4_
  56.2 1.5 %collective-permute-start.16 = (bf16[3,128,256]{2,1,0:T(8,128)(2,1)S(1)}, bf16[3,128,256]{2,1,0:T(8,128)(2,1)S(1)}, u32[]{:S(2)}, u32[]{:S(2)}) collective-permute-start(bf16[3,128,256]{2,1,0:T(8,128)(2,1)S(1)} %get-tuple-element.127), channel_id=1, source_target_pairs={{0,2},{1,3},{2,0},{3,1},{4,6},{5,7},{6,4},{7,5},{8,10},{9,11},{10,... | collective-permute-start | bytes 589832 | tf_op jit(solution)/shard_map/ppermute | solution.py:605
  57.7 0.0 collective-permute-done.10.refs_3_
  57.7 1.5 %collective-permute-start.17 = (bf16[3,128,256]{2,1,0:T(8,128)(2,1)S(1)}, bf16[3,128,256]{2,1,0:T(8,128)(2,1)S(1)}, u32[]{:S(2)}, u32[]{:S(2)}) collective-permute-start(bf16[3,128,256]{2,1,0:T(8,128)(2,1)S(1)} %get-tuple-element.128), channel_id=1, source_target_pairs={{0,4},{1,5},{2,6},{3,7},{4,0},{5,1},{6,2},{7,3},{8,12},{9,13},{10,... | collective-permute-start | bytes 589832 | tf_op jit(solution)/shard_map/ppermute | solution.py:605
  59.2 0.8 collective-permute-start.23
  60.0 10.1 %attention.3 = (bf16[8,3,128,256]{3,2,1,0:T(8,128)(2,1)}, f32[16,256]{1,0:T(8,128)S(1)}, f32[16,256]{1,0:T(8,128)S(1)}, f32[16,256]{1,0:T(8,128)S(1)}, f32[16,256]{1,0:T(8,128)S(1)}, /*index=5*/f32[16,256]{1,0:T(8,128)S(1)}) custom-call(s32[1,4]{1,0:T(1,128)S(1)} %copy-done.4, bf16[8,256]{1,0:T(8,128)(2,1)S(1)} %get-tuple-element.172.upq_ref, ...), custom_call_target="tpu_custom_call" | custom-call | flops 10000000000 | tf_op jit(solution)/shard_map/attention/pallas_call | solution.py:378
  70.2 2.5 %collective-permute-start.18 = (f32[16,256]{1,0:T(8,128)S(1)}, f32[16,256]{1,0:T(8,128)S(1)}, u32[]{:S(2)}, u32[]{:S(2)}) collective-permute-start(f32[16,256]{1,0:T(8,128)S(1)} %get-tuple-element.133), channel_id=1, source_target_pairs={{0,6},{1,7},{2,4},{3,5},{4,2},{5,3},{6,0},{7,1},{8,14},{9,15},{10,... | collective-permute-start | bytes 49160 | tf_op jit(solution)/shard_map/ppermute | solution.py:708
  72.7 0.5 collective-permute-start.19
  73.2 0.5 collective-permute-start.20
  73.7 1.1 collective-permute-done.18.refs_1_
  74.9 1.5 %collective-permute-done.19.refs_2_ = f32[16,256]{1,0:T(8,128)S(1)} collective-permute-done((f32[16,256]{1,0:T(8,128)S(1)}, f32[16,256]{1,0:T(8,128)S(1)}, u32[]{:S(2)}, u32[]{:S(2)}) %collective-permute-start.19) | collective-permute-done | bytes 16416 | tf_op jit(solution)/shard_map/ppermute | solution.py:708
  76.4 0.5 collective-permute-done.20.refs_3_
  77.0 0.1 collective-permute-start.21
  77.1 1.2 %collective-permute-done.21.other_ref = f32[16,768]{1,0:T(8,128)S(1)} collective-permute-done((f32[16,768]{1,0:T(8,128)S(1)}, f32[16,768]{1,0:T(8,128)S(1)}, u32[]{:S(2)}, u32[]{:S(2)}) %collective-permute-start.21) | collective-permute-done | bytes 49184 | tf_op jit(solution)/shard_map/ppermute | solution.py:708
  78.2 0.8 down_terms.1
  79.1 4.3 %all-to-all-start = ((bf16[8,3,128,256]{3,2,1,0:T(8,128)(2,1)}), bf16[8,3,128,256]{3,2,1,0:T(8,128)(2,1)}, u32[]{:S(2)}, u32[]{:S(2)}) async-start(bf16[8,3,128,256]{3,2,1,0:T(8,128)(2,1)} %get-tuple-element.155), calls=%async_computation | async-start | bytes 3145728 | tf_op jit(solution)/shard_map/all_to_all | solution.py:603
  83.5 2.6 %collective-permute-start.30 = (bf16[3,128,256]{2,1,0:T(8,128)(2,1)S(1)}, bf16[3,128,256]{2,1,0:T(8,128)(2,1)S(1)}, u32[]{:S(2)}, u32[]{:S(2)}) collective-permute-start(bf16[3,128,256]{2,1,0:T(8,128)(2,1)S(1)} %get-tuple-element.150), channel_id=1, source_target_pairs={{0,7},{1,6},{2,5},{3,4},{4,3},{5,2},{6,1},{7,0},{8,15},{9,14},{10,... | collective-permute-start | bytes 589832 | tf_op jit(solution)/shard_map/ppermute | solution.py:605
  86.0 0.4 collective-permute-start.31
  86.4 1.6 %collective-permute-start.25 = (f32[8,2304]{1,0:T(8,128)S(1)}, f32[8,2304]{1,0:T(8,128)S(1)}, u32[]{:S(2)}, u32[]{:S(2)}) collective-permute-start(f32[8,2304]{1,0:T(8,128)S(1)} %get-tuple-element.148), channel_id=1, source_target_pairs={{0,16},{8,24},{16,0},{24,8},{1,17},{9,25},{17,1},{25,9},{2,18},{10... | collective-permute-start | bytes 221192 | tf_op jit(solution)/shard_map/ppermute | solution.py:605
  88.0 2.8 %collective-permute-start.26 = (f32[8,2304]{1,0:T(8,128)S(1)}, f32[8,2304]{1,0:T(8,128)S(1)}, u32[]{:S(2)}, u32[]{:S(2)}) collective-permute-start(f32[8,2304]{1,0:T(8,128)S(1)} %get-tuple-element.149), channel_id=1, source_target_pairs={{0,24},{8,16},{16,8},{24,0},{1,25},{9,17},{17,9},{25,1},{2,26},{10... | collective-permute-start | bytes 221192 | tf_op jit(solution)/shard_map/ppermute | solution.py:605
  90.8 1.3 %collective-permute-done.24.refs_1_ = f32[8,2304]{1,0:T(8,128)S(1)} collective-permute-done((f32[8,2304]{1,0:T(8,128)S(1)}, f32[8,2304]{1,0:T(8,128)S(1)}, u32[]{:S(2)}, u32[]{:S(2)}) %collective-permute-start.24) | collective-permute-done | bytes 73760 | tf_op jit(solution)/shard_map/ppermute | solution.py:605
  92.1 3.2 %collective-permute-done.25.refs_2_ = f32[8,2304]{1,0:T(8,128)S(1)} collective-permute-done((f32[8,2304]{1,0:T(8,128)S(1)}, f32[8,2304]{1,0:T(8,128)S(1)}, u32[]{:S(2)}, u32[]{:S(2)}) %collective-permute-start.25) | collective-permute-done | bytes 73760 | tf_op jit(solution)/shard_map/ppermute | solution.py:605
  95.3 0.6 collective-permute-start.29
  95.9 0.3 collective-permute-start.28
  96.2 2.6 %collective-permute-start.27 = (f32[8,2304]{1,0:T(8,128)S(1)}, f32[8,2304]{1,0:T(8,128)S(1)}, u32[]{:S(2)}, u32[]{:S(2)}) collective-permute-start(f32[8,2304]{1,0:T(8,128)S(1)} %sum_packs.1.refs_0_), channel_id=1, source_target_pairs={{0,6},{1,7},{2,4},{3,5},{4,2},{5,3},{6,0},{7,1},{8,14},{9,15},{10,... | collective-permute-start | bytes 221192 | tf_op jit(solution)/shard_map/ppermute | solution.py:708
  98.8 10.4 %collective-permute-done.29.refs_3_ = f32[8,2304]{1,0:T(8,128)S(1)} collective-permute-done((f32[8,2304]{1,0:T(8,128)S(1)}, f32[8,2304]{1,0:T(8,128)S(1)}, u32[]{:S(2)}, u32[]{:S(2)}) %collective-permute-start.29) | collective-permute-done | bytes 73760 | tf_op jit(solution)/shard_map/ppermute | solution.py:708
  109.2 0.6 collective-permute-done.28.refs_2_
  109.8 2.0 %collective-permute-done.27.refs_1_ = f32[8,2304]{1,0:T(8,128)S(1)} collective-permute-done((f32[8,2304]{1,0:T(8,128)S(1)}, f32[8,2304]{1,0:T(8,128)S(1)}, u32[]{:S(2)}, u32[]{:S(2)}) %collective-permute-start.27) | collective-permute-done | bytes 73760 | tf_op jit(solution)/shard_map/ppermute | solution.py:708
  111.9 0.1 collective-permute-start.32
  112.0 0.6 copy-done.10
  112.5 0.1 copy-done.11
  112.6 3.4 %unpack.1 = (bf16[128,4096]{1,0:T(8,128)(2,1)}, bf16[128,4096]{1,0:T(8,128)(2,1)}, bf16[128,4096]{1,0:T(8,128)(2,1)}) custom-call(bf16[3,128,256]{2,1,0:T(8,128)(2,1)} %copy-done.1, bf16[3,128,256]{2,1,0:T(8,128)(2,1)} %copy-done.5, bf16[3,128,256]{2,1,0:T(8,128)(2,1)} %copy-done.6, bf16[3,128,256]{2,1,0:T(8,128)(2,1)} %copy-done.7, ...), custom_call_target="tpu_custom_call" | custom-call | tf_op jit(solution)/shard_map/unpack/pallas_call | solution.py:582
  116.0 0.7 finish.1
  (49 shorter events, 0.2 us)
Async XLA Ops:
  0.6 12.0 %copy-start.4 = (s32[1,4]{1,0:T(1,128)S(1)}, s32[1,4]{1,0:T(1,128)}, u32[]{:S(2)}) copy-start(s32[1,4]{1,0:T(1,128)} %lengths_ref.3) | copy-start | bytes 52
  0.6 13.1 %collective-permute-start = (bf16[128,5120]{1,0:T(8,128)(2,1)}, bf16[128,5120]{1,0:T(8,128)(2,1)S(1)}, u32[]{:S(2)}, u32[]{:S(2)}) collective-permute-start(bf16[128,5120]{1,0:T(8,128)(2,1)} %hidden_ref.1), channel_id=1, source_target_pairs={{0,1},{1,0},{2,3},{3,2},{4,5},{5,4},{6,7},{7,6},{8,9},{9,8},{10,11... | collective-permute-start | bytes 3932168 | tf_op jit(solution)/shard_map/ppermute | solution.py:647
  7.3 23.3 %collective-permute-start.1 = (bf16[1056,128]{1,0:T(8,128)(2,1)}, bf16[1056,128]{1,0:T(8,128)(2,1)S(1)}, u32[]{:S(2)}, u32[]{:S(2)}) collective-permute-start(bf16[1056,128]{1,0:T(8,128)(2,1)} %get-tuple-element.95), channel_id=1, source_target_pairs={{0,6},{1,7},{2,4},{3,5},{4,2},{5,3},{6,0},{7,1},{8,14},{9,15},{10,... | collective-permute-start | bytes 811016 | tf_op jit(solution)/shard_map/ppermute | solution.py:605
  10.9 19.8 %collective-permute-start.2 = (bf16[1056,128]{1,0:T(8,128)(2,1)}, bf16[1056,128]{1,0:T(8,128)(2,1)S(1)}, u32[]{:S(2)}, u32[]{:S(2)}) collective-permute-start(bf16[1056,128]{1,0:T(8,128)(2,1)} %get-tuple-element.101), channel_id=1, source_target_pairs={{0,2},{1,3},{2,0},{3,1},{4,6},{5,7},{6,4},{7,5},{8,10},{9,11},{10,... | collective-permute-start | bytes 811016 | tf_op jit(solution)/shard_map/ppermute | solution.py:605
  11.4 12.7 %collective-permute-start.3 = (bf16[1056,128]{1,0:T(8,128)(2,1)}, bf16[1056,128]{1,0:T(8,128)(2,1)S(1)}, u32[]{:S(2)}, u32[]{:S(2)}) collective-permute-start(bf16[1056,128]{1,0:T(8,128)(2,1)} %get-tuple-element.104), channel_id=1, source_target_pairs={{0,4},{1,5},{2,6},{3,7},{4,0},{5,1},{6,2},{7,3},{8,12},{9,13},{10,... | collective-permute-start | bytes 811016 | tf_op jit(solution)/shard_map/ppermute | solution.py:605
  11.5 18.1 %collective-permute-start.4 = (bf16[1056,128]{1,0:T(8,128)(2,1)}, bf16[1056,128]{1,0:T(8,128)(2,1)S(1)}, u32[]{:S(2)}, u32[]{:S(2)}) collective-permute-start(bf16[1056,128]{1,0:T(8,128)(2,1)} %get-tuple-element.107), channel_id=1, source_target_pairs={{0,3},{1,2},{2,1},{3,0},{4,7},{5,6},{6,5},{7,4},{8,11},{9,10},{10,... | collective-permute-start | bytes 811016 | tf_op jit(solution)/shard_map/ppermute | solution.py:605
  13.7 19.5 %collective-permute-start.5 = (bf16[1056,128]{1,0:T(8,128)(2,1)}, bf16[1056,128]{1,0:T(8,128)(2,1)S(1)}, u32[]{:S(2)}, u32[]{:S(2)}) collective-permute-start(bf16[1056,128]{1,0:T(8,128)(2,1)} %get-tuple-element.109), channel_id=1, source_target_pairs={{0,5},{1,4},{2,7},{3,6},{4,1},{5,0},{6,3},{7,2},{8,13},{9,12},{10,... | collective-permute-start | bytes 811016 | tf_op jit(solution)/shard_map/ppermute | solution.py:605
  15.8 8.3 %copy-start.13 = (bf16[1056,128]{1,0:T(8,128)(2,1)S(1)}, bf16[1056,128]{1,0:T(8,128)(2,1)}, u32[]{:S(2)}) copy-start(bf16[1056,128]{1,0:T(8,128)(2,1)} %get-tuple-element.110) | copy-start | bytes 811012
  15.8 13.9 %copy-start.12 = (bf16[1056,128]{1,0:T(8,128)(2,1)S(1)}, bf16[1056,128]{1,0:T(8,128)(2,1)}, u32[]{:S(2)}) copy-start(bf16[1056,128]{1,0:T(8,128)(2,1)} %get-tuple-element.111) | copy-start | bytes 811012
  15.8 27.8 %copy-start.2 = (bf16[1056,128]{1,0:T(8,128)(2,1)S(1)}, bf16[1056,128]{1,0:T(8,128)(2,1)}, u32[]{:S(2)}) copy-start(bf16[1056,128]{1,0:T(8,128)(2,1)} %get-tuple-element.86.refs_0_.refs_8_) | copy-start | bytes 811012
  24.1 11.3 %collective-permute-start.6 = (bf16[1056,128]{1,0:T(8,128)(2,1)S(1)}, bf16[1056,128]{1,0:T(8,128)(2,1)S(1)}, u32[]{:S(2)}, u32[]{:S(2)}) collective-permute-start(bf16[1056,128]{1,0:T(8,128)(2,1)S(1)} %copy-done.13), channel_id=1, source_target_pairs={{0,7},{1,6},{2,5},{3,4},{4,3},{5,2},{6,1},{7,0},{8,15},{9,14},{10,... | collective-permute-start | bytes 811016 | tf_op jit(solution)/shard_map/ppermute | solution.py:605
  29.7 7.8 %collective-permute-start.7 = (bf16[1056,128]{1,0:T(8,128)(2,1)S(1)}, bf16[1056,128]{1,0:T(8,128)(2,1)S(1)}, u32[]{:S(2)}, u32[]{:S(2)}) collective-permute-start(bf16[1056,128]{1,0:T(8,128)(2,1)S(1)} %copy-done.12), channel_id=1, source_target_pairs={{0,1},{1,0},{2,3},{3,2},{4,5},{5,4},{6,7},{7,6},{8,9},{9,8},{10,11... | collective-permute-start | bytes 811016 | tf_op jit(solution)/shard_map/ppermute | solution.py:605
  30.6 8.3 %collective-permute-start.14 = (bf16[1024,128]{1,0:T(8,128)(2,1)}, bf16[1024,128]{1,0:T(8,128)(2,1)S(1)}, u32[]{:S(2)}, u32[]{:S(2)}) collective-permute-start(bf16[1024,128]{1,0:T(8,128)(2,1)} %get-tuple-element.120), channel_id=1, source_target_pairs={{0,1},{1,0},{2,3},{3,2},{4,5},{5,4},{6,7},{7,6},{8,9},{9,8},{10,11... | collective-permute-start | bytes 786440 | tf_op jit(solution)/shard_map/ppermute | solution.py:605
  30.7 10.4 %collective-permute-start.13 = (bf16[1024,128]{1,0:T(8,128)(2,1)}, bf16[1024,128]{1,0:T(8,128)(2,1)S(1)}, u32[]{:S(2)}, u32[]{:S(2)}) collective-permute-start(bf16[1024,128]{1,0:T(8,128)(2,1)} %get-tuple-element.119), channel_id=1, source_target_pairs={{0,7},{1,6},{2,5},{3,4},{4,3},{5,2},{6,1},{7,0},{8,15},{9,14},{10,... | collective-permute-start | bytes 786440 | tf_op jit(solution)/shard_map/ppermute | solution.py:605
  33.2 22.5 %collective-permute-start.12 = (bf16[1024,128]{1,0:T(8,128)(2,1)}, bf16[1024,128]{1,0:T(8,128)(2,1)S(1)}, u32[]{:S(2)}, u32[]{:S(2)}) collective-permute-start(bf16[1024,128]{1,0:T(8,128)(2,1)} %get-tuple-element.118), channel_id=1, source_target_pairs={{0,5},{1,4},{2,7},{3,6},{4,1},{5,0},{6,3},{7,2},{8,13},{9,12},{10,... | collective-permute-start | bytes 786440 | tf_op jit(solution)/shard_map/ppermute | solution.py:605
  35.4 20.8 %collective-permute-start.11 = (bf16[1024,128]{1,0:T(8,128)(2,1)}, bf16[1024,128]{1,0:T(8,128)(2,1)S(1)}, u32[]{:S(2)}, u32[]{:S(2)}) collective-permute-start(bf16[1024,128]{1,0:T(8,128)(2,1)} %get-tuple-element.117), channel_id=1, source_target_pairs={{0,3},{1,2},{2,1},{3,0},{4,7},{5,6},{6,5},{7,4},{8,11},{9,10},{10,... | collective-permute-start | bytes 786440 | tf_op jit(solution)/shard_map/ppermute | solution.py:605
  37.5 20.2 %collective-permute-start.10 = (bf16[1024,128]{1,0:T(8,128)(2,1)}, bf16[1024,128]{1,0:T(8,128)(2,1)S(1)}, u32[]{:S(2)}, u32[]{:S(2)}) collective-permute-start(bf16[1024,128]{1,0:T(8,128)(2,1)} %get-tuple-element.116), channel_id=1, source_target_pairs={{0,4},{1,5},{2,6},{3,7},{4,0},{5,1},{6,2},{7,3},{8,12},{9,13},{10,... | collective-permute-start | bytes 786440 | tf_op jit(solution)/shard_map/ppermute | solution.py:605
  39.0 20.2 %collective-permute-start.9 = (bf16[1024,128]{1,0:T(8,128)(2,1)}, bf16[1024,128]{1,0:T(8,128)(2,1)S(1)}, u32[]{:S(2)}, u32[]{:S(2)}) collective-permute-start(bf16[1024,128]{1,0:T(8,128)(2,1)} %get-tuple-element.115), channel_id=1, source_target_pairs={{0,2},{1,3},{2,0},{3,1},{4,6},{5,7},{6,4},{7,5},{8,10},{9,11},{10,... | collective-permute-start | bytes 786440 | tf_op jit(solution)/shard_map/ppermute | solution.py:605
  41.1 18.1 %collective-permute-start.8 = (bf16[1024,128]{1,0:T(8,128)(2,1)}, bf16[1024,128]{1,0:T(8,128)(2,1)S(1)}, u32[]{:S(2)}, u32[]{:S(2)}) collective-permute-start(bf16[1024,128]{1,0:T(8,128)(2,1)} %get-tuple-element.114), channel_id=1, source_target_pairs={{0,6},{1,7},{2,4},{3,5},{4,2},{5,3},{6,0},{7,1},{8,14},{9,15},{10,... | collective-permute-start | bytes 786440 | tf_op jit(solution)/shard_map/ppermute | solution.py:605
  43.6 16.5 %copy-start.3 = (bf16[1024,128]{1,0:T(8,128)(2,1)S(1)}, bf16[1024,128]{1,0:T(8,128)(2,1)}, u32[]{:S(2)}) copy-start(bf16[1024,128]{1,0:T(8,128)(2,1)} %get-tuple-element.113.refs_0_) | copy-start | bytes 786436
  55.0 0.7 copy-start.1
  55.7 14.4 %collective-permute-start.15 = (bf16[3,128,256]{2,1,0:T(8,128)(2,1)S(1)}, bf16[3,128,256]{2,1,0:T(8,128)(2,1)S(1)}, u32[]{:S(2)}, u32[]{:S(2)}) collective-permute-start(bf16[3,128,256]{2,1,0:T(8,128)(2,1)S(1)} %get-tuple-element.126), channel_id=1, source_target_pairs={{0,6},{1,7},{2,4},{3,5},{4,2},{5,3},{6,0},{7,1},{8,14},{9,15},{10,... | collective-permute-start | bytes 589832 | tf_op jit(solution)/shard_map/ppermute | solution.py:605
  56.2 13.9 %collective-permute-start.16 = (bf16[3,128,256]{2,1,0:T(8,128)(2,1)S(1)}, bf16[3,128,256]{2,1,0:T(8,128)(2,1)S(1)}, u32[]{:S(2)}, u32[]{:S(2)}) collective-permute-start(bf16[3,128,256]{2,1,0:T(8,128)(2,1)S(1)} %get-tuple-element.127), channel_id=1, source_target_pairs={{0,2},{1,3},{2,0},{3,1},{4,6},{5,7},{6,4},{7,5},{8,10},{9,11},{10,... | collective-permute-start | bytes 589832 | tf_op jit(solution)/shard_map/ppermute | solution.py:605
  57.7 12.4 %collective-permute-start.17 = (bf16[3,128,256]{2,1,0:T(8,128)(2,1)S(1)}, bf16[3,128,256]{2,1,0:T(8,128)(2,1)S(1)}, u32[]{:S(2)}, u32[]{:S(2)}) collective-permute-start(bf16[3,128,256]{2,1,0:T(8,128)(2,1)S(1)} %get-tuple-element.128), channel_id=1, source_target_pairs={{0,4},{1,5},{2,6},{3,7},{4,0},{5,1},{6,2},{7,3},{8,12},{9,13},{10,... | collective-permute-start | bytes 589832 | tf_op jit(solution)/shard_map/ppermute | solution.py:605
  59.2 17.8 %collective-permute-start.22 = (bf16[3,128,256]{2,1,0:T(8,128)(2,1)S(1)}, bf16[3,128,256]{2,1,0:T(8,128)(2,1)S(1)}, u32[]{:S(2)}, u32[]{:S(2)}) collective-permute-start(bf16[3,128,256]{2,1,0:T(8,128)(2,1)S(1)} %get-tuple-element.138), channel_id=1, source_target_pairs={{0,3},{1,2},{2,1},{3,0},{4,7},{5,6},{6,5},{7,4},{8,11},{9,10},{10,... | collective-permute-start | bytes 589832 | tf_op jit(solution)/shard_map/ppermute | solution.py:605
  59.2 17.8 %collective-permute-start.23 = (bf16[3,128,256]{2,1,0:T(8,128)(2,1)S(1)}, bf16[3,128,256]{2,1,0:T(8,128)(2,1)S(1)}, u32[]{:S(2)}, u32[]{:S(2)}) collective-permute-start(bf16[3,128,256]{2,1,0:T(8,128)(2,1)S(1)} %get-tuple-element.139), channel_id=1, source_target_pairs={{0,5},{1,4},{2,7},{3,6},{4,1},{5,0},{6,3},{7,2},{8,13},{9,12},{10,... | collective-permute-start | bytes 589832 | tf_op jit(solution)/shard_map/ppermute | solution.py:605
  60.0 18.2 %copy-start = (bf16[128,5120]{1,0:T(8,128)(2,1)S(1)}, bf16[128,5120]{1,0:T(8,128)(2,1)}, u32[]{:S(2)}) copy-start(bf16[128,5120]{1,0:T(8,128)(2,1)} %hidden_ref.1) | copy-start | bytes 3932164
  70.1 9.0 %copy-start.5 = (bf16[3,128,256]{2,1,0:T(8,128)(2,1)}, bf16[3,128,256]{2,1,0:T(8,128)(2,1)S(1)}, u32[]{:S(2)}) copy-start(bf16[3,128,256]{2,1,0:T(8,128)(2,1)S(1)} %collective-permute-done.15.refs_1_) | copy-start | bytes 589828
  70.1 9.0 %copy-start.6 = (bf16[3,128,256]{2,1,0:T(8,128)(2,1)}, bf16[3,128,256]{2,1,0:T(8,128)(2,1)S(1)}, u32[]{:S(2)}) copy-start(bf16[3,128,256]{2,1,0:T(8,128)(2,1)S(1)} %collective-permute-done.16.refs_2_) | copy-start | bytes 589828
  70.2 9.0 %copy-start.7 = (bf16[3,128,256]{2,1,0:T(8,128)(2,1)}, bf16[3,128,256]{2,1,0:T(8,128)(2,1)S(1)}, u32[]{:S(2)}) copy-start(bf16[3,128,256]{2,1,0:T(8,128)(2,1)S(1)} %collective-permute-done.17.refs_3_) | copy-start | bytes 589828
  70.2 4.7 %collective-permute-start.18 = (f32[16,256]{1,0:T(8,128)S(1)}, f32[16,256]{1,0:T(8,128)S(1)}, u32[]{:S(2)}, u32[]{:S(2)}) collective-permute-start(f32[16,256]{1,0:T(8,128)S(1)} %get-tuple-element.133), channel_id=1, source_target_pairs={{0,6},{1,7},{2,4},{3,5},{4,2},{5,3},{6,0},{7,1},{8,14},{9,15},{10,... | collective-permute-start | bytes 49160 | tf_op jit(solution)/shard_map/ppermute | solution.py:708
  72.7 3.7 %collective-permute-start.19 = (f32[16,256]{1,0:T(8,128)S(1)}, f32[16,256]{1,0:T(8,128)S(1)}, u32[]{:S(2)}, u32[]{:S(2)}) collective-permute-start(f32[16,256]{1,0:T(8,128)S(1)} %get-tuple-element.134), channel_id=1, source_target_pairs={{0,2},{1,3},{2,0},{3,1},{4,6},{5,7},{6,4},{7,5},{8,10},{9,11},{10,... | collective-permute-start | bytes 49160 | tf_op jit(solution)/shard_map/ppermute | solution.py:708
  73.2 3.7 %collective-permute-start.20 = (f32[16,256]{1,0:T(8,128)S(1)}, f32[16,256]{1,0:T(8,128)S(1)}, u32[]{:S(2)}, u32[]{:S(2)}) collective-permute-start(f32[16,256]{1,0:T(8,128)S(1)} %get-tuple-element.135), channel_id=1, source_target_pairs={{0,4},{1,5},{2,6},{3,7},{4,0},{5,1},{6,2},{7,3},{8,12},{9,13},{10,... | collective-permute-start | bytes 49160 | tf_op jit(solution)/shard_map/ppermute | solution.py:708
  77.0 1.3 %collective-permute-start.21 = (f32[16,768]{1,0:T(8,128)S(1)}, f32[16,768]{1,0:T(8,128)S(1)}, u32[]{:S(2)}, u32[]{:S(2)}) collective-permute-start(f32[16,768]{1,0:T(8,128)S(1)} %fold.1.own_ref), channel_id=1, source_target_pairs={{0,1},{1,0},{2,3},{3,2},{4,5},{5,4},{6,7},{7,6},{8,9},{9,8},{10,11... | collective-permute-start | bytes 147464 | tf_op jit(solution)/shard_map/ppermute | solution.py:708
  77.0 2.1 %copy-start.8 = (bf16[3,128,256]{2,1,0:T(8,128)(2,1)}, bf16[3,128,256]{2,1,0:T(8,128)(2,1)S(1)}, u32[]{:S(2)}) copy-start(bf16[3,128,256]{2,1,0:T(8,128)(2,1)S(1)} %collective-permute-done.22.refs_4_) | copy-start | bytes 589828
  77.1 2.1 %copy-start.9 = (bf16[3,128,256]{2,1,0:T(8,128)(2,1)}, bf16[3,128,256]{2,1,0:T(8,128)(2,1)S(1)}, u32[]{:S(2)}) copy-start(bf16[3,128,256]{2,1,0:T(8,128)(2,1)S(1)} %collective-permute-done.23.refs_5_) | copy-start | bytes 589828
  79.1 32.7 %all-to-all-start = ((bf16[8,3,128,256]{3,2,1,0:T(8,128)(2,1)}), bf16[8,3,128,256]{3,2,1,0:T(8,128)(2,1)}, u32[]{:S(2)}, u32[]{:S(2)}) async-start(bf16[8,3,128,256]{3,2,1,0:T(8,128)(2,1)} %get-tuple-element.155), calls=%async_computation | async-start | bytes 3145728 | tf_op jit(solution)/shard_map/all_to_all | solution.py:603
  83.5 28.4 %collective-permute-start.30 = (bf16[3,128,256]{2,1,0:T(8,128)(2,1)S(1)}, bf16[3,128,256]{2,1,0:T(8,128)(2,1)S(1)}, u32[]{:S(2)}, u32[]{:S(2)}) collective-permute-start(bf16[3,128,256]{2,1,0:T(8,128)(2,1)S(1)} %get-tuple-element.150), channel_id=1, source_target_pairs={{0,7},{1,6},{2,5},{3,4},{4,3},{5,2},{6,1},{7,0},{8,15},{9,14},{10,... | collective-permute-start | bytes 589832 | tf_op jit(solution)/shard_map/ppermute | solution.py:605
  86.0 25.8 %collective-permute-start.31 = (bf16[3,128,256]{2,1,0:T(8,128)(2,1)S(1)}, bf16[3,128,256]{2,1,0:T(8,128)(2,1)S(1)}, u32[]{:S(2)}, u32[]{:S(2)}) collective-permute-start(bf16[3,128,256]{2,1,0:T(8,128)(2,1)S(1)} %get-tuple-element.151), channel_id=1, source_target_pairs={{0,1},{1,0},{2,3},{3,2},{4,5},{5,4},{6,7},{7,6},{8,9},{9,8},{10,11... | collective-permute-start | bytes 589832 | tf_op jit(solution)/shard_map/ppermute | solution.py:605
  86.4 5.7 %collective-permute-start.24 = (f32[8,2304]{1,0:T(8,128)S(1)}, f32[8,2304]{1,0:T(8,128)S(1)}, u32[]{:S(2)}, u32[]{:S(2)}) collective-permute-start(f32[8,2304]{1,0:T(8,128)S(1)} %get-tuple-element.147), channel_id=1, source_target_pairs={{0,8},{8,0},{16,24},{24,16},{1,9},{9,1},{17,25},{25,17},{2,10},{10... | collective-permute-start | bytes 221192 | tf_op jit(solution)/shard_map/ppermute | solution.py:605
  86.4 8.8 %collective-permute-start.25 = (f32[8,2304]{1,0:T(8,128)S(1)}, f32[8,2304]{1,0:T(8,128)S(1)}, u32[]{:S(2)}, u32[]{:S(2)}) collective-permute-start(f32[8,2304]{1,0:T(8,128)S(1)} %get-tuple-element.148), channel_id=1, source_target_pairs={{0,16},{8,24},{16,0},{24,8},{1,17},{9,25},{17,1},{25,9},{2,18},{10... | collective-permute-start | bytes 221192 | tf_op jit(solution)/shard_map/ppermute | solution.py:605
  88.0 7.3 %collective-permute-start.26 = (f32[8,2304]{1,0:T(8,128)S(1)}, f32[8,2304]{1,0:T(8,128)S(1)}, u32[]{:S(2)}, u32[]{:S(2)}) collective-permute-start(f32[8,2304]{1,0:T(8,128)S(1)} %get-tuple-element.149), channel_id=1, source_target_pairs={{0,24},{8,16},{16,8},{24,0},{1,25},{9,17},{17,9},{25,1},{2,26},{10... | collective-permute-start | bytes 221192 | tf_op jit(solution)/shard_map/ppermute | solution.py:605
  95.3 14.0 %collective-permute-start.29 = (f32[8,2304]{1,0:T(8,128)S(1)}, f32[8,2304]{1,0:T(8,128)S(1)}, u32[]{:S(2)}, u32[]{:S(2)}) collective-permute-start(f32[8,2304]{1,0:T(8,128)S(1)} %sum_packs.1.refs_0_), channel_id=1, source_target_pairs={{0,4},{1,5},{2,6},{3,7},{4,0},{5,1},{6,2},{7,3},{8,12},{9,13},{10,... | collective-permute-start | bytes 221192 | tf_op jit(solution)/shard_map/ppermute | solution.py:708
  95.9 13.9 %collective-permute-start.28 = (f32[8,2304]{1,0:T(8,128)S(1)}, f32[8,2304]{1,0:T(8,128)S(1)}, u32[]{:S(2)}, u32[]{:S(2)}) collective-permute-start(f32[8,2304]{1,0:T(8,128)S(1)} %sum_packs.1.refs_0_), channel_id=1, source_target_pairs={{0,2},{1,3},{2,0},{3,1},{4,6},{5,7},{6,4},{7,5},{8,10},{9,11},{10,... | collective-permute-start | bytes 221192 | tf_op jit(solution)/shard_map/ppermute | solution.py:708
  96.2 15.6 %collective-permute-start.27 = (f32[8,2304]{1,0:T(8,128)S(1)}, f32[8,2304]{1,0:T(8,128)S(1)}, u32[]{:S(2)}, u32[]{:S(2)}) collective-permute-start(f32[8,2304]{1,0:T(8,128)S(1)} %sum_packs.1.refs_0_), channel_id=1, source_target_pairs={{0,6},{1,7},{2,4},{3,5},{4,2},{5,3},{6,0},{7,1},{8,14},{9,15},{10,... | collective-permute-start | bytes 221192 | tf_op jit(solution)/shard_map/ppermute | solution.py:708
  111.8 0.7 copy-start.10
  111.9 0.7 copy-start.11
  111.9 4.2 %collective-permute-start.32 = (f32[8,2304]{1,0:T(8,128)S(1)}, f32[8,2304]{1,0:T(8,128)S(1)}, u32[]{:S(2)}, u32[]{:S(2)}) collective-permute-start(f32[8,2304]{1,0:T(8,128)S(1)} %sum_chips.1.own_ref), channel_id=1, source_target_pairs={{0,1},{1,0},{2,3},{3,2},{4,5},{5,4},{6,7},{7,6},{8,9},{9,8},{10,11... | collective-permute-start | bytes 221192 | tf_op jit(solution)/shard_map/ppermute | solution.py:708

commit v5 on v4

--- a/solution.py
+++ b/solution.py
@@ -21,7 +21,7 @@
 COST = pl.CostEstimate(flops=0, bytes_accessed=0, transcendentals=0)
 ATTENTION_COST = pl.CostEstimate(flops=10**10, bytes_accessed=0, transcendentals=0)
 LAST_HEADS = 2
-LATE_OUT = 1
+LATE_OUT = 0
 WHOLE_IN = (False, False)
 WHOLE_OUT = (False, True)
 ORDER = (6, 2, 4, 3, 5, 7, 1)

time: 116 us -> 115 us (level); the launches traced: 117 us -> 114 us
  waiting for transfers between devices: 33.1 us -> 30.7 us
  Pallas kernels: 35.8 us -> 33.4 us
  starting transfers between devices: 43.5 us -> 45.2 us
    ppermute x8, waiting for transfers between devices: 17.4 us -> 13.8 us  [swap(): return lax.ppermute(value, 'seq', [(i, i ^ offset) for i in range(members)])]
    pallas_call x2, Pallas kernels: 21.5 us -> 19.1 us  [attention(): pl.pallas_call(functools.partial(attention_kernel, members, heads_here, f...]
    ppermute x24, starting transfers between devices: 31.5 us -> 33 us  [exchange(): lax.ppermute(message, axis, [(i, i ^ offset) for i in range(count)])]
    ppermute x24, waiting for transfers between devices: 15.7 us -> 17 us  [exchange(): lax.ppermute(message, axis, [(i, i ^ offset) for i in range(count)])]
where the time goes in v5:
time: 115 us; the launch traced here: 114 us
  starting transfers between devices  45.2 us (39%)
  Pallas kernels  33.4 us (29%)
  waiting for transfers between devices  30.7 us (27%)
  local copies, waits for them, and re-layouts  2.11 us (2%)
  other arithmetic  1.27 us (1%)
    ppermute x24, starting transfers between devices, exchange(): lax.ppermute(message, axis, [(i, i ^ offset) for i in range(count)])  33 us
    pallas_call x2, Pallas kernels, attention(): pl.pallas_call(functools.partial(attention_kernel, members, heads_here, f...  19.1 us
    ppermute x24, waiting for transfers between devices, exchange(): lax.ppermute(message, axis, [(i, i ^ offset) for i in range(count)])  17 us
    ppermute x8, waiting for transfers between devices, swap(): return lax.ppermute(value, 'seq', [(i, i ^ offset) for i in range(members)])  13.8 us
    pallas_call x2, Pallas kernels, pack(): pl.pallas_call(functools.partial(pack_kernel, members, heads_here, first_...  9.27 us
    ppermute x8, starting transfers between devices, swap(): return lax.ppermute(value, 'seq', [(i, i ^ offset) for i in range(members)])  7.24 us
    all_to_all x1, starting transfers between devices, exchange(): lax.all_to_all(messages[0], axis, split_axis=0, concat_axis=0, tiled=True)  4.44 us
    pallas_call x1, Pallas kernels, unpack(): pl.pallas_call(functools.partial(unpack_kernel, members, heads_here, stag...  3.43 us
  transfers between devices with their start and end apart: 34, of which 13 were waited for; matrix products, arithmetic and copies ran while one was open for 2% of the time, Pallas kernels for 29%

profile of v5, /device:TPU:0, one launch (start us, length us, event | category | flops | bytes accessed | tf_op | source)
XLA Modules:
  0.0 113.6 jit_solution(685024271144797685)
XLA Ops:
  0.6 0.5 collective-permute-start
  1.2 6.2 %pack.2 = (bf16[1056,128]{1,0:T(8,128)(2,1)}, bf16[1056,128]{1,0:T(8,128)(2,1)}, bf16[1056,128]{1,0:T(8,128)(2,1)}, bf16[1056,128]{1,0:T(8,128)(2,1)}, bf16[1056...) custom-call(bf16[128,4096]{1,0:T(8,128)(2,1)} %refs_0_.2, ...), custom_call_target="tpu_custom_call" | custom-call | tf_op jit(solution)/shard_map/pack/pallas_call | solution.py:165
  7.3 3.5 %collective-permute-start.1 = (bf16[1056,128]{1,0:T(8,128)(2,1)}, bf16[1056,128]{1,0:T(8,128)(2,1)S(1)}, u32[]{:S(2)}, u32[]{:S(2)}) collective-permute-start(bf16[1056,128]{1,0:T(8,128)(2,1)} %get-tuple-element.95), channel_id=1, source_target_pairs={{0,6},{1,7},{2,4},{3,5},{4,2},{5,3},{6,0},{7,1},{8,14},{9,15},{10,... | collective-permute-start | bytes 811016 | tf_op jit(solution)/shard_map/ppermute | solution.py:605
  10.9 0.5 collective-permute-start.2
  11.4 0.1 collective-permute-start.3
  11.5 1.1 collective-permute-start.4
  12.7 0.2 reduce-window_clone.1
  12.8 0.1 select_reduce_fusion
  12.9 0.7 constant_dynamic-slice_fusion
  13.7 0.0 collective-permute-done.beside_ref
  13.7 2.1 %collective-permute-start.5 = (bf16[1056,128]{1,0:T(8,128)(2,1)}, bf16[1056,128]{1,0:T(8,128)(2,1)S(1)}, u32[]{:S(2)}, u32[]{:S(2)}) collective-permute-start(bf16[1056,128]{1,0:T(8,128)(2,1)} %get-tuple-element.109), channel_id=1, source_target_pairs={{0,5},{1,4},{2,7},{3,6},{4,1},{5,0},{6,3},{7,2},{8,13},{9,12},{10,... | collective-permute-start | bytes 811016 | tf_op jit(solution)/shard_map/ppermute | solution.py:605
  15.8 3.1 %pack.3 = (bf16[1024,128]{1,0:T(8,128)(2,1)}, bf16[1024,128]{1,0:T(8,128)(2,1)}, bf16[1024,128]{1,0:T(8,128)(2,1)}, bf16[1024,128]{1,0:T(8,128)(2,1)}, bf16[1024...) custom-call(bf16[128,4096]{1,0:T(8,128)(2,1)} %refs_0_.2, ...), custom_call_target="tpu_custom_call" | custom-call | tf_op jit(solution)/shard_map/pack/pallas_call | solution.py:165
  18.9 5.2 %collective-permute-done.3.refs_3_.refs_11_ = bf16[1056,128]{1,0:T(8,128)(2,1)S(1)} collective-permute-done((bf16[1056,128]{1,0:T(8,128)(2,1)}, bf16[1056,128]{1,0:T(8,128)(2,1)S(1)}, u32[]{:S(2)}, u32[]{:S(2)}) %collective-permute-start.3) | collective-permute-done | bytes 270368 | tf_op jit(solution)/shard_map/ppermute | solution.py:605
  24.1 2.2 %collective-permute-start.6 = (bf16[1056,128]{1,0:T(8,128)(2,1)S(1)}, bf16[1056,128]{1,0:T(8,128)(2,1)S(1)}, u32[]{:S(2)}, u32[]{:S(2)}) collective-permute-start(bf16[1056,128]{1,0:T(8,128)(2,1)S(1)} %copy-done.13), channel_id=1, source_target_pairs={{0,7},{1,6},{2,5},{3,4},{4,3},{5,2},{6,1},{7,0},{8,15},{9,14},{10,... | collective-permute-start | bytes 811016 | tf_op jit(solution)/shard_map/ppermute | solution.py:605
  26.3 3.4 %collective-permute-done.4.refs_4_.refs_12_ = bf16[1056,128]{1,0:T(8,128)(2,1)S(1)} collective-permute-done((bf16[1056,128]{1,0:T(8,128)(2,1)}, bf16[1056,128]{1,0:T(8,128)(2,1)S(1)}, u32[]{:S(2)}, u32[]{:S(2)}) %collective-permute-start.4) | collective-permute-done | bytes 270368 | tf_op jit(solution)/shard_map/ppermute | solution.py:605
  29.7 1.0 collective-permute-start.7
  30.6 0.0 collective-permute-done.1.refs_1_.refs_9_
  30.6 0.1 collective-permute-start.14
  30.7 1.5 %collective-permute-start.13 = (bf16[1024,128]{1,0:T(8,128)(2,1)}, bf16[1024,128]{1,0:T(8,128)(2,1)S(1)}, u32[]{:S(2)}, u32[]{:S(2)}) collective-permute-start(bf16[1024,128]{1,0:T(8,128)(2,1)} %get-tuple-element.119), channel_id=1, source_target_pairs={{0,7},{1,6},{2,5},{3,4},{4,3},{5,2},{6,1},{7,0},{8,15},{9,14},{10,... | collective-permute-start | bytes 786440 | tf_op jit(solution)/shard_map/ppermute | solution.py:605
  32.2 1.0 multiply_sine_fusion
  33.2 0.0 collective-permute-done.5.refs_5_.refs_13_
  33.2 1.3 %collective-permute-start.12 = (bf16[1024,128]{1,0:T(8,128)(2,1)}, bf16[1024,128]{1,0:T(8,128)(2,1)S(1)}, u32[]{:S(2)}, u32[]{:S(2)}) collective-permute-start(bf16[1024,128]{1,0:T(8,128)(2,1)} %get-tuple-element.118), channel_id=1, source_target_pairs={{0,5},{1,4},{2,7},{3,6},{4,1},{5,0},{6,3},{7,2},{8,13},{9,12},{10,... | collective-permute-start | bytes 786440 | tf_op jit(solution)/shard_map/ppermute | solution.py:605
  34.5 0.9 collective-permute-done.6.refs_6_.refs_14_
  35.4 2.0 %collective-permute-start.11 = (bf16[1024,128]{1,0:T(8,128)(2,1)}, bf16[1024,128]{1,0:T(8,128)(2,1)S(1)}, u32[]{:S(2)}, u32[]{:S(2)}) collective-permute-start(bf16[1024,128]{1,0:T(8,128)(2,1)} %get-tuple-element.117), channel_id=1, source_target_pairs={{0,3},{1,2},{2,1},{3,0},{4,7},{5,6},{6,5},{7,4},{8,11},{9,10},{10,... | collective-permute-start | bytes 786440 | tf_op jit(solution)/shard_map/ppermute | solution.py:605
  37.5 1.5 %collective-permute-start.10 = (bf16[1024,128]{1,0:T(8,128)(2,1)}, bf16[1024,128]{1,0:T(8,128)(2,1)S(1)}, u32[]{:S(2)}, u32[]{:S(2)}) collective-permute-start(bf16[1024,128]{1,0:T(8,128)(2,1)} %get-tuple-element.116), channel_id=1, source_target_pairs={{0,4},{1,5},{2,6},{3,7},{4,0},{5,1},{6,2},{7,3},{8,12},{9,13},{10,... | collective-permute-start | bytes 786440 | tf_op jit(solution)/shard_map/ppermute | solution.py:605
  39.0 0.5 collective-permute-start.9
  39.5 1.6 %collective-permute-done.13.refs_6_ = bf16[1024,128]{1,0:T(8,128)(2,1)S(1)} collective-permute-done((bf16[1024,128]{1,0:T(8,128)(2,1)}, bf16[1024,128]{1,0:T(8,128)(2,1)S(1)}, u32[]{:S(2)}, u32[]{:S(2)}) %collective-permute-start.13) | collective-permute-done | bytes 262176 | tf_op jit(solution)/shard_map/ppermute | solution.py:605
  41.1 2.4 %collective-permute-start.8 = (bf16[1024,128]{1,0:T(8,128)(2,1)}, bf16[1024,128]{1,0:T(8,128)(2,1)S(1)}, u32[]{:S(2)}, u32[]{:S(2)}) collective-permute-start(bf16[1024,128]{1,0:T(8,128)(2,1)} %get-tuple-element.114), channel_id=1, source_target_pairs={{0,6},{1,7},{2,4},{3,5},{4,2},{5,3},{6,0},{7,1},{8,14},{9,15},{10,... | collective-permute-start | bytes 786440 | tf_op jit(solution)/shard_map/ppermute | solution.py:605
  43.6 10.3 %attention.2 = (bf16[3,128,256]{2,1,0:T(8,128)(2,1)S(1)}, bf16[3,128,256]{2,1,0:T(8,128)(2,1)S(1)}, bf16[3,128,256]{2,1,0:T(8,128)(2,1)S(1)}, bf16[3,128,256]{2,...) custom-call(s32[1,4]{1,0:T(1,128)S(1)} %copy-done.4, ...), custom_call_target="tpu_custom_call" | custom-call | flops 10000000000 | tf_op jit(solution)/shard_map/attention/pallas_call | solution.py:378
  53.8 0.7 copy-done.1
  54.5 0.5 collective-permute-start.15
  55.0 1.5 %collective-permute-start.16 = (bf16[3,128,256]{2,1,0:T(8,128)(2,1)S(1)}, bf16[3,128,256]{2,1,0:T(8,128)(2,1)S(1)}, u32[]{:S(2)}, u32[]{:S(2)}) collective-permute-start(bf16[3,128,256]{2,1,0:T(8,128)(2,1)S(1)} %get-tuple-element.127), channel_id=1, source_target_pairs={{0,2},{1,3},{2,0},{3,1},{4,6},{5,7},{6,4},{7,5},{8,10},{9,11},{10,... | collective-permute-start | bytes 589832 | tf_op jit(solution)/shard_map/ppermute | solution.py:605
  56.5 1.5 %collective-permute-start.17 = (bf16[3,128,256]{2,1,0:T(8,128)(2,1)S(1)}, bf16[3,128,256]{2,1,0:T(8,128)(2,1)S(1)}, u32[]{:S(2)}, u32[]{:S(2)}) collective-permute-start(bf16[3,128,256]{2,1,0:T(8,128)(2,1)S(1)} %get-tuple-element.128), channel_id=1, source_target_pairs={{0,4},{1,5},{2,6},{3,7},{4,0},{5,1},{6,2},{7,3},{8,12},{9,13},{10,... | collective-permute-start | bytes 589832 | tf_op jit(solution)/shard_map/ppermute | solution.py:605
  58.0 0.1 collective-permute-done.8.refs_1_
  58.2 1.0 collective-permute-start.23
  59.2 8.9 %attention.3 = (bf16[8,3,128,256]{3,2,1,0:T(8,128)(2,1)}, f32[16,256]{1,0:T(8,128)S(1)}, f32[16,256]{1,0:T(8,128)S(1)}, f32[16,256]{1,0:T(8,128)S(1)}, f32[16,256]{1,0:T(8,128)S(1)}, /*index=5*/f32[16,256]{1,0:T(8,128)S(1)}) custom-call(s32[1,4]{1,0:T(1,128)S(1)} %copy-done.4, bf16[8,256]{1,0:T(8,128)(2,1)S(1)} %get-tuple-element.172.upq_ref, ...), custom_call_target="tpu_custom_call" | custom-call | flops 10000000000 | tf_op jit(solution)/shard_map/attention/pallas_call | solution.py:378
  68.1 2.2 %collective-permute-start.18 = (f32[16,256]{1,0:T(8,128)S(1)}, f32[16,256]{1,0:T(8,128)S(1)}, u32[]{:S(2)}, u32[]{:S(2)}) collective-permute-start(f32[16,256]{1,0:T(8,128)S(1)} %get-tuple-element.133), channel_id=1, source_target_pairs={{0,6},{1,7},{2,4},{3,5},{4,2},{5,3},{6,0},{7,1},{8,14},{9,15},{10,... | collective-permute-start | bytes 49160 | tf_op jit(solution)/shard_map/ppermute | solution.py:708
  70.3 0.5 collective-permute-start.19
  70.8 0.8 collective-permute-start.20
  71.6 1.1 %collective-permute-done.18.refs_1_ = f32[16,256]{1,0:T(8,128)S(1)} collective-permute-done((f32[16,256]{1,0:T(8,128)S(1)}, f32[16,256]{1,0:T(8,128)S(1)}, u32[]{:S(2)}, u32[]{:S(2)}) %collective-permute-start.18) | collective-permute-done | bytes 16416 | tf_op jit(solution)/shard_map/ppermute | solution.py:708
  72.8 1.3 %collective-permute-done.19.refs_2_ = f32[16,256]{1,0:T(8,128)S(1)} collective-permute-done((f32[16,256]{1,0:T(8,128)S(1)}, f32[16,256]{1,0:T(8,128)S(1)}, u32[]{:S(2)}, u32[]{:S(2)}) %collective-permute-start.19) | collective-permute-done | bytes 16416 | tf_op jit(solution)/shard_map/ppermute | solution.py:708
  74.1 0.5 collective-permute-done.20.refs_3_
  74.5 0.1 collective-permute-start.21
  74.7 1.2 %collective-permute-done.21.other_ref = f32[16,768]{1,0:T(8,128)S(1)} collective-permute-done((f32[16,768]{1,0:T(8,128)S(1)}, f32[16,768]{1,0:T(8,128)S(1)}, u32[]{:S(2)}, u32[]{:S(2)}) %collective-permute-start.21) | collective-permute-done | bytes 49184 | tf_op jit(solution)/shard_map/ppermute | solution.py:708
  75.8 0.0 copy-start
  75.9 4.4 %all-to-all-start = ((bf16[8,3,128,256]{3,2,1,0:T(8,128)(2,1)}), bf16[8,3,128,256]{3,2,1,0:T(8,128)(2,1)}, u32[]{:S(2)}, u32[]{:S(2)}) async-start(bf16[8,3,128,256]{3,2,1,0:T(8,128)(2,1)} %get-tuple-element.155), calls=%async_computation | async-start | bytes 3145728 | tf_op jit(solution)/shard_map/all_to_all | solution.py:603
  80.3 2.6 %collective-permute-start.30 = (bf16[3,128,256]{2,1,0:T(8,128)(2,1)S(1)}, bf16[3,128,256]{2,1,0:T(8,128)(2,1)S(1)}, u32[]{:S(2)}, u32[]{:S(2)}) collective-permute-start(bf16[3,128,256]{2,1,0:T(8,128)(2,1)S(1)} %get-tuple-element.150), channel_id=1, source_target_pairs={{0,7},{1,6},{2,5},{3,4},{4,3},{5,2},{6,1},{7,0},{8,15},{9,14},{10,... | collective-permute-start | bytes 589832 | tf_op jit(solution)/shard_map/ppermute | solution.py:605
  82.9 0.4 collective-permute-start.31
  83.3 0.8 down_terms.1
  84.1 3.2 %collective-permute-start.24 = (f32[8,2304]{1,0:T(8,128)S(1)}, f32[8,2304]{1,0:T(8,128)S(1)}, u32[]{:S(2)}, u32[]{:S(2)}) collective-permute-start(f32[8,2304]{1,0:T(8,128)S(1)} %get-tuple-element.147), channel_id=1, source_target_pairs={{0,8},{8,0},{16,24},{24,16},{1,9},{9,1},{17,25},{25,17},{2,10},{10... | collective-permute-start | bytes 221192 | tf_op jit(solution)/shard_map/ppermute | solution.py:605
  87.3 1.0 collective-permute-start.25
  88.4 1.4 %collective-permute-start.26 = (f32[8,2304]{1,0:T(8,128)S(1)}, f32[8,2304]{1,0:T(8,128)S(1)}, u32[]{:S(2)}, u32[]{:S(2)}) collective-permute-start(f32[8,2304]{1,0:T(8,128)S(1)} %get-tuple-element.149), channel_id=1, source_target_pairs={{0,24},{8,16},{16,8},{24,0},{1,25},{9,17},{17,9},{25,1},{2,26},{10... | collective-permute-start | bytes 221192 | tf_op jit(solution)/shard_map/ppermute | solution.py:605
  89.8 0.2 collective-permute-done.24.refs_1_
  90.0 5.4 %collective-permute-done.25.refs_2_ = f32[8,2304]{1,0:T(8,128)S(1)} collective-permute-done((f32[8,2304]{1,0:T(8,128)S(1)}, f32[8,2304]{1,0:T(8,128)S(1)}, u32[]{:S(2)}, u32[]{:S(2)}) %collective-permute-start.25) | collective-permute-done | bytes 73760 | tf_op jit(solution)/shard_map/ppermute | solution.py:605
  95.4 0.6 collective-permute-start.29
  96.0 0.3 collective-permute-start.28
  96.3 2.6 %collective-permute-start.27 = (f32[8,2304]{1,0:T(8,128)S(1)}, f32[8,2304]{1,0:T(8,128)S(1)}, u32[]{:S(2)}, u32[]{:S(2)}) collective-permute-start(f32[8,2304]{1,0:T(8,128)S(1)} %sum_packs.1.refs_0_), channel_id=1, source_target_pairs={{0,6},{1,7},{2,4},{3,5},{4,2},{5,3},{6,0},{7,1},{8,14},{9,15},{10,... | collective-permute-start | bytes 221192 | tf_op jit(solution)/shard_map/ppermute | solution.py:708
  99.0 8.5 %collective-permute-done.29.refs_3_ = f32[8,2304]{1,0:T(8,128)S(1)} collective-permute-done((f32[8,2304]{1,0:T(8,128)S(1)}, f32[8,2304]{1,0:T(8,128)S(1)}, u32[]{:S(2)}, u32[]{:S(2)}) %collective-permute-start.29) | collective-permute-done | bytes 73760 | tf_op jit(solution)/shard_map/ppermute | solution.py:708
  107.5 1.2 %collective-permute-done.27.refs_1_ = f32[8,2304]{1,0:T(8,128)S(1)} collective-permute-done((f32[8,2304]{1,0:T(8,128)S(1)}, f32[8,2304]{1,0:T(8,128)S(1)}, u32[]{:S(2)}, u32[]{:S(2)}) %collective-permute-start.27) | collective-permute-done | bytes 73760 | tf_op jit(solution)/shard_map/ppermute | solution.py:708
  108.7 0.1 collective-permute-start.32
  108.8 0.6 copy-done.10
  109.4 0.1 copy-done.11
  109.5 3.4 %unpack.1 = (bf16[128,4096]{1,0:T(8,128)(2,1)}, bf16[128,4096]{1,0:T(8,128)(2,1)}, bf16[128,4096]{1,0:T(8,128)(2,1)}) custom-call(bf16[3,128,256]{2,1,0:T(8,128)(2,1)} %copy-done.1, bf16[3,128,256]{2,1,0:T(8,128)(2,1)} %copy-done.5, bf16[3,128,256]{2,1,0:T(8,128)(2,1)} %copy-done.6, bf16[3,128,256]{2,1,0:T(8,128)(2,1)} %copy-done.7, ...), custom_call_target="tpu_custom_call" | custom-call | tf_op jit(solution)/shard_map/unpack/pallas_call | solution.py:582
  112.9 0.7 finish.1
  (49 shorter events, 0.2 us)
Async XLA Ops:
  0.6 12.0 %copy-start.4 = (s32[1,4]{1,0:T(1,128)S(1)}, s32[1,4]{1,0:T(1,128)}, u32[]{:S(2)}) copy-start(s32[1,4]{1,0:T(1,128)} %lengths_ref.3) | copy-start | bytes 52
  0.6 13.1 %collective-permute-start = (bf16[128,5120]{1,0:T(8,128)(2,1)}, bf16[128,5120]{1,0:T(8,128)(2,1)S(1)}, u32[]{:S(2)}, u32[]{:S(2)}) collective-permute-start(bf16[128,5120]{1,0:T(8,128)(2,1)} %hidden_ref.1), channel_id=1, source_target_pairs={{0,1},{1,0},{2,3},{3,2},{4,5},{5,4},{6,7},{7,6},{8,9},{9,8},{10,11... | collective-permute-start | bytes 3932168 | tf_op jit(solution)/shard_map/ppermute | solution.py:647
  7.3 23.3 %collective-permute-start.1 = (bf16[1056,128]{1,0:T(8,128)(2,1)}, bf16[1056,128]{1,0:T(8,128)(2,1)S(1)}, u32[]{:S(2)}, u32[]{:S(2)}) collective-permute-start(bf16[1056,128]{1,0:T(8,128)(2,1)} %get-tuple-element.95), channel_id=1, source_target_pairs={{0,6},{1,7},{2,4},{3,5},{4,2},{5,3},{6,0},{7,1},{8,14},{9,15},{10,... | collective-permute-start | bytes 811016 | tf_op jit(solution)/shard_map/ppermute | solution.py:605
  10.9 19.8 %collective-permute-start.2 = (bf16[1056,128]{1,0:T(8,128)(2,1)}, bf16[1056,128]{1,0:T(8,128)(2,1)S(1)}, u32[]{:S(2)}, u32[]{:S(2)}) collective-permute-start(bf16[1056,128]{1,0:T(8,128)(2,1)} %get-tuple-element.101), channel_id=1, source_target_pairs={{0,2},{1,3},{2,0},{3,1},{4,6},{5,7},{6,4},{7,5},{8,10},{9,11},{10,... | collective-permute-start | bytes 811016 | tf_op jit(solution)/shard_map/ppermute | solution.py:605
  11.4 12.7 %collective-permute-start.3 = (bf16[1056,128]{1,0:T(8,128)(2,1)}, bf16[1056,128]{1,0:T(8,128)(2,1)S(1)}, u32[]{:S(2)}, u32[]{:S(2)}) collective-permute-start(bf16[1056,128]{1,0:T(8,128)(2,1)} %get-tuple-element.104), channel_id=1, source_target_pairs={{0,4},{1,5},{2,6},{3,7},{4,0},{5,1},{6,2},{7,3},{8,12},{9,13},{10,... | collective-permute-start | bytes 811016 | tf_op jit(solution)/shard_map/ppermute | solution.py:605
  11.5 18.1 %collective-permute-start.4 = (bf16[1056,128]{1,0:T(8,128)(2,1)}, bf16[1056,128]{1,0:T(8,128)(2,1)S(1)}, u32[]{:S(2)}, u32[]{:S(2)}) collective-permute-start(bf16[1056,128]{1,0:T(8,128)(2,1)} %get-tuple-element.107), channel_id=1, source_target_pairs={{0,3},{1,2},{2,1},{3,0},{4,7},{5,6},{6,5},{7,4},{8,11},{9,10},{10,... | collective-permute-start | bytes 811016 | tf_op jit(solution)/shard_map/ppermute | solution.py:605
  13.7 19.5 %collective-permute-start.5 = (bf16[1056,128]{1,0:T(8,128)(2,1)}, bf16[1056,128]{1,0:T(8,128)(2,1)S(1)}, u32[]{:S(2)}, u32[]{:S(2)}) collective-permute-start(bf16[1056,128]{1,0:T(8,128)(2,1)} %get-tuple-element.109), channel_id=1, source_target_pairs={{0,5},{1,4},{2,7},{3,6},{4,1},{5,0},{6,3},{7,2},{8,13},{9,12},{10,... | collective-permute-start | bytes 811016 | tf_op jit(solution)/shard_map/ppermute | solution.py:605
  15.8 8.3 %copy-start.13 = (bf16[1056,128]{1,0:T(8,128)(2,1)S(1)}, bf16[1056,128]{1,0:T(8,128)(2,1)}, u32[]{:S(2)}) copy-start(bf16[1056,128]{1,0:T(8,128)(2,1)} %get-tuple-element.110) | copy-start | bytes 811012
  15.8 13.9 %copy-start.12 = (bf16[1056,128]{1,0:T(8,128)(2,1)S(1)}, bf16[1056,128]{1,0:T(8,128)(2,1)}, u32[]{:S(2)}) copy-start(bf16[1056,128]{1,0:T(8,128)(2,1)} %get-tuple-element.111) | copy-start | bytes 811012
  15.8 27.8 %copy-start.2 = (bf16[1056,128]{1,0:T(8,128)(2,1)S(1)}, bf16[1056,128]{1,0:T(8,128)(2,1)}, u32[]{:S(2)}) copy-start(bf16[1056,128]{1,0:T(8,128)(2,1)} %get-tuple-element.86.refs_0_.refs_8_) | copy-start | bytes 811012
  24.1 11.3 %collective-permute-start.6 = (bf16[1056,128]{1,0:T(8,128)(2,1)S(1)}, bf16[1056,128]{1,0:T(8,128)(2,1)S(1)}, u32[]{:S(2)}, u32[]{:S(2)}) collective-permute-start(bf16[1056,128]{1,0:T(8,128)(2,1)S(1)} %copy-done.13), channel_id=1, source_target_pairs={{0,7},{1,6},{2,5},{3,4},{4,3},{5,2},{6,1},{7,0},{8,15},{9,14},{10,... | collective-permute-start | bytes 811016 | tf_op jit(solution)/shard_map/ppermute | solution.py:605
  29.7 7.8 %collective-permute-start.7 = (bf16[1056,128]{1,0:T(8,128)(2,1)S(1)}, bf16[1056,128]{1,0:T(8,128)(2,1)S(1)}, u32[]{:S(2)}, u32[]{:S(2)}) collective-permute-start(bf16[1056,128]{1,0:T(8,128)(2,1)S(1)} %copy-done.12), channel_id=1, source_target_pairs={{0,1},{1,0},{2,3},{3,2},{4,5},{5,4},{6,7},{7,6},{8,9},{9,8},{10,11... | collective-permute-start | bytes 811016 | tf_op jit(solution)/shard_map/ppermute | solution.py:605
  30.6 8.3 %collective-permute-start.14 = (bf16[1024,128]{1,0:T(8,128)(2,1)}, bf16[1024,128]{1,0:T(8,128)(2,1)S(1)}, u32[]{:S(2)}, u32[]{:S(2)}) collective-permute-start(bf16[1024,128]{1,0:T(8,128)(2,1)} %get-tuple-element.120), channel_id=1, source_target_pairs={{0,1},{1,0},{2,3},{3,2},{4,5},{5,4},{6,7},{7,6},{8,9},{9,8},{10,11... | collective-permute-start | bytes 786440 | tf_op jit(solution)/shard_map/ppermute | solution.py:605
  30.7 10.4 %collective-permute-start.13 = (bf16[1024,128]{1,0:T(8,128)(2,1)}, bf16[1024,128]{1,0:T(8,128)(2,1)S(1)}, u32[]{:S(2)}, u32[]{:S(2)}) collective-permute-start(bf16[1024,128]{1,0:T(8,128)(2,1)} %get-tuple-element.119), channel_id=1, source_target_pairs={{0,7},{1,6},{2,5},{3,4},{4,3},{5,2},{6,1},{7,0},{8,15},{9,14},{10,... | collective-permute-start | bytes 786440 | tf_op jit(solution)/shard_map/ppermute | solution.py:605
  33.2 21.3 %collective-permute-start.12 = (bf16[1024,128]{1,0:T(8,128)(2,1)}, bf16[1024,128]{1,0:T(8,128)(2,1)S(1)}, u32[]{:S(2)}, u32[]{:S(2)}) collective-permute-start(bf16[1024,128]{1,0:T(8,128)(2,1)} %get-tuple-element.118), channel_id=1, source_target_pairs={{0,5},{1,4},{2,7},{3,6},{4,1},{5,0},{6,3},{7,2},{8,13},{9,12},{10,... | collective-permute-start | bytes 786440 | tf_op jit(solution)/shard_map/ppermute | solution.py:605
  35.4 19.6 %collective-permute-start.11 = (bf16[1024,128]{1,0:T(8,128)(2,1)}, bf16[1024,128]{1,0:T(8,128)(2,1)S(1)}, u32[]{:S(2)}, u32[]{:S(2)}) collective-permute-start(bf16[1024,128]{1,0:T(8,128)(2,1)} %get-tuple-element.117), channel_id=1, source_target_pairs={{0,3},{1,2},{2,1},{3,0},{4,7},{5,6},{6,5},{7,4},{8,11},{9,10},{10,... | collective-permute-start | bytes 786440 | tf_op jit(solution)/shard_map/ppermute | solution.py:605
  37.5 19.0 %collective-permute-start.10 = (bf16[1024,128]{1,0:T(8,128)(2,1)}, bf16[1024,128]{1,0:T(8,128)(2,1)S(1)}, u32[]{:S(2)}, u32[]{:S(2)}) collective-permute-start(bf16[1024,128]{1,0:T(8,128)(2,1)} %get-tuple-element.116), channel_id=1, source_target_pairs={{0,4},{1,5},{2,6},{3,7},{4,0},{5,1},{6,2},{7,3},{8,12},{9,13},{10,... | collective-permute-start | bytes 786440 | tf_op jit(solution)/shard_map/ppermute | solution.py:605
  39.0 19.0 %collective-permute-start.9 = (bf16[1024,128]{1,0:T(8,128)(2,1)}, bf16[1024,128]{1,0:T(8,128)(2,1)S(1)}, u32[]{:S(2)}, u32[]{:S(2)}) collective-permute-start(bf16[1024,128]{1,0:T(8,128)(2,1)} %get-tuple-element.115), channel_id=1, source_target_pairs={{0,2},{1,3},{2,0},{3,1},{4,6},{5,7},{6,4},{7,5},{8,10},{9,11},{10,... | collective-permute-start | bytes 786440 | tf_op jit(solution)/shard_map/ppermute | solution.py:605
  41.1 17.0 %collective-permute-start.8 = (bf16[1024,128]{1,0:T(8,128)(2,1)}, bf16[1024,128]{1,0:T(8,128)(2,1)S(1)}, u32[]{:S(2)}, u32[]{:S(2)}) collective-permute-start(bf16[1024,128]{1,0:T(8,128)(2,1)} %get-tuple-element.114), channel_id=1, source_target_pairs={{0,6},{1,7},{2,4},{3,5},{4,2},{5,3},{6,0},{7,1},{8,14},{9,15},{10,... | collective-permute-start | bytes 786440 | tf_op jit(solution)/shard_map/ppermute | solution.py:605
  43.6 15.6 %copy-start.3 = (bf16[1024,128]{1,0:T(8,128)(2,1)S(1)}, bf16[1024,128]{1,0:T(8,128)(2,1)}, u32[]{:S(2)}) copy-start(bf16[1024,128]{1,0:T(8,128)(2,1)} %get-tuple-element.113.refs_0_) | copy-start | bytes 786436
  53.8 0.7 copy-start.1
  54.5 13.5 %collective-permute-start.15 = (bf16[3,128,256]{2,1,0:T(8,128)(2,1)S(1)}, bf16[3,128,256]{2,1,0:T(8,128)(2,1)S(1)}, u32[]{:S(2)}, u32[]{:S(2)}) collective-permute-start(bf16[3,128,256]{2,1,0:T(8,128)(2,1)S(1)} %get-tuple-element.126), channel_id=1, source_target_pairs={{0,6},{1,7},{2,4},{3,5},{4,2},{5,3},{6,0},{7,1},{8,14},{9,15},{10,... | collective-permute-start | bytes 589832 | tf_op jit(solution)/shard_map/ppermute | solution.py:605
  55.0 13.0 %collective-permute-start.16 = (bf16[3,128,256]{2,1,0:T(8,128)(2,1)S(1)}, bf16[3,128,256]{2,1,0:T(8,128)(2,1)S(1)}, u32[]{:S(2)}, u32[]{:S(2)}) collective-permute-start(bf16[3,128,256]{2,1,0:T(8,128)(2,1)S(1)} %get-tuple-element.127), channel_id=1, source_target_pairs={{0,2},{1,3},{2,0},{3,1},{4,6},{5,7},{6,4},{7,5},{8,10},{9,11},{10,... | collective-permute-start | bytes 589832 | tf_op jit(solution)/shard_map/ppermute | solution.py:605
  56.5 11.6 %collective-permute-start.17 = (bf16[3,128,256]{2,1,0:T(8,128)(2,1)S(1)}, bf16[3,128,256]{2,1,0:T(8,128)(2,1)S(1)}, u32[]{:S(2)}, u32[]{:S(2)}) collective-permute-start(bf16[3,128,256]{2,1,0:T(8,128)(2,1)S(1)} %get-tuple-element.128), channel_id=1, source_target_pairs={{0,4},{1,5},{2,6},{3,7},{4,0},{5,1},{6,2},{7,3},{8,12},{9,13},{10,... | collective-permute-start | bytes 589832 | tf_op jit(solution)/shard_map/ppermute | solution.py:605
  58.0 16.6 %collective-permute-start.22 = (bf16[3,128,256]{2,1,0:T(8,128)(2,1)S(1)}, bf16[3,128,256]{2,1,0:T(8,128)(2,1)S(1)}, u32[]{:S(2)}, u32[]{:S(2)}) collective-permute-start(bf16[3,128,256]{2,1,0:T(8,128)(2,1)S(1)} %get-tuple-element.138), channel_id=1, source_target_pairs={{0,3},{1,2},{2,1},{3,0},{4,7},{5,6},{6,5},{7,4},{8,11},{9,10},{10,... | collective-permute-start | bytes 589832 | tf_op jit(solution)/shard_map/ppermute | solution.py:605
  58.2 16.5 %collective-permute-start.23 = (bf16[3,128,256]{2,1,0:T(8,128)(2,1)S(1)}, bf16[3,128,256]{2,1,0:T(8,128)(2,1)S(1)}, u32[]{:S(2)}, u32[]{:S(2)}) collective-permute-start(bf16[3,128,256]{2,1,0:T(8,128)(2,1)S(1)} %get-tuple-element.139), channel_id=1, source_target_pairs={{0,5},{1,4},{2,7},{3,6},{4,1},{5,0},{6,3},{7,2},{8,13},{9,12},{10,... | collective-permute-start | bytes 589832 | tf_op jit(solution)/shard_map/ppermute | solution.py:605
  68.0 7.8 %copy-start.5 = (bf16[3,128,256]{2,1,0:T(8,128)(2,1)}, bf16[3,128,256]{2,1,0:T(8,128)(2,1)S(1)}, u32[]{:S(2)}) copy-start(bf16[3,128,256]{2,1,0:T(8,128)(2,1)S(1)} %collective-permute-done.15.refs_1_) | copy-start | bytes 589828
  68.1 7.8 %copy-start.6 = (bf16[3,128,256]{2,1,0:T(8,128)(2,1)}, bf16[3,128,256]{2,1,0:T(8,128)(2,1)S(1)}, u32[]{:S(2)}) copy-start(bf16[3,128,256]{2,1,0:T(8,128)(2,1)S(1)} %collective-permute-done.16.refs_2_) | copy-start | bytes 589828
  68.1 7.8 %copy-start.7 = (bf16[3,128,256]{2,1,0:T(8,128)(2,1)}, bf16[3,128,256]{2,1,0:T(8,128)(2,1)S(1)}, u32[]{:S(2)}) copy-start(bf16[3,128,256]{2,1,0:T(8,128)(2,1)S(1)} %collective-permute-done.17.refs_3_) | copy-start | bytes 589828
  68.1 4.7 %collective-permute-start.18 = (f32[16,256]{1,0:T(8,128)S(1)}, f32[16,256]{1,0:T(8,128)S(1)}, u32[]{:S(2)}, u32[]{:S(2)}) collective-permute-start(f32[16,256]{1,0:T(8,128)S(1)} %get-tuple-element.133), channel_id=1, source_target_pairs={{0,6},{1,7},{2,4},{3,5},{4,2},{5,3},{6,0},{7,1},{8,14},{9,15},{10,... | collective-permute-start | bytes 49160 | tf_op jit(solution)/shard_map/ppermute | solution.py:708
  70.3 3.7 %collective-permute-start.19 = (f32[16,256]{1,0:T(8,128)S(1)}, f32[16,256]{1,0:T(8,128)S(1)}, u32[]{:S(2)}, u32[]{:S(2)}) collective-permute-start(f32[16,256]{1,0:T(8,128)S(1)} %get-tuple-element.134), channel_id=1, source_target_pairs={{0,2},{1,3},{2,0},{3,1},{4,6},{5,7},{6,4},{7,5},{8,10},{9,11},{10,... | collective-permute-start | bytes 49160 | tf_op jit(solution)/shard_map/ppermute | solution.py:708
  70.8 3.7 %collective-permute-start.20 = (f32[16,256]{1,0:T(8,128)S(1)}, f32[16,256]{1,0:T(8,128)S(1)}, u32[]{:S(2)}, u32[]{:S(2)}) collective-permute-start(f32[16,256]{1,0:T(8,128)S(1)} %get-tuple-element.135), channel_id=1, source_target_pairs={{0,4},{1,5},{2,6},{3,7},{4,0},{5,1},{6,2},{7,3},{8,12},{9,13},{10,... | collective-permute-start | bytes 49160 | tf_op jit(solution)/shard_map/ppermute | solution.py:708
  74.5 1.3 %collective-permute-start.21 = (f32[16,768]{1,0:T(8,128)S(1)}, f32[16,768]{1,0:T(8,128)S(1)}, u32[]{:S(2)}, u32[]{:S(2)}) collective-permute-start(f32[16,768]{1,0:T(8,128)S(1)} %fold.1.own_ref), channel_id=1, source_target_pairs={{0,1},{1,0},{2,3},{3,2},{4,5},{5,4},{6,7},{7,6},{8,9},{9,8},{10,11... | collective-permute-start | bytes 147464 | tf_op jit(solution)/shard_map/ppermute | solution.py:708
  74.6 1.2 %copy-start.8 = (bf16[3,128,256]{2,1,0:T(8,128)(2,1)}, bf16[3,128,256]{2,1,0:T(8,128)(2,1)S(1)}, u32[]{:S(2)}) copy-start(bf16[3,128,256]{2,1,0:T(8,128)(2,1)S(1)} %collective-permute-done.22.refs_4_) | copy-start | bytes 589828
  74.6 1.2 %copy-start.9 = (bf16[3,128,256]{2,1,0:T(8,128)(2,1)}, bf16[3,128,256]{2,1,0:T(8,128)(2,1)S(1)}, u32[]{:S(2)}) copy-start(bf16[3,128,256]{2,1,0:T(8,128)(2,1)S(1)} %collective-permute-done.23.refs_5_) | copy-start | bytes 589828
  75.8 7.4 %copy-start = (bf16[128,5120]{1,0:T(8,128)(2,1)S(1)}, bf16[128,5120]{1,0:T(8,128)(2,1)}, u32[]{:S(2)}) copy-start(bf16[128,5120]{1,0:T(8,128)(2,1)} %hidden_ref.1) | copy-start | bytes 3932164
  75.9 32.9 %all-to-all-start = ((bf16[8,3,128,256]{3,2,1,0:T(8,128)(2,1)}), bf16[8,3,128,256]{3,2,1,0:T(8,128)(2,1)}, u32[]{:S(2)}, u32[]{:S(2)}) async-start(bf16[8,3,128,256]{3,2,1,0:T(8,128)(2,1)} %get-tuple-element.155), calls=%async_computation | async-start | bytes 3145728 | tf_op jit(solution)/shard_map/all_to_all | solution.py:603
  80.3 28.4 %collective-permute-start.30 = (bf16[3,128,256]{2,1,0:T(8,128)(2,1)S(1)}, bf16[3,128,256]{2,1,0:T(8,128)(2,1)S(1)}, u32[]{:S(2)}, u32[]{:S(2)}) collective-permute-start(bf16[3,128,256]{2,1,0:T(8,128)(2,1)S(1)} %get-tuple-element.150), channel_id=1, source_target_pairs={{0,7},{1,6},{2,5},{3,4},{4,3},{5,2},{6,1},{7,0},{8,15},{9,14},{10,... | collective-permute-start | bytes 589832 | tf_op jit(solution)/shard_map/ppermute | solution.py:605
  82.9 25.8 %collective-permute-start.31 = (bf16[3,128,256]{2,1,0:T(8,128)(2,1)S(1)}, bf16[3,128,256]{2,1,0:T(8,128)(2,1)S(1)}, u32[]{:S(2)}, u32[]{:S(2)}) collective-permute-start(bf16[3,128,256]{2,1,0:T(8,128)(2,1)S(1)} %get-tuple-element.151), channel_id=1, source_target_pairs={{0,1},{1,0},{2,3},{3,2},{4,5},{5,4},{6,7},{7,6},{8,9},{9,8},{10,11... | collective-permute-start | bytes 589832 | tf_op jit(solution)/shard_map/ppermute | solution.py:605
  84.1 5.9 %collective-permute-start.24 = (f32[8,2304]{1,0:T(8,128)S(1)}, f32[8,2304]{1,0:T(8,128)S(1)}, u32[]{:S(2)}, u32[]{:S(2)}) collective-permute-start(f32[8,2304]{1,0:T(8,128)S(1)} %get-tuple-element.147), channel_id=1, source_target_pairs={{0,8},{8,0},{16,24},{24,16},{1,9},{9,1},{17,25},{25,17},{2,10},{10... | collective-permute-start | bytes 221192 | tf_op jit(solution)/shard_map/ppermute | solution.py:605
  87.3 8.1 %collective-permute-start.25 = (f32[8,2304]{1,0:T(8,128)S(1)}, f32[8,2304]{1,0:T(8,128)S(1)}, u32[]{:S(2)}, u32[]{:S(2)}) collective-permute-start(f32[8,2304]{1,0:T(8,128)S(1)} %get-tuple-element.148), channel_id=1, source_target_pairs={{0,16},{8,24},{16,0},{24,8},{1,17},{9,25},{17,1},{25,9},{2,18},{10... | collective-permute-start | bytes 221192 | tf_op jit(solution)/shard_map/ppermute | solution.py:605
  88.4 7.0 %collective-permute-start.26 = (f32[8,2304]{1,0:T(8,128)S(1)}, f32[8,2304]{1,0:T(8,128)S(1)}, u32[]{:S(2)}, u32[]{:S(2)}) collective-permute-start(f32[8,2304]{1,0:T(8,128)S(1)} %get-tuple-element.149), channel_id=1, source_target_pairs={{0,24},{8,16},{16,8},{24,0},{1,25},{9,17},{17,9},{25,1},{2,26},{10... | collective-permute-start | bytes 221192 | tf_op jit(solution)/shard_map/ppermute | solution.py:605
  95.4 12.0 %collective-permute-start.29 = (f32[8,2304]{1,0:T(8,128)S(1)}, f32[8,2304]{1,0:T(8,128)S(1)}, u32[]{:S(2)}, u32[]{:S(2)}) collective-permute-start(f32[8,2304]{1,0:T(8,128)S(1)} %sum_packs.1.refs_0_), channel_id=1, source_target_pairs={{0,4},{1,5},{2,6},{3,7},{4,0},{5,1},{6,2},{7,3},{8,12},{9,13},{10,... | collective-permute-start | bytes 221192 | tf_op jit(solution)/shard_map/ppermute | solution.py:708
  96.0 11.4 %collective-permute-start.28 = (f32[8,2304]{1,0:T(8,128)S(1)}, f32[8,2304]{1,0:T(8,128)S(1)}, u32[]{:S(2)}, u32[]{:S(2)}) collective-permute-start(f32[8,2304]{1,0:T(8,128)S(1)} %sum_packs.1.refs_0_), channel_id=1, source_target_pairs={{0,2},{1,3},{2,0},{3,1},{4,6},{5,7},{6,4},{7,5},{8,10},{9,11},{10,... | collective-permute-start | bytes 221192 | tf_op jit(solution)/shard_map/ppermute | solution.py:708
  96.3 12.3 %collective-permute-start.27 = (f32[8,2304]{1,0:T(8,128)S(1)}, f32[8,2304]{1,0:T(8,128)S(1)}, u32[]{:S(2)}, u32[]{:S(2)}) collective-permute-start(f32[8,2304]{1,0:T(8,128)S(1)} %sum_packs.1.refs_0_), channel_id=1, source_target_pairs={{0,6},{1,7},{2,4},{3,5},{4,2},{5,3},{6,0},{7,1},{8,14},{9,15},{10,... | collective-permute-start | bytes 221192 | tf_op jit(solution)/shard_map/ppermute | solution.py:708
  108.7 0.7 copy-start.10
  108.7 0.7 copy-start.11
  108.7 4.2 %collective-permute-start.32 = (f32[8,2304]{1,0:T(8,128)S(1)}, f32[8,2304]{1,0:T(8,128)S(1)}, u32[]{:S(2)}, u32[]{:S(2)}) collective-permute-start(f32[8,2304]{1,0:T(8,128)S(1)} %sum_chips.1.own_ref), channel_id=1, source_target_pairs={{0,1},{1,0},{2,3},{3,2},{4,5},{5,4},{6,7},{7,6},{8,9},{9,8},{10,11... | collective-permute-start | bytes 221192 | tf_op jit(solution)/shard_map/ppermute | solution.py:708

commit v6 on v5

--- a/solution.py
+++ b/solution.py
@@ -533,36 +533,27 @@
     return small_call(kernel, shapes, own, other, name="finish")
 
 
-def unpack_kernel(members, heads_here, stages, counts, *refs):
-    count = sum(counts)
-    groups = [refs[sum(counts[:i]) : sum(counts[: i + 1])] for i in range(len(counts))]
-    outs = refs[count : count + 3]
-    held = refs[count + 3 : count + 3 + len(stages)]
-    in_sems, out_sems = refs[count + 3 + len(stages) :]
+def unpack_kernel(heads_here, stages, items, count, *refs):
+    outs = refs[-6:-3]
+    held, in_sems, out_sems = refs[-3:]
     me = lax.axis_index("seq")
     reads = []
     writes = []
-    for stage, (first_head, stage_heads) in enumerate(stages):
-        for offset in range(members):
-            source = me ^ offset
-            start = pl.multiple_of((source * heads_here + first_head) * HD, HD)
-            reads.append(
+    for slot, (index, stage, offset, whole) in enumerate(items):
+        first_head, stage_heads = stages[stage]
+        start = pl.multiple_of(((me ^ offset) * heads_here + first_head) * HD, HD)
+        message = refs[index].at[me ^ offset] if whole else refs[index]
+        reads.append(pltpu.make_async_copy(message, held.at[slot], in_sems.at[slot]))
+        writes.append(
+            [
                 pltpu.make_async_copy(
-                    part_of(groups[stage], me, offset),
-                    held[stage].at[offset],
-                    in_sems.at[stage, offset],
+                    held.at[slot, which],
+                    outs[which].at[:, pl.ds(start, stage_heads * HD)],
+                    out_sems.at[slot, which],
                 )
-            )
-            writes.append(
-                [
-                    pltpu.make_async_copy(
-                        held[stage].at[offset, which],
-                        outs[which].at[:, pl.ds(start, stage_heads * HD)],
-                        out_sems.at[stage, offset, which],
-                    )
-                    for which in range(3)
-                ]
-            )
+                for which in range(3)
+            ]
+        )
     for copy in reads:
         copy.start()
     for copy, followers in zip(reads, writes):
@@ -574,27 +565,33 @@
             follower.wait()
 
 
-def unpack(groups, members, heads_here, stages):
-    rows = groups[0][0].shape[-2]
-    counts = [len(group) for group in groups]
-    messages = [message for group in groups for message in group]
-    width = members * heads_here * HD
+def unpack(home, members, heads_here, stages, chosen, earlier):
+    messages, items = [], []
+    for stage, group in enumerate(home):
+        for place, offset in enumerate(offsets_of(members)):
+            whole = len(group) == 1
+            if (stage, offset) in chosen:
+                if not whole or place == 0:
+                    messages.append(group[0 if whole else place])
+                items.append((len(messages) - 1, stage, offset, whole))
+    rows = messages[0].shape[-2]
+    shape = jax.ShapeDtypeStruct((rows, members * heads_here * HD), BF16)
+    count = len(messages)
     return pl.pallas_call(
-        functools.partial(unpack_kernel, members, heads_here, stages, counts),
-        out_shape=[jax.ShapeDtypeStruct((rows, width), BF16)] * 3,
-        in_specs=any_specs(len(messages)),
+        functools.partial(unpack_kernel, heads_here, stages, items, count),
+        out_shape=[shape] * 3,
+        in_specs=any_specs(count + len(earlier)),
         out_specs=any_specs(3),
+        input_output_aliases={count + place: place for place in range(len(earlier))},
         scratch_shapes=[
-            pltpu.VMEM((members, 3, rows, stage_heads * HD), BF16) for _, stage_heads in stages
-        ]
-        + [
-            pltpu.SemaphoreType.DMA((len(stages), members)),
-            pltpu.SemaphoreType.DMA((len(stages), members, 3)),
+            pltpu.VMEM((len(items), 3, rows, stages[0][1] * HD), BF16),
+            pltpu.SemaphoreType.DMA((len(items),)),
+            pltpu.SemaphoreType.DMA((len(items), 3)),
         ],
         compiler_params=params(56),
         cost_estimate=COST,
         name="unpack",
-    )(*messages)
+    )(*messages, *earlier)
 
 
 def exchange(messages, axis):
@@ -737,11 +734,19 @@
             summed = summed + swap(summed, step)
             step *= 2
         pieces = [summed, swap(summed, step)]
+    everything = [(stage, offset) for stage in range(len(stages)) for offset in range(members)]
+    early, earlier = [], ()
+    if planned:
+        early = [(0, offset) for offset in (0, 6, 2, 4, 3, 5)]
+        earlier = tuple(unpack(home, members, heads_here, stages, early, ()))
+        pieces, earlier = lax.optimization_barrier((pieces, earlier))
     summed = planned_after(sum_chips(pieces), 4)
     down_query_grad, up_query_grad, down_value_grad, up_value_grad = finish(
         summed, swap(summed, 1), down_cols
     )
-    grad_queries, grad_keys, value_gradients = unpack(home, members, heads_here, stages)
+    grad_queries, grad_keys, value_gradients = unpack(
+        home, members, heads_here, stages, [at for at in everything if at not in early], earlier
+    )
     return (
         grad_queries,
         grad_keys,

time: 115 us -> 113 us (0.983)
  starting transfers between devices: 45.2 us -> 44 us
    ppermute x8, waiting for transfers between devices: 13.8 us -> 12 us  [swap(): return lax.ppermute(value, 'seq', [(i, i ^ offset) for i in range(members)])]
    pallas_call x1 -> x2, Pallas kernels: 3.43 us -> 4.85 us  [unpack(): pl.pallas_call(functools.partial(unpack_kernel, heads_here, stages, items...]
    ppermute x24, starting transfers between devices: 33 us -> 31.8 us  [exchange(): lax.ppermute(message, axis, [(i, i ^ offset) for i in range(count)])]
  transfers between devices with their start and end apart: 34 -> 34, of which waited for: 13 -> 13; matrix products, arithmetic and copies ran while one was open for 2% -> 2% of each run, Pallas kernels for 29% -> 30%
where the time goes in v6:
time: 113 us
  starting transfers between devices  44 us (39%)
  Pallas kernels  34.4 us (30%)
  waiting for transfers between devices  29.9 us (26%)
  local copies, waits for them, and re-layouts  2.09 us (2%)
  other arithmetic  1.27 us (1%)
    ppermute x24, starting transfers between devices, exchange(): lax.ppermute(message, axis, [(i, i ^ offset) for i in range(count)])  31.8 us
    pallas_call x2, Pallas kernels, attention(): pl.pallas_call(functools.partial(attention_kernel, members, heads_here, f...  18.7 us
    ppermute x24, waiting for transfers between devices, exchange(): lax.ppermute(message, axis, [(i, i ^ offset) for i in range(count)])  17.8 us
    ppermute x8, waiting for transfers between devices, swap(): return lax.ppermute(value, 'seq', [(i, i ^ offset) for i in range(members)])  12 us
    pallas_call x2, Pallas kernels, pack(): pl.pallas_call(functools.partial(pack_kernel, members, heads_here, first_...  9.26 us
    ppermute x8, starting transfers between devices, swap(): return lax.ppermute(value, 'seq', [(i, i ^ offset) for i in range(members)])  7.24 us
    pallas_call x2, Pallas kernels, unpack(): pl.pallas_call(functools.partial(unpack_kernel, heads_here, stages, items...  4.85 us
    all_to_all x1, starting transfers between devices, exchange(): lax.all_to_all(messages[0], axis, split_axis=0, concat_axis=0, tiled=True)  4.44 us
  transfers between devices with their start and end apart: 34, of which 13 were waited for; matrix products, arithmetic and copies ran while one was open for 2% of the time, Pallas kernels for 30%

profile of v6, /device:TPU:0, one launch (start us, length us, event | category | flops | bytes accessed | tf_op | source)
XLA Modules:
  0.0 112.5 jit_solution(588051533130089918)
XLA Ops:
  0.6 0.5 collective-permute-start
  1.2 6.2 %pack.2 = (bf16[1056,128]{1,0:T(8,128)(2,1)}, bf16[1056,128]{1,0:T(8,128)(2,1)}, bf16[1056,128]{1,0:T(8,128)(2,1)}, bf16[1056,128]{1,0:T(8,128)(2,1)}, bf16[1056...) custom-call(bf16[128,4096]{1,0:T(8,128)(2,1)} %refs_0_.2, ...), custom_call_target="tpu_custom_call" | custom-call | tf_op jit(solution)/shard_map/pack/pallas_call | solution.py:165
  7.3 3.5 %collective-permute-start.1 = (bf16[1056,128]{1,0:T(8,128)(2,1)}, bf16[1056,128]{1,0:T(8,128)(2,1)S(1)}, u32[]{:S(2)}, u32[]{:S(2)}) collective-permute-start(bf16[1056,128]{1,0:T(8,128)(2,1)} %get-tuple-element.103), channel_id=1, source_target_pairs={{0,6},{1,7},{2,4},{3,5},{4,2},{5,3},{6,0},{7,1},{8,14},{9,15},{10,... | collective-permute-start | bytes 811016 | tf_op jit(solution)/shard_map/ppermute | solution.py:602
  10.9 0.5 collective-permute-start.6
  11.4 0.1 collective-permute-start.8
  11.5 1.1 collective-permute-start.10
  12.7 0.2 reduce-window_clone.1
  12.8 0.1 select_reduce_fusion
  12.9 0.7 constant_dynamic-slice_fusion
  13.7 0.0 collective-permute-done.beside_ref
  13.7 2.1 %collective-permute-start.12 = (bf16[1056,128]{1,0:T(8,128)(2,1)}, bf16[1056,128]{1,0:T(8,128)(2,1)S(1)}, u32[]{:S(2)}, u32[]{:S(2)}) collective-permute-start(bf16[1056,128]{1,0:T(8,128)(2,1)} %get-tuple-element.127), channel_id=1, source_target_pairs={{0,5},{1,4},{2,7},{3,6},{4,1},{5,0},{6,3},{7,2},{8,13},{9,12},{10,... | collective-permute-start | bytes 811016 | tf_op jit(solution)/shard_map/ppermute | solution.py:602
  15.8 3.1 %pack.3 = (bf16[1024,128]{1,0:T(8,128)(2,1)}, bf16[1024,128]{1,0:T(8,128)(2,1)}, bf16[1024,128]{1,0:T(8,128)(2,1)}, bf16[1024,128]{1,0:T(8,128)(2,1)}, bf16[1024...) custom-call(bf16[128,4096]{1,0:T(8,128)(2,1)} %refs_0_.2, ...), custom_call_target="tpu_custom_call" | custom-call | tf_op jit(solution)/shard_map/pack/pallas_call | solution.py:165
  18.9 5.2 %collective-permute-done.8.refs_3_.refs_11_ = bf16[1056,128]{1,0:T(8,128)(2,1)S(1)} collective-permute-done((bf16[1056,128]{1,0:T(8,128)(2,1)}, bf16[1056,128]{1,0:T(8,128)(2,1)S(1)}, u32[]{:S(2)}, u32[]{:S(2)}) %collective-permute-start.8) | collective-permute-done | bytes 270368 | tf_op jit(solution)/shard_map/ppermute | solution.py:602
  24.1 2.2 %collective-permute-start.13 = (bf16[1056,128]{1,0:T(8,128)(2,1)S(1)}, bf16[1056,128]{1,0:T(8,128)(2,1)S(1)}, u32[]{:S(2)}, u32[]{:S(2)}) collective-permute-start(bf16[1056,128]{1,0:T(8,128)(2,1)S(1)} %copy-done.13), channel_id=1, source_target_pairs={{0,7},{1,6},{2,5},{3,4},{4,3},{5,2},{6,1},{7,0},{8,15},{9,14},{10,... | collective-permute-start | bytes 811016 | tf_op jit(solution)/shard_map/ppermute | solution.py:602
  26.3 3.4 %collective-permute-done.10.refs_4_.refs_12_ = bf16[1056,128]{1,0:T(8,128)(2,1)S(1)} collective-permute-done((bf16[1056,128]{1,0:T(8,128)(2,1)}, bf16[1056,128]{1,0:T(8,128)(2,1)S(1)}, u32[]{:S(2)}, u32[]{:S(2)}) %collective-permute-start.10) | collective-permute-done | bytes 270368 | tf_op jit(solution)/shard_map/ppermute | solution.py:602
  29.7 1.0 collective-permute-start.14
  30.6 0.0 collective-permute-done.1.refs_1_.refs_9_
  30.6 0.1 collective-permute-start.11
  30.7 1.5 %collective-permute-start.9 = (bf16[1024,128]{1,0:T(8,128)(2,1)}, bf16[1024,128]{1,0:T(8,128)(2,1)S(1)}, u32[]{:S(2)}, u32[]{:S(2)}) collective-permute-start(bf16[1024,128]{1,0:T(8,128)(2,1)} %get-tuple-element.119), channel_id=1, source_target_pairs={{0,7},{1,6},{2,5},{3,4},{4,3},{5,2},{6,1},{7,0},{8,15},{9,14},{10,... | collective-permute-start | bytes 786440 | tf_op jit(solution)/shard_map/ppermute | solution.py:602
  32.2 1.0 multiply_sine_fusion
  33.2 0.0 collective-permute-done.12.refs_5_.refs_13_
  33.2 1.3 %collective-permute-start.7 = (bf16[1024,128]{1,0:T(8,128)(2,1)}, bf16[1024,128]{1,0:T(8,128)(2,1)S(1)}, u32[]{:S(2)}, u32[]{:S(2)}) collective-permute-start(bf16[1024,128]{1,0:T(8,128)(2,1)} %get-tuple-element.116), channel_id=1, source_target_pairs={{0,5},{1,4},{2,7},{3,6},{4,1},{5,0},{6,3},{7,2},{8,13},{9,12},{10,... | collective-permute-start | bytes 786440 | tf_op jit(solution)/shard_map/ppermute | solution.py:602
  34.5 0.9 collective-permute-done.13.refs_6_.refs_14_
  35.4 2.0 %collective-permute-start.5 = (bf16[1024,128]{1,0:T(8,128)(2,1)}, bf16[1024,128]{1,0:T(8,128)(2,1)S(1)}, u32[]{:S(2)}, u32[]{:S(2)}) collective-permute-start(bf16[1024,128]{1,0:T(8,128)(2,1)} %get-tuple-element.113), channel_id=1, source_target_pairs={{0,3},{1,2},{2,1},{3,0},{4,7},{5,6},{6,5},{7,4},{8,11},{9,10},{10,... | collective-permute-start | bytes 786440 | tf_op jit(solution)/shard_map/ppermute | solution.py:602
  37.5 1.5 %collective-permute-start.4 = (bf16[1024,128]{1,0:T(8,128)(2,1)}, bf16[1024,128]{1,0:T(8,128)(2,1)S(1)}, u32[]{:S(2)}, u32[]{:S(2)}) collective-permute-start(bf16[1024,128]{1,0:T(8,128)(2,1)} %get-tuple-element.110), channel_id=1, source_target_pairs={{0,4},{1,5},{2,6},{3,7},{4,0},{5,1},{6,2},{7,3},{8,12},{9,13},{10,... | collective-permute-start | bytes 786440 | tf_op jit(solution)/shard_map/ppermute | solution.py:602
  39.0 0.5 collective-permute-start.3
  39.5 1.6 %collective-permute-done.9.refs_6_ = bf16[1024,128]{1,0:T(8,128)(2,1)S(1)} collective-permute-done((bf16[1024,128]{1,0:T(8,128)(2,1)}, bf16[1024,128]{1,0:T(8,128)(2,1)S(1)}, u32[]{:S(2)}, u32[]{:S(2)}) %collective-permute-start.9) | collective-permute-done | bytes 262176 | tf_op jit(solution)/shard_map/ppermute | solution.py:602
  41.1 2.4 %collective-permute-start.2 = (bf16[1024,128]{1,0:T(8,128)(2,1)}, bf16[1024,128]{1,0:T(8,128)(2,1)S(1)}, u32[]{:S(2)}, u32[]{:S(2)}) collective-permute-start(bf16[1024,128]{1,0:T(8,128)(2,1)} %get-tuple-element.104), channel_id=1, source_target_pairs={{0,6},{1,7},{2,4},{3,5},{4,2},{5,3},{6,0},{7,1},{8,14},{9,15},{10,... | collective-permute-start | bytes 786440 | tf_op jit(solution)/shard_map/ppermute | solution.py:602
  43.6 10.1 %attention.2 = (bf16[3,128,256]{2,1,0:T(8,128)(2,1)S(1)}, bf16[3,128,256]{2,1,0:T(8,128)(2,1)S(1)}, bf16[3,128,256]{2,1,0:T(8,128)(2,1)S(1)}, bf16[3,128,256]{2,...) custom-call(s32[1,4]{1,0:T(1,128)S(1)} %copy-done.4, ...), custom_call_target="tpu_custom_call" | custom-call | flops 10000000000 | tf_op jit(solution)/shard_map/attention/pallas_call | solution.py:378
  53.6 0.7 copy-done.1
  54.3 0.5 collective-permute-start.15
  54.8 1.5 %collective-permute-start.16 = (bf16[3,128,256]{2,1,0:T(8,128)(2,1)S(1)}, bf16[3,128,256]{2,1,0:T(8,128)(2,1)S(1)}, u32[]{:S(2)}, u32[]{:S(2)}) collective-permute-start(bf16[3,128,256]{2,1,0:T(8,128)(2,1)S(1)} %get-tuple-element.136), channel_id=1, source_target_pairs={{0,2},{1,3},{2,0},{3,1},{4,6},{5,7},{6,4},{7,5},{8,10},{9,11},{10,... | collective-permute-start | bytes 589832 | tf_op jit(solution)/shard_map/ppermute | solution.py:602
  56.3 1.5 %collective-permute-start.17 = (bf16[3,128,256]{2,1,0:T(8,128)(2,1)S(1)}, bf16[3,128,256]{2,1,0:T(8,128)(2,1)S(1)}, u32[]{:S(2)}, u32[]{:S(2)}) collective-permute-start(bf16[3,128,256]{2,1,0:T(8,128)(2,1)S(1)} %get-tuple-element.137), channel_id=1, source_target_pairs={{0,4},{1,5},{2,6},{3,7},{4,0},{5,1},{6,2},{7,3},{8,12},{9,13},{10,... | collective-permute-start | bytes 589832 | tf_op jit(solution)/shard_map/ppermute | solution.py:602
  57.8 0.3 collective-permute-done.2.refs_1_
  58.2 1.0 collective-permute-start.23
  59.2 8.7 %attention.3 = (bf16[8,3,128,256]{3,2,1,0:T(8,128)(2,1)}, f32[16,256]{1,0:T(8,128)S(1)}, f32[16,256]{1,0:T(8,128)S(1)}, f32[16,256]{1,0:T(8,128)S(1)}, f32[16,256]{1,0:T(8,128)S(1)}, /*index=5*/f32[16,256]{1,0:T(8,128)S(1)}) custom-call(s32[1,4]{1,0:T(1,128)S(1)} %copy-done.4, bf16[8,256]{1,0:T(8,128)(2,1)S(1)} %get-tuple-element.191.upq_ref, ...), custom_call_target="tpu_custom_call" | custom-call | flops 10000000000 | tf_op jit(solution)/shard_map/attention/pallas_call | solution.py:378
  67.9 2.2 %collective-permute-start.18 = (f32[16,256]{1,0:T(8,128)S(1)}, f32[16,256]{1,0:T(8,128)S(1)}, u32[]{:S(2)}, u32[]{:S(2)}) collective-permute-start(f32[16,256]{1,0:T(8,128)S(1)} %get-tuple-element.139), channel_id=1, source_target_pairs={{0,6},{1,7},{2,4},{3,5},{4,2},{5,3},{6,0},{7,1},{8,14},{9,15},{10,... | collective-permute-start | bytes 49160 | tf_op jit(solution)/shard_map/ppermute | solution.py:705
  70.1 0.4 collective-permute-start.19
  70.6 0.9 collective-permute-start.20
  71.5 1.1 %collective-permute-done.18.refs_1_ = f32[16,256]{1,0:T(8,128)S(1)} collective-permute-done((f32[16,256]{1,0:T(8,128)S(1)}, f32[16,256]{1,0:T(8,128)S(1)}, u32[]{:S(2)}, u32[]{:S(2)}) %collective-permute-start.18) | collective-permute-done | bytes 16416 | tf_op jit(solution)/shard_map/ppermute | solution.py:705
  72.6 1.3 %collective-permute-done.19.refs_2_ = f32[16,256]{1,0:T(8,128)S(1)} collective-permute-done((f32[16,256]{1,0:T(8,128)S(1)}, f32[16,256]{1,0:T(8,128)S(1)}, u32[]{:S(2)}, u32[]{:S(2)}) %collective-permute-start.19) | collective-permute-done | bytes 16416 | tf_op jit(solution)/shard_map/ppermute | solution.py:705
  73.9 0.4 collective-permute-done.20.refs_3_
  74.3 0.1 collective-permute-start.21
  74.4 1.2 %collective-permute-done.21.other_ref = f32[16,768]{1,0:T(8,128)S(1)} collective-permute-done((f32[16,768]{1,0:T(8,128)S(1)}, f32[16,768]{1,0:T(8,128)S(1)}, u32[]{:S(2)}, u32[]{:S(2)}) %collective-permute-start.21) | collective-permute-done | bytes 49184 | tf_op jit(solution)/shard_map/ppermute | solution.py:705
  75.6 0.0 copy-start
  75.7 4.4 %all-to-all-start = ((bf16[8,3,128,256]{3,2,1,0:T(8,128)(2,1)}), bf16[8,3,128,256]{3,2,1,0:T(8,128)(2,1)}, u32[]{:S(2)}, u32[]{:S(2)}) async-start(bf16[8,3,128,256]{3,2,1,0:T(8,128)(2,1)} %get-tuple-element.172), calls=%async_computation | async-start | bytes 3145728 | tf_op jit(solution)/shard_map/all_to_all | solution.py:600
  80.1 2.6 %collective-permute-start.30 = (bf16[3,128,256]{2,1,0:T(8,128)(2,1)S(1)}, bf16[3,128,256]{2,1,0:T(8,128)(2,1)S(1)}, u32[]{:S(2)}, u32[]{:S(2)}) collective-permute-start(bf16[3,128,256]{2,1,0:T(8,128)(2,1)S(1)} %get-tuple-element.167), channel_id=1, source_target_pairs={{0,7},{1,6},{2,5},{3,4},{4,3},{5,2},{6,1},{7,0},{8,15},{9,14},{10,... | collective-permute-start | bytes 589832 | tf_op jit(solution)/shard_map/ppermute | solution.py:602
  82.7 0.4 collective-permute-start.31
  83.1 0.8 down_terms.1
  83.9 1.9 %collective-permute-start.24 = (f32[8,2304]{1,0:T(8,128)S(1)}, f32[8,2304]{1,0:T(8,128)S(1)}, u32[]{:S(2)}, u32[]{:S(2)}) collective-permute-start(f32[8,2304]{1,0:T(8,128)S(1)} %get-tuple-element.151), channel_id=1, source_target_pairs={{0,8},{8,0},{16,24},{24,16},{1,9},{9,1},{17,25},{25,17},{2,10},{10... | collective-permute-start | bytes 221192 | tf_op jit(solution)/shard_map/ppermute | solution.py:602
  85.8 2.6 %collective-permute-start.25 = (f32[8,2304]{1,0:T(8,128)S(1)}, f32[8,2304]{1,0:T(8,128)S(1)}, u32[]{:S(2)}, u32[]{:S(2)}) collective-permute-start(f32[8,2304]{1,0:T(8,128)S(1)} %get-tuple-element.152), channel_id=1, source_target_pairs={{0,16},{8,24},{16,0},{24,8},{1,17},{9,25},{17,1},{25,9},{2,18},{10... | collective-permute-start | bytes 221192 | tf_op jit(solution)/shard_map/ppermute | solution.py:602
  88.4 6.3 %collective-permute-done.25.refs_2_ = f32[8,2304]{1,0:T(8,128)S(1)} collective-permute-done((f32[8,2304]{1,0:T(8,128)S(1)}, f32[8,2304]{1,0:T(8,128)S(1)}, u32[]{:S(2)}, u32[]{:S(2)}) %collective-permute-start.25) | collective-permute-done | bytes 73760 | tf_op jit(solution)/shard_map/ppermute | solution.py:602
  94.7 0.6 collective-permute-start.29
  95.3 0.3 collective-permute-start.28
  95.5 2.7 %collective-permute-start.27 = (f32[8,2304]{1,0:T(8,128)S(1)}, f32[8,2304]{1,0:T(8,128)S(1)}, u32[]{:S(2)}, u32[]{:S(2)}) collective-permute-start(f32[8,2304]{1,0:T(8,128)S(1)} %sum_packs.1.refs_0_), channel_id=1, source_target_pairs={{0,6},{1,7},{2,4},{3,5},{4,2},{5,3},{6,0},{7,1},{8,14},{9,15},{10,... | collective-permute-start | bytes 221192 | tf_op jit(solution)/shard_map/ppermute | solution.py:705
  98.2 2.2 %unpack.2 = (bf16[128,4096]{1,0:T(8,128)(2,1)}, bf16[128,4096]{1,0:T(8,128)(2,1)}, bf16[128,4096]{1,0:T(8,128)(2,1)}) custom-call(bf16[3,128,256]{2,1,0:T(8,128)(2,1)} %copy-done.1, bf16[3,128,256]{2,1,0:T(8,128)(2,1)} %copy-done.7, bf16[3,128,256]{2,1,0:T(8,128)(2,1)} %copy-done.8, bf16[3,128,256]{2,1,0:T(8,128)(2,1)} %copy-done.9, ...), custom_call_target="tpu_custom_call" | custom-call | tf_op jit(solution)/shard_map/unpack/pallas_call | solution.py:580
  100.4 5.6 %collective-permute-done.29.refs_3_ = f32[8,2304]{1,0:T(8,128)S(1)} collective-permute-done((f32[8,2304]{1,0:T(8,128)S(1)}, f32[8,2304]{1,0:T(8,128)S(1)}, u32[]{:S(2)}, u32[]{:S(2)}) %collective-permute-start.29) | collective-permute-done | bytes 73760 | tf_op jit(solution)/shard_map/ppermute | solution.py:705
  106.0 0.4 collective-permute-done.28.refs_2_
  106.4 2.0 %collective-permute-done.27.refs_1_ = f32[8,2304]{1,0:T(8,128)S(1)} collective-permute-done((f32[8,2304]{1,0:T(8,128)S(1)}, f32[8,2304]{1,0:T(8,128)S(1)}, u32[]{:S(2)}, u32[]{:S(2)}) %collective-permute-start.27) | collective-permute-done | bytes 73760 | tf_op jit(solution)/shard_map/ppermute | solution.py:705
  108.5 0.1 collective-permute-start.32
  108.6 0.6 copy-done.5
  109.2 0.1 copy-done.6
  109.2 2.6 %unpack.3 = (bf16[128,4096]{1,0:T(8,128)(2,1)}, bf16[128,4096]{1,0:T(8,128)(2,1)}, bf16[128,4096]{1,0:T(8,128)(2,1)}) custom-call(bf16[3,128,256]{2,1,0:T(8,128)(2,1)} %copy-done.5, bf16[3,128,256]{2,1,0:T(8,128)(2,1)} %copy-done.6, bf16[8,3,128,256]{3,2,1,0:T(8,128)(2,1)} %all-to-all-done.refs_2_, ...), custom_call_target="tpu_custom_call", output_to_operand_aliasing={{0}: (3, {}), {1}: (4, {}), {2}: (5, {})} | custom-call | tf_op jit(solution)/shard_map/unpack/pallas_call | solution.py:580
  111.9 0.7 finish.1
  (50 shorter events, 0.2 us)
Async XLA Ops:
  0.6 12.0 %copy-start.4 = (s32[1,4]{1,0:T(1,128)S(1)}, s32[1,4]{1,0:T(1,128)}, u32[]{:S(2)}) copy-start(s32[1,4]{1,0:T(1,128)} %lengths_ref.3) | copy-start | bytes 52
  0.6 13.1 %collective-permute-start = (bf16[128,5120]{1,0:T(8,128)(2,1)}, bf16[128,5120]{1,0:T(8,128)(2,1)S(1)}, u32[]{:S(2)}, u32[]{:S(2)}) collective-permute-start(bf16[128,5120]{1,0:T(8,128)(2,1)} %hidden_ref.1), channel_id=1, source_target_pairs={{0,1},{1,0},{2,3},{3,2},{4,5},{5,4},{6,7},{7,6},{8,9},{9,8},{10,11... | collective-permute-start | bytes 3932168 | tf_op jit(solution)/shard_map/ppermute | solution.py:644
  7.3 23.3 %collective-permute-start.1 = (bf16[1056,128]{1,0:T(8,128)(2,1)}, bf16[1056,128]{1,0:T(8,128)(2,1)S(1)}, u32[]{:S(2)}, u32[]{:S(2)}) collective-permute-start(bf16[1056,128]{1,0:T(8,128)(2,1)} %get-tuple-element.103), channel_id=1, source_target_pairs={{0,6},{1,7},{2,4},{3,5},{4,2},{5,3},{6,0},{7,1},{8,14},{9,15},{10,... | collective-permute-start | bytes 811016 | tf_op jit(solution)/shard_map/ppermute | solution.py:602
  10.9 19.8 %collective-permute-start.6 = (bf16[1056,128]{1,0:T(8,128)(2,1)}, bf16[1056,128]{1,0:T(8,128)(2,1)S(1)}, u32[]{:S(2)}, u32[]{:S(2)}) collective-permute-start(bf16[1056,128]{1,0:T(8,128)(2,1)} %get-tuple-element.115), channel_id=1, source_target_pairs={{0,2},{1,3},{2,0},{3,1},{4,6},{5,7},{6,4},{7,5},{8,10},{9,11},{10,... | collective-permute-start | bytes 811016 | tf_op jit(solution)/shard_map/ppermute | solution.py:602
  11.4 12.7 %collective-permute-start.8 = (bf16[1056,128]{1,0:T(8,128)(2,1)}, bf16[1056,128]{1,0:T(8,128)(2,1)S(1)}, u32[]{:S(2)}, u32[]{:S(2)}) collective-permute-start(bf16[1056,128]{1,0:T(8,128)(2,1)} %get-tuple-element.118), channel_id=1, source_target_pairs={{0,4},{1,5},{2,6},{3,7},{4,0},{5,1},{6,2},{7,3},{8,12},{9,13},{10,... | collective-permute-start | bytes 811016 | tf_op jit(solution)/shard_map/ppermute | solution.py:602
  11.5 18.1 %collective-permute-start.10 = (bf16[1056,128]{1,0:T(8,128)(2,1)}, bf16[1056,128]{1,0:T(8,128)(2,1)S(1)}, u32[]{:S(2)}, u32[]{:S(2)}) collective-permute-start(bf16[1056,128]{1,0:T(8,128)(2,1)} %get-tuple-element.121), channel_id=1, source_target_pairs={{0,3},{1,2},{2,1},{3,0},{4,7},{5,6},{6,5},{7,4},{8,11},{9,10},{10,... | collective-permute-start | bytes 811016 | tf_op jit(solution)/shard_map/ppermute | solution.py:602
  13.7 19.5 %collective-permute-start.12 = (bf16[1056,128]{1,0:T(8,128)(2,1)}, bf16[1056,128]{1,0:T(8,128)(2,1)S(1)}, u32[]{:S(2)}, u32[]{:S(2)}) collective-permute-start(bf16[1056,128]{1,0:T(8,128)(2,1)} %get-tuple-element.127), channel_id=1, source_target_pairs={{0,5},{1,4},{2,7},{3,6},{4,1},{5,0},{6,3},{7,2},{8,13},{9,12},{10,... | collective-permute-start | bytes 811016 | tf_op jit(solution)/shard_map/ppermute | solution.py:602
  15.8 8.3 %copy-start.13 = (bf16[1056,128]{1,0:T(8,128)(2,1)S(1)}, bf16[1056,128]{1,0:T(8,128)(2,1)}, u32[]{:S(2)}) copy-start(bf16[1056,128]{1,0:T(8,128)(2,1)} %get-tuple-element.128) | copy-start | bytes 811012
  15.8 13.9 %copy-start.12 = (bf16[1056,128]{1,0:T(8,128)(2,1)S(1)}, bf16[1056,128]{1,0:T(8,128)(2,1)}, u32[]{:S(2)}) copy-start(bf16[1056,128]{1,0:T(8,128)(2,1)} %get-tuple-element.129) | copy-start | bytes 811012
  15.8 27.8 %copy-start.2 = (bf16[1056,128]{1,0:T(8,128)(2,1)S(1)}, bf16[1056,128]{1,0:T(8,128)(2,1)}, u32[]{:S(2)}) copy-start(bf16[1056,128]{1,0:T(8,128)(2,1)} %get-tuple-element.96.refs_0_.refs_8_) | copy-start | bytes 811012
  24.1 11.3 %collective-permute-start.13 = (bf16[1056,128]{1,0:T(8,128)(2,1)S(1)}, bf16[1056,128]{1,0:T(8,128)(2,1)S(1)}, u32[]{:S(2)}, u32[]{:S(2)}) collective-permute-start(bf16[1056,128]{1,0:T(8,128)(2,1)S(1)} %copy-done.13), channel_id=1, source_target_pairs={{0,7},{1,6},{2,5},{3,4},{4,3},{5,2},{6,1},{7,0},{8,15},{9,14},{10,... | collective-permute-start | bytes 811016 | tf_op jit(solution)/shard_map/ppermute | solution.py:602
  29.7 7.8 %collective-permute-start.14 = (bf16[1056,128]{1,0:T(8,128)(2,1)S(1)}, bf16[1056,128]{1,0:T(8,128)(2,1)S(1)}, u32[]{:S(2)}, u32[]{:S(2)}) collective-permute-start(bf16[1056,128]{1,0:T(8,128)(2,1)S(1)} %copy-done.12), channel_id=1, source_target_pairs={{0,1},{1,0},{2,3},{3,2},{4,5},{5,4},{6,7},{7,6},{8,9},{9,8},{10,11... | collective-permute-start | bytes 811016 | tf_op jit(solution)/shard_map/ppermute | solution.py:602
  30.6 8.3 %collective-permute-start.11 = (bf16[1024,128]{1,0:T(8,128)(2,1)}, bf16[1024,128]{1,0:T(8,128)(2,1)S(1)}, u32[]{:S(2)}, u32[]{:S(2)}) collective-permute-start(bf16[1024,128]{1,0:T(8,128)(2,1)} %get-tuple-element.122), channel_id=1, source_target_pairs={{0,1},{1,0},{2,3},{3,2},{4,5},{5,4},{6,7},{7,6},{8,9},{9,8},{10,11... | collective-permute-start | bytes 786440 | tf_op jit(solution)/shard_map/ppermute | solution.py:602
  30.7 10.4 %collective-permute-start.9 = (bf16[1024,128]{1,0:T(8,128)(2,1)}, bf16[1024,128]{1,0:T(8,128)(2,1)S(1)}, u32[]{:S(2)}, u32[]{:S(2)}) collective-permute-start(bf16[1024,128]{1,0:T(8,128)(2,1)} %get-tuple-element.119), channel_id=1, source_target_pairs={{0,7},{1,6},{2,5},{3,4},{4,3},{5,2},{6,1},{7,0},{8,15},{9,14},{10,... | collective-permute-start | bytes 786440 | tf_op jit(solution)/shard_map/ppermute | solution.py:602
  33.2 21.1 %collective-permute-start.7 = (bf16[1024,128]{1,0:T(8,128)(2,1)}, bf16[1024,128]{1,0:T(8,128)(2,1)S(1)}, u32[]{:S(2)}, u32[]{:S(2)}) collective-permute-start(bf16[1024,128]{1,0:T(8,128)(2,1)} %get-tuple-element.116), channel_id=1, source_target_pairs={{0,5},{1,4},{2,7},{3,6},{4,1},{5,0},{6,3},{7,2},{8,13},{9,12},{10,... | collective-permute-start | bytes 786440 | tf_op jit(solution)/shard_map/ppermute | solution.py:602
  35.4 19.4 %collective-permute-start.5 = (bf16[1024,128]{1,0:T(8,128)(2,1)}, bf16[1024,128]{1,0:T(8,128)(2,1)S(1)}, u32[]{:S(2)}, u32[]{:S(2)}) collective-permute-start(bf16[1024,128]{1,0:T(8,128)(2,1)} %get-tuple-element.113), channel_id=1, source_target_pairs={{0,3},{1,2},{2,1},{3,0},{4,7},{5,6},{6,5},{7,4},{8,11},{9,10},{10,... | collective-permute-start | bytes 786440 | tf_op jit(solution)/shard_map/ppermute | solution.py:602
  37.5 18.8 %collective-permute-start.4 = (bf16[1024,128]{1,0:T(8,128)(2,1)}, bf16[1024,128]{1,0:T(8,128)(2,1)S(1)}, u32[]{:S(2)}, u32[]{:S(2)}) collective-permute-start(bf16[1024,128]{1,0:T(8,128)(2,1)} %get-tuple-element.110), channel_id=1, source_target_pairs={{0,4},{1,5},{2,6},{3,7},{4,0},{5,1},{6,2},{7,3},{8,12},{9,13},{10,... | collective-permute-start | bytes 786440 | tf_op jit(solution)/shard_map/ppermute | solution.py:602
  39.0 18.8 %collective-permute-start.3 = (bf16[1024,128]{1,0:T(8,128)(2,1)}, bf16[1024,128]{1,0:T(8,128)(2,1)S(1)}, u32[]{:S(2)}, u32[]{:S(2)}) collective-permute-start(bf16[1024,128]{1,0:T(8,128)(2,1)} %get-tuple-element.107), channel_id=1, source_target_pairs={{0,2},{1,3},{2,0},{3,1},{4,6},{5,7},{6,4},{7,5},{8,10},{9,11},{10,... | collective-permute-start | bytes 786440 | tf_op jit(solution)/shard_map/ppermute | solution.py:602
  41.1 17.0 %collective-permute-start.2 = (bf16[1024,128]{1,0:T(8,128)(2,1)}, bf16[1024,128]{1,0:T(8,128)(2,1)S(1)}, u32[]{:S(2)}, u32[]{:S(2)}) collective-permute-start(bf16[1024,128]{1,0:T(8,128)(2,1)} %get-tuple-element.104), channel_id=1, source_target_pairs={{0,6},{1,7},{2,4},{3,5},{4,2},{5,3},{6,0},{7,1},{8,14},{9,15},{10,... | collective-permute-start | bytes 786440 | tf_op jit(solution)/shard_map/ppermute | solution.py:602
  43.6 15.6 %copy-start.3 = (bf16[1024,128]{1,0:T(8,128)(2,1)S(1)}, bf16[1024,128]{1,0:T(8,128)(2,1)}, u32[]{:S(2)}) copy-start(bf16[1024,128]{1,0:T(8,128)(2,1)} %get-tuple-element.101.refs_0_) | copy-start | bytes 786436
  53.6 0.7 copy-start.1
  54.3 13.5 %collective-permute-start.15 = (bf16[3,128,256]{2,1,0:T(8,128)(2,1)S(1)}, bf16[3,128,256]{2,1,0:T(8,128)(2,1)S(1)}, u32[]{:S(2)}, u32[]{:S(2)}) collective-permute-start(bf16[3,128,256]{2,1,0:T(8,128)(2,1)S(1)} %get-tuple-element.135), channel_id=1, source_target_pairs={{0,6},{1,7},{2,4},{3,5},{4,2},{5,3},{6,0},{7,1},{8,14},{9,15},{10,... | collective-permute-start | bytes 589832 | tf_op jit(solution)/shard_map/ppermute | solution.py:602
  54.8 13.0 %collective-permute-start.16 = (bf16[3,128,256]{2,1,0:T(8,128)(2,1)S(1)}, bf16[3,128,256]{2,1,0:T(8,128)(2,1)S(1)}, u32[]{:S(2)}, u32[]{:S(2)}) collective-permute-start(bf16[3,128,256]{2,1,0:T(8,128)(2,1)S(1)} %get-tuple-element.136), channel_id=1, source_target_pairs={{0,2},{1,3},{2,0},{3,1},{4,6},{5,7},{6,4},{7,5},{8,10},{9,11},{10,... | collective-permute-start | bytes 589832 | tf_op jit(solution)/shard_map/ppermute | solution.py:602
  56.3 11.6 %collective-permute-start.17 = (bf16[3,128,256]{2,1,0:T(8,128)(2,1)S(1)}, bf16[3,128,256]{2,1,0:T(8,128)(2,1)S(1)}, u32[]{:S(2)}, u32[]{:S(2)}) collective-permute-start(bf16[3,128,256]{2,1,0:T(8,128)(2,1)S(1)} %get-tuple-element.137), channel_id=1, source_target_pairs={{0,4},{1,5},{2,6},{3,7},{4,0},{5,1},{6,2},{7,3},{8,12},{9,13},{10,... | collective-permute-start | bytes 589832 | tf_op jit(solution)/shard_map/ppermute | solution.py:602
  57.8 16.6 %collective-permute-start.22 = (bf16[3,128,256]{2,1,0:T(8,128)(2,1)S(1)}, bf16[3,128,256]{2,1,0:T(8,128)(2,1)S(1)}, u32[]{:S(2)}, u32[]{:S(2)}) collective-permute-start(bf16[3,128,256]{2,1,0:T(8,128)(2,1)S(1)} %get-tuple-element.144), channel_id=1, source_target_pairs={{0,3},{1,2},{2,1},{3,0},{4,7},{5,6},{6,5},{7,4},{8,11},{9,10},{10,... | collective-permute-start | bytes 589832 | tf_op jit(solution)/shard_map/ppermute | solution.py:602
  58.2 16.3 %collective-permute-start.23 = (bf16[3,128,256]{2,1,0:T(8,128)(2,1)S(1)}, bf16[3,128,256]{2,1,0:T(8,128)(2,1)S(1)}, u32[]{:S(2)}, u32[]{:S(2)}) collective-permute-start(bf16[3,128,256]{2,1,0:T(8,128)(2,1)S(1)} %get-tuple-element.145), channel_id=1, source_target_pairs={{0,5},{1,4},{2,7},{3,6},{4,1},{5,0},{6,3},{7,2},{8,13},{9,12},{10,... | collective-permute-start | bytes 589832 | tf_op jit(solution)/shard_map/ppermute | solution.py:602
  67.9 7.8 %copy-start.7 = (bf16[3,128,256]{2,1,0:T(8,128)(2,1)}, bf16[3,128,256]{2,1,0:T(8,128)(2,1)S(1)}, u32[]{:S(2)}) copy-start(bf16[3,128,256]{2,1,0:T(8,128)(2,1)S(1)} %collective-permute-done.15.refs_1_) | copy-start | bytes 589828
  67.9 7.7 %copy-start.8 = (bf16[3,128,256]{2,1,0:T(8,128)(2,1)}, bf16[3,128,256]{2,1,0:T(8,128)(2,1)S(1)}, u32[]{:S(2)}) copy-start(bf16[3,128,256]{2,1,0:T(8,128)(2,1)S(1)} %collective-permute-done.16.refs_2_) | copy-start | bytes 589828
  67.9 7.7 %copy-start.9 = (bf16[3,128,256]{2,1,0:T(8,128)(2,1)}, bf16[3,128,256]{2,1,0:T(8,128)(2,1)S(1)}, u32[]{:S(2)}) copy-start(bf16[3,128,256]{2,1,0:T(8,128)(2,1)S(1)} %collective-permute-done.17.refs_3_) | copy-start | bytes 589828
  67.9 4.7 %collective-permute-start.18 = (f32[16,256]{1,0:T(8,128)S(1)}, f32[16,256]{1,0:T(8,128)S(1)}, u32[]{:S(2)}, u32[]{:S(2)}) collective-permute-start(f32[16,256]{1,0:T(8,128)S(1)} %get-tuple-element.139), channel_id=1, source_target_pairs={{0,6},{1,7},{2,4},{3,5},{4,2},{5,3},{6,0},{7,1},{8,14},{9,15},{10,... | collective-permute-start | bytes 49160 | tf_op jit(solution)/shard_map/ppermute | solution.py:705
  70.1 3.7 %collective-permute-start.19 = (f32[16,256]{1,0:T(8,128)S(1)}, f32[16,256]{1,0:T(8,128)S(1)}, u32[]{:S(2)}, u32[]{:S(2)}) collective-permute-start(f32[16,256]{1,0:T(8,128)S(1)} %get-tuple-element.140), channel_id=1, source_target_pairs={{0,2},{1,3},{2,0},{3,1},{4,6},{5,7},{6,4},{7,5},{8,10},{9,11},{10,... | collective-permute-start | bytes 49160 | tf_op jit(solution)/shard_map/ppermute | solution.py:705
  70.6 3.7 %collective-permute-start.20 = (f32[16,256]{1,0:T(8,128)S(1)}, f32[16,256]{1,0:T(8,128)S(1)}, u32[]{:S(2)}, u32[]{:S(2)}) collective-permute-start(f32[16,256]{1,0:T(8,128)S(1)} %get-tuple-element.141), channel_id=1, source_target_pairs={{0,4},{1,5},{2,6},{3,7},{4,0},{5,1},{6,2},{7,3},{8,12},{9,13},{10,... | collective-permute-start | bytes 49160 | tf_op jit(solution)/shard_map/ppermute | solution.py:705
  74.3 1.3 %collective-permute-start.21 = (f32[16,768]{1,0:T(8,128)S(1)}, f32[16,768]{1,0:T(8,128)S(1)}, u32[]{:S(2)}, u32[]{:S(2)}) collective-permute-start(f32[16,768]{1,0:T(8,128)S(1)} %fold.1.own_ref), channel_id=1, source_target_pairs={{0,1},{1,0},{2,3},{3,2},{4,5},{5,4},{6,7},{7,6},{8,9},{9,8},{10,11... | collective-permute-start | bytes 147464 | tf_op jit(solution)/shard_map/ppermute | solution.py:705
  74.4 1.2 %copy-start.10 = (bf16[3,128,256]{2,1,0:T(8,128)(2,1)}, bf16[3,128,256]{2,1,0:T(8,128)(2,1)S(1)}, u32[]{:S(2)}) copy-start(bf16[3,128,256]{2,1,0:T(8,128)(2,1)S(1)} %collective-permute-done.22.refs_4_) | copy-start | bytes 589828
  74.4 1.2 %copy-start.11 = (bf16[3,128,256]{2,1,0:T(8,128)(2,1)}, bf16[3,128,256]{2,1,0:T(8,128)(2,1)S(1)}, u32[]{:S(2)}) copy-start(bf16[3,128,256]{2,1,0:T(8,128)(2,1)S(1)} %collective-permute-done.23.refs_5_) | copy-start | bytes 589828
  75.6 7.4 %copy-start = (bf16[128,5120]{1,0:T(8,128)(2,1)S(1)}, bf16[128,5120]{1,0:T(8,128)(2,1)}, u32[]{:S(2)}) copy-start(bf16[128,5120]{1,0:T(8,128)(2,1)} %hidden_ref.1) | copy-start | bytes 3932164
  75.7 32.9 %all-to-all-start = ((bf16[8,3,128,256]{3,2,1,0:T(8,128)(2,1)}), bf16[8,3,128,256]{3,2,1,0:T(8,128)(2,1)}, u32[]{:S(2)}, u32[]{:S(2)}) async-start(bf16[8,3,128,256]{3,2,1,0:T(8,128)(2,1)} %get-tuple-element.172), calls=%async_computation | async-start | bytes 3145728 | tf_op jit(solution)/shard_map/all_to_all | solution.py:600
  80.1 28.4 %collective-permute-start.30 = (bf16[3,128,256]{2,1,0:T(8,128)(2,1)S(1)}, bf16[3,128,256]{2,1,0:T(8,128)(2,1)S(1)}, u32[]{:S(2)}, u32[]{:S(2)}) collective-permute-start(bf16[3,128,256]{2,1,0:T(8,128)(2,1)S(1)} %get-tuple-element.167), channel_id=1, source_target_pairs={{0,7},{1,6},{2,5},{3,4},{4,3},{5,2},{6,1},{7,0},{8,15},{9,14},{10,... | collective-permute-start | bytes 589832 | tf_op jit(solution)/shard_map/ppermute | solution.py:602
  82.7 25.8 %collective-permute-start.31 = (bf16[3,128,256]{2,1,0:T(8,128)(2,1)S(1)}, bf16[3,128,256]{2,1,0:T(8,128)(2,1)S(1)}, u32[]{:S(2)}, u32[]{:S(2)}) collective-permute-start(bf16[3,128,256]{2,1,0:T(8,128)(2,1)S(1)} %get-tuple-element.168), channel_id=1, source_target_pairs={{0,1},{1,0},{2,3},{3,2},{4,5},{5,4},{6,7},{7,6},{8,9},{9,8},{10,11... | collective-permute-start | bytes 589832 | tf_op jit(solution)/shard_map/ppermute | solution.py:602
  83.9 4.5 %collective-permute-start.24 = (f32[8,2304]{1,0:T(8,128)S(1)}, f32[8,2304]{1,0:T(8,128)S(1)}, u32[]{:S(2)}, u32[]{:S(2)}) collective-permute-start(f32[8,2304]{1,0:T(8,128)S(1)} %get-tuple-element.151), channel_id=1, source_target_pairs={{0,8},{8,0},{16,24},{24,16},{1,9},{9,1},{17,25},{25,17},{2,10},{10... | collective-permute-start | bytes 221192 | tf_op jit(solution)/shard_map/ppermute | solution.py:602
  85.8 8.9 %collective-permute-start.25 = (f32[8,2304]{1,0:T(8,128)S(1)}, f32[8,2304]{1,0:T(8,128)S(1)}, u32[]{:S(2)}, u32[]{:S(2)}) collective-permute-start(f32[8,2304]{1,0:T(8,128)S(1)} %get-tuple-element.152), channel_id=1, source_target_pairs={{0,16},{8,24},{16,0},{24,8},{1,17},{9,25},{17,1},{25,9},{2,18},{10... | collective-permute-start | bytes 221192 | tf_op jit(solution)/shard_map/ppermute | solution.py:602
  88.4 6.3 %collective-permute-start.26 = (f32[8,2304]{1,0:T(8,128)S(1)}, f32[8,2304]{1,0:T(8,128)S(1)}, u32[]{:S(2)}, u32[]{:S(2)}) collective-permute-start(f32[8,2304]{1,0:T(8,128)S(1)} %get-tuple-element.153), channel_id=1, source_target_pairs={{0,24},{8,16},{16,8},{24,0},{1,25},{9,17},{17,9},{25,1},{2,26},{10... | collective-permute-start | bytes 221192 | tf_op jit(solution)/shard_map/ppermute | solution.py:602
  94.7 11.4 %collective-permute-start.29 = (f32[8,2304]{1,0:T(8,128)S(1)}, f32[8,2304]{1,0:T(8,128)S(1)}, u32[]{:S(2)}, u32[]{:S(2)}) collective-permute-start(f32[8,2304]{1,0:T(8,128)S(1)} %sum_packs.1.refs_0_), channel_id=1, source_target_pairs={{0,4},{1,5},{2,6},{3,7},{4,0},{5,1},{6,2},{7,3},{8,12},{9,13},{10,... | collective-permute-start | bytes 221192 | tf_op jit(solution)/shard_map/ppermute | solution.py:705
  95.3 11.2 %collective-permute-start.28 = (f32[8,2304]{1,0:T(8,128)S(1)}, f32[8,2304]{1,0:T(8,128)S(1)}, u32[]{:S(2)}, u32[]{:S(2)}) collective-permute-start(f32[8,2304]{1,0:T(8,128)S(1)} %sum_packs.1.refs_0_), channel_id=1, source_target_pairs={{0,2},{1,3},{2,0},{3,1},{4,6},{5,7},{6,4},{7,5},{8,10},{9,11},{10,... | collective-permute-start | bytes 221192 | tf_op jit(solution)/shard_map/ppermute | solution.py:705
  95.5 12.9 %collective-permute-start.27 = (f32[8,2304]{1,0:T(8,128)S(1)}, f32[8,2304]{1,0:T(8,128)S(1)}, u32[]{:S(2)}, u32[]{:S(2)}) collective-permute-start(f32[8,2304]{1,0:T(8,128)S(1)} %sum_packs.1.refs_0_), channel_id=1, source_target_pairs={{0,6},{1,7},{2,4},{3,5},{4,2},{5,3},{6,0},{7,1},{8,14},{9,15},{10,... | collective-permute-start | bytes 221192 | tf_op jit(solution)/shard_map/ppermute | solution.py:705
  108.5 0.7 copy-start.5
  108.5 0.7 copy-start.6
  108.5 3.3 %collective-permute-start.32 = (f32[8,2304]{1,0:T(8,128)S(1)}, f32[8,2304]{1,0:T(8,128)S(1)}, u32[]{:S(2)}, u32[]{:S(2)}) collective-permute-start(f32[8,2304]{1,0:T(8,128)S(1)} %sum_chips.1.own_ref), channel_id=1, source_target_pairs={{0,1},{1,0},{2,3},{3,2},{4,5},{5,4},{6,7},{7,6},{8,9},{9,8},{10,11... | collective-permute-start | bytes 221192 | tf_op jit(solution)/shard_map/ppermute | solution.py:705
